TPU v7x, 32 devices: a whole 2x2x4 slice. The times are simulated.
32 devices in a mesh: prompt: 4 (over y, x), vocab: 8 (over z, core).
Axes of the slice: x: 2, y: 2, z: 4, core: 2. Of those that a mesh axis runs over, the one named last changes fastest.
Arguments:
- hidden: bfloat16 [512, 8192], P('prompt')
- head: bfloat16 [8192, 65536], P('prompt', 'vocab')
- gain: float32 [8192], replicated, may hold values from 0.25 to 1.75
- refusal_ids: int32 [512, 16], P('prompt'), may hold values from 0 to 65535, as said below
- refusal_count: int32 [512], P('prompt'), may hold values from 1 to 16
- loss_scale: float32 [512], P('prompt'), may hold values from 8 to 32
Outputs:
- grad_hidden: float32 [512, 8192], P('prompt', 'vocab')
- log_refusal: float32 [512], P('prompt')
Inputs may be any that keep to these rules, and one draw needn't show every extreme that they name: `refusal_ids`: the first refusal_count entries of a prompt's list are distinct ids below 65536; later entries are ignored.
All inputs are finite; a program needn't handle non-finite values.
Results may differ from a plain program's by a relative error of at most 0.0027.
The roundings to bfloat16 on the way count: a program that leaves them out, or rounds other values in their place, can miss the bound.
Values may be sent and summed in bfloat16 or wider, within the bound.
No kernel may reach another device: no remote copies, remote signals or barrier semaphores. Data moves between devices by JAX's collectives and lax.ppermute only.
A program may use at most 256 MiB of HBM per device.

v0:
```python
import jax
import jax.numpy as jnp
from jax import lax
from jax.sharding import PartitionSpec as P

epsilon = 1e-05
lowest = -1e30


def shards(hidden, head, gain, refusal_ids, refusal_count, loss_scale):
    row_count, model_width = hidden.shape
    vocab_local = head.shape[1]
    list_length = refusal_ids.shape[1]
    hidden_f = hidden.astype(jnp.float32)
    inverse_rms = lax.rsqrt(jnp.mean(hidden_f * hidden_f, axis=1, keepdims=True) + epsilon)
    normed = (hidden_f * inverse_rms * gain).astype(jnp.bfloat16)
    logits = jnp.dot(
        normed,
        lax.all_gather(head, "prompt", axis=0, tiled=True),
        preferred_element_type=jnp.float32,
    )
    vocab_start = lax.axis_index("vocab") * vocab_local
    shifted_ids = refusal_ids - vocab_start
    in_list = jnp.arange(list_length)[None, :] < refusal_count[:, None]
    is_local = in_list & (shifted_ids >= 0) & (shifted_ids < vocab_local)
    safe_ids = jnp.clip(shifted_ids, 0, vocab_local - 1)
    picked = jnp.take_along_axis(logits, safe_ids, axis=1)
    peak_all = jnp.max(logits, axis=1)
    peak_ref = jnp.max(jnp.where(is_local, picked, lowest), axis=1)
    peak_all, peak_ref = lax.pmax((peak_all, peak_ref), "vocab")
    sum_all = jnp.sum(jnp.exp(logits - peak_all[:, None]), axis=1)
    sum_ref = jnp.sum(jnp.exp(jnp.where(is_local, picked - peak_ref[:, None], lowest)), axis=1)
    sum_all, sum_ref = lax.psum((sum_all, sum_ref), "vocab")
    lse_all = peak_all + jnp.log(sum_all)
    lse_ref = peak_ref + jnp.log(sum_ref)
    log_refusal = lse_ref - lse_all
    member = jnp.any(
        (safe_ids[:, :, None] == jnp.arange(vocab_local)[None, None, :]) & is_local[:, :, None],
        axis=1,
    )
    grad_logits = loss_scale[:, None] * (
        jnp.exp(jnp.where(member, logits - lse_ref[:, None], lowest))
        - jnp.exp(logits - lse_all[:, None])
    )
    grad_b = grad_logits.astype(jnp.bfloat16)
    slice_width = model_width // lax.axis_size("vocab")
    col_start = lax.axis_index("vocab") * slice_width
    grad_full = lax.dot_general(
        grad_b,
        lax.all_gather(head, "prompt", axis=0, tiled=True),
        (((1,), (1,)), ((), ())),
        preferred_element_type=jnp.float32,
    )
    grad_cols = lax.psum_scatter(grad_full, "vocab", scatter_dimension=1, tiled=True)
    normed_cols = lax.dynamic_slice_in_dim(normed, col_start, slice_width, 1).astype(jnp.float32)
    row_term = lax.psum(jnp.sum(grad_cols * normed_cols, axis=1), "vocab")
    hidden_cols = lax.dynamic_slice_in_dim(hidden_f, col_start, slice_width, 1)
    gain_cols = lax.dynamic_slice_in_dim(gain, col_start, slice_width, 0)
    grad_hidden = (
        inverse_rms * gain_cols * grad_cols
        - hidden_cols * (inverse_rms * inverse_rms / model_width) * row_term[:, None]
    )
    return (grad_hidden, log_refusal)


def solution(mesh):
    return jax.shard_map(
        shards,
        mesh=mesh,
        in_specs=(
            P("prompt", None),
            P("prompt", "vocab"),
            P(),
            P("prompt", None),
            P("prompt"),
            P("prompt"),
        ),
        out_specs=(P("prompt", "vocab"), P("prompt")),
        check_vma=False,
    )
```

profile of v0, /device:TPU:2, one launch (start us, length us, event | category | flops | bytes accessed | tf_op | source)
XLA Modules:
  0.0 1453.7 jit_solution(495029840252945237)
XLA Ops:
  7.2 0.0 copy-start.3
  7.2 0.0 copy-start
  7.2 0.0 copy-start.2
  7.2 0.0 all-gather.2.cloned.1.call-start
  7.2 0.7 all-gather.2.cloned.1.call-update
  7.9 0.0 reduce-scatter.2.cloned.1.call-start
  8.0 0.0 copy-done.3
  8.0 0.1 copy.11
  8.1 0.1 reshape.39
  8.2 0.6 copy-done
  8.8 0.5 multiply_reduce_fusion
  9.3 0.0 copy-done.2
  9.3 2.0 multiply_convert_fusion.1
  11.3 1135.8 %all-gather.2.cloned.1.call-done = bf16[8192,8192]{1,0:T(8,128)(2,1)} async-done(((bf16[2048,8192]{1,0:T(8,128)(2,1)}), bf16[8192,8192]{1,0:T(8,128)(2,1)}) %all-gather.2.cloned.1.call-update) | async-done | bytes 134217744 | tf_op jit(solution)/shard_map/all_gather | solution.py:19
  1147.1 45.8 %fusion.12 = (f32[128]{0:T(128)S(1)}, f32[128,8192]{1,0:T(8,128)}) fusion(bf16[128,8192]{1,0:T(8,128)(2,1)} %multiply_convert_fusion.1, bf16[8192,8192]{1,0:T(8,128)(2,1)} %all-gather.2.cloned.1.call-done), kind=kOutput, calls=%fused_computation.30 | convolution fusion | flops 17180917760 | bytes 140509696 | tf_op jit(solution)/shard_map/dot_general | solution.py:17
  1192.9 0.0 copy-start.4
  1192.9 82.0 %gather_fusion = f32[2048]{0:T(1024)S(1)} fusion(f32[128,8192]{1,0:T(8,128)} %get-tuple-element.16, s32[2048]{0:T(1024)S(1)} %reshape.39), kind=kCustom, calls=%fused_computation | custom fusion | bytes 32768 | tf_op jit(solution)/shard_map/jit(take_along_axis)/gather | solution.py:27
  1274.9 0.0 copy-start.1
  1274.9 0.1 reshape.42
  1274.9 0.0 copy-done.4
  1275.0 0.2 select_reduce_fusion
  1275.1 18.1 %fusion.1 = pred[128,8192]{1,0:T(8,128)(4,1)S(1)} fusion(s32[128,16]{1,0:T(8,128)S(1)} %get-tuple-element.12, pred[128,16]{1,0:T(8,128)(4,1)S(1)} %get-tuple-element.10), kind=kLoop, calls=%fused_computation.3 | loop fusion | flops 49283072 | bytes 1058816 | tf_op jit(solution)/shard_map/reduce_or | solution.py:37
  1293.2 15.8 %all-reduce.1 = (f32[128]{0:T(128)S(1)}, f32[128]{0:T(128)S(1)}) all-reduce(f32[128]{0:T(128)S(1)} %get-tuple-element.15, f32[128]{0:T(128)S(1)} %get-tuple-element.9), channel_id=1, replica_groups=mesh['prompt'=4,'vocab'=8] {'vocab'}, use_global_device_ids=true, to_apply=%region_7.8 | all-reduce | flops 256 | bytes 2048 | tf_op jit(solution)/shard_map/pmax | solution.py:30
  1309.1 0.2 exponential_reduce_fusion.1
  1309.3 2.9 exponential_reduce_fusion
  1312.2 13.6 all-reduce
  1325.8 0.5 fusion.10
  1326.3 0.0 copy-done.1
  1326.3 55.6 %fusion.2 = f32[128,8192]{1,0:T(8,128)} fusion(bf16[8192,8192]{1,0:T(8,128)(2,1)} %all-gather.2.cloned.1.call-done, f32[128,8192]{1,0:T(8,128)} %get-tuple-element.16, pred[128,8192]{1,0:T(8,128)(4,1)S(1)} %fusion.1, f32[128]{0:T(128)S(1)} %get-tuple-element.8, f32[128]{0:T(128)S(1)} %get-tuple-element.7, f32[128]{0:T(128)S(1)} %copy-done.1), kind=kOutput, calls=%fused_computation.8 | convolution fusion | flops 17186160640 | bytes 143656448 | tf_op jit(solution)/shard_map/dot_general | solution.py:48
  1381.8 0.0 reduce-scatter.2.cloned.1.call-update
  1381.9 2.4 convert_element_type.12
  1384.2 45.5 %reduce-scatter.2.cloned.1.call-done = f32[128,1024]{1,0:T(8,128)} async-done(((f32[128,8192]{1,0:T(8,128)}), f32[128,1024]{1,0:T(8,128)}) %reduce-scatter.2.cloned.1.call-update) | async-done | bytes 524304 | tf_op jit(solution)/shard_map/reduce_scatter | solution.py:54
  1429.7 1.2 multiply_reduce_fusion.1
  1431.0 13.8 psum.23
  1444.7 2.2 multiply_subtract_fusion
  (3 shorter events, 0.0 us)
Async XLA Ops:
  7.2 0.8 copy-start.3
  7.2 1.6 copy-start
  7.2 2.1 copy-start.2
  7.2 1139.9 %all-gather.2.cloned.1.call-start = ((), (), s32[]{:S(2)}) async-start(), calls=%async_computation.1 | async-start | bytes 167772160 | tf_op jit(solution)/shard_map/all_gather | solution.py:19
  7.9 1421.8 %reduce-scatter.2.cloned.1.call-start = ((), (), s32[]{:S(2)}) async-start(), calls=%async_computation.2 | async-start | bytes 4718592 | tf_op jit(solution)/shard_map/reduce_scatter | solution.py:54
  1192.9 82.1 %copy-start.4 = (s32[128]{0:T(128)S(1)}, s32[128]{0:T(128)}, u32[]{:S(2)}) copy-start(s32[128]{0:T(128)} %param.10) | copy-start | bytes 1540
  1274.9 51.4 %copy-start.1 = (f32[128]{0:T(128)S(1)}, f32[128]{0:T(128)}, u32[]{:S(2)}) copy-start(f32[128]{0:T(128)} %param.11) | copy-start | bytes 1540
Sparse Core Ops, SparseCore 0:
  9.9 1137.1 all-gather.1
  1382.0 47.6 reduce-scatter.1
where the time goes:
time: 1460 us; the launch traced here: 1450 us
  waiting for transfers between devices  1180 us (81%)
  matrix products  101 us (7%)
  local copies, waits for them, and re-layouts  82.8 us (6%)
  blocking collectives  43.2 us (3%)
  other arithmetic  30.2 us (2%)
    all_gather x1, waiting for transfers between devices, shards(): lax.all_gather(head, 'prompt', axis=0, tiled=True)  1140 us
    gather x3, local copies, waits for them, and re-layouts, shards(): picked = jnp.take_along_axis(logits, safe_ids, axis=1)  82.1 us
    dot_general x1, matrix products, shards(): lax.dot_general(grad_b, lax.all_gather(head, 'prompt', axis=0, tiled=True...  55.6 us
    dot_general x1, matrix products, shards(): jnp.dot(normed, lax.all_gather(head, 'prompt', axis=0, tiled=True), prefe...  45.8 us
    reduce_scatter x1, waiting for transfers between devices, shards(): lax.psum_scatter(grad_full, 'vocab', scatter_dimension=1, tiled=True)  45.5 us
  transfers between devices with their start and end apart: 2, of which 2 were waited for; matrix products, arithmetic and copies ran while one was open for 0% of the time, Pallas kernels for 0%

commit v1 on v0

v1 whole, which is shorter than its diff:
```python
import jax
import jax.numpy as jnp
from jax import lax
from jax.experimental import pallas as pl
from jax.experimental.pallas import tpu as pltpu
from jax.sharding import PartitionSpec as P

epsilon = 1e-05
lowest = -1e30


def members(ids, start, width):
    rows = ids.shape[0]
    column = lax.broadcasted_iota(jnp.int32, (rows, width), 1) + start
    found = column == ids[:, 0:1]
    for k in range(1, ids.shape[1]):
        found = found | (column == ids[:, k : k + 1])
    return found


def stats_kernel(chunk, logits_ref, ids_ref, out_ref):
    rows, width = logits_ref.shape
    ids = ids_ref[...]
    peak_all = jnp.full((rows, 1), lowest, jnp.float32)
    peak_ref = jnp.full((rows, 1), lowest, jnp.float32)
    for start in range(0, width, chunk):
        piece = logits_ref[:, start : start + chunk]
        found = members(ids, start, chunk)
        peak_all = jnp.maximum(peak_all, jnp.max(piece, axis=1, keepdims=True))
        peak_ref = jnp.maximum(
            peak_ref, jnp.max(jnp.where(found, piece, lowest), axis=1, keepdims=True)
        )
    sum_all = jnp.zeros((rows, 1), jnp.float32)
    sum_ref = jnp.zeros((rows, 1), jnp.float32)
    for start in range(0, width, chunk):
        piece = logits_ref[:, start : start + chunk]
        found = members(ids, start, chunk)
        sum_all = sum_all + jnp.sum(jnp.exp(piece - peak_all), axis=1, keepdims=True)
        sum_ref = sum_ref + jnp.sum(
            jnp.exp(jnp.where(found, piece - peak_ref, lowest)), axis=1, keepdims=True
        )
    lane = lax.broadcasted_iota(jnp.int32, out_ref.shape, 1)
    out_ref[...] = jnp.where(
        lane == 0, peak_all, jnp.where(lane == 1, peak_ref, jnp.where(lane == 2, sum_all, sum_ref))
    )


def row_stats(logits, ids):
    rows, width = logits.shape
    block = min(rows, 16)
    return pl.pallas_call(
        lambda *refs: stats_kernel(min(width, 1024), *refs),
        grid=(rows // block,),
        in_specs=[
            pl.BlockSpec((block, width), lambda i: (i, 0)),
            pl.BlockSpec((block, ids.shape[1]), lambda i: (i, 0)),
        ],
        out_specs=pl.BlockSpec((block, 128), lambda i: (i, 0)),
        out_shape=jax.ShapeDtypeStruct((rows, 128), jnp.float32),
        name="row_stats",
    )(logits, ids)


def grad_kernel(chunk, logits_ref, ids_ref, scalars_ref, out_ref, term_ref):
    rows, width = logits_ref.shape
    ids = ids_ref[...]
    lse_ref = scalars_ref[:, 0:1]
    lse_all = scalars_ref[:, 1:2]
    scale = scalars_ref[:, 2:3]
    term = jnp.zeros((rows, 1), jnp.float32)
    for start in range(0, width, chunk):
        piece = logits_ref[:, start : start + chunk]
        found = members(ids, start, chunk)
        grad = scale * (
            jnp.exp(jnp.where(found, piece - lse_ref, lowest)) - jnp.exp(piece - lse_all)
        )
        grad = grad.astype(jnp.bfloat16)
        out_ref[:, start : start + chunk] = grad
        term = term + jnp.sum(grad.astype(jnp.float32) * piece, axis=1, keepdims=True)
    term_ref[...] = jnp.broadcast_to(term, term_ref.shape)


def logit_grads(logits, ids, scalars):
    rows, width = logits.shape
    block = min(rows, 16)
    return pl.pallas_call(
        lambda *refs: grad_kernel(min(width, 1024), *refs),
        grid=(rows // block,),
        in_specs=[
            pl.BlockSpec((block, width), lambda i: (i, 0)),
            pl.BlockSpec((block, ids.shape[1]), lambda i: (i, 0)),
            pl.BlockSpec((block, scalars.shape[1]), lambda i: (i, 0)),
        ],
        out_specs=[
            pl.BlockSpec((block, width), lambda i: (i, 0)),
            pl.BlockSpec((block, 128), lambda i: (i, 0)),
        ],
        out_shape=[
            jax.ShapeDtypeStruct((rows, width), jnp.bfloat16),
            jax.ShapeDtypeStruct((rows, 128), jnp.float32),
        ],
        name="logit_grads",
    )(logits, ids, scalars)


def shards(hidden, head, gain, refusal_ids, refusal_count, loss_scale):
    row_count, model_width = hidden.shape
    vocab_local = head.shape[1]
    list_length = refusal_ids.shape[1]
    prompt_size = lax.axis_size("prompt")
    vocab_size = lax.axis_size("vocab")
    group = vocab_size // prompt_size

    hidden_f = hidden.astype(jnp.float32)
    inverse_rms = lax.rsqrt(jnp.mean(hidden_f * hidden_f, axis=1, keepdims=True) + epsilon)
    normed = (hidden_f * inverse_rms * gain).astype(jnp.bfloat16)
    normed_all = lax.all_to_all(normed, "prompt", split_axis=1, concat_axis=0, tiled=True)
    partial = jnp.dot(normed_all, head, preferred_element_type=jnp.float32)
    logits = lax.psum_scatter(partial, "prompt", scatter_dimension=0, tiled=True)

    vocab_start = lax.axis_index("vocab") * vocab_local
    in_list = jnp.arange(list_length)[None, :] < refusal_count[:, None]
    ids = jnp.where(in_list, refusal_ids - vocab_start, -1)

    stats = row_stats(logits, ids)[:, :4].T
    stats = lax.all_gather(stats, "vocab", axis=0)
    peaks = jnp.max(stats[:, :2], axis=0)
    sums = jnp.sum(stats[:, 2:] * jnp.exp(stats[:, :2] - peaks[None]), axis=0)
    lse_all, lse_ref = peaks + jnp.log(sums)
    log_refusal = lse_ref - lse_all

    scalars = jnp.stack([lse_ref, lse_all, loss_scale, loss_scale], axis=1)
    grad_b, term = logit_grads(logits, ids, scalars)
    row_term = lax.psum(term[:, 0], "vocab")

    grad_all = lax.all_gather(grad_b, "prompt", axis=0, tiled=True)
    grad_part = lax.dot_general(
        grad_all, head, (((1,), (1,)), ((), ())), preferred_element_type=jnp.float32
    )
    grad_rows = lax.psum_scatter(grad_part, "vocab", scatter_dimension=0, tiled=True)
    moves = []
    for p in range(prompt_size):
        for r in range(prompt_size):
            for i in range(group):
                moves.append((p * vocab_size + r * group + i, r * vocab_size + p * group + i))
    grad_rows = lax.ppermute(grad_rows, ("prompt", "vocab"), moves)
    groups = [[p * group + i for i in range(group)] for p in range(prompt_size)]
    grad_cols = lax.all_to_all(
        grad_rows, "vocab", split_axis=1, concat_axis=0, axis_index_groups=groups, tiled=True
    )

    slice_width = model_width // vocab_size
    col_start = lax.axis_index("vocab") * slice_width
    hidden_cols = lax.dynamic_slice_in_dim(hidden, col_start, slice_width, 1).astype(jnp.float32)
    gain_cols = lax.dynamic_slice_in_dim(gain, col_start, slice_width, 0)
    grad_hidden = (
        inverse_rms * gain_cols * grad_cols
        - hidden_cols * (inverse_rms * inverse_rms / model_width) * row_term[:, None]
    )
    return (grad_hidden, log_refusal)


def solution(mesh):
    return jax.shard_map(
        shards,
        mesh=mesh,
        in_specs=(
            P("prompt", None),
            P("prompt", "vocab"),
            P(),
            P("prompt", None),
            P("prompt"),
            P("prompt"),
        ),
        out_specs=(P("prompt", "vocab"), P("prompt")),
        check_vma=False,
    )
```

time: 1460 us -> 489 us (0.33)
  waiting for transfers between devices: 1180 us -> 300 us
  local copies, waits for them, and re-layouts: 82.8 us -> 8.64 us
  matrix products: 101 us -> 52.1 us
  blocking collectives: 43.2 us -> 69.7 us
  Pallas kernels: 0 us -> 25.7 us
  other arithmetic: 30.2 us -> 8.09 us
    all_gather x1, waiting for transfers between devices: 1140 us -> 86.5 us  [shards(): grad_all = lax.all_gather(grad_b, 'prompt', axis=0, tiled=True)]
    reduce_scatter x1 -> x2, waiting for transfers between devices: 45.5 us -> 203 us  [the longest x1 153 us: shards(): lax.psum_scatter(partial, 'prompt', scatter_dimension=0, tiled=True)]
    gather x3 -> x0, local copies, waits for them, and re-layouts: 82.1 us -> none  [shards(): picked = jnp.take_along_axis(logits, safe_ids, axis=1)]
    dot_general x2, matrix products: 101 us -> 52.1 us  [the longest x1 27.2 us: shards(): partial = jnp.dot(normed_all, head, preferred_element_type=jnp.float32)]
    all_to_all x0 -> x2, blocking collectives: none -> 32.5 us  [the longest x1 28.3 us: shards(): lax.all_to_all(normed, 'prompt', split_axis=1, concat_axis=0, tiled=True)]
    pallas_call x0 -> x2, Pallas kernels: none -> 25.7 us  [the longest x1 13.3 us: row_stats(): pl.pallas_call(lambda *refs: stats_kernel(min(width, 1024), *refs), grid=...]
    reduce_or x1 -> x0, other arithmetic: 18.1 us -> none  [shards(): jnp.any((safe_ids[:, :, None] == jnp.arange(vocab_local)[None, None, :])...]
    pmax x1 -> x0, blocking collectives: 15.8 us -> none  [shards(): peak_all, peak_ref = lax.pmax((peak_all, peak_ref), 'vocab')]
  transfers between devices with their start and end apart: 2 -> 4, of which waited for: 2 -> 4; matrix products, arithmetic and copies ran while one was open for 0% -> 0% of each run, Pallas kernels for 0% -> 0%
where the time goes in v1:
time: 489 us; the launch traced here: 480 us
  waiting for transfers between devices  300 us (61%)
  blocking collectives  69.7 us (14%)
  matrix products  52.1 us (11%)
  Pallas kernels  25.7 us (5%)
  between operations  13.8 us (3%)
  local copies, waits for them, and re-layouts  8.64 us (2%)
  other arithmetic  8.09 us (2%)
    reduce_scatter x1, waiting for transfers between devices, shards(): lax.psum_scatter(partial, 'prompt', scatter_dimension=0, tiled=True)  153 us
    all_gather x1, waiting for transfers between devices, shards(): grad_all = lax.all_gather(grad_b, 'prompt', axis=0, tiled=True)  86.5 us
    reduce_scatter x1, waiting for transfers between devices, shards(): lax.psum_scatter(grad_part, 'vocab', scatter_dimension=0, tiled=True)  50.2 us
    all_to_all x1, blocking collectives, shards(): lax.all_to_all(normed, 'prompt', split_axis=1, concat_axis=0, tiled=True)  28.3 us
    dot_general x1, matrix products, shards(): partial = jnp.dot(normed_all, head, preferred_element_type=jnp.float32)  27.2 us
    dot_general x1, matrix products, shards(): lax.dot_general(grad_all, head, (((1,), (1,)), ((), ())), preferred_eleme...  24.9 us
    psum x1, blocking collectives, shards(): row_term = lax.psum(term[:, 0], 'vocab')  24.3 us
    pallas_call x1, Pallas kernels, row_stats(): pl.pallas_call(lambda *refs: stats_kernel(min(width, 1024), *refs), grid=...  13.3 us
  transfers between devices with their start and end apart: 4, of which 4 were waited for; matrix products, arithmetic and copies ran while one was open for 0% of the time, Pallas kernels for 0%

profile of v1, /device:TPU:2, one launch (start us, length us, event | category | flops | bytes accessed | tf_op | source)
XLA Modules:
  0.0 480.3 jit_solution(1616257556543876728)
XLA Ops:
  7.2 0.0 copy-start.1
  7.2 0.0 reduce-scatter.3.cloned.1.call-start
  7.2 3.2 copy.54
  10.5 1.1 fusion
  11.6 0.0 copy-done.1
  11.6 3.5 fusion.2
  15.1 28.3 %all_to_all.38 = bf16[128,4,2048]{0,2,1:T(8,128)(2,1)S(1)} all-to-all(bf16[128,4,2048]{0,2,1:T(8,128)(2,1)S(1)} %bitcast.24), channel_id=1, replica_groups=mesh['prompt'=4,'vocab'=8] {'prompt'}, dimensions={1} | all-to-all | bytes 4194304 | tf_op jit(solution)/shard_map/all_to_all | solution.py:117
  43.4 2.7 copy.55
  46.1 27.2 %fusion.6 = f32[512,8192]{1,0:T(8,128)} fusion(bf16[512,2048]{1,0:T(8,128)(2,1)} %bitcast.26, bf16[2048,8192]{1,0:T(8,128)(2,1)} %param.7), kind=kOutput, calls=%fused_computation.23 | convolution fusion | flops 17179869184 | bytes 52428800 | tf_op jit(solution)/shard_map/dot_general | solution.py:118
  73.3 0.0 copy-start.2
  73.3 0.0 copy-start.3
  73.3 0.0 reduce-scatter.3.cloned.1.call-update
  73.3 0.0 copy-start.4
  73.3 0.0 all-gather.4.cloned.1.call-start
  73.4 0.6 copy-done.2
  74.0 0.1 copy.56
  74.1 0.0 copy-done.3
  74.1 0.7 fusion.4.refs_1_
  74.8 152.7 %reduce-scatter.3.cloned.1.call-done.refs_0_ = f32[128,8192]{1,0:T(8,128)} async-done(((f32[512,8192]{1,0:T(8,128)}), f32[128,8192]{1,0:T(8,128)}) %reduce-scatter.3.cloned.1.call-update) | async-done | bytes 4194320 | tf_op jit(solution)/shard_map/reduce_scatter | solution.py:119
  227.4 13.3 %row_stats.1 = f32[128,128]{1,0:T(8,128)} custom-call(f32[128,8192]{1,0:T(8,128)} %reduce-scatter.3.cloned.1.call-done.refs_0_, s32[128,16]{1,0:T(8,128)} %fusion.4.refs_1_), custom_call_target="tpu_custom_call" | custom-call | tf_op jit(solution)/shard_map/row_stats/pallas_call | solution.py:51
  240.8 0.8 slice_bitcast_fusion
  241.6 0.1 copy.57
  241.7 13.0 %all-gather.1 = f32[8,4,128]{2,1,0:T(4,128)S(1)} all-gather(f32[1,4,128]{2,1,0:T(4,128)S(1)} %copy.57), channel_id=2, replica_groups=mesh['prompt'=4,'vocab'=8] {'vocab'}, dimensions={0}, use_global_device_ids=true | all-gather | bytes 18432 | tf_op jit(solution)/shard_map/all_gather | solution.py:126
  254.7 0.1 copy.63
  254.8 0.1 copy.64
  254.9 0.7 subtract_reduce_fusion
  255.6 0.0 copy-done.4
  255.6 0.7 copy.61.refs_2_
  256.4 12.4 %logit_grads.1 = (bf16[128,8192]{1,0:T(8,128)(2,1)}, f32[128,128]{1,0:T(8,128)}) custom-call(f32[128,8192]{1,0:T(8,128)} %reduce-scatter.3.cloned.1.call-done.refs_0_, s32[128,16]{1,0:T(8,128)} %fusion.4.refs_1_, f32[128,4]{1,0:T(8,128)} %copy.61.refs_2_), custom_call_target="tpu_custom_call" | custom-call | tf_op jit(solution)/shard_map/logit_grads/pallas_call | solution.py:86
  268.8 0.0 all-gather.4.cloned.1.call-update
  268.8 0.0 reduce-scatter.5.cloned.1.call-start
  268.8 86.5 %all-gather.4.cloned.1.call-done = bf16[512,8192]{1,0:T(8,128)(2,1)} async-done(((bf16[128,8192]{1,0:T(8,128)(2,1)}), bf16[512,8192]{1,0:T(8,128)(2,1)}) %all-gather.4.cloned.1.call-update) | async-done | bytes 8388624 | tf_op jit(solution)/shard_map/all_gather | solution.py:136
  355.3 24.9 %fusion.7 = f32[512,2048]{1,0:T(8,128)} fusion(bf16[512,8192]{1,0:T(8,128)(2,1)} %all-gather.4.cloned.1.call-done, bf16[2048,8192]{1,0:T(8,128)(2,1)} %param.7), kind=kOutput, calls=%fused_computation.24 | convolution fusion | flops 17179869184 | bytes 46137344 | tf_op jit(solution)/shard_map/dot_general | solution.py:137
  380.3 0.0 copy-start
  380.3 0.0 reduce-scatter.5.cloned.1.call-update
  380.3 50.2 %reduce-scatter.5.cloned.1.call-done = f32[64,2048]{1,0:T(8,128)} async-done(((f32[512,2048]{1,0:T(8,128)}), f32[64,2048]{1,0:T(8,128)}) %reduce-scatter.5.cloned.1.call-update) | async-done | bytes 524304 | tf_op jit(solution)/shard_map/reduce_scatter | solution.py:140
  430.5 1.9 collective-permute-start
  432.4 0.0 copy-done
  432.4 0.1 slice_reduce_fusion
  432.5 24.3 %psum.7 = f32[128]{0:T(128)S(1)} all-reduce(f32[128]{0:T(128)S(1)} %slice_reduce_fusion), channel_id=1, replica_groups=mesh['prompt'=4,'vocab'=8] {'vocab'}, use_global_device_ids=true, to_apply=%region_5.6 | all-reduce | flops 128 | bytes 1024 | tf_op jit(solution)/shard_map/psum | solution.py:134
  456.8 10.8 %collective-permute-done = f32[64,2048]{1,0:T(8,128)S(1)} collective-permute-done((f32[64,2048]{1,0:T(8,128)}, f32[64,2048]{1,0:T(8,128)S(1)}, u32[]{:S(2)}, u32[]{:S(2)}) %collective-permute-start) | collective-permute-done | bytes 524320 | tf_op jit(solution)/shard_map/ppermute | solution.py:146
  467.6 4.2 all_to_all.39
  471.8 2.0 fusion.3
  (8 shorter events, 0.1 us)
Async XLA Ops:
  7.2 4.4 copy-start.1
  7.2 220.3 %reduce-scatter.3.cloned.1.call-start = ((), (), s32[]{:S(2)}) async-start(), calls=%async_computation.4 | async-start | bytes 20971520 | tf_op jit(solution)/shard_map/reduce_scatter | solution.py:119
  73.3 0.7 copy-start.2
  73.3 0.8 copy-start.3
  73.3 182.3 %copy-start.4 = (f32[128]{0:T(128)S(1)}, f32[128]{0:T(128)}, u32[]{:S(2)}) copy-start(f32[128]{0:T(128)} %param.11) | copy-start | bytes 1540
  73.3 282.0 %all-gather.4.cloned.1.call-start = ((), (), s32[]{:S(2)}) async-start(), calls=%async_computation.5 | async-start | bytes 10485760 | tf_op jit(solution)/shard_map/all_gather | solution.py:136
  268.8 161.7 %reduce-scatter.5.cloned.1.call-start = ((), (), s32[]{:S(2)}) async-start(), calls=%async_computation.6 | async-start | bytes 4718592 | tf_op jit(solution)/shard_map/reduce_scatter | solution.py:140
  380.3 52.1 %copy-start = (f32[128,128]{1,0:T(8,128)S(1)}, f32[128,128]{1,0:T(8,128)}, u32[]{:S(2)}) copy-start(f32[128,128]{1,0:T(8,128)} %get-tuple-element.5) | copy-start | bytes 196612
  430.5 37.1 %collective-permute-start = (f32[64,2048]{1,0:T(8,128)}, f32[64,2048]{1,0:T(8,128)S(1)}, u32[]{:S(2)}, u32[]{:S(2)}) collective-permute-start(f32[64,2048]{1,0:T(8,128)} %reduce-scatter.5.cloned.1.call-done), channel_id=1, source_target_pairs={{0,0},{1,1},{2,8},{3,9},{4,16},{5,17},{6,24},{7,25},{8,2},{9,3},{1... | collective-permute-start | bytes 1572872 | tf_op jit(solution)/shard_map/ppermute | solution.py:146
Sparse Core Ops, SparseCore 0:
  73.4 153.9 reduce-scatter.2
  268.9 86.3 all-gather.3
  380.4 50.0 reduce-scatter.4

commit v2 on v1

v2 whole, which is shorter than its diff:
```python
import functools
import math

import jax
import jax.numpy as jnp
from jax import lax
from jax.experimental import pallas as pl
from jax.experimental.pallas import tpu as pltpu
from jax.sharding import PartitionSpec as P

epsilon = 1e-05
lowest = -1e30
tail = 128
steps = 64
code_top = 32000.0
per_step = math.log(2.0) / steps
megabyte = 1024 * 1024


def encode(value):
    top = jnp.max(jnp.abs(value), axis=1, keepdims=True)
    power = jnp.ceil(jnp.log(jnp.maximum(top, 1e-30) * (1.0 / code_top)) * (1.0 / per_step))
    code = jnp.round(value * jnp.exp(power * -per_step))
    return code.astype(jnp.int32).astype(jnp.int16), power


def decode(codes_ref, tile, width, vocab_local, rows=slice(None)):
    powers = codes_ref[rows, vocab_local : vocab_local + tail].astype(jnp.int32).astype(jnp.float32)
    lane = lax.broadcasted_iota(jnp.int32, powers.shape, 1)
    power = jnp.sum(jnp.where(lane == tile, powers, 0.0), axis=1, keepdims=True)
    start = tile * width
    if not isinstance(start, int):
        start = pl.multiple_of(start, width)
    codes = codes_ref[rows, pl.ds(start, width)].astype(jnp.int32).astype(jnp.float32)
    return codes * jnp.exp(power * per_step)


def put(out_ref, powers_ref, rows, tile, width, vocab_local, value):
    code, power = encode(value)
    out_ref[:, pl.ds(pl.multiple_of(tile * width, width), width)] = code
    lane = lax.broadcasted_iota(jnp.int32, (value.shape[0], tail), 1)
    powers = jnp.where(lane >= tile, power, powers_ref[rows, :])
    powers_ref[rows, :] = powers
    out_ref[:, vocab_local:] = powers.astype(jnp.int32).astype(jnp.int16)


def dot(a, b):
    return jnp.dot(a, b, preferred_element_type=jnp.float32)


def far_kernel(width, vocab_local, x_ref, head_ref, first_ref, second_ref, powers_ref):
    tile = pl.program_id(0)
    value = dot(x_ref[...], head_ref[...])
    half = value.shape[0] // 2
    put(first_ref, powers_ref, slice(0, half), tile, width, vocab_local, value[:half])
    put(second_ref, powers_ref, slice(half, 2 * half), tile, width, vocab_local, value[half:])


def far_codes(rows_in, head, width):
    rows, depth = rows_in.shape
    vocab_local = head.shape[1]
    return pl.pallas_call(
        functools.partial(far_kernel, width, vocab_local),
        grid=(vocab_local // width,),
        in_specs=[
            pl.BlockSpec((rows, depth), lambda j: (0, 0)),
            pl.BlockSpec((depth, width), lambda j: (0, j)),
        ],
        out_specs=[pl.BlockSpec((rows // 2, vocab_local + tail), lambda j: (0, 0))] * 2,
        out_shape=[jax.ShapeDtypeStruct((rows // 2, vocab_local + tail), jnp.int16)] * 2,
        scratch_shapes=[pltpu.VMEM((rows, tail), jnp.float32)],
        compiler_params=pltpu.CompilerParams(vmem_limit_bytes=40 * megabyte),
        cost_estimate=pl.CostEstimate(
            flops=2 * rows * depth * vocab_local,
            bytes_accessed=2 * depth * vocab_local,
            transcendentals=0,
        ),
        name="far_codes",
    )(rows_in, head)


def near_kernel(
    width, vocab_local, x_ref, y_ref, head_ref, by_x_ref, by_y_ref, to_x_ref, to_y_ref, powers_ref
):
    tile = pl.program_id(0)
    rows = x_ref.shape[0]
    half = rows // 2
    value = dot(jnp.concatenate([x_ref[...], y_ref[...]], axis=0), head_ref[...])
    for_x, for_y = value[:rows], value[rows:]
    more_x = decode(by_y_ref, tile, width, vocab_local)
    more_y = decode(by_x_ref, tile, width, vocab_local)
    for_x = jnp.concatenate([for_x[:half], for_x[half:] + more_x], axis=0)
    for_y = jnp.concatenate([for_y[:half] + more_y, for_y[half:]], axis=0)
    put(to_x_ref, powers_ref, slice(0, rows), tile, width, vocab_local, for_x)
    put(to_y_ref, powers_ref, slice(rows, 2 * rows), tile, width, vocab_local, for_y)


def near_codes(part, rows_x, rows_y, head, by_x, by_y, width):
    depth = rows_x.shape[1]
    rows = rows_x.shape[0] // 2
    vocab_local = head.shape[1]
    whole = lambda r: pl.BlockSpec((r, vocab_local + tail), lambda j: (0, 0))
    return pl.pallas_call(
        functools.partial(near_kernel, width, vocab_local),
        grid=(vocab_local // width,),
        in_specs=[
            pl.BlockSpec((rows, depth), lambda j: (part, 0)),
            pl.BlockSpec((rows, depth), lambda j: (part, 0)),
            pl.BlockSpec((depth, width), lambda j: (0, j)),
            whole(rows // 2),
            whole(rows // 2),
        ],
        out_specs=[whole(rows)] * 2,
        out_shape=[jax.ShapeDtypeStruct((rows, vocab_local + tail), jnp.int16)] * 2,
        scratch_shapes=[pltpu.VMEM((2 * rows, tail), jnp.float32)],
        compiler_params=pltpu.CompilerParams(vmem_limit_bytes=40 * megabyte),
        cost_estimate=pl.CostEstimate(
            flops=4 * rows * depth * vocab_local,
            bytes_accessed=2 * depth * vocab_local,
            transcendentals=0,
        ),
        name="near_codes",
    )(rows_x, rows_y, head, by_x, by_y)


def own_kernel(x_ref, head_ref, out_ref):
    out_ref[...] = dot(x_ref[...], head_ref[...])


def own_logits(rows_in, head, width):
    rows, depth = rows_in.shape
    vocab_local = head.shape[1]
    return pl.pallas_call(
        own_kernel,
        grid=(vocab_local // width,),
        in_specs=[
            pl.BlockSpec((rows, depth), lambda j: (0, 0)),
            pl.BlockSpec((depth, width), lambda j: (0, j)),
        ],
        out_specs=pl.BlockSpec((rows, width), lambda j: (0, j)),
        out_shape=jax.ShapeDtypeStruct((rows, vocab_local), jnp.float32),
        compiler_params=pltpu.CompilerParams(vmem_limit_bytes=40 * megabyte),
        cost_estimate=pl.CostEstimate(
            flops=2 * rows * depth * vocab_local,
            bytes_accessed=2 * depth * vocab_local,
            transcendentals=0,
        ),
        name="own_logits",
    )(rows_in, head)


def members(ids, start, width):
    rows = ids.shape[0]
    column = lax.broadcasted_iota(jnp.int32, (rows, width), 1) + start
    found = column == ids[:, 0:1]
    for k in range(1, ids.shape[1]):
        found = found | (column == ids[:, k : k + 1])
    return found


def stats_kernel(width, vocab_local, own_ref, by_x_ref, by_y_ref, ids_ref, logits_ref, listed_ref, out_ref):
    rows = own_ref.shape[0]
    ids = ids_ref[...]
    top_all = jnp.full((rows, width), lowest, jnp.float32)
    top_ref = jnp.full((rows, width), lowest, jnp.float32)
    for tile in range(vocab_local // width):
        at = slice(tile * width, (tile + 1) * width)
        piece = (
            own_ref[:, at]
            + decode(by_x_ref, tile, width, vocab_local)
            + decode(by_y_ref, tile, width, vocab_local)
        )
        listed = jnp.where(members(ids, tile * width, width), piece, lowest)
        logits_ref[:, at] = piece
        listed_ref[:, at] = listed
        top_all = jnp.maximum(top_all, piece)
        top_ref = jnp.maximum(top_ref, listed)
    peak_all = jnp.max(top_all, axis=1, keepdims=True)
    peak_ref = jnp.max(top_ref, axis=1, keepdims=True)
    sum_all = jnp.zeros((rows, width), jnp.float32)
    sum_ref = jnp.zeros((rows, width), jnp.float32)
    for tile in range(vocab_local // width):
        at = slice(tile * width, (tile + 1) * width)
        sum_all = sum_all + jnp.exp(logits_ref[:, at] - peak_all)
        sum_ref = sum_ref + jnp.exp(listed_ref[:, at] - peak_ref)
    sum_all = jnp.sum(sum_all, axis=1, keepdims=True)
    sum_ref = jnp.sum(sum_ref, axis=1, keepdims=True)
    lane = lax.broadcasted_iota(jnp.int32, out_ref.shape, 1)
    out_ref[...] = jnp.where(
        lane == 0, peak_all, jnp.where(lane == 1, peak_ref, jnp.where(lane == 2, sum_all, sum_ref))
    )


def row_stats(part, own, by_x, by_y, ids, width):
    rows = by_x.shape[0]
    vocab_local = own.shape[1]
    block = 16
    skip = part * (rows // block)
    return pl.pallas_call(
        functools.partial(stats_kernel, width, vocab_local),
        grid=(rows // block,),
        in_specs=[
            pl.BlockSpec((block, vocab_local), lambda i: (i + skip, 0)),
            pl.BlockSpec((block, vocab_local + tail), lambda i: (i, 0)),
            pl.BlockSpec((block, vocab_local + tail), lambda i: (i, 0)),
            pl.BlockSpec((block, ids.shape[1]), lambda i: (i + skip, 0)),
        ],
        out_specs=[
            pl.BlockSpec((block, vocab_local), lambda i: (i, 0)),
            pl.BlockSpec((block, vocab_local), lambda i: (i, 0)),
            pl.BlockSpec((block, 128), lambda i: (i, 0)),
        ],
        out_shape=[
            jax.ShapeDtypeStruct((rows, vocab_local), jnp.float32),
            jax.ShapeDtypeStruct((rows, vocab_local), jnp.float32),
            jax.ShapeDtypeStruct((rows, 128), jnp.float32),
        ],
        compiler_params=pltpu.CompilerParams(vmem_limit_bytes=40 * megabyte),
        cost_estimate=pl.CostEstimate(
            flops=64 * rows * vocab_local,
            bytes_accessed=16 * rows * vocab_local,
            transcendentals=2 * rows * vocab_local,
        ),
        name="row_stats",
    )(own, by_x, by_y, ids)


def grad_kernel(width, logits_ref, listed_ref, scalars_ref, out_ref, term_ref):
    rows, vocab_local = logits_ref.shape
    lse_ref = scalars_ref[:, 0:1]
    lse_all = scalars_ref[:, 1:2]
    scale = scalars_ref[:, 2:3]
    term = jnp.zeros((rows, width), jnp.float32)
    for start in range(0, vocab_local, width):
        at = slice(start, start + width)
        piece = logits_ref[:, at]
        grad = scale * (jnp.exp(listed_ref[:, at] - lse_ref) - jnp.exp(piece - lse_all))
        grad = grad.astype(jnp.bfloat16)
        out_ref[:, at] = grad
        term = term + grad.astype(jnp.float32) * piece
    term_ref[...] = jnp.broadcast_to(jnp.sum(term, axis=1, keepdims=True), term_ref.shape)


def logit_grads(logits, listed, scalars, width):
    rows, vocab_local = logits.shape
    block = 16
    return pl.pallas_call(
        functools.partial(grad_kernel, width),
        grid=(rows // block,),
        in_specs=[
            pl.BlockSpec((block, vocab_local), lambda i: (i, 0)),
            pl.BlockSpec((block, vocab_local), lambda i: (i, 0)),
            pl.BlockSpec((block, scalars.shape[1]), lambda i: (i, 0)),
        ],
        out_specs=[
            pl.BlockSpec((block, vocab_local), lambda i: (i, 0)),
            pl.BlockSpec((block, 128), lambda i: (i, 0)),
        ],
        out_shape=[
            jax.ShapeDtypeStruct((rows, vocab_local), jnp.bfloat16),
            jax.ShapeDtypeStruct((rows, 128), jnp.float32),
        ],
        compiler_params=pltpu.CompilerParams(vmem_limit_bytes=40 * megabyte),
        cost_estimate=pl.CostEstimate(
            flops=8 * rows * vocab_local,
            bytes_accessed=10 * rows * vocab_local,
            transcendentals=2 * rows * vocab_local,
        ),
        name="logit_grads",
    )(logits, listed, scalars)


def after(value, *others):
    return lax.optimization_barrier((value, *others))[0]


def shards(hidden, head, gain, refusal_ids, refusal_count, loss_scale):
    row_count, model_width = hidden.shape
    depth, vocab_local = head.shape
    list_length = refusal_ids.shape[1]
    prompt_size = lax.axis_size("prompt")
    vocab_size = lax.axis_size("vocab")
    group = vocab_size // prompt_size
    width = min(1024, vocab_local)
    half = row_count // 2
    me = lax.axis_index("prompt")
    to_x, to_y, to_far = ([(p, p ^ k) for p in range(prompt_size)] for k in (1, 2, 3))
    send = lambda value, pairs: lax.ppermute(value, "prompt", pairs)

    hidden_f = hidden.astype(jnp.float32)
    inverse_rms = lax.rsqrt(jnp.mean(hidden_f * hidden_f, axis=1, keepdims=True) + epsilon)
    normed = (hidden_f * inverse_rms * gain).astype(jnp.bfloat16)
    columns = lambda p: lax.dynamic_slice_in_dim(normed, p * depth, depth, 1)
    for_far = columns(me ^ 3)
    far = [send(for_far[:half], to_far), send(for_far[half:], to_far)]
    rows_x = send(columns(me ^ 1), to_x)
    rows_y = send(columns(me ^ 2), to_y)

    far_a = far_codes(far[0], head, width)
    by_x_a, by_y_a = send(far_a[0], to_x), send(far_a[1], to_y)
    far_b = far_codes(after(far[1], *far_a), head, width)
    by_x_b, by_y_b = send(far_b[0], to_x), send(far_b[1], to_y)
    near_a = near_codes(0, rows_x, rows_y, head, by_x_a, by_y_a, width)
    sums_a = send(near_a[0], to_x), send(near_a[1], to_y)
    near_b = near_codes(1, rows_x, rows_y, head, by_x_b, by_y_b, width)
    own = own_logits(after(columns(me), *near_b), head, width)
    sums_b = send(near_b[0], to_x), send(near_b[1], to_y)

    vocab_start = lax.axis_index("vocab") * vocab_local
    in_list = jnp.arange(list_length)[None, :] < refusal_count[:, None]
    ids = jnp.where(in_list, refusal_ids - vocab_start, -1)

    moves = []
    for p in range(prompt_size):
        for r in range(prompt_size):
            for i in range(group):
                moves.append((p * vocab_size + r * group + i, r * vocab_size + p * group + i))
    groups = [[p * group + i for i in range(group)] for p in range(prompt_size)]

    grads, terms, logs = [], [], []
    for part, sums in enumerate((sums_a, sums_b)):
        logits, listed, stats = row_stats(part, own, *sums, ids, width)
        stats = lax.all_gather(stats[:, :4].T, "vocab", axis=0)
        peaks = jnp.max(stats[:, :2], axis=0)
        sums = jnp.sum(stats[:, 2:] * jnp.exp(stats[:, :2] - peaks[None]), axis=0)
        lse_all, lse_ref = peaks + jnp.log(sums)
        logs.append(lse_ref - lse_all)
        scale = loss_scale[part * half : (part + 1) * half]
        scalars = jnp.stack([lse_ref, lse_all, scale, scale], axis=1)
        grad_b, term = logit_grads(logits, listed, scalars, width)
        terms.append(term[:, 0])
        grad_all = lax.all_gather(grad_b, "prompt", axis=0, tiled=True)
        grad_part = lax.dot_general(
            grad_all, head, (((1,), (1,)), ((), ())), preferred_element_type=jnp.float32
        )
        grads.append(lax.psum_scatter(grad_part, "vocab", scatter_dimension=0, tiled=True))
    row_term = lax.psum(jnp.concatenate(terms), "vocab")
    log_refusal = jnp.concatenate(logs)

    grad_cols = []
    for grad_rows in grads:
        grad_rows = lax.ppermute(grad_rows, ("prompt", "vocab"), moves)
        grad_cols.append(
            lax.all_to_all(
                grad_rows, "vocab", split_axis=1, concat_axis=0, axis_index_groups=groups, tiled=True
            )
        )
    grad_cols = jnp.concatenate(grad_cols)

    slice_width = model_width // vocab_size
    col_start = lax.axis_index("vocab") * slice_width
    hidden_cols = lax.dynamic_slice_in_dim(hidden, col_start, slice_width, 1).astype(jnp.float32)
    gain_cols = lax.dynamic_slice_in_dim(gain, col_start, slice_width, 0)
    grad_hidden = (
        inverse_rms * gain_cols * grad_cols
        - hidden_cols * (inverse_rms * inverse_rms / model_width) * row_term[:, None]
    )
    return (grad_hidden, log_refusal)


def solution(mesh):
    return jax.shard_map(
        shards,
        mesh=mesh,
        in_specs=(
            P("prompt", None),
            P("prompt", "vocab"),
            P(),
            P("prompt", None),
            P("prompt"),
            P("prompt"),
        ),
        out_specs=(P("prompt", "vocab"), P("prompt")),
        check_vma=False,
    )
```

time: 489 us -> 412 us (0.84)
  the two profiles are of different devices: /device:TPU:2 before, /device:TPU:0 now
where the time goes in v2:
time: 412 us; the launch traced here: 411 us
  waiting for transfers between devices  172 us (42%)
  Pallas kernels  92 us (22%)
  blocking collectives  52 us (13%)
  matrix products  34.8 us (8%)
  starting transfers between devices  24.4 us (6%)
  local copies, waits for them, and re-layouts  14.1 us (3%)
  between operations  14 us (3%)
  other arithmetic  6.87 us (2%)
    all_gather x2, waiting for transfers between devices, shards(): grad_all = lax.all_gather(grad_b, 'prompt', axis=0, tiled=True)  82.8 us
    reduce_scatter x2, waiting for transfers between devices, shards(): lax.psum_scatter(grad_part, 'vocab', scatter_dimension=0, tiled=True)  63 us
    dot_general x2, matrix products, shards(): lax.dot_general(grad_all, head, (((1,), (1,)), ((), ())), preferred_eleme...  34.8 us
    pallas_call x2, Pallas kernels, far_codes(): pl.pallas_call(functools.partial(far_kernel, width, vocab_local), grid=(v...  31 us
    pallas_call x2, Pallas kernels, near_codes(): pl.pallas_call(functools.partial(near_kernel, width, vocab_local), grid=(...  29.8 us
    all_gather x2, blocking collectives, shards(): stats = lax.all_gather(stats[:, :4].T, 'vocab', axis=0)  25.6 us
    ppermute x12, waiting for transfers between devices, shards(): send = lambda value, pairs: lax.ppermute(value, 'prompt', pairs)  25.1 us
    psum x1, blocking collectives, shards(): row_term = lax.psum(jnp.concatenate(terms), 'vocab')  22.4 us
  transfers between devices with their start and end apart: 19, of which 7 were waited for; matrix products, arithmetic and copies ran while one was open for 9% of the time, Pallas kernels for 16%

profile of v2, /device:TPU:0, one launch (start us, length us, event | category | flops | bytes accessed | tf_op | source)
XLA Modules:
  0.0 410.6 jit_solution(7567632582688367783)
XLA Ops:
  7.2 2.2 fusion
  9.5 1.4 fusion.2
  10.9 4.0 collective-permute-start.3
  14.9 1.2 collective-permute-start.2
  16.1 5.9 %collective-permute-done.3.x_ref = bf16[64,2048]{1,0:T(8,128)(2,1)S(1)} collective-permute-done((bf16[64,2048]{1,0:T(8,128)(2,1)S(1)}, bf16[64,2048]{1,0:T(8,128)(2,1)S(1)}, u32[]{:S(2)}, u32[]{:S(2)}) %collective-permute-start.3) | collective-permute-done | bytes 262176 | tf_op jit(solution)/shard_map/ppermute | solution.py:288
  22.0 15.5 %far_codes.2 = (s16[32,8320]{1,0:T(8,128)(2,1)}, s16[32,8320]{1,0:T(8,128)(2,1)}) custom-call(bf16[64,2048]{1,0:T(8,128)(2,1)S(1)} %collective-permute-done.3.x_ref, bf16[2048,8192]{1,0:T(8,128)(2,1)} %head_ref.9), custom_call_target="tpu_custom_call" | custom-call | flops 2147483648 | bytes 33554432 | tf_op jit(solution)/shard_map/far_codes/pallas_call | solution.py:62
  37.6 15.5 %far_codes.3 = (s16[32,8320]{1,0:T(8,128)(2,1)}, s16[32,8320]{1,0:T(8,128)(2,1)S(1)}) custom-call(bf16[64,2048]{1,0:T(8,128)(2,1)S(1)} %collective-permute-done.2.x_ref, bf16[2048,8192]{1,0:T(8,128)(2,1)} %head_ref.9), custom_call_target="tpu_custom_call" | custom-call | flops 2147483648 | bytes 33554432 | tf_op jit(solution)/shard_map/far_codes/pallas_call | solution.py:62
  53.1 2.0 collective-permute-start.4
  55.1 1.5 collective-permute-start.5
  56.6 1.1 constant_dynamic-slice_fusion.1
  57.7 0.6 collective-permute-start
  58.3 0.1 copy.64
  58.4 2.0 collective-permute-start.6
  60.4 19.1 %collective-permute-done.x_ref = bf16[128,2048]{1,0:T(8,128)(2,1)S(1)} collective-permute-done((bf16[128,2048]{1,0:T(8,128)(2,1)}, bf16[128,2048]{1,0:T(8,128)(2,1)S(1)}, u32[]{:S(2)}, u32[]{:S(2)}) %collective-permute-start) | collective-permute-done | bytes 524320 | tf_op jit(solution)/shard_map/ppermute | solution.py:288
  79.6 2.0 collective-permute-start.7
  81.6 14.2 %near_codes.2 = (s16[64,8320]{1,0:T(8,128)(2,1)S(1)}, s16[64,8320]{1,0:T(8,128)(2,1)S(1)}) custom-call(bf16[128,2048]{1,0:T(8,128)(2,1)S(1)} %collective-permute-done.x_ref, bf16[128,2048]{1,0:T(8,128)(2,1)S(1)} %collective-permute-done.1.y_ref, bf16[2048,8192]{1,0:T(8,128)(2,1)} %head_ref.9, s16[32,8320]{1,0:T(8,128)(2,1)S(1)} %collective-permute-done.4.by_x_ref, ...), custom_call_target="tpu_custom_call" | custom-call | flops 4294967296 | bytes 33554432 | tf_op jit(solution)/shard_map/near_codes/pallas_call | solution.py:103
  95.9 1.5 collective-permute-start.11
  97.4 0.5 collective-permute-start.12
  97.9 0.1 fusion.4.ids_ref
  98.0 15.6 %near_codes.3 = (s16[64,8320]{1,0:T(8,128)(2,1)}, s16[64,8320]{1,0:T(8,128)(2,1)}) custom-call(bf16[128,2048]{1,0:T(8,128)(2,1)S(1)} %collective-permute-done.x_ref, bf16[128,2048]{1,0:T(8,128)(2,1)S(1)} %collective-permute-done.1.y_ref, bf16[2048,8192]{1,0:T(8,128)(2,1)} %head_ref.9, s16[32,8320]{1,0:T(8,128)(2,1)S(1)} %collective-permute-done.6.by_x_ref, ...), custom_call_target="tpu_custom_call" | custom-call | flops 4294967296 | bytes 33554432 | tf_op jit(solution)/shard_map/near_codes/pallas_call | solution.py:103
  113.7 2.0 collective-permute-start.9
  115.7 13.8 %own_logits.1.own_ref = f32[128,8192]{1,0:T(8,128)S(1)} custom-call(bf16[128,2048]{1,0:T(8,128)(2,1)S(1)} %get-tuple-element.29.x_ref, bf16[2048,8192]{1,0:T(8,128)(2,1)} %head_ref.9), custom_call_target="tpu_custom_call" | custom-call | flops 4294967296 | bytes 33554432 | tf_op jit(solution)/shard_map/own_logits/pallas_call | solution.py:133
  129.6 5.9 %row_stats.3 = (f32[64,8192]{1,0:T(8,128)S(1)}, f32[64,8192]{1,0:T(8,128)S(1)}, f32[64,128]{1,0:T(8,128)S(1)}) custom-call(f32[128,8192]{1,0:T(8,128)S(1)} %own_logits.1.own_ref, s16[64,8320]{1,0:T(8,128)(2,1)S(1)} %collective-permute-done.11.by_x_ref, s16[64,8320]{1,0:T(8,128)(2,1)S(1)} %collective-permute-done.12.by_y_ref, s32[128,16]{1,0:T(8,128)S(1)} %fusion.4.ids_ref), custom_call_target="tpu_custom_call" | custom-call | flops 33554432 | bytes 8388608 | tf_op jit(solution)/shard_map/row_stats/pallas_call | solution.py:199
  135.4 1.4 copy-done.2
  136.8 0.1 copy.71
  136.9 12.9 %all-gather.3 = f32[8,4,64]{2,1,0:T(4,128)S(1)} all-gather(f32[1,4,64]{2,1,0:T(4,128)S(1)} %copy.71), channel_id=3, replica_groups=mesh['prompt'=4,'vocab'=8] {'vocab'}, dimensions={0}, use_global_device_ids=true | all-gather | bytes 9216 | tf_op jit(solution)/shard_map/all_gather | solution.py:323
  149.9 0.1 copy.79
  150.0 2.2 copy-done.1
  152.2 6.8 %row_stats.2 = (f32[64,8192]{1,0:T(8,128)S(1)}, f32[64,8192]{1,0:T(8,128)S(1)}, f32[64,128]{1,0:T(8,128)S(1)}) custom-call(f32[128,8192]{1,0:T(8,128)S(1)} %copy-done.1, s16[64,8320]{1,0:T(8,128)(2,1)S(1)} %collective-permute-done.8.by_x_ref, s16[64,8320]{1,0:T(8,128)(2,1)} %collective-permute-done.9.by_y_ref, s32[128,16]{1,0:T(8,128)S(1)} %fusion.4.ids_ref), custom_call_target="tpu_custom_call" | custom-call | flops 33554432 | bytes 8388608 | tf_op jit(solution)/shard_map/row_stats/pallas_call | solution.py:199
  159.0 1.4 copy-done.4
  160.4 1.3 copy-done.6
  161.7 0.1 copy.65
  161.8 12.7 %all-gather.2 = f32[8,4,64]{2,1,0:T(4,128)S(1)} all-gather(f32[1,4,64]{2,1,0:T(4,128)S(1)} %copy.65), channel_id=2, replica_groups=mesh['prompt'=4,'vocab'=8] {'vocab'}, dimensions={0}, use_global_device_ids=true | all-gather | bytes 9216 | tf_op jit(solution)/shard_map/all_gather | solution.py:323
  174.5 0.1 copy.77
  174.6 0.1 copy.80
  174.8 0.2 subtract_reduce_fusion
  175.0 0.1 copy.78
  175.1 0.2 subtract_reduce_fusion.1
  175.3 0.1 copy.69.scalars_ref
  175.4 1.6 copy-done.5
  177.0 1.6 copy-done.7
  178.6 2.4 logit_grads.2
  181.0 0.1 copy.75.scalars_ref
  181.1 1.6 copy-done.3
  182.7 2.4 logit_grads.3
  185.1 0.2 reduce-scatter.3.cloned.1.call-start
  185.3 46.1 %all-gather.7.cloned.1.call-done = bf16[256,8192]{1,0:T(8,128)(2,1)} async-done(((bf16[64,8192]{1,0:T(8,128)(2,1)}), bf16[256,8192]{1,0:T(8,128)(2,1)}) %all-gather.7.cloned.1.call-update) | async-done | bytes 4194320 | tf_op jit(solution)/shard_map/all_gather | solution.py:332
  231.5 17.8 %fusion.7 = f32[256,2048]{1,0:T(8,128)} fusion(bf16[256,8192]{1,0:T(8,128)(2,1)} %all-gather.7.cloned.1.call-done, bf16[2048,8192]{1,0:T(8,128)(2,1)} %head_ref.9), kind=kOutput, calls=%fused_computation.42 | convolution fusion | flops 8589934592 | bytes 39845888 | tf_op jit(solution)/shard_map/dot_general | solution.py:333
  249.4 36.7 %all-gather.9.cloned.1.call-done = bf16[256,8192]{1,0:T(8,128)(2,1)} async-done(((bf16[64,8192]{1,0:T(8,128)(2,1)}), bf16[256,8192]{1,0:T(8,128)(2,1)}) %all-gather.9.cloned.1.call-update) | async-done | bytes 4194320 | tf_op jit(solution)/shard_map/all_gather | solution.py:332
  286.1 16.9 %fusion.8 = f32[256,2048]{1,0:T(8,128)} fusion(bf16[256,8192]{1,0:T(8,128)(2,1)} %all-gather.9.cloned.1.call-done, bf16[2048,8192]{1,0:T(8,128)(2,1)} %head_ref.9), kind=kOutput, calls=%fused_computation.43 | convolution fusion | flops 8589934592 | bytes 39845888 | tf_op jit(solution)/shard_map/dot_general | solution.py:333
  303.0 0.1 slice_reduce_fusion.1
  303.1 21.0 %reduce-scatter.3.cloned.1.call-done = f32[32,2048]{1,0:T(8,128)} async-done(((f32[256,2048]{1,0:T(8,128)}), f32[32,2048]{1,0:T(8,128)}) %reduce-scatter.3.cloned.1.call-update) | async-done | bytes 262160 | tf_op jit(solution)/shard_map/reduce_scatter | solution.py:336
  324.2 1.6 collective-permute-start.10
  325.8 42.0 %reduce-scatter.5.cloned.1.call-done = f32[32,2048]{1,0:T(8,128)} async-done(((f32[256,2048]{1,0:T(8,128)}), f32[32,2048]{1,0:T(8,128)}) %reduce-scatter.5.cloned.1.call-update) | async-done | bytes 262160 | tf_op jit(solution)/shard_map/reduce_scatter | solution.py:336
  367.7 1.6 collective-permute-start.13
  369.3 0.1 slice_reduce_fusion
  369.4 0.1 pad_maximum_fusion.2
  369.5 22.4 %psum.7 = f32[128]{0:T(128)S(1)} all-reduce(f32[128]{0:T(128)S(1)} %pad_maximum_fusion.2), channel_id=1, replica_groups=mesh['prompt'=4,'vocab'=8] {'vocab'}, use_global_device_ids=true, to_apply=%region_7.8 | all-reduce | flops 128 | bytes 1024 | tf_op jit(solution)/shard_map/psum | solution.py:337
  391.9 0.6 pad_maximum_fusion.3
  392.5 0.7 copy.86
  393.2 3.4 all-to-all-start
  396.7 1.5 all-to-all-done
  398.2 3.9 all_to_all.38
  402.2 1.9 fusion.3
  (58 shorter events, 0.6 us)
Async XLA Ops:
  7.2 2.3 copy-start.8
  7.2 224.3 %all-gather.7.cloned.1.call-start = ((), (), s32[]{:S(2)}) async-start(), calls=%async_computation.4 | async-start | bytes 5242880 | tf_op jit(solution)/shard_map/all_gather | solution.py:332
  10.9 4.0 copy-start.9
  10.9 11.1 %collective-permute-start.3 = (bf16[64,2048]{1,0:T(8,128)(2,1)S(1)}, bf16[64,2048]{1,0:T(8,128)(2,1)S(1)}, u32[]{:S(2)}, u32[]{:S(2)}) collective-permute-start(bf16[64,2048]{1,0:T(8,128)(2,1)S(1)} %get-tuple-element.48), channel_id=1, source_target_pairs={{0,24},{8,16},{16,8},{24,0},{1,25},{9,17},{17,9},{25,1},{2,26},{10... | collective-permute-start | bytes 786440 | tf_op jit(solution)/shard_map/ppermute | solution.py:288
  14.9 22.7 %collective-permute-start.2 = (bf16[64,2048]{1,0:T(8,128)(2,1)S(1)}, bf16[64,2048]{1,0:T(8,128)(2,1)S(1)}, u32[]{:S(2)}, u32[]{:S(2)}) collective-permute-start(bf16[64,2048]{1,0:T(8,128)(2,1)S(1)} %get-tuple-element.49), channel_id=1, source_target_pairs={{0,24},{8,16},{16,8},{24,0},{1,25},{9,17},{17,9},{25,1},{2,26},{10... | collective-permute-start | bytes 786440 | tf_op jit(solution)/shard_map/ppermute | solution.py:288
  37.6 19.0 %copy-start.10 = (bf16[128,8192]{1,0:T(8,128)(2,1)S(1)}, bf16[128,8192]{1,0:T(8,128)(2,1)}, u32[]{:S(2)}) copy-start(bf16[128,8192]{1,0:T(8,128)(2,1)} %copy-done.9) | copy-start | bytes 6291460
  53.1 5.2 %copy-start.11 = (s32[128,16]{0,1:T(8,128)S(1)}, s32[128,16]{0,1:T(8,128)}, u32[]{:S(2)}) copy-start(s32[128,16]{0,1:T(8,128)} %param.9) | copy-start | bytes 24580
  53.1 28.5 %collective-permute-start.4 = (s16[32,8320]{1,0:T(8,128)(2,1)}, s16[32,8320]{1,0:T(8,128)(2,1)S(1)}, u32[]{:S(2)}, u32[]{:S(2)}) collective-permute-start(s16[32,8320]{1,0:T(8,128)(2,1)} %get-tuple-element.25), channel_id=1, source_target_pairs={{0,8},{8,0},{16,24},{24,16},{1,9},{9,1},{17,25},{25,17},{2,10},{10... | collective-permute-start | bytes 1597448 | tf_op jit(solution)/shard_map/ppermute | solution.py:288
  55.1 26.5 %collective-permute-start.5 = (s16[32,8320]{1,0:T(8,128)(2,1)S(1)}, s16[32,8320]{1,0:T(8,128)(2,1)S(1)}, u32[]{:S(2)}, u32[]{:S(2)}) collective-permute-start(s16[32,8320]{1,0:T(8,128)(2,1)S(1)} %get-tuple-element.26), channel_id=1, source_target_pairs={{0,16},{8,24},{16,0},{24,8},{1,17},{9,25},{17,1},{25,9},{2,18},{10... | collective-permute-start | bytes 1597448 | tf_op jit(solution)/shard_map/ppermute | solution.py:288
  57.7 21.8 %collective-permute-start = (bf16[128,2048]{1,0:T(8,128)(2,1)}, bf16[128,2048]{1,0:T(8,128)(2,1)S(1)}, u32[]{:S(2)}, u32[]{:S(2)}) collective-permute-start(bf16[128,2048]{1,0:T(8,128)(2,1)} %get-tuple-element.51), channel_id=1, source_target_pairs={{0,8},{8,0},{16,24},{24,16},{1,9},{9,1},{17,25},{25,17},{2,10},{10... | collective-permute-start | bytes 1572872 | tf_op jit(solution)/shard_map/ppermute | solution.py:288
  58.3 23.3 %collective-permute-start.1 = (bf16[128,2048]{1,0:T(8,128)(2,1)}, bf16[128,2048]{1,0:T(8,128)(2,1)S(1)}, u32[]{:S(2)}, u32[]{:S(2)}) collective-permute-start(bf16[128,2048]{1,0:T(8,128)(2,1)} %get-tuple-element.50), channel_id=1, source_target_pairs={{0,16},{8,24},{16,0},{24,8},{1,17},{9,25},{17,1},{25,9},{2,18},{10... | collective-permute-start | bytes 1572872 | tf_op jit(solution)/shard_map/ppermute | solution.py:288
  58.4 39.5 %copy-start.13 = (s32[128]{0:T(128)S(1)}, s32[128]{0:T(128)}, u32[]{:S(2)}) copy-start(s32[128]{0:T(128)} %param.10) | copy-start | bytes 1540
  58.4 39.6 %collective-permute-start.6 = (s16[32,8320]{1,0:T(8,128)(2,1)}, s16[32,8320]{1,0:T(8,128)(2,1)S(1)}, u32[]{:S(2)}, u32[]{:S(2)}) collective-permute-start(s16[32,8320]{1,0:T(8,128)(2,1)} %get-tuple-element.22), channel_id=1, source_target_pairs={{0,8},{8,0},{16,24},{24,16},{1,9},{9,1},{17,25},{25,17},{2,10},{10... | collective-permute-start | bytes 1597448 | tf_op jit(solution)/shard_map/ppermute | solution.py:288
  79.6 18.5 %collective-permute-start.7 = (s16[32,8320]{1,0:T(8,128)(2,1)}, s16[32,8320]{1,0:T(8,128)(2,1)S(1)}, u32[]{:S(2)}, u32[]{:S(2)}) collective-permute-start(s16[32,8320]{1,0:T(8,128)(2,1)} %get-tuple-element.23), channel_id=1, source_target_pairs={{0,16},{8,24},{16,0},{24,8},{1,17},{9,25},{17,1},{25,9},{2,18},{10... | collective-permute-start | bytes 1597448 | tf_op jit(solution)/shard_map/ppermute | solution.py:288
  95.9 33.7 %collective-permute-start.11 = (s16[64,8320]{1,0:T(8,128)(2,1)S(1)}, s16[64,8320]{1,0:T(8,128)(2,1)S(1)}, u32[]{:S(2)}, u32[]{:S(2)}) collective-permute-start(s16[64,8320]{1,0:T(8,128)(2,1)S(1)} %get-tuple-element.27), channel_id=1, source_target_pairs={{0,8},{8,0},{16,24},{24,16},{1,9},{9,1},{17,25},{25,17},{2,10},{10... | collective-permute-start | bytes 3194888 | tf_op jit(solution)/shard_map/ppermute | solution.py:288
  97.4 32.1 %collective-permute-start.12 = (s16[64,8320]{1,0:T(8,128)(2,1)S(1)}, s16[64,8320]{1,0:T(8,128)(2,1)S(1)}, u32[]{:S(2)}, u32[]{:S(2)}) collective-permute-start(s16[64,8320]{1,0:T(8,128)(2,1)S(1)} %get-tuple-element.28), channel_id=1, source_target_pairs={{0,16},{8,24},{16,0},{24,8},{1,17},{9,25},{17,1},{25,9},{2,18},{10... | collective-permute-start | bytes 3194888 | tf_op jit(solution)/shard_map/ppermute | solution.py:288
  98.0 17.7 %copy-start.12 = (f32[128]{0:T(128)S(1)}, f32[128]{0:T(128)}, u32[]{:S(2)}) copy-start(f32[128]{0:T(128)} %param.11) | copy-start | bytes 1540
  113.6 36.4 %collective-permute-start.8 = (s16[64,8320]{1,0:T(8,128)(2,1)}, s16[64,8320]{1,0:T(8,128)(2,1)S(1)}, u32[]{:S(2)}, u32[]{:S(2)}) collective-permute-start(s16[64,8320]{1,0:T(8,128)(2,1)} %get-tuple-element.30), channel_id=1, source_target_pairs={{0,8},{8,0},{16,24},{24,16},{1,9},{9,1},{17,25},{25,17},{2,10},{10... | collective-permute-start | bytes 3194888 | tf_op jit(solution)/shard_map/ppermute | solution.py:288
  113.7 36.3 %collective-permute-start.9 = (s16[64,8320]{1,0:T(8,128)(2,1)}, s16[64,8320]{1,0:T(8,128)(2,1)}, u32[]{:S(2)}, u32[]{:S(2)}) collective-permute-start(s16[64,8320]{1,0:T(8,128)(2,1)} %get-tuple-element.31), channel_id=1, source_target_pairs={{0,16},{8,24},{16,0},{24,8},{1,17},{9,25},{17,1},{25,9},{2,18},{10... | collective-permute-start | bytes 3194888 | tf_op jit(solution)/shard_map/ppermute | solution.py:288
  129.5 5.9 %copy-start = (f32[128,8192]{1,0:T(8,128)}, f32[128,8192]{1,0:T(8,128)S(1)}, u32[]{:S(2)}) copy-start(f32[128,8192]{1,0:T(8,128)S(1)} %own_logits.1.own_ref) | copy-start | bytes 12582916
  135.4 1.4 copy-start.2
  150.0 2.2 copy-start.1
  159.0 1.4 copy-start.4
  160.4 1.3 copy-start.6
  175.4 1.6 copy-start.5
  177.0 1.6 copy-start.7
  181.0 105.1 %all-gather.9.cloned.1.call-start = ((), (), s32[]{:S(2)}) async-start(), calls=%async_computation.6 | async-start | bytes 5242880 | tf_op jit(solution)/shard_map/all_gather | solution.py:332
  181.1 1.6 copy-start.3
  185.1 139.1 %reduce-scatter.3.cloned.1.call-start = ((), (), s32[]{:S(2)}) async-start(), calls=%async_computation.5 | async-start | bytes 2359296 | tf_op jit(solution)/shard_map/reduce_scatter | solution.py:336
  249.3 118.4 %reduce-scatter.5.cloned.1.call-start = ((), (), s32[]{:S(2)}) async-start(), calls=%async_computation.7 | async-start | bytes 2359296 | tf_op jit(solution)/shard_map/reduce_scatter | solution.py:336
  303.0 99.2 %dynamic-slice-start = ((f32[8192]{0:T(1024)}, s32[]{:T(128)}), f32[1024]{0:T(1024)S(1)}, s32[]{:S(2)}) async-start(f32[8192]{0:T(1024)} %param.8, s32[]{:T(128)} %select_n.20), calls=%async_computation.8 | async-start | bytes 8704 | tf_op jit(solution)/shard_map/dynamic_slice | solution.py:353
  324.2 68.4 %collective-permute-start.10 = (f32[32,2048]{1,0:T(8,128)}, f32[32,2048]{1,0:T(8,128)S(1)}, u32[]{:S(2)}, u32[]{:S(2)}) collective-permute-start(f32[32,2048]{1,0:T(8,128)} %reduce-scatter.3.cloned.1.call-done), channel_id=1, source_target_pairs={{0,0},{1,1},{2,8},{3,9},{4,16},{5,17},{6,24},{7,25},{8,2},{9,3},{1... | collective-permute-start | bytes 786440 | tf_op jit(solution)/shard_map/ppermute | solution.py:342
  367.7 29.0 %collective-permute-start.13 = (f32[32,2048]{1,0:T(8,128)}, f32[32,2048]{1,0:T(8,128)S(1)}, u32[]{:S(2)}, u32[]{:S(2)}) collective-permute-start(f32[32,2048]{1,0:T(8,128)} %reduce-scatter.5.cloned.1.call-done), channel_id=1, source_target_pairs={{0,0},{1,1},{2,8},{3,9},{4,16},{5,17},{6,24},{7,25},{8,2},{9,3},{1... | collective-permute-start | bytes 786440 | tf_op jit(solution)/shard_map/ppermute | solution.py:342
  393.2 5.0 %all-to-all-start = ((f32[32,2,1024]{2,0,1:T(8,128)}), f32[32,2,1024]{2,0,1:T(8,128)S(1)}, u32[]{:S(2)}, u32[]{:S(2)}) async-start(f32[32,2,1024]{2,0,1:T(8,128)} %bitcast.33), calls=%async_computation.1 | async-start | bytes 524288 | tf_op jit(solution)/shard_map/all_to_all | solution.py:344
Sparse Core Ops, SparseCore 0:
  181.1 50.3 all-gather.6
  233.3 52.6 all-gather.8
  288.4 35.7 reduce-scatter.2
  326.3 41.3 reduce-scatter.4

commit v3 on v0

v3 whole, which is shorter than its diff:
```python
import functools
import math

import jax
import jax.numpy as jnp
from jax import lax
from jax.experimental import pallas as pl
from jax.experimental.pallas import tpu as pltpu
from jax.sharding import PartitionSpec as P

epsilon = 1e-05
lowest = -1e30
tail = 128
steps = 64
code_top = 32000.0
per_step = math.log(2.0) / steps
megabyte = 1024 * 1024


def encode(value):
    top = jnp.max(jnp.abs(value), axis=1, keepdims=True)
    power = jnp.ceil(jnp.log(jnp.maximum(top, 1e-30) * (1.0 / code_top)) * (1.0 / per_step))
    code = jnp.round(value * jnp.exp(power * -per_step))
    return code.astype(jnp.int32).astype(jnp.int16), power


def decode(codes_ref, tile, width, vocab_local, rows=slice(None)):
    powers = codes_ref[rows, vocab_local : vocab_local + tail].astype(jnp.int32).astype(jnp.float32)
    lane = lax.broadcasted_iota(jnp.int32, powers.shape, 1)
    power = jnp.sum(jnp.where(lane == tile, powers, 0.0), axis=1, keepdims=True)
    start = tile * width
    if not isinstance(start, int):
        start = pl.multiple_of(start, width)
    codes = codes_ref[rows, pl.ds(start, width)].astype(jnp.int32).astype(jnp.float32)
    return codes * jnp.exp(power * per_step)


def put(out_ref, powers_ref, rows, tile, width, vocab_local, value):
    code, power = encode(value)
    out_ref[:, pl.ds(pl.multiple_of(tile * width, width), width)] = code
    lane = lax.broadcasted_iota(jnp.int32, (value.shape[0], tail), 1)
    powers = jnp.where(lane >= tile, power, powers_ref[rows, :])
    powers_ref[rows, :] = powers
    out_ref[:, vocab_local:] = powers.astype(jnp.int32).astype(jnp.int16)


def dot(a, b):
    return jnp.dot(a, b, preferred_element_type=jnp.float32)


def compiler_params():
    return pltpu.CompilerParams(vmem_limit_bytes=40 * megabyte)


def small_cost():
    return pl.CostEstimate(flops=1024, bytes_accessed=1024, transcendentals=0)


def constant(*shape):
    return pl.BlockSpec(shape, lambda *_: (0,) * len(shape))


def far_kernel(width, x_ref, head_ref, first_ref, second_ref, powers_ref):
    tile = pl.program_id(0)
    columns = first_ref.shape[1] - tail
    value = dot(x_ref[...], head_ref[...])
    q = value.shape[0] // 4
    first = jnp.concatenate([value[:q], value[2 * q : 3 * q]], axis=0)
    second = jnp.concatenate([value[q : 2 * q], value[3 * q :]], axis=0)
    put(first_ref, powers_ref, slice(0, 2 * q), tile, width, columns, first)
    put(second_ref, powers_ref, slice(2 * q, 4 * q), tile, width, columns, second)


def far_codes(rows_in, head, width, skip, tiles):
    rows, depth = rows_in.shape
    columns = tiles * width
    return pl.pallas_call(
        functools.partial(far_kernel, width),
        grid=(tiles,),
        in_specs=[
            constant(rows, depth),
            pl.BlockSpec((depth, width), lambda j: (0, j + skip)),
        ],
        out_specs=[constant(rows // 2, columns + tail)] * 2,
        out_shape=[jax.ShapeDtypeStruct((rows // 2, columns + tail), jnp.int16)] * 2,
        scratch_shapes=[pltpu.VMEM((rows, tail), jnp.float32)],
        compiler_params=compiler_params(),
        cost_estimate=small_cost(),
        name="far_codes",
    )(rows_in, head)


def decode_any(refs, tile, width):
    columns = refs[0].shape[1] - tail
    if len(refs) == 1:
        return decode(refs[0], tile, width, columns)
    each = columns // width
    if isinstance(tile, int):
        return decode(refs[tile // each], tile % each, width, columns)
    low = decode(refs[0], jnp.minimum(tile, each - 1), width, columns)
    high = decode(refs[1], jnp.maximum(tile - each, 0), width, columns)
    return jnp.where(tile < each, low, high)


def near_kernel(width, parts, x_ref, y_ref, own_ref, head_ref, *refs):
    by_x_refs, by_y_refs = refs[:parts], refs[parts : 2 * parts]
    to_x_ref, to_y_ref, out_ref, powers_ref = refs[2 * parts :]
    tile = pl.program_id(0)
    rows = x_ref.shape[0]
    half = rows // 2
    columns = to_x_ref.shape[1] - tail
    value = dot(jnp.concatenate([x_ref[...], y_ref[...], own_ref[...]], axis=0), head_ref[...])
    out_ref[...] = value[2 * rows :]
    more_x = decode_any(by_y_refs, tile, width)
    more_y = decode_any(by_x_refs, tile, width)
    for_x = jnp.concatenate([value[:half], value[half:rows] + more_x], axis=0)
    for_y = jnp.concatenate([value[rows : rows + half] + more_y, value[rows + half : 2 * rows]], axis=0)
    put(to_x_ref, powers_ref, slice(0, rows), tile, width, columns, for_x)
    put(to_y_ref, powers_ref, slice(rows, 2 * rows), tile, width, columns, for_y)


def near_codes(part, rows_x, rows_y, rows_own, head, by_x, by_y, width, skip, tiles):
    depth = rows_x.shape[1]
    rows = rows_x.shape[0] // 2
    columns = tiles * width
    received = pl.BlockSpec((rows // 2, by_x[0].shape[1]), lambda j: (part, 0))
    return pl.pallas_call(
        functools.partial(near_kernel, width, len(by_x)),
        grid=(tiles,),
        in_specs=[pl.BlockSpec((rows, depth), lambda j: (part, 0))] * 3
        + [pl.BlockSpec((depth, width), lambda j: (0, j + skip))]
        + [received] * (2 * len(by_x)),
        out_specs=[constant(rows, columns + tail)] * 2 + [pl.BlockSpec((rows, width), lambda j: (0, j))],
        out_shape=[jax.ShapeDtypeStruct((rows, columns + tail), jnp.int16)] * 2
        + [jax.ShapeDtypeStruct((rows, columns), jnp.float32)],
        scratch_shapes=[pltpu.VMEM((2 * rows, tail), jnp.float32)],
        compiler_params=compiler_params(),
        cost_estimate=small_cost(),
        name="near_codes",
    )(rows_x, rows_y, rows_own, head, *by_x, *by_y)


def members(ids, start, width):
    rows = ids.shape[0]
    column = lax.broadcasted_iota(jnp.int32, (rows, width), 1) + start
    found = column == ids[:, 0:1]
    for k in range(1, ids.shape[1]):
        found = found | (column == ids[:, k : k + 1])
    return found


def stats_kernel(width, parts, *refs):
    own_refs, by_x_refs, by_y_refs = refs[:parts], refs[parts : 2 * parts], refs[2 * parts : 3 * parts]
    ids_ref, logits_ref, listed_ref, out_ref = refs[3 * parts :]
    rows, columns = logits_ref.shape
    each = columns // parts
    ids = ids_ref[...]
    top_all = jnp.full((rows, width), lowest, jnp.float32)
    top_ref = jnp.full((rows, width), lowest, jnp.float32)
    for start in range(0, columns, width):
        at = slice(start, start + width)
        inner = start % each
        piece = own_refs[start // each][:, inner : inner + width]
        piece = piece + decode_any(by_x_refs, start // width, width)
        piece = piece + decode_any(by_y_refs, start // width, width)
        listed = jnp.where(members(ids, start, width), piece, lowest)
        logits_ref[:, at] = piece
        listed_ref[:, at] = listed
        top_all = jnp.maximum(top_all, piece)
        top_ref = jnp.maximum(top_ref, listed)
    peak_all = jnp.max(top_all, axis=1, keepdims=True)
    peak_ref = jnp.max(top_ref, axis=1, keepdims=True)
    sum_all = jnp.zeros((rows, width), jnp.float32)
    sum_ref = jnp.zeros((rows, width), jnp.float32)
    for start in range(0, columns, width):
        at = slice(start, start + width)
        sum_all = sum_all + jnp.exp(logits_ref[:, at] - peak_all)
        sum_ref = sum_ref + jnp.exp(listed_ref[:, at] - peak_ref)
    sum_all = jnp.sum(sum_all, axis=1, keepdims=True)
    sum_ref = jnp.sum(sum_ref, axis=1, keepdims=True)
    lane = lax.broadcasted_iota(jnp.int32, out_ref.shape, 1)
    out_ref[...] = jnp.where(
        lane == 0, peak_all, jnp.where(lane == 1, peak_ref, jnp.where(lane == 2, sum_all, sum_ref))
    )


def row_stats(part, own, by_x, by_y, ids, width):
    rows = own[0].shape[0]
    parts = len(own)
    columns = own[0].shape[1] * parts
    block = min(rows, 16)
    skip = part * (rows // block)
    across = lambda array: pl.BlockSpec((block, array.shape[1]), lambda i: (i, 0))
    return pl.pallas_call(
        functools.partial(stats_kernel, width, parts),
        grid=(rows // block,),
        in_specs=[across(a) for a in (*own, *by_x, *by_y)]
        + [pl.BlockSpec((block, ids.shape[1]), lambda i: (i + skip, 0))],
        out_specs=[
            pl.BlockSpec((block, columns), lambda i: (i, 0)),
            pl.BlockSpec((block, columns), lambda i: (i, 0)),
            pl.BlockSpec((block, 128), lambda i: (i, 0)),
        ],
        out_shape=[
            jax.ShapeDtypeStruct((rows, columns), jnp.float32),
            jax.ShapeDtypeStruct((rows, columns), jnp.float32),
            jax.ShapeDtypeStruct((rows, 128), jnp.float32),
        ],
        compiler_params=compiler_params(),
        cost_estimate=small_cost(),
        name="row_stats",
    )(*own, *by_x, *by_y, ids)


def grad_kernel(width, logits_ref, listed_ref, stats_ref, scale_ref, out_ref, info_ref):
    rows, columns = logits_ref.shape
    stats = [stats_ref[v] for v in range(stats_ref.shape[0])]
    peaks = functools.reduce(jnp.maximum, [s[:, :2] for s in stats])
    sums = functools.reduce(jnp.add, [s[:, 2:4] * jnp.exp(s[:, :2] - peaks) for s in stats])
    lse = peaks + jnp.log(sums)
    lse_all, lse_ref = lse[:, 0:1], lse[:, 1:2]
    scale = scale_ref[...]
    term = jnp.zeros((rows, width), jnp.float32)
    for start in range(0, columns, width):
        at = slice(start, start + width)
        piece = logits_ref[:, at]
        grad = scale * (jnp.exp(listed_ref[:, at] - lse_ref) - jnp.exp(piece - lse_all))
        grad = grad.astype(jnp.bfloat16)
        out_ref[:, at] = grad
        term = term + grad.astype(jnp.float32) * piece
    lane = lax.broadcasted_iota(jnp.int32, info_ref.shape, 1)
    info_ref[...] = jnp.where(lane == 0, jnp.sum(term, axis=1, keepdims=True), lse_ref - lse_all)


def logit_grads(part, logits, listed, stats, scale, width):
    rows, columns = logits.shape
    block = min(rows, 16)
    skip = part * (rows // block)
    return pl.pallas_call(
        functools.partial(grad_kernel, width),
        grid=(rows // block,),
        in_specs=[
            pl.BlockSpec((block, columns), lambda i: (i, 0)),
            pl.BlockSpec((block, columns), lambda i: (i, 0)),
            pl.BlockSpec((stats.shape[0], block, 128), lambda i: (0, i, 0)),
            pl.BlockSpec((block, 1), lambda i: (i + skip, 0)),
        ],
        out_specs=[
            pl.BlockSpec((block, columns), lambda i: (i, 0)),
            pl.BlockSpec((block, 128), lambda i: (i, 0)),
        ],
        out_shape=[
            jax.ShapeDtypeStruct((rows, columns), jnp.bfloat16),
            jax.ShapeDtypeStruct((rows, 128), jnp.float32),
        ],
        compiler_params=compiler_params(),
        cost_estimate=small_cost(),
        name="logit_grads",
    )(logits, listed, stats, scale)


def put_row(out_ref, value):
    code, power = encode(value)
    width = value.shape[1]
    out_ref[:, :width] = code
    out_ref[:, width:] = jnp.broadcast_to(power, (value.shape[0], tail)).astype(jnp.int32).astype(jnp.int16)


def take_row(codes_ref):
    width = codes_ref.shape[1] - tail
    power = codes_ref[:, width:].astype(jnp.int32).astype(jnp.float32)[:, 0:1]
    return codes_ref[:, :width].astype(jnp.int32).astype(jnp.float32) * jnp.exp(power * per_step)


def back_kernel(tiles, started, ends, place_ref, *refs):
    grads, head_ref, refs = refs[:5], refs[5], refs[6:]
    so_far_ref, refs = (refs[0], refs[1:]) if started else (None, refs)
    total_ref, refs = refs[-1], refs[:-1]
    tile = pl.program_id(0)

    @pl.when(tile == 0)
    def _():
        total_ref[...] = so_far_ref[...] if started else jnp.zeros_like(total_ref)

    grad = jnp.concatenate([g[...] for g in grads], axis=0)
    total_ref[...] += lax.dot_general(
        grad, head_ref[...], (((1,), (1,)), ((), ())), preferred_element_type=jnp.float32
    )

    @pl.when(tile == tiles - 1)
    def _():
        if not ends:
            refs[0][...] = total_ref[...]
            return
        keep_ref, sends = refs[0], refs[1:]
        width = keep_ref.shape[1]
        block = lambda b: total_ref[:, pl.ds(pl.multiple_of(b * width, width), width)]
        mine = place_ref[0]
        keep_ref[...] = block(mine)
        for k, send_ref in enumerate(sends, 1):
            put_row(send_ref, block(mine ^ k))


def back(grads, head, so_far, place, width, skip, tiles, group):
    depth = head.shape[0]
    rows = sum(g.shape[0] for g in grads)
    across = lambda g: pl.BlockSpec(
        (g.shape[0], width), (lambda j: (0, j + skip)) if g.shape[1] > tiles * width else (lambda j: (0, j))
    )
    started = [] if so_far is None else [so_far]
    if group:
        part = depth // group
        shapes = [((rows, part), jnp.float32)] + [((rows, part + tail), jnp.int16)] * (group - 1)
    else:
        shapes = [((rows, depth), jnp.float32)]
    return pl.pallas_call(
        functools.partial(back_kernel, tiles, bool(started), bool(group)),
        grid=(tiles,),
        in_specs=[pl.BlockSpec(memory_space=pltpu.SMEM)]
        + [across(g) for g in grads]
        + [pl.BlockSpec((depth, width), lambda j: (0, j + skip))]
        + [constant(rows, depth)] * len(started),
        out_specs=[constant(*shape) for shape, _ in shapes],
        out_shape=[jax.ShapeDtypeStruct(*s) for s in shapes],
        scratch_shapes=[pltpu.VMEM((rows, depth), jnp.float32)],
        compiler_params=compiler_params(),
        cost_estimate=small_cost(),
        name="grad_rows",
    )(place, *grads, head, *started)


def group_kernel(place_ref, keep_ref, *refs):
    total_ref = refs[-1]
    count = place_ref.shape[0] - 1
    out_ref, sends, received = refs[-2 - count], refs[-1 - count : -1], refs[: -2 - count]
    total = keep_ref[...]
    for codes_ref in received:
        total = total + take_row(codes_ref)
    total_ref[...] = total
    rows = out_ref.shape[0]
    block = lambda b: total_ref[pl.ds(pl.multiple_of(b * rows, rows), rows), :]
    out_ref[...] = block(place_ref[0])
    for k, send_ref in enumerate(sends, 1):
        put_row(send_ref, block(place_ref[k]))


def group_sum(place, keep, received):
    blocks = place.shape[0]
    rows, width = keep.shape
    own = (rows // blocks, width)
    coded = (rows // blocks, width + tail)
    return pl.pallas_call(
        group_kernel,
        in_specs=[pl.BlockSpec(memory_space=pltpu.SMEM)]
        + [pl.BlockSpec(memory_space=pltpu.VMEM)] * (1 + len(received)),
        out_specs=[pl.BlockSpec(memory_space=pltpu.VMEM)] * blocks,
        out_shape=[jax.ShapeDtypeStruct(own, jnp.float32)]
        + [jax.ShapeDtypeStruct(coded, jnp.int16)] * (blocks - 1),
        scratch_shapes=[pltpu.VMEM((rows, width), jnp.float32)],
        compiler_params=compiler_params(),
        cost_estimate=small_cost(),
        name="group_sum",
    )(place, keep, *received)


def after(value, *others):
    return lax.optimization_barrier((value, *others))[0]


def last_kernel(keep_ref, *refs):
    total = keep_ref[...]
    for codes_ref in refs[:-1]:
        total = total + take_row(codes_ref)
    put_row(refs[-1], total)


def last_sum(keep, received):
    rows, width = keep.shape
    return pl.pallas_call(
        last_kernel,
        in_specs=[pl.BlockSpec(memory_space=pltpu.VMEM)] * (1 + len(received)),
        out_specs=pl.BlockSpec(memory_space=pltpu.VMEM),
        out_shape=jax.ShapeDtypeStruct((rows, width + tail), jnp.int16),
        compiler_params=compiler_params(),
        cost_estimate=small_cost(),
        name="last_sum",
    )(keep, *received)


def shards(hidden, head, gain, refusal_ids, refusal_count, loss_scale):
    row_count, model_width = hidden.shape
    depth, vocab_local = head.shape
    list_length = refusal_ids.shape[1]
    prompt_size = lax.axis_size("prompt")
    vocab_size = lax.axis_size("vocab")
    group = vocab_size // prompt_size
    width = min(1024, vocab_local // 2)
    tiles = vocab_local // width
    half = row_count // 2
    me = lax.axis_index("prompt")
    shard = lax.axis_index("vocab")
    to_x, to_y, to_far = ([(p, p ^ k) for p in range(prompt_size)] for k in (1, 2, 3))
    send = lambda value, pairs: lax.ppermute(value, "prompt", pairs)

    hidden_f = hidden.astype(jnp.float32)
    inverse_rms = lax.rsqrt(jnp.mean(hidden_f * hidden_f, axis=1, keepdims=True) + epsilon)
    normed = (hidden_f * inverse_rms * gain).astype(jnp.bfloat16)
    columns = lambda p: lax.dynamic_slice_in_dim(normed, p * depth, depth, 1)
    rows_far = send(columns(me ^ 3), to_far)
    rows_x = send(columns(me ^ 1), to_x)
    rows_y = send(columns(me ^ 2), to_y)
    rows_own = columns(me)

    by_x, by_y = [], []
    for skip in (0, tiles // 2):
        first, second = far_codes(rows_far, head, width, skip, tiles // 2)
        by_x.append(send(first, to_x))
        by_y.append(send(second, to_y))
    own_a, sums_x_a, sums_y_a = [], [], []
    for c, skip in enumerate((0, tiles // 2)):
        codes_x, codes_y, own = near_codes(
            0, rows_x, rows_y, rows_own, head, [by_x[c]], [by_y[c]], width, skip, tiles // 2
        )
        own_a.append(own)
        sums_x_a.append(send(codes_x, to_x))
        sums_y_a.append(send(codes_y, to_y))
    codes_x, codes_y, own = near_codes(
        1, rows_x, rows_y, after(rows_own, *own_a), head, by_x, by_y, width, 0, tiles
    )
    halves = (
        (own_a, sums_x_a, sums_y_a),
        ([own], [send(codes_x, to_x)], [send(codes_y, to_y)]),
    )

    in_list = jnp.arange(list_length)[None, :] < refusal_count[:, None]
    ids = jnp.where(in_list, refusal_ids - shard * vocab_local, -1)

    block, member = shard // group, shard % group
    place_group = jnp.stack([member]).astype(jnp.int32)
    place_block = jnp.stack([block ^ k ^ me for k in range(prompt_size)]).astype(jnp.int32)
    to_member = [[(v, v ^ k) for v in range(vocab_size)] for k in range(1, group)]
    to_block = [
        [(v, ((v // group) ^ k) * group + v % group) for v in range(vocab_size)]
        for k in range(1, prompt_size)
    ]
    moves = []
    for p in range(prompt_size):
        for r in range(prompt_size):
            for i in range(group):
                moves.append((p * vocab_size + r * group + i, r * vocab_size + p * group + i))

    infos, grad_cols, grads, turns, before_back = [], [], [], [], []
    for part, (own, sums_x, sums_y) in enumerate(halves):
        logits, listed, stats = row_stats(part, own, sums_x, sums_y, after(ids, *infos), width)
        stats = lax.all_gather(stats, "vocab", axis=0)
        grad, info = logit_grads(part, logits, listed, stats, loss_scale[:, None], width)
        infos.append(info)
        grads.append((grad, send(grad, to_x), send(grad, to_y)))
    info = jnp.concatenate(infos)
    terms = lax.all_gather(info, "vocab", axis=0)

    for part, (grad, grad_x, grad_y) in enumerate(grads):
        quarter = half // 2
        pieces = 1 + part
        so_far = None
        grad_x, grad_y = after(grad_x, *turns), after(grad_y, *turns)
        for c in range(pieces):
            at = slice(c * vocab_local // pieces, (c + 1) * vocab_local // pieces)
            far_0 = send(grad_y[:quarter, at], to_x)
            far_1 = send(grad_x[quarter:, at], to_y)
            so_far = back(
                (grad, grad_x, grad_y, far_0, far_1),
                head,
                so_far,
                after(place_group, *before_back),
                width,
                c * tiles // pieces,
                tiles // pieces,
                group if c == pieces - 1 else 0,
            )
            if c < pieces - 1:
                so_far = so_far[0]
        keep, *codes = so_far
        turns = [keep]
        keep, *codes = group_sum(
            place_block, keep, [lax.ppermute(c, "vocab", to) for c, to in zip(codes, to_member)]
        )
        before_back = [keep, terms]
        codes = last_sum(keep, [lax.ppermute(c, "vocab", to) for c, to in zip(codes, to_block)])
        grad_cols.append(lax.ppermute(codes, ("prompt", "vocab"), moves))
    row_term = jnp.sum(terms[:, :, 0], axis=0)
    log_refusal = info[:, 1]

    slice_width = model_width // vocab_size
    col_start = shard * slice_width
    codes = jnp.concatenate(grad_cols)
    power = codes[:, slice_width : slice_width + 1].astype(jnp.float32)
    grad_cols = codes[:, :slice_width].astype(jnp.float32) * jnp.exp(power * per_step)
    hidden_cols = lax.dynamic_slice_in_dim(hidden, col_start, slice_width, 1).astype(jnp.float32)
    gain_cols = lax.dynamic_slice_in_dim(gain, col_start, slice_width, 0)
    grad_hidden = (
        inverse_rms * gain_cols * grad_cols
        - hidden_cols * (inverse_rms * inverse_rms / model_width) * row_term[:, None]
    )
    return (grad_hidden, log_refusal)


def solution(mesh):
    return jax.shard_map(
        shards,
        mesh=mesh,
        in_specs=(
            P("prompt", None),
            P("prompt", "vocab"),
            P(),
            P("prompt", None),
            P("prompt"),
            P("prompt"),
        ),
        out_specs=(P("prompt", "vocab"), P("prompt")),
        check_vma=False,
    )
```

time: 1460 us -> 310 us (0.21)
  waiting for transfers between devices: 1180 us -> 87.9 us
  Pallas kernels: 0 us -> 107 us
  matrix products: 101 us -> 0 us
  local copies, waits for them, and re-layouts: 82.8 us -> 17.7 us
  starting transfers between devices: 0.08 us -> 44.6 us
  other arithmetic: 30.2 us -> 6.53 us
    all_gather x1 -> x0, waiting for transfers between devices: 1140 us -> none  [shards(): lax.all_gather(head, 'prompt', axis=0, tiled=True)]
    pallas_call x0 -> x16, Pallas kernels: none -> 107 us  [the longest x3 35.5 us: back(): pl.pallas_call(functools.partial(back_kernel, tiles, bool(started), bool(...]
    dot_general x2 -> x0, matrix products: 101 us -> none  [the longest x1 55.6 us: shards(): lax.dot_general(grad_b, lax.all_gather(head, 'prompt', axis=0, tiled=True...]
    ppermute x0 -> x33, waiting for transfers between devices: none -> 87.9 us  [the longest x23 59.8 us: shards(): send = lambda value, pairs: lax.ppermute(value, 'prompt', pairs)]
    gather x3 -> x0, local copies, waits for them, and re-layouts: 82.1 us -> none  [shards(): picked = jnp.take_along_axis(logits, safe_ids, axis=1)]
    reduce_scatter x1 -> x0, waiting for transfers between devices: 45.5 us -> none  [shards(): lax.psum_scatter(grad_full, 'vocab', scatter_dimension=1, tiled=True)]
    ppermute x0 -> x33, starting transfers between devices: none -> 44.6 us  [the longest x23 25.8 us: shards(): send = lambda value, pairs: lax.ppermute(value, 'prompt', pairs)]
    all_gather x0 -> x3, blocking collectives: none -> 44.5 us  [the longest x2 28.7 us: shards(): stats = lax.all_gather(stats, 'vocab', axis=0)]
  transfers between devices with their start and end apart: 2 -> 33, of which waited for: 2 -> 9; matrix products, arithmetic and copies ran while one was open for 0% -> 1% of each run, Pallas kernels for 0% -> 29%
where the time goes in v3:
time: 310 us; the launch traced here: 309 us
  Pallas kernels  107 us (35%)
  waiting for transfers between devices  87.9 us (28%)
  starting transfers between devices  44.6 us (14%)
  blocking collectives  44.5 us (14%)
  local copies, waits for them, and re-layouts  17.7 us (6%)
  other arithmetic  6.53 us (2%)
    ppermute x23, waiting for transfers between devices, shards(): send = lambda value, pairs: lax.ppermute(value, 'prompt', pairs)  59.8 us
    pallas_call x3, Pallas kernels, back(): pl.pallas_call(functools.partial(back_kernel, tiles, bool(started), bool(...  35.5 us
    pallas_call x3, Pallas kernels, near_codes(): pl.pallas_call(functools.partial(near_kernel, width, len(by_x)), grid=(ti...  34.7 us
    all_gather x2, blocking collectives, shards(): stats = lax.all_gather(stats, 'vocab', axis=0)  28.7 us
    ppermute x23, starting transfers between devices, shards(): send = lambda value, pairs: lax.ppermute(value, 'prompt', pairs)  25.8 us
    ppermute x8, waiting for transfers between devices, shards(): lax.ppermute(c, 'vocab', to)  20.6 us
    all_gather x1, blocking collectives, shards(): terms = lax.all_gather(info, 'vocab', axis=0)  15.8 us
    pallas_call x2, Pallas kernels, far_codes(): pl.pallas_call(functools.partial(far_kernel, width), grid=(tiles,), in_sp...  15.4 us
  transfers between devices with their start and end apart: 33, of which 9 were waited for; matrix products, arithmetic and copies ran while one was open for 1% of the time, Pallas kernels for 29%

profile of v3, /device:TPU:2, one launch (start us, length us, event | category | flops | bytes accessed | tf_op | source)
XLA Modules:
  0.0 308.7 jit_solution(1118192721636599007)
XLA Ops:
  0.7 2.2 fusion
  2.9 1.9 fusion.2
  4.9 1.7 constant_dynamic-slice_fusion
  6.6 1.6 collective-permute-start.2
  8.1 13.1 %collective-permute-done.2.x_ref = bf16[128,2048]{1,0:T(8,128)(2,1)S(1)} collective-permute-done((bf16[128,2048]{1,0:T(8,128)(2,1)S(1)}, bf16[128,2048]{1,0:T(8,128)(2,1)S(1)}, u32[]{:S(2)}, u32[]{:S(2)}) %collective-permute-start.2) | collective-permute-done | bytes 524320 | tf_op jit(solution)/shard_map/ppermute | solution.py:403
  21.2 7.7 %far_codes.2 = (s16[64,4224]{1,0:T(8,128)(2,1)S(1)}, s16[64,4224]{1,0:T(8,128)(2,1)S(1)}) custom-call(bf16[128,2048]{1,0:T(8,128)(2,1)S(1)} %collective-permute-done.2.x_ref, bf16[2048,8192]{1,0:T(8,128)(2,1)} %refs_5_.5), custom_call_target="tpu_custom_call" | custom-call | flops 1024 | bytes 1024 | tf_op jit(solution)/shard_map/far_codes/pallas_call | solution.py:77
  29.3 1.7 collective-permute-start.4
  31.0 1.5 collective-permute-start
  33.0 7.7 %far_codes.3 = (s16[64,4224]{1,0:T(8,128)(2,1)S(1)}, s16[64,4224]{1,0:T(8,128)(2,1)S(1)}) custom-call(bf16[128,2048]{1,0:T(8,128)(2,1)S(1)} %collective-permute-done.2.x_ref, bf16[2048,8192]{1,0:T(8,128)(2,1)} %refs_5_.5), custom_call_target="tpu_custom_call" | custom-call | flops 1024 | bytes 1024 | tf_op jit(solution)/shard_map/far_codes/pallas_call | solution.py:77
  41.1 14.3 %collective-permute-done.x_ref = bf16[128,2048]{1,0:T(8,128)(2,1)S(1)} collective-permute-done((bf16[128,2048]{1,0:T(8,128)(2,1)S(1)}, bf16[128,2048]{1,0:T(8,128)(2,1)S(1)}, u32[]{:S(2)}, u32[]{:S(2)}) %collective-permute-start) | collective-permute-done | bytes 524320 | tf_op jit(solution)/shard_map/ppermute | solution.py:403
  55.4 1.5 collective-permute-start.6
  56.9 9.0 %near_codes.3 = (s16[64,4224]{1,0:T(8,128)(2,1)S(1)}, s16[64,4224]{1,0:T(8,128)(2,1)}, f32[64,4096]{1,0:T(8,128)S(1)}) custom-call(bf16[128,2048]{1,0:T(8,128)(2,1)S(1)} %collective-permute-done.x_ref, bf16[128,2048]{1,0:T(8,128)(2,1)S(1)} %collective-permute-done.1.y_ref, bf16[128,2048]{1,0:T(8,128)(2,1)S(1)} %get-tuple-element.63.own_ref, ...), custom_call_target="tpu_custom_call" | custom-call | flops 1024 | bytes 1024 | tf_op jit(solution)/shard_map/near_codes/pallas_call | solution.py:127
  66.5 9.2 %near_codes.4 = (s16[64,4224]{1,0:T(8,128)(2,1)}, s16[64,4224]{1,0:T(8,128)(2,1)}, f32[64,4096]{1,0:T(8,128)S(1)}) custom-call(bf16[128,2048]{1,0:T(8,128)(2,1)S(1)} %collective-permute-done.x_ref, bf16[128,2048]{1,0:T(8,128)(2,1)S(1)} %collective-permute-done.1.y_ref, bf16[128,2048]{1,0:T(8,128)(2,1)S(1)} %get-tuple-element.63.own_ref, ...), custom_call_target="tpu_custom_call" | custom-call | flops 1024 | bytes 1024 | tf_op jit(solution)/shard_map/near_codes/pallas_call | solution.py:127
  75.6 1.0 copy-done.10
  76.7 1.5 collective-permute-start.8
  78.6 1.5 collective-permute-start.10
  80.2 16.6 %near_codes.5 = (s16[64,8320]{1,0:T(8,128)(2,1)}, s16[64,8320]{1,0:T(8,128)(2,1)}, f32[64,8192]{1,0:T(8,128)S(1)}) custom-call(bf16[128,2048]{1,0:T(8,128)(2,1)S(1)} %collective-permute-done.x_ref, bf16[128,2048]{1,0:T(8,128)(2,1)S(1)} %collective-permute-done.1.y_ref, bf16[128,2048]{1,0:T(8,128)(2,1)S(1)} %get-tuple-element.63.own_ref, ...), custom_call_target="tpu_custom_call" | custom-call | flops 1024 | bytes 1024 | tf_op jit(solution)/shard_map/near_codes/pallas_call | solution.py:127
  97.3 0.8 copy-done.12
  98.1 1.6 collective-permute-start.21
  100.0 3.4 %collective-permute-done.10.refs_5_ = s16[64,4224]{1,0:T(8,128)(2,1)} collective-permute-done((s16[64,4224]{1,0:T(8,128)(2,1)}, s16[64,4224]{1,0:T(8,128)(2,1)}, u32[]{:S(2)}, u32[]{:S(2)}) %collective-permute-start.10) | collective-permute-done | bytes 540704 | tf_op jit(solution)/shard_map/ppermute | solution.py:403
  103.4 1.2 copy-done.9
  104.6 1.2 copy-done.11
  105.9 1.0 copy-done.13
  106.9 6.9 %row_stats.2 = (f32[64,8192]{1,0:T(8,128)S(1)}, f32[64,8192]{1,0:T(8,128)S(1)}, f32[64,128]{1,0:T(8,128)S(1)}) custom-call(f32[64,4096]{1,0:T(8,128)S(1)} %copy-done.9, f32[64,4096]{1,0:T(8,128)S(1)} %copy-done.11, s16[64,4224]{1,0:T(8,128)(2,1)S(1)} %copy-done.13, s16[64,4224]{1,0:T(8,128)(2,1)} %collective-permute-done.8.refs_3_, ...), custom_call_target="tpu_custom_call" | custom-call | flops 1024 | bytes 1024 | tf_op jit(solution)/shard_map/row_stats/pallas_call | solution.py:194
  113.8 14.2 %all-gather = f32[512,128]{1,0:T(8,128)S(1)} all-gather(f32[64,128]{1,0:T(8,128)S(1)} %get-tuple-element.54), channel_id=2, replica_groups=mesh['prompt'=4,'vocab'=8] {'vocab'}, dimensions={0}, use_global_device_ids=true | all-gather | bytes 294912 | tf_op jit(solution)/shard_map/all_gather | solution.py:455
  128.1 2.1 logit_grads.2
  130.2 0.9 collective-permute-start.12
  131.1 2.8 collective-permute-start.11
  133.9 6.8 %row_stats.3 = (f32[64,8192]{1,0:T(8,128)S(1)}, f32[64,8192]{1,0:T(8,128)S(1)}, f32[64,128]{1,0:T(8,128)S(1)}) custom-call(f32[64,8192]{1,0:T(8,128)S(1)} %get-tuple-element.64.refs_0_, s16[64,8320]{1,0:T(8,128)(2,1)S(1)} %collective-permute-done.20.refs_1_, s16[64,8320]{1,0:T(8,128)(2,1)} %collective-permute-done.21.refs_2_, ...), custom_call_target="tpu_custom_call" | custom-call | flops 1024 | bytes 1024 | tf_op jit(solution)/shard_map/row_stats/pallas_call | solution.py:194
  140.8 14.4 %all-gather.1 = f32[512,128]{1,0:T(8,128)S(1)} all-gather(f32[64,128]{1,0:T(8,128)S(1)} %get-tuple-element.70), channel_id=3, replica_groups=mesh['prompt'=4,'vocab'=8] {'vocab'}, dimensions={0}, use_global_device_ids=true | all-gather | bytes 294912 | tf_op jit(solution)/shard_map/all_gather | solution.py:455
  155.2 2.1 logit_grads.3
  157.8 0.8 slice.40
  158.7 1.0 copy-done
  159.7 1.8 collective-permute-start.13
  161.5 0.8 slice.41
  162.3 1.0 copy-done.2
  163.3 1.8 collective-permute-start.14
  165.2 28.9 %collective-permute-done.13.refs_3_ = bf16[32,8192]{1,0:T(8,128)(2,1)} collective-permute-done((bf16[32,8192]{1,0:T(8,128)(2,1)}, bf16[32,8192]{1,0:T(8,128)(2,1)}, u32[]{:S(2)}, u32[]{:S(2)}) %collective-permute-start.13) | collective-permute-done | bytes 524320 | tf_op jit(solution)/shard_map/ppermute | solution.py:403
  194.2 1.2 copy-done.1
  195.4 1.2 copy-done.3
  196.7 1.2 copy-done.5
  197.9 16.7 %grad_rows.3 = (f32[256,1024]{1,0:T(8,128)S(1)}, s16[256,1152]{1,0:T(8,128)(2,1)S(1)}) custom-call(s32[1]{0:T(128)} %bitcast.4.place_ref, bf16[64,8192]{1,0:T(8,128)(2,1)S(1)} %copy-done.5, bf16[64,8192]{1,0:T(8,128)(2,1)S(1)} %copy-done.3, bf16[64,8192]{1,0:T(8,128)(2,1)S(1)} %copy-done.1, bf16[32,8192]{1,0:T(8,128)(2,1)} %collective-permute-done.13.refs_3_, ...), custom_call_target="tpu_custom_call" | custom-call | flops 1024 | bytes 1024 | tf_op jit(solution)/shard_map/grad_rows/pallas_call | solution.py:316
  214.7 1.7 collective-permute-start.24
  217.2 1.7 collective-permute-start.27
  218.9 15.8 %all-gather.2 = f32[1024,128]{1,0:T(8,128)} all-gather(f32[128,128]{1,0:T(8,128)S(1)} %constant_dynamic-update-slice_fusion), channel_id=4, replica_groups=mesh['prompt'=4,'vocab'=8] {'vocab'}, dimensions={0}, use_global_device_ids=true | all-gather | bytes 589824 | tf_op jit(solution)/shard_map/all_gather | solution.py:460
  234.8 1.6 group_sum.2
  236.4 8.9 %grad_rows.4.refs_6_ = f32[256,2048]{1,0:T(8,128)S(1)} custom-call(s32[1]{0:T(128)} %bitcast.4.place_ref, bf16[64,8192]{1,0:T(8,128)(2,1)S(1)} %get-tuple-element.73.refs_0_, bf16[64,8192]{1,0:T(8,128)(2,1)S(1)} %collective-permute-done.22.refs_1_, bf16[64,8192]{1,0:T(8,128)(2,1)S(1)} %collective-permute-done.23.refs_2_, ...), custom_call_target="tpu_custom_call" | custom-call | flops 1024 | bytes 1024 | tf_op jit(solution)/shard_map/grad_rows/pallas_call | solution.py:316
  245.3 9.9 %grad_rows.5 = (f32[256,1024]{1,0:T(8,128)S(1)}, s16[256,1152]{1,0:T(8,128)(2,1)}) custom-call(s32[1]{0:T(128)} %bitcast.4.place_ref, bf16[64,8192]{1,0:T(8,128)(2,1)S(1)} %get-tuple-element.73.refs_0_, bf16[64,8192]{1,0:T(8,128)(2,1)S(1)} %collective-permute-done.22.refs_1_, bf16[64,8192]{1,0:T(8,128)(2,1)S(1)} %collective-permute-done.23.refs_2_, ...), custom_call_target="tpu_custom_call" | custom-call | flops 1024 | bytes 1024 | tf_op jit(solution)/shard_map/grad_rows/pallas_call | solution.py:316
  255.2 1.0 copy-done.6
  256.6 1.1 collective-permute-start.16
  257.7 2.4 collective-permute-start.17
  260.2 0.8 collective-permute-start.18
  261.0 4.2 %collective-permute-done.16.refs_0_ = s16[64,1152]{1,0:T(8,128)(2,1)S(1)} collective-permute-done((s16[64,1152]{1,0:T(8,128)(2,1)}, s16[64,1152]{1,0:T(8,128)(2,1)S(1)}, u32[]{:S(2)}, u32[]{:S(2)}) %collective-permute-start.16) | collective-permute-done | bytes 147488 | tf_op jit(solution)/shard_map/ppermute | solution.py:489
  265.1 6.8 %collective-permute-done.17.refs_1_ = s16[64,1152]{1,0:T(8,128)(2,1)S(1)} collective-permute-done((s16[64,1152]{1,0:T(8,128)(2,1)}, s16[64,1152]{1,0:T(8,128)(2,1)S(1)}, u32[]{:S(2)}, u32[]{:S(2)}) %collective-permute-start.17) | collective-permute-done | bytes 147488 | tf_op jit(solution)/shard_map/ppermute | solution.py:489
  272.2 5.7 %collective-permute-start.19 = (s16[64,1152]{1,0:T(8,128)(2,1)S(1)}, s16[64,1152]{1,0:T(8,128)(2,1)S(1)}, u32[]{:S(2)}, u32[]{:S(2)}) collective-permute-start(s16[64,1152]{1,0:T(8,128)(2,1)S(1)} %last_sum.2), channel_id=1, source_target_pairs={{0,0},{1,1},{2,8},{3,9},{4,16},{5,17},{6,24},{7,25},{8,2},{9,3},{1... | collective-permute-start | bytes 442376 | tf_op jit(solution)/shard_map/ppermute | solution.py:490
  277.9 1.2 copy-done.7
  279.1 0.9 group_sum.3
  280.1 1.7 collective-permute-start.30
  281.8 2.7 collective-permute-start.31
  284.5 0.7 slice_reduce_fusion.1
  285.3 9.7 %collective-permute-done.30.refs_1_ = s16[64,1152]{1,0:T(8,128)(2,1)S(1)} collective-permute-done((s16[64,1152]{1,0:T(8,128)(2,1)S(1)}, s16[64,1152]{1,0:T(8,128)(2,1)S(1)}, u32[]{:S(2)}, u32[]{:S(2)}) %collective-permute-start.30) | collective-permute-done | bytes 147488 | tf_op jit(solution)/shard_map/ppermute | solution.py:489
  295.2 3.9 %collective-permute-start.32 = (s16[64,1152]{1,0:T(8,128)(2,1)S(1)}, s16[64,1152]{1,0:T(8,128)(2,1)S(1)}, u32[]{:S(2)}, u32[]{:S(2)}) collective-permute-start(s16[64,1152]{1,0:T(8,128)(2,1)S(1)} %last_sum.3), channel_id=1, source_target_pairs={{0,0},{1,1},{2,8},{3,9},{4,16},{5,17},{6,24},{7,25},{8,2},{9,3},{1... | collective-permute-start | bytes 442376 | tf_op jit(solution)/shard_map/ppermute | solution.py:490
  299.1 7.5 %collective-permute-done.32 = s16[64,1152]{1,0:T(8,128)(2,1)S(1)} collective-permute-done((s16[64,1152]{1,0:T(8,128)(2,1)S(1)}, s16[64,1152]{1,0:T(8,128)(2,1)S(1)}, u32[]{:S(2)}, u32[]{:S(2)}) %collective-permute-start.32) | collective-permute-done | bytes 147488 | tf_op jit(solution)/shard_map/ppermute | solution.py:490
  306.7 2.0 multiply_subtract_fusion
  (84 shorter events, 6.0 us)
Async XLA Ops:
  0.6 2.3 copy-start.14
  0.6 2.3 copy-start.16
  6.6 14.6 %collective-permute-start.2 = (bf16[128,2048]{1,0:T(8,128)(2,1)S(1)}, bf16[128,2048]{1,0:T(8,128)(2,1)S(1)}, u32[]{:S(2)}, u32[]{:S(2)}) collective-permute-start(bf16[128,2048]{1,0:T(8,128)(2,1)S(1)} %get-tuple-element.82), channel_id=1, source_target_pairs={{0,24},{8,16},{16,8},{24,0},{1,25},{9,17},{17,9},{25,1},{2,26},{10... | collective-permute-start | bytes 1572872 | tf_op jit(solution)/shard_map/ppermute | solution.py:403
  28.9 28.0 %collective-permute-start.3 = (s16[64,4224]{1,0:T(8,128)(2,1)S(1)}, s16[64,4224]{1,0:T(8,128)(2,1)S(1)}, u32[]{:S(2)}, u32[]{:S(2)}) collective-permute-start(s16[64,4224]{1,0:T(8,128)(2,1)S(1)} %get-tuple-element.42), channel_id=1, source_target_pairs={{0,8},{8,0},{16,24},{24,16},{1,9},{9,1},{17,25},{25,17},{2,10},{10... | collective-permute-start | bytes 1622024 | tf_op jit(solution)/shard_map/ppermute | solution.py:403
  29.3 27.6 %collective-permute-start.4 = (s16[64,4224]{1,0:T(8,128)(2,1)S(1)}, s16[64,4224]{1,0:T(8,128)(2,1)S(1)}, u32[]{:S(2)}, u32[]{:S(2)}) collective-permute-start(s16[64,4224]{1,0:T(8,128)(2,1)S(1)} %get-tuple-element.43), channel_id=1, source_target_pairs={{0,16},{8,24},{16,0},{24,8},{1,17},{9,25},{17,1},{25,9},{2,18},{10... | collective-permute-start | bytes 1622024 | tf_op jit(solution)/shard_map/ppermute | solution.py:403
  31.0 24.4 %collective-permute-start = (bf16[128,2048]{1,0:T(8,128)(2,1)S(1)}, bf16[128,2048]{1,0:T(8,128)(2,1)S(1)}, u32[]{:S(2)}, u32[]{:S(2)}) collective-permute-start(bf16[128,2048]{1,0:T(8,128)(2,1)S(1)} %get-tuple-element.85), channel_id=1, source_target_pairs={{0,8},{8,0},{16,24},{24,16},{1,9},{9,1},{17,25},{25,17},{2,10},{10... | collective-permute-start | bytes 1572872 | tf_op jit(solution)/shard_map/ppermute | solution.py:403
  32.5 24.4 %collective-permute-start.1 = (bf16[128,2048]{1,0:T(8,128)(2,1)S(1)}, bf16[128,2048]{1,0:T(8,128)(2,1)S(1)}, u32[]{:S(2)}, u32[]{:S(2)}) collective-permute-start(bf16[128,2048]{1,0:T(8,128)(2,1)S(1)} %get-tuple-element.84), channel_id=1, source_target_pairs={{0,16},{8,24},{16,0},{24,8},{1,17},{9,25},{17,1},{25,9},{2,18},{10... | collective-permute-start | bytes 1572872 | tf_op jit(solution)/shard_map/ppermute | solution.py:403
  40.7 25.7 %collective-permute-start.5 = (s16[64,4224]{1,0:T(8,128)(2,1)S(1)}, s16[64,4224]{1,0:T(8,128)(2,1)S(1)}, u32[]{:S(2)}, u32[]{:S(2)}) collective-permute-start(s16[64,4224]{1,0:T(8,128)(2,1)S(1)} %get-tuple-element.45), channel_id=1, source_target_pairs={{0,8},{8,0},{16,24},{24,16},{1,9},{9,1},{17,25},{25,17},{2,10},{10... | collective-permute-start | bytes 1622024 | tf_op jit(solution)/shard_map/ppermute | solution.py:403
  55.4 11.1 %collective-permute-start.6 = (s16[64,4224]{1,0:T(8,128)(2,1)S(1)}, s16[64,4224]{1,0:T(8,128)(2,1)S(1)}, u32[]{:S(2)}, u32[]{:S(2)}) collective-permute-start(s16[64,4224]{1,0:T(8,128)(2,1)S(1)} %get-tuple-element.46), channel_id=1, source_target_pairs={{0,16},{8,24},{16,0},{24,8},{1,17},{9,25},{17,1},{25,9},{2,18},{10... | collective-permute-start | bytes 1622024 | tf_op jit(solution)/shard_map/ppermute | solution.py:403
  65.9 9.7 %copy-start.8 = (f32[64,4096]{1,0:T(8,128)}, f32[64,4096]{1,0:T(8,128)S(1)}, u32[]{:S(2)}) copy-start(f32[64,4096]{1,0:T(8,128)S(1)} %get-tuple-element.44.refs_0_) | copy-start | bytes 3145732
  65.9 31.4 %collective-permute-start.7 = (s16[64,4224]{1,0:T(8,128)(2,1)S(1)}, s16[64,4224]{1,0:T(8,128)(2,1)S(1)}, u32[]{:S(2)}, u32[]{:S(2)}) collective-permute-start(s16[64,4224]{1,0:T(8,128)(2,1)S(1)} %get-tuple-element.48), channel_id=1, source_target_pairs={{0,8},{8,0},{16,24},{24,16},{1,9},{9,1},{17,25},{25,17},{2,10},{10... | collective-permute-start | bytes 1622024 | tf_op jit(solution)/shard_map/ppermute | solution.py:403
  75.6 1.0 copy-start.10
  76.7 23.4 %collective-permute-start.8 = (s16[64,4224]{1,0:T(8,128)(2,1)}, s16[64,4224]{1,0:T(8,128)(2,1)}, u32[]{:S(2)}, u32[]{:S(2)}) collective-permute-start(s16[64,4224]{1,0:T(8,128)(2,1)} %get-tuple-element.49), channel_id=1, source_target_pairs={{0,8},{8,0},{16,24},{24,16},{1,9},{9,1},{17,25},{25,17},{2,10},{10... | collective-permute-start | bytes 1622024 | tf_op jit(solution)/shard_map/ppermute | solution.py:403
  78.1 21.9 %collective-permute-start.9 = (s16[64,4224]{1,0:T(8,128)(2,1)}, s16[64,4224]{1,0:T(8,128)(2,1)}, u32[]{:S(2)}, u32[]{:S(2)}) collective-permute-start(s16[64,4224]{1,0:T(8,128)(2,1)} %get-tuple-element.50), channel_id=1, source_target_pairs={{0,16},{8,24},{16,0},{24,8},{1,17},{9,25},{17,1},{25,9},{2,18},{10... | collective-permute-start | bytes 1622024 | tf_op jit(solution)/shard_map/ppermute | solution.py:403
  78.6 24.8 %collective-permute-start.10 = (s16[64,4224]{1,0:T(8,128)(2,1)}, s16[64,4224]{1,0:T(8,128)(2,1)}, u32[]{:S(2)}, u32[]{:S(2)}) collective-permute-start(s16[64,4224]{1,0:T(8,128)(2,1)} %get-tuple-element.51), channel_id=1, source_target_pairs={{0,16},{8,24},{16,0},{24,8},{1,17},{9,25},{17,1},{25,9},{2,18},{10... | collective-permute-start | bytes 1622024 | tf_op jit(solution)/shard_map/ppermute | solution.py:403
  80.2 19.5 %copy-start.17 = (s32[128,16]{0,1:T(8,128)S(1)}, s32[128,16]{0,1:T(8,128)}, u32[]{:S(2)}) copy-start(s32[128,16]{0,1:T(8,128)} %param.9) | copy-start | bytes 24580
  80.2 19.6 %copy-start.18 = (s32[128]{0:T(128)S(1)}, s32[128]{0:T(128)}, u32[]{:S(2)}) copy-start(s32[128]{0:T(128)} %param.10) | copy-start | bytes 1540
  80.2 19.7 %copy-start.19 = (f32[128]{0:T(128)S(1)}, f32[128]{0:T(128)}, u32[]{:S(2)}) copy-start(f32[128]{0:T(128)} %param.11) | copy-start | bytes 1540
  96.7 37.2 %collective-permute-start.20 = (s16[64,8320]{1,0:T(8,128)(2,1)}, s16[64,8320]{1,0:T(8,128)(2,1)S(1)}, u32[]{:S(2)}, u32[]{:S(2)}) collective-permute-start(s16[64,8320]{1,0:T(8,128)(2,1)} %get-tuple-element.65), channel_id=1, source_target_pairs={{0,8},{8,0},{16,24},{24,16},{1,9},{9,1},{17,25},{25,17},{2,10},{10... | collective-permute-start | bytes 3194888 | tf_op jit(solution)/shard_map/ppermute | solution.py:403
  97.3 0.8 copy-start.12
  98.1 35.9 %collective-permute-start.21 = (s16[64,8320]{1,0:T(8,128)(2,1)}, s16[64,8320]{1,0:T(8,128)(2,1)}, u32[]{:S(2)}, u32[]{:S(2)}) collective-permute-start(s16[64,8320]{1,0:T(8,128)(2,1)} %get-tuple-element.66), channel_id=1, source_target_pairs={{0,16},{8,24},{16,0},{24,8},{1,17},{9,25},{17,1},{25,9},{2,18},{10... | collective-permute-start | bytes 3194888 | tf_op jit(solution)/shard_map/ppermute | solution.py:403
  103.4 1.2 copy-start.9
  104.6 1.2 copy-start.11
  105.9 1.0 copy-start.13
  130.2 10.5 %copy-start.4 = (bf16[64,8192]{1,0:T(8,128)(2,1)}, bf16[64,8192]{1,0:T(8,128)(2,1)S(1)}, u32[]{:S(2)}) copy-start(bf16[64,8192]{1,0:T(8,128)(2,1)S(1)} %get-tuple-element.55.refs_0_) | copy-start | bytes 3145732
  130.2 27.6 %collective-permute-start.12 = (bf16[64,8192]{1,0:T(8,128)(2,1)S(1)}, bf16[64,8192]{1,0:T(8,128)(2,1)S(1)}, u32[]{:S(2)}, u32[]{:S(2)}) collective-permute-start(bf16[64,8192]{1,0:T(8,128)(2,1)S(1)} %get-tuple-element.55.refs_0_), channel_id=1, source_target_pairs={{0,16},{8,24},{16,0},{24,8},{1,17},{9,25},{17,1},{25,9},{2,18},{10... | collective-permute-start | bytes 3145736 | tf_op jit(solution)/shard_map/ppermute | solution.py:403
  131.1 30.4 %collective-permute-start.11 = (bf16[64,8192]{1,0:T(8,128)(2,1)S(1)}, bf16[64,8192]{1,0:T(8,128)(2,1)S(1)}, u32[]{:S(2)}, u32[]{:S(2)}) collective-permute-start(bf16[64,8192]{1,0:T(8,128)(2,1)S(1)} %get-tuple-element.55.refs_0_), channel_id=1, source_target_pairs={{0,8},{8,0},{16,24},{24,16},{1,9},{9,1},{17,25},{25,17},{2,10},{10... | collective-permute-start | bytes 3145736 | tf_op jit(solution)/shard_map/ppermute | solution.py:403
  157.4 57.3 %collective-permute-start.22 = (bf16[64,8192]{1,0:T(8,128)(2,1)S(1)}, bf16[64,8192]{1,0:T(8,128)(2,1)S(1)}, u32[]{:S(2)}, u32[]{:S(2)}) collective-permute-start(bf16[64,8192]{1,0:T(8,128)(2,1)S(1)} %get-tuple-element.73.refs_0_), channel_id=1, source_target_pairs={{0,8},{8,0},{16,24},{24,16},{1,9},{9,1},{17,25},{25,17},{2,10},{10... | collective-permute-start | bytes 3145736 | tf_op jit(solution)/shard_map/ppermute | solution.py:403
  157.4 57.3 %collective-permute-start.23 = (bf16[64,8192]{1,0:T(8,128)(2,1)S(1)}, bf16[64,8192]{1,0:T(8,128)(2,1)S(1)}, u32[]{:S(2)}, u32[]{:S(2)}) collective-permute-start(bf16[64,8192]{1,0:T(8,128)(2,1)S(1)} %get-tuple-element.73.refs_0_), channel_id=1, source_target_pairs={{0,16},{8,24},{16,0},{24,8},{1,17},{9,25},{17,1},{25,9},{2,18},{10... | collective-permute-start | bytes 3145736 | tf_op jit(solution)/shard_map/ppermute | solution.py:403
  158.7 1.0 copy-start
  159.7 34.5 %collective-permute-start.13 = (bf16[32,8192]{1,0:T(8,128)(2,1)}, bf16[32,8192]{1,0:T(8,128)(2,1)}, u32[]{:S(2)}, u32[]{:S(2)}) collective-permute-start(bf16[32,8192]{1,0:T(8,128)(2,1)} %slice.40), channel_id=1, source_target_pairs={{0,8},{8,0},{16,24},{24,16},{1,9},{9,1},{17,25},{25,17},{2,10},{10... | collective-permute-start | bytes 1572872 | tf_op jit(solution)/shard_map/ppermute | solution.py:403
  162.3 1.0 copy-start.2
  163.3 30.9 %collective-permute-start.14 = (bf16[32,8192]{1,0:T(8,128)(2,1)}, bf16[32,8192]{1,0:T(8,128)(2,1)}, u32[]{:S(2)}, u32[]{:S(2)}) collective-permute-start(bf16[32,8192]{1,0:T(8,128)(2,1)} %slice.41), channel_id=1, source_target_pairs={{0,16},{8,24},{16,0},{24,8},{1,17},{9,25},{17,1},{25,9},{2,18},{10... | collective-permute-start | bytes 1572872 | tf_op jit(solution)/shard_map/ppermute | solution.py:403
  194.2 1.2 copy-start.1
  195.4 1.2 copy-start.3
  196.7 1.2 copy-start.5
  214.6 20.2 %collective-permute-start.15 = (s16[256,1152]{1,0:T(8,128)(2,1)S(1)}, s16[256,1152]{1,0:T(8,128)(2,1)S(1)}, u32[]{:S(2)}, u32[]{:S(2)}) collective-permute-start(s16[256,1152]{1,0:T(8,128)(2,1)S(1)} %get-tuple-element.57), channel_id=1, source_target_pairs={{0,1},{1,0},{2,3},{3,2},{4,5},{5,4},{6,7},{7,6},{8,9},{9,8},{10,11... | collective-permute-start | bytes 1769480 | tf_op jit(solution)/shard_map/ppermute | solution.py:486
  214.7 30.6 %collective-permute-start.24 = (bf16[32,4096]{1,0:T(8,128)(2,1)S(1)}, bf16[32,4096]{1,0:T(8,128)(2,1)S(1)}, u32[]{:S(2)}, u32[]{:S(2)}) collective-permute-start(bf16[32,4096]{1,0:T(8,128)(2,1)S(1)} %get-tuple-element.89), channel_id=1, source_target_pairs={{0,8},{8,0},{16,24},{24,16},{1,9},{9,1},{17,25},{25,17},{2,10},{10... | collective-permute-start | bytes 786440 | tf_op jit(solution)/shard_map/ppermute | solution.py:403
  216.5 28.8 %collective-permute-start.25 = (bf16[32,4096]{1,0:T(8,128)(2,1)S(1)}, bf16[32,4096]{1,0:T(8,128)(2,1)S(1)}, u32[]{:S(2)}, u32[]{:S(2)}) collective-permute-start(bf16[32,4096]{1,0:T(8,128)(2,1)S(1)} %get-tuple-element.87), channel_id=1, source_target_pairs={{0,16},{8,24},{16,0},{24,8},{1,17},{9,25},{17,1},{25,9},{2,18},{10... | collective-permute-start | bytes 786440 | tf_op jit(solution)/shard_map/ppermute | solution.py:403
  216.8 19.6 %collective-permute-start.26 = (bf16[32,4096]{1,0:T(8,128)(2,1)S(1)}, bf16[32,4096]{1,0:T(8,128)(2,1)S(1)}, u32[]{:S(2)}, u32[]{:S(2)}) collective-permute-start(bf16[32,4096]{1,0:T(8,128)(2,1)S(1)} %get-tuple-element.88), channel_id=1, source_target_pairs={{0,8},{8,0},{16,24},{24,16},{1,9},{9,1},{17,25},{25,17},{2,10},{10... | collective-permute-start | bytes 786440 | tf_op jit(solution)/shard_map/ppermute | solution.py:403
  217.2 19.2 %collective-permute-start.27 = (bf16[32,4096]{1,0:T(8,128)(2,1)S(1)}, bf16[32,4096]{1,0:T(8,128)(2,1)S(1)}, u32[]{:S(2)}, u32[]{:S(2)}) collective-permute-start(bf16[32,4096]{1,0:T(8,128)(2,1)S(1)} %get-tuple-element.86), channel_id=1, source_target_pairs={{0,16},{8,24},{16,0},{24,8},{1,17},{9,25},{17,1},{25,9},{2,18},{10... | collective-permute-start | bytes 786440 | tf_op jit(solution)/shard_map/ppermute | solution.py:403
  255.2 1.0 copy-start.6
  256.2 28.9 %copy-start.15 = (f32[1024,128]{1,0:T(8,128)S(1)}, f32[1024,128]{1,0:T(8,128)}, u32[]{:S(2)}) copy-start(f32[1024,128]{1,0:T(8,128)} %all-gather.2) | copy-start | bytes 1572868
  256.2 21.6 %collective-permute-start.28 = (s16[256,1152]{1,0:T(8,128)(2,1)}, s16[256,1152]{1,0:T(8,128)(2,1)S(1)}, u32[]{:S(2)}, u32[]{:S(2)}) collective-permute-start(s16[256,1152]{1,0:T(8,128)(2,1)} %get-tuple-element.77), channel_id=1, source_target_pairs={{0,1},{1,0},{2,3},{3,2},{4,5},{5,4},{6,7},{7,6},{8,9},{9,8},{10,11... | collective-permute-start | bytes 1769480 | tf_op jit(solution)/shard_map/ppermute | solution.py:486
  256.6 8.6 %collective-permute-start.16 = (s16[64,1152]{1,0:T(8,128)(2,1)}, s16[64,1152]{1,0:T(8,128)(2,1)S(1)}, u32[]{:S(2)}, u32[]{:S(2)}) collective-permute-start(s16[64,1152]{1,0:T(8,128)(2,1)} %get-tuple-element.59), channel_id=1, source_target_pairs={{0,2},{1,3},{2,0},{3,1},{4,6},{5,7},{6,4},{7,5},{8,10},{9,11},{10,... | collective-permute-start | bytes 442376 | tf_op jit(solution)/shard_map/ppermute | solution.py:489
  257.7 14.2 %collective-permute-start.17 = (s16[64,1152]{1,0:T(8,128)(2,1)}, s16[64,1152]{1,0:T(8,128)(2,1)S(1)}, u32[]{:S(2)}, u32[]{:S(2)}) collective-permute-start(s16[64,1152]{1,0:T(8,128)(2,1)} %get-tuple-element.60), channel_id=1, source_target_pairs={{0,4},{1,5},{2,6},{3,7},{4,0},{5,1},{6,2},{7,3},{8,12},{9,13},{10,... | collective-permute-start | bytes 442376 | tf_op jit(solution)/shard_map/ppermute | solution.py:489
  260.2 11.7 %collective-permute-start.18 = (s16[64,1152]{1,0:T(8,128)(2,1)}, s16[64,1152]{1,0:T(8,128)(2,1)S(1)}, u32[]{:S(2)}, u32[]{:S(2)}) collective-permute-start(s16[64,1152]{1,0:T(8,128)(2,1)} %get-tuple-element.61), channel_id=1, source_target_pairs={{0,6},{1,7},{2,4},{3,5},{4,2},{5,3},{6,0},{7,1},{8,14},{9,15},{10,... | collective-permute-start | bytes 442376 | tf_op jit(solution)/shard_map/ppermute | solution.py:489
  261.0 45.7 %dynamic-slice-start = ((f32[8192]{0:T(1024)}, s32[]{:T(128)}), f32[1024]{0:T(1024)S(1)}, s32[]{:S(2)}) async-start(f32[8192]{0:T(1024)} %param.8, s32[]{:T(128)} %select_n.31), calls=%async_computation | async-start | bytes 8704 | tf_op jit(solution)/shard_map/dynamic_slice | solution.py:500
  272.2 26.9 %collective-permute-start.19 = (s16[64,1152]{1,0:T(8,128)(2,1)S(1)}, s16[64,1152]{1,0:T(8,128)(2,1)S(1)}, u32[]{:S(2)}, u32[]{:S(2)}) collective-permute-start(s16[64,1152]{1,0:T(8,128)(2,1)S(1)} %last_sum.2), channel_id=1, source_target_pairs={{0,0},{1,1},{2,8},{3,9},{4,16},{5,17},{6,24},{7,25},{8,2},{9,3},{1... | collective-permute-start | bytes 442376 | tf_op jit(solution)/shard_map/ppermute | solution.py:490
  277.9 1.2 copy-start.7
  280.0 5.3 %collective-permute-start.29 = (s16[64,1152]{1,0:T(8,128)(2,1)S(1)}, s16[64,1152]{1,0:T(8,128)(2,1)S(1)}, u32[]{:S(2)}, u32[]{:S(2)}) collective-permute-start(s16[64,1152]{1,0:T(8,128)(2,1)S(1)} %get-tuple-element.79), channel_id=1, source_target_pairs={{0,2},{1,3},{2,0},{3,1},{4,6},{5,7},{6,4},{7,5},{8,10},{9,11},{10,... | collective-permute-start | bytes 442376 | tf_op jit(solution)/shard_map/ppermute | solution.py:489
  280.1 14.9 %collective-permute-start.30 = (s16[64,1152]{1,0:T(8,128)(2,1)S(1)}, s16[64,1152]{1,0:T(8,128)(2,1)S(1)}, u32[]{:S(2)}, u32[]{:S(2)}) collective-permute-start(s16[64,1152]{1,0:T(8,128)(2,1)S(1)} %get-tuple-element.80), channel_id=1, source_target_pairs={{0,4},{1,5},{2,6},{3,7},{4,0},{5,1},{6,2},{7,3},{8,12},{9,13},{10,... | collective-permute-start | bytes 442376 | tf_op jit(solution)/shard_map/ppermute | solution.py:489
  281.8 13.2 %collective-permute-start.31 = (s16[64,1152]{1,0:T(8,128)(2,1)S(1)}, s16[64,1152]{1,0:T(8,128)(2,1)S(1)}, u32[]{:S(2)}, u32[]{:S(2)}) collective-permute-start(s16[64,1152]{1,0:T(8,128)(2,1)S(1)} %get-tuple-element.81), channel_id=1, source_target_pairs={{0,6},{1,7},{2,4},{3,5},{4,2},{5,3},{6,0},{7,1},{8,14},{9,15},{10,... | collective-permute-start | bytes 442376 | tf_op jit(solution)/shard_map/ppermute | solution.py:489
  295.2 11.4 %collective-permute-start.32 = (s16[64,1152]{1,0:T(8,128)(2,1)S(1)}, s16[64,1152]{1,0:T(8,128)(2,1)S(1)}, u32[]{:S(2)}, u32[]{:S(2)}) collective-permute-start(s16[64,1152]{1,0:T(8,128)(2,1)S(1)} %last_sum.3), channel_id=1, source_target_pairs={{0,0},{1,1},{2,8},{3,9},{4,16},{5,17},{6,24},{7,25},{8,2},{9,3},{1... | collective-permute-start | bytes 442376 | tf_op jit(solution)/shard_map/ppermute | solution.py:490

commit v4 on v3

--- a/solution.py
+++ b/solution.py
@@ -49,7 +49,7 @@
 
 
 def compiler_params():
-    return pltpu.CompilerParams(vmem_limit_bytes=40 * megabyte)
+    return pltpu.CompilerParams(vmem_limit_bytes=20 * megabyte)
 
 
 def small_cost():
@@ -102,24 +102,23 @@
     return jnp.where(tile < each, low, high)
 
 
-def near_kernel(width, parts, x_ref, y_ref, own_ref, head_ref, *refs):
+def near_kernel(width, parts, x_ref, y_ref, head_ref, *refs):
     by_x_refs, by_y_refs = refs[:parts], refs[parts : 2 * parts]
-    to_x_ref, to_y_ref, out_ref, powers_ref = refs[2 * parts :]
+    to_x_ref, to_y_ref, powers_ref = refs[2 * parts :]
     tile = pl.program_id(0)
     rows = x_ref.shape[0]
     half = rows // 2
     columns = to_x_ref.shape[1] - tail
-    value = dot(jnp.concatenate([x_ref[...], y_ref[...], own_ref[...]], axis=0), head_ref[...])
-    out_ref[...] = value[2 * rows :]
+    value = dot(jnp.concatenate([x_ref[...], y_ref[...]], axis=0), head_ref[...])
     more_x = decode_any(by_y_refs, tile, width)
     more_y = decode_any(by_x_refs, tile, width)
     for_x = jnp.concatenate([value[:half], value[half:rows] + more_x], axis=0)
-    for_y = jnp.concatenate([value[rows : rows + half] + more_y, value[rows + half : 2 * rows]], axis=0)
+    for_y = jnp.concatenate([value[rows : rows + half] + more_y, value[rows + half :]], axis=0)
     put(to_x_ref, powers_ref, slice(0, rows), tile, width, columns, for_x)
     put(to_y_ref, powers_ref, slice(rows, 2 * rows), tile, width, columns, for_y)
 
 
-def near_codes(part, rows_x, rows_y, rows_own, head, by_x, by_y, width, skip, tiles):
+def near_codes(part, rows_x, rows_y, head, by_x, by_y, width, skip, tiles):
     depth = rows_x.shape[1]
     rows = rows_x.shape[0] // 2
     columns = tiles * width
@@ -127,17 +126,38 @@
     return pl.pallas_call(
         functools.partial(near_kernel, width, len(by_x)),
         grid=(tiles,),
-        in_specs=[pl.BlockSpec((rows, depth), lambda j: (part, 0))] * 3
+        in_specs=[pl.BlockSpec((rows, depth), lambda j: (part, 0))] * 2
         + [pl.BlockSpec((depth, width), lambda j: (0, j + skip))]
         + [received] * (2 * len(by_x)),
-        out_specs=[constant(rows, columns + tail)] * 2 + [pl.BlockSpec((rows, width), lambda j: (0, j))],
-        out_shape=[jax.ShapeDtypeStruct((rows, columns + tail), jnp.int16)] * 2
-        + [jax.ShapeDtypeStruct((rows, columns), jnp.float32)],
+        out_specs=[constant(rows, columns + tail)] * 2,
+        out_shape=[jax.ShapeDtypeStruct((rows, columns + tail), jnp.int16)] * 2,
         scratch_shapes=[pltpu.VMEM((2 * rows, tail), jnp.float32)],
         compiler_params=compiler_params(),
         cost_estimate=small_cost(),
         name="near_codes",
-    )(rows_x, rows_y, rows_own, head, *by_x, *by_y)
+    )(rows_x, rows_y, head, *by_x, *by_y)
+
+
+def own_kernel(x_ref, head_ref, out_ref):
+    out_ref[...] = dot(x_ref[...], head_ref[...])
+
+
+def own_logits(rows_in, head, width):
+    rows, depth = rows_in.shape
+    columns = head.shape[1]
+    return pl.pallas_call(
+        own_kernel,
+        grid=(columns // width,),
+        in_specs=[
+            constant(rows, depth),
+            pl.BlockSpec((depth, width), lambda j: (0, j)),
+        ],
+        out_specs=pl.BlockSpec((rows, width), lambda j: (0, j)),
+        out_shape=jax.ShapeDtypeStruct((rows, columns), jnp.float32),
+        compiler_params=compiler_params(),
+        cost_estimate=small_cost(),
+        name="own_logits",
+    )(rows_in, head)
 
 
 def members(ids, start, width):
@@ -150,18 +170,15 @@
 
 
 def stats_kernel(width, parts, *refs):
-    own_refs, by_x_refs, by_y_refs = refs[:parts], refs[parts : 2 * parts], refs[2 * parts : 3 * parts]
-    ids_ref, logits_ref, listed_ref, out_ref = refs[3 * parts :]
+    own_ref, by_x_refs, by_y_refs = refs[0], refs[1 : 1 + parts], refs[1 + parts : 1 + 2 * parts]
+    ids_ref, logits_ref, listed_ref, out_ref = refs[1 + 2 * parts :]
     rows, columns = logits_ref.shape
-    each = columns // parts
     ids = ids_ref[...]
     top_all = jnp.full((rows, width), lowest, jnp.float32)
     top_ref = jnp.full((rows, width), lowest, jnp.float32)
     for start in range(0, columns, width):
         at = slice(start, start + width)
-        inner = start % each
-        piece = own_refs[start // each][:, inner : inner + width]
-        piece = piece + decode_any(by_x_refs, start // width, width)
+        piece = own_ref[:, at] + decode_any(by_x_refs, start // width, width)
         piece = piece + decode_any(by_y_refs, start // width, width)
         listed = jnp.where(members(ids, start, width), piece, lowest)
         logits_ref[:, at] = piece
@@ -185,16 +202,17 @@
 
 
 def row_stats(part, own, by_x, by_y, ids, width):
-    rows = own[0].shape[0]
-    parts = len(own)
-    columns = own[0].shape[1] * parts
+    rows = by_x[0].shape[0]
+    parts = len(by_x)
+    columns = own.shape[1]
     block = min(rows, 16)
     skip = part * (rows // block)
     across = lambda array: pl.BlockSpec((block, array.shape[1]), lambda i: (i, 0))
     return pl.pallas_call(
         functools.partial(stats_kernel, width, parts),
         grid=(rows // block,),
-        in_specs=[across(a) for a in (*own, *by_x, *by_y)]
+        in_specs=[pl.BlockSpec((block, columns), lambda i: (i + skip, 0))]
+        + [across(a) for a in (*by_x, *by_y)]
         + [pl.BlockSpec((block, ids.shape[1]), lambda i: (i + skip, 0))],
         out_specs=[
             pl.BlockSpec((block, columns), lambda i: (i, 0)),
@@ -209,7 +227,7 @@
         compiler_params=compiler_params(),
         cost_estimate=small_cost(),
         name="row_stats",
-    )(*own, *by_x, *by_y, ids)
+    )(own, *by_x, *by_y, ids)
 
 
 def grad_kernel(width, logits_ref, listed_ref, stats_ref, scale_ref, out_ref, info_ref):
@@ -229,7 +247,13 @@
         out_ref[:, at] = grad
         term = term + grad.astype(jnp.float32) * piece
     lane = lax.broadcasted_iota(jnp.int32, info_ref.shape, 1)
-    info_ref[...] = jnp.where(lane == 0, jnp.sum(term, axis=1, keepdims=True), lse_ref - lse_all)
+    info_ref[...] = jnp.broadcast_to(lse_ref - lse_all, info_ref.shape)
+    term = jnp.sum(term, axis=1, keepdims=True)
+    high = term.astype(jnp.bfloat16).astype(jnp.float32)
+    middle = (term - high).astype(jnp.bfloat16).astype(jnp.float32)
+    low = term - high - middle
+    term = jnp.where(lane == 0, high, jnp.where(lane == 1, middle, jnp.where(lane == 2, low, 0.0)))
+    out_ref[:, columns:] = term.astype(jnp.bfloat16)
 
 
 def logit_grads(part, logits, listed, stats, scale, width):
@@ -246,11 +270,11 @@
             pl.BlockSpec((block, 1), lambda i: (i + skip, 0)),
         ],
         out_specs=[
-            pl.BlockSpec((block, columns), lambda i: (i, 0)),
+            pl.BlockSpec((block, columns + tail), lambda i: (i, 0)),
             pl.BlockSpec((block, 128), lambda i: (i, 0)),
         ],
         out_shape=[
-            jax.ShapeDtypeStruct((rows, columns), jnp.bfloat16),
+            jax.ShapeDtypeStruct((rows, columns + tail), jnp.bfloat16),
             jax.ShapeDtypeStruct((rows, 128), jnp.float32),
         ],
         compiler_params=compiler_params(),
@@ -260,27 +284,30 @@
 
 
 def put_row(out_ref, value):
-    code, power = encode(value)
-    width = value.shape[1]
+    width = value.shape[1] - tail
+    code, power = encode(value[:, :width])
+    term, term_power = encode(value[:, width : width + 1])
+    lane = lax.broadcasted_iota(jnp.int32, (value.shape[0], tail), 1)
+    beside = jnp.where(lane == 0, power, jnp.where(lane == 1, term.astype(jnp.int32).astype(jnp.float32), term_power))
     out_ref[:, :width] = code
-    out_ref[:, width:] = jnp.broadcast_to(power, (value.shape[0], tail)).astype(jnp.int32).astype(jnp.int16)
+    out_ref[:, width:] = beside.astype(jnp.int32).astype(jnp.int16)
 
 
 def take_row(codes_ref):
     width = codes_ref.shape[1] - tail
-    power = codes_ref[:, width:].astype(jnp.int32).astype(jnp.float32)[:, 0:1]
-    return codes_ref[:, :width].astype(jnp.int32).astype(jnp.float32) * jnp.exp(power * per_step)
-
-
-def back_kernel(tiles, started, ends, place_ref, *refs):
-    grads, head_ref, refs = refs[:5], refs[5], refs[6:]
-    so_far_ref, refs = (refs[0], refs[1:]) if started else (None, refs)
-    total_ref, refs = refs[-1], refs[:-1]
+    beside = codes_ref[:, width:].astype(jnp.int32).astype(jnp.float32)
+    value = codes_ref[:, :width].astype(jnp.int32).astype(jnp.float32) * jnp.exp(beside[:, 0:1] * per_step)
+    term = beside[:, 1:2] * jnp.exp(beside[:, 2:3] * per_step)
+    return value, jnp.broadcast_to(term, beside.shape)
+
+
+def back_kernel(tiles, keeps, place_ref, *refs):
+    grads, terms, head_ref, outs, total_ref = refs[:5], refs[5:10], refs[10], refs[11:-1], refs[-1]
     tile = pl.program_id(0)
 
     @pl.when(tile == 0)
     def _():
-        total_ref[...] = so_far_ref[...] if started else jnp.zeros_like(total_ref)
+        total_ref[...] = jnp.zeros_like(total_ref)
 
     grad = jnp.concatenate([g[...] for g in grads], axis=0)
     total_ref[...] += lax.dot_general(
@@ -289,54 +316,55 @@
 
     @pl.when(tile == tiles - 1)
     def _():
-        if not ends:
-            refs[0][...] = total_ref[...]
-            return
-        keep_ref, sends = refs[0], refs[1:]
-        width = keep_ref.shape[1]
-        block = lambda b: total_ref[:, pl.ds(pl.multiple_of(b * width, width), width)]
-        mine = place_ref[0]
-        keep_ref[...] = block(mine)
-        for k, send_ref in enumerate(sends, 1):
-            put_row(send_ref, block(mine ^ k))
-
-
-def back(grads, head, so_far, place, width, skip, tiles, group):
-    depth = head.shape[0]
+        term = jnp.concatenate([t[...].astype(jnp.float32) for t in terms], axis=0)
+        term = jnp.broadcast_to(term[:, 0:1] + term[:, 1:2] + term[:, 2:3], (term.shape[0], tail))
+        width = outs[0].shape[1] - tail
+        for k, out_ref in enumerate(outs):
+            start = pl.multiple_of((place_ref[1] ^ k) * width, width)
+            if k == 0 and keeps:
+                out_ref[:, :width] = total_ref[:, pl.ds(start, width)]
+                out_ref[:, width:] = term
+            else:
+                put_row(out_ref, jnp.concatenate([total_ref[:, pl.ds(start, width)], term], axis=1))
+
+
+def back(grads, head, place, width, group, keeps):
+    depth, columns = head.shape
     rows = sum(g.shape[0] for g in grads)
-    across = lambda g: pl.BlockSpec(
-        (g.shape[0], width), (lambda j: (0, j + skip)) if g.shape[1] > tiles * width else (lambda j: (0, j))
-    )
-    started = [] if so_far is None else [so_far]
-    if group:
-        part = depth // group
-        shapes = [((rows, part), jnp.float32)] + [((rows, part + tail), jnp.int16)] * (group - 1)
-    else:
-        shapes = [((rows, depth), jnp.float32)]
-    return pl.pallas_call(
-        functools.partial(back_kernel, tiles, bool(started), bool(group)),
-        grid=(tiles,),
-        in_specs=[pl.BlockSpec(memory_space=pltpu.SMEM)]
-        + [across(g) for g in grads]
-        + [pl.BlockSpec((depth, width), lambda j: (0, j + skip))]
-        + [constant(rows, depth)] * len(started),
-        out_specs=[constant(*shape) for shape, _ in shapes],
-        out_shape=[jax.ShapeDtypeStruct(*s) for s in shapes],
-        scratch_shapes=[pltpu.VMEM((rows, depth), jnp.float32)],
+    blocks = max(group // 2, 1)
+    part = depth // group
+    types = [jnp.float32 if keeps and k == 0 else jnp.int16 for k in range(blocks)]
+    across = lambda g: pl.BlockSpec((g.shape[0], width), lambda j, place: (0, j))
+    beside = lambda g: pl.BlockSpec((g.shape[0], tail), lambda j, place: (0, columns // tail))
+    return pl.pallas_call(
+        functools.partial(back_kernel, columns // width, keeps),
+        grid_spec=pltpu.PrefetchScalarGridSpec(
+            num_scalar_prefetch=1,
+            grid=(columns // width,),
+            in_specs=[across(g) for g in grads]
+            + [beside(g) for g in grads]
+            + [pl.BlockSpec((blocks * part, width), lambda j, place: (place[0], j))],
+            out_specs=[constant(rows, part + tail)] * blocks,
+            scratch_shapes=[pltpu.VMEM((rows, blocks * part), jnp.float32)],
+        ),
+        out_shape=[jax.ShapeDtypeStruct((rows, part + tail), t) for t in types],
         compiler_params=compiler_params(),
         cost_estimate=small_cost(),
         name="grad_rows",
-    )(place, *grads, head, *started)
+    )(place, *grads, *grads, head)
 
 
 def group_kernel(place_ref, keep_ref, *refs):
     total_ref = refs[-1]
     count = place_ref.shape[0] - 1
     out_ref, sends, received = refs[-2 - count], refs[-1 - count : -1], refs[: -2 - count]
-    total = keep_ref[...]
+    width = keep_ref.shape[1] - tail
+    total, term = keep_ref[:, :width], keep_ref[:, width:]
     for codes_ref in received:
-        total = total + take_row(codes_ref)
-    total_ref[...] = total
+        more, more_term = take_row(codes_ref)
+        total, term = total + more, term + more_term
+    total_ref[:, :width] = total
+    total_ref[:, width:] = term
     rows = out_ref.shape[0]
     block = lambda b: total_ref[pl.ds(pl.multiple_of(b * rows, rows), rows), :]
     out_ref[...] = block(place_ref[0])
@@ -347,15 +375,14 @@
 def group_sum(place, keep, received):
     blocks = place.shape[0]
     rows, width = keep.shape
-    own = (rows // blocks, width)
-    coded = (rows // blocks, width + tail)
+    each = (rows // blocks, width)
     return pl.pallas_call(
         group_kernel,
         in_specs=[pl.BlockSpec(memory_space=pltpu.SMEM)]
         + [pl.BlockSpec(memory_space=pltpu.VMEM)] * (1 + len(received)),
         out_specs=[pl.BlockSpec(memory_space=pltpu.VMEM)] * blocks,
-        out_shape=[jax.ShapeDtypeStruct(own, jnp.float32)]
-        + [jax.ShapeDtypeStruct(coded, jnp.int16)] * (blocks - 1),
+        out_shape=[jax.ShapeDtypeStruct(each, jnp.float32)]
+        + [jax.ShapeDtypeStruct(each, jnp.int16)] * (blocks - 1),
         scratch_shapes=[pltpu.VMEM((rows, width), jnp.float32)],
         compiler_params=compiler_params(),
         cost_estimate=small_cost(),
@@ -363,28 +390,29 @@
     )(place, keep, *received)
 
 
-def after(value, *others):
-    return lax.optimization_barrier((value, *others))[0]
-
-
 def last_kernel(keep_ref, *refs):
-    total = keep_ref[...]
+    width = keep_ref.shape[1] - tail
+    total, term = keep_ref[:, :width], keep_ref[:, width:]
     for codes_ref in refs[:-1]:
-        total = total + take_row(codes_ref)
-    put_row(refs[-1], total)
+        more, more_term = take_row(codes_ref)
+        total, term = total + more, term + more_term
+    put_row(refs[-1], jnp.concatenate([total, term], axis=1))
 
 
 def last_sum(keep, received):
-    rows, width = keep.shape
     return pl.pallas_call(
         last_kernel,
         in_specs=[pl.BlockSpec(memory_space=pltpu.VMEM)] * (1 + len(received)),
         out_specs=pl.BlockSpec(memory_space=pltpu.VMEM),
-        out_shape=jax.ShapeDtypeStruct((rows, width + tail), jnp.int16),
+        out_shape=jax.ShapeDtypeStruct(keep.shape, jnp.int16),
         compiler_params=compiler_params(),
         cost_estimate=small_cost(),
         name="last_sum",
     )(keep, *received)
+
+
+def after(value, *others):
+    return lax.optimization_barrier((value, *others))[0]
 
 
 def shards(hidden, head, gain, refusal_ids, refusal_count, loss_scale):
@@ -409,34 +437,32 @@
     rows_far = send(columns(me ^ 3), to_far)
     rows_x = send(columns(me ^ 1), to_x)
     rows_y = send(columns(me ^ 2), to_y)
-    rows_own = columns(me)
+    own = own_logits(columns(me), head, width)
+    rows_far = after(rows_far, rows_x, rows_y, own)
 
     by_x, by_y = [], []
     for skip in (0, tiles // 2):
         first, second = far_codes(rows_far, head, width, skip, tiles // 2)
         by_x.append(send(first, to_x))
         by_y.append(send(second, to_y))
-    own_a, sums_x_a, sums_y_a = [], [], []
+    sums_x_a, sums_y_a = [], []
     for c, skip in enumerate((0, tiles // 2)):
-        codes_x, codes_y, own = near_codes(
-            0, rows_x, rows_y, rows_own, head, [by_x[c]], [by_y[c]], width, skip, tiles // 2
+        codes_x, codes_y = near_codes(
+            0, rows_x, rows_y, head, [by_x[c]], [by_y[c]], width, skip, tiles // 2
         )
-        own_a.append(own)
         sums_x_a.append(send(codes_x, to_x))
         sums_y_a.append(send(codes_y, to_y))
-    codes_x, codes_y, own = near_codes(
-        1, rows_x, rows_y, after(rows_own, *own_a), head, by_x, by_y, width, 0, tiles
-    )
-    halves = (
-        (own_a, sums_x_a, sums_y_a),
-        ([own], [send(codes_x, to_x)], [send(codes_y, to_y)]),
-    )
+    rows_x = after(rows_x, codes_x, sums_x_a[0], sums_y_a[0])
+    codes_x, codes_y = near_codes(1, rows_x, rows_y, head, by_x, by_y, width, 0, tiles)
+    halves = ((sums_x_a, sums_y_a), ([send(codes_x, to_x)], [send(codes_y, to_y)]))
 
     in_list = jnp.arange(list_length)[None, :] < refusal_count[:, None]
     ids = jnp.where(in_list, refusal_ids - shard * vocab_local, -1)
 
     block, member = shard // group, shard % group
-    place_group = jnp.stack([member]).astype(jnp.int32)
+    spread = max(group // 2, 1)
+    place_other = jnp.stack([(member // spread) ^ 1, member % spread]).astype(jnp.int32)
+    place_mine = jnp.stack([member // spread, member % spread]).astype(jnp.int32)
     place_block = jnp.stack([block ^ k ^ me for k in range(prompt_size)]).astype(jnp.int32)
     to_member = [[(v, v ^ k) for v in range(vocab_size)] for k in range(1, group)]
     to_block = [
@@ -449,53 +475,42 @@
             for i in range(group):
                 moves.append((p * vocab_size + r * group + i, r * vocab_size + p * group + i))
 
-    infos, grad_cols, grads, turns, before_back = [], [], [], [], []
-    for part, (own, sums_x, sums_y) in enumerate(halves):
+    infos, grads = [], []
+    for part, (sums_x, sums_y) in enumerate(halves):
         logits, listed, stats = row_stats(part, own, sums_x, sums_y, after(ids, *infos), width)
         stats = lax.all_gather(stats, "vocab", axis=0)
         grad, info = logit_grads(part, logits, listed, stats, loss_scale[:, None], width)
         infos.append(info)
         grads.append((grad, send(grad, to_x), send(grad, to_y)))
-    info = jnp.concatenate(infos)
-    terms = lax.all_gather(info, "vocab", axis=0)
-
-    for part, (grad, grad_x, grad_y) in enumerate(grads):
-        quarter = half // 2
-        pieces = 1 + part
-        so_far = None
-        grad_x, grad_y = after(grad_x, *turns), after(grad_y, *turns)
-        for c in range(pieces):
-            at = slice(c * vocab_local // pieces, (c + 1) * vocab_local // pieces)
-            far_0 = send(grad_y[:quarter, at], to_x)
-            far_1 = send(grad_x[quarter:, at], to_y)
-            so_far = back(
-                (grad, grad_x, grad_y, far_0, far_1),
-                head,
-                so_far,
-                after(place_group, *before_back),
-                width,
-                c * tiles // pieces,
-                tiles // pieces,
-                group if c == pieces - 1 else 0,
-            )
-            if c < pieces - 1:
-                so_far = so_far[0]
-        keep, *codes = so_far
-        turns = [keep]
-        keep, *codes = group_sum(
-            place_block, keep, [lax.ppermute(c, "vocab", to) for c, to in zip(codes, to_member)]
-        )
-        before_back = [keep, terms]
-        codes = last_sum(keep, [lax.ppermute(c, "vocab", to) for c, to in zip(codes, to_block)])
+    log_refusal = jnp.concatenate([info[:, 0] for info in infos])
+
+    quarter = half // 2
+    gathered = []
+    for grad, grad_x, grad_y in grads:
+        far_0 = send(grad_y[:quarter], to_x)
+        far_1 = send(grad_x[quarter:], to_y)
+        gathered.append((grad, grad_x, grad_y, far_0, far_1))
+    (_, grad_x, grad_y, far_0, far_1) = gathered[1]
+    waits_other, waits_mine = [grad_x, grad_y], [far_0, far_1]
+    grad_cols = []
+    for parts in gathered:
+        others = back(parts, head, after(place_other, *waits_other), width, group, False)
+        received = [lax.ppermute(c, "vocab", to) for c, to in zip(others, to_member[spread - 1 :])]
+        keep, *codes = back(parts, head, after(place_mine, *others, *waits_mine), width, group, True)
+        received += [lax.ppermute(c, "vocab", to) for c, to in zip(codes, to_member)]
+        keep, *codes = group_sum(place_block, keep, received)
+        received = [lax.ppermute(c, "vocab", to) for c, to in zip(codes, to_block)]
+        waits_other, waits_mine = [keep], received
+        codes = last_sum(keep, received)
         grad_cols.append(lax.ppermute(codes, ("prompt", "vocab"), moves))
-    row_term = jnp.sum(terms[:, :, 0], axis=0)
-    log_refusal = info[:, 1]
 
     slice_width = model_width // vocab_size
     col_start = shard * slice_width
     codes = jnp.concatenate(grad_cols)
     power = codes[:, slice_width : slice_width + 1].astype(jnp.float32)
     grad_cols = codes[:, :slice_width].astype(jnp.float32) * jnp.exp(power * per_step)
+    term = codes[:, slice_width + 1 : slice_width + 3].astype(jnp.float32)
+    row_term = term[:, 0] * jnp.exp(term[:, 1] * per_step)
     hidden_cols = lax.dynamic_slice_in_dim(hidden, col_start, slice_width, 1).astype(jnp.float32)
     gain_cols = lax.dynamic_slice_in_dim(gain, col_start, slice_width, 0)
     grad_hidden = (

time: 310 us -> 325 us (1.048)
  Pallas kernels: 107 us -> 129 us
  blocking collectives: 44.5 us -> 29.1 us
  local copies, waits for them, and re-layouts: 17.7 us -> 28.3 us
  starting transfers between devices: 44.6 us -> 40.8 us
    pallas_call x3 -> x5, Pallas kernels: 35.5 us -> 64.5 us  [the longest x4 50.8 us: back(): pl.pallas_call(functools.partial(back_kernel, columns // width, keeps), g...]
    ppermute x8 -> x2, waiting for transfers between devices: 20.6 us -> 0.01 us  [shards(): lax.ppermute(c, 'vocab', to)]
    ppermute x0 -> x6, waiting for transfers between devices: none -> 19.9 us  [shards(): received = [lax.ppermute(c, 'vocab', to) for c, to in zip(codes, to_block)]]
    all_gather x1 -> x0, blocking collectives: 15.8 us -> none  [shards(): terms = lax.all_gather(info, 'vocab', axis=0)]
    unnamed x42 -> x39, local copies, waits for them, and re-layouts: 13.3 us -> 22.7 us
    ppermute x8 -> x2, starting transfers between devices: 9.25 us -> 0.07 us  [shards(): lax.ppermute(c, 'vocab', to)]
    ppermute x0 -> x6, starting transfers between devices: none -> 8.9 us  [shards(): received = [lax.ppermute(c, 'vocab', to) for c, to in zip(codes, to_block)]]
    pallas_call x2, Pallas kernels: 15.4 us -> 9.18 us  [far_codes(): pl.pallas_call(functools.partial(far_kernel, width), grid=(tiles,), in_sp...]
  transfers between devices with their start and end apart: 33 -> 31, of which waited for: 9 -> 17; matrix products, arithmetic and copies ran while one was open for 1% -> 1% of each run, Pallas kernels for 29% -> 30%
where the time goes in v4:
time: 325 us; the launch traced here: 324 us
  Pallas kernels  129 us (40%)
  waiting for transfers between devices  89 us (27%)
  starting transfers between devices  40.8 us (13%)
  blocking collectives  29.1 us (9%)
  local copies, waits for them, and re-layouts  28.3 us (9%)
  other arithmetic  7.3 us (2%)
    ppermute x21, waiting for transfers between devices, shards(): send = lambda value, pairs: lax.ppermute(value, 'prompt', pairs)  60.7 us
    pallas_call x4, Pallas kernels, back(): pl.pallas_call(functools.partial(back_kernel, columns // width, keeps), g...  50.8 us
    pallas_call x3, Pallas kernels, near_codes(): pl.pallas_call(functools.partial(near_kernel, width, len(by_x)), grid=(ti...  32.1 us
    all_gather x2, blocking collectives, shards(): stats = lax.all_gather(stats, 'vocab', axis=0)  29.1 us
    unnamed x39, local copies, waits for them, and re-layouts  22.7 us
    ppermute x21, starting transfers between devices, shards(): send = lambda value, pairs: lax.ppermute(value, 'prompt', pairs)  21.9 us
    ppermute x6, waiting for transfers between devices, shards(): received = [lax.ppermute(c, 'vocab', to) for c, to in zip(codes, to_block)]  19.9 us
    pallas_call x1, Pallas kernels, own_logits(): pl.pallas_call(own_kernel, grid=(columns // width,), in_specs=[constant(r...  13.8 us
  transfers between devices with their start and end apart: 31, of which 17 were waited for; matrix products, arithmetic and copies ran while one was open for 1% of the time, Pallas kernels for 30%

profile of v4, /device:TPU:2, one launch (start us, length us, event | category | flops | bytes accessed | tf_op | source)
XLA Modules:
  0.0 324.0 jit_solution(13922326613703928406)
XLA Ops:
  0.7 2.2 fusion
  2.9 1.9 fusion.2
  4.8 1.8 constant_dynamic-slice_fusion
  6.7 2.0 collective-permute-start.1
  8.7 1.4 collective-permute-start.2
  10.2 13.8 %own_logits.1.refs_0_ = f32[128,8192]{1,0:T(8,128)S(1)} custom-call(bf16[128,2048]{1,0:T(8,128)(2,1)S(1)} %get-tuple-element.75.x_ref, bf16[2048,8192]{1,0:T(8,128)(2,1)} %refs_10_.7), custom_call_target="tpu_custom_call" | custom-call | flops 1024 | bytes 1024 | tf_op jit(solution)/shard_map/own_logits/pallas_call | solution.py:148
  23.9 2.0 copy-done.1
  25.9 5.0 %collective-permute-done.1.y_ref = bf16[128,2048]{1,0:T(8,128)(2,1)S(1)} collective-permute-done((bf16[128,2048]{1,0:T(8,128)(2,1)S(1)}, bf16[128,2048]{1,0:T(8,128)(2,1)S(1)}, u32[]{:S(2)}, u32[]{:S(2)}) %collective-permute-start.1) | collective-permute-done | bytes 524320 | tf_op jit(solution)/shard_map/ppermute | solution.py:431
  30.9 1.6 collective-permute-done.2.x_ref
  32.5 10.5 %copy-done = bf16[2048,8192]{1,0:T(8,128)(2,1)S(1)} copy-done((bf16[2048,8192]{1,0:T(8,128)(2,1)S(1)}, bf16[2048,8192]{1,0:T(8,128)(2,1)}, u32[]{:S(2)}) %copy-start) | copy-done | bytes 33554456
  43.1 4.6 %far_codes.3 = (s16[64,4224]{1,0:T(8,128)(2,1)S(1)}, s16[64,4224]{1,0:T(8,128)(2,1)S(1)}) custom-call(bf16[128,2048]{1,0:T(8,128)(2,1)S(1)} %collective-permute-done.2.x_ref, bf16[2048,8192]{1,0:T(8,128)(2,1)S(1)} %copy-done), custom_call_target="tpu_custom_call" | custom-call | flops 1024 | bytes 1024 | tf_op jit(solution)/shard_map/far_codes/pallas_call | solution.py:77
  48.5 1.5 collective-permute-start.6
  50.1 4.6 %far_codes.2 = (s16[64,4224]{1,0:T(8,128)(2,1)S(1)}, s16[64,4224]{1,0:T(8,128)(2,1)S(1)}) custom-call(bf16[128,2048]{1,0:T(8,128)(2,1)S(1)} %collective-permute-done.2.x_ref, bf16[2048,8192]{1,0:T(8,128)(2,1)S(1)} %copy-done), custom_call_target="tpu_custom_call" | custom-call | flops 1024 | bytes 1024 | tf_op jit(solution)/shard_map/far_codes/pallas_call | solution.py:77
  55.3 1.2 collective-permute-start.4
  56.5 6.5 %collective-permute-done.5.refs_0_ = s16[64,4224]{1,0:T(8,128)(2,1)S(1)} collective-permute-done((s16[64,4224]{1,0:T(8,128)(2,1)S(1)}, s16[64,4224]{1,0:T(8,128)(2,1)S(1)}, u32[]{:S(2)}, u32[]{:S(2)}) %collective-permute-start.5) | collective-permute-done | bytes 540704 | tf_op jit(solution)/shard_map/ppermute | solution.py:431
  63.7 7.7 %near_codes.4 = (s16[64,4224]{1,0:T(8,128)(2,1)S(1)}, s16[64,4224]{1,0:T(8,128)(2,1)S(1)}) custom-call(bf16[128,2048]{1,0:T(8,128)(2,1)S(1)} %collective-permute-done.x_ref, bf16[128,2048]{1,0:T(8,128)(2,1)S(1)} %collective-permute-done.1.y_ref, bf16[2048,8192]{1,0:T(8,128)(2,1)} %refs_10_.7, s16[64,4224]{1,0:T(8,128)(2,1)S(1)} %collective-permute-done.5.refs_0_, ...), custom_call_target="tpu_custom_call" | custom-call | flops 1024 | bytes 1024 | tf_op jit(solution)/shard_map/near_codes/pallas_call | solution.py:126
  71.4 1.3 collective-permute-start.7
  73.5 1.0 collective-permute-done.3.refs_0_.refs_1_
  75.0 8.7 %near_codes.3 = (s16[64,4224]{1,0:T(8,128)(2,1)}, s16[64,4224]{1,0:T(8,128)(2,1)}) custom-call(bf16[128,2048]{1,0:T(8,128)(2,1)S(1)} %collective-permute-done.x_ref, bf16[128,2048]{1,0:T(8,128)(2,1)S(1)} %collective-permute-done.1.y_ref, bf16[2048,8192]{1,0:T(8,128)(2,1)} %refs_10_.7, s16[64,4224]{1,0:T(8,128)(2,1)S(1)} %collective-permute-done.3.refs_0_.refs_1_, ...), custom_call_target="tpu_custom_call" | custom-call | flops 1024 | bytes 1024 | tf_op jit(solution)/shard_map/near_codes/pallas_call | solution.py:126
  83.7 1.5 collective-permute-start.11
  86.1 15.7 %near_codes.5 = (s16[64,8320]{1,0:T(8,128)(2,1)}, s16[64,8320]{1,0:T(8,128)(2,1)}) custom-call(bf16[128,2048]{1,0:T(8,128)(2,1)S(1)} %collective-permute-done.x_ref, bf16[128,2048]{1,0:T(8,128)(2,1)S(1)} %collective-permute-done.1.y_ref, bf16[2048,8192]{1,0:T(8,128)(2,1)} %refs_10_.7, s16[64,4224]{1,0:T(8,128)(2,1)S(1)} %collective-permute-done.5.refs_0_, ...), custom_call_target="tpu_custom_call" | custom-call | flops 1024 | bytes 1024 | tf_op jit(solution)/shard_map/near_codes/pallas_call | solution.py:126
  101.8 1.7 collective-permute-start.9
  104.6 2.2 copy-done.2
  106.8 1.0 copy-done.11
  107.9 6.8 %row_stats.2 = (f32[64,8192]{1,0:T(8,128)S(1)}, f32[64,8192]{1,0:T(8,128)S(1)}, f32[64,128]{1,0:T(8,128)S(1)}) custom-call(f32[128,8192]{1,0:T(8,128)S(1)} %copy-done.2, s16[64,4224]{1,0:T(8,128)(2,1)S(1)} %collective-permute-done.7.refs_1_, s16[64,4224]{1,0:T(8,128)(2,1)} %collective-permute-done.11.refs_2_, s16[64,4224]{1,0:T(8,128)(2,1)S(1)} %copy-done.11, ...), custom_call_target="tpu_custom_call" | custom-call | flops 1024 | bytes 1024 | tf_op jit(solution)/shard_map/row_stats/pallas_call | solution.py:211
  114.7 14.6 %all-gather = f32[512,128]{1,0:T(8,128)S(1)} all-gather(f32[64,128]{1,0:T(8,128)S(1)} %get-tuple-element.51), channel_id=2, replica_groups=mesh['prompt'=4,'vocab'=8] {'vocab'}, dimensions={0}, use_global_device_ids=true | all-gather | bytes 294912 | tf_op jit(solution)/shard_map/all_gather | solution.py:481
  129.2 2.2 logit_grads.2
  131.4 1.3 collective-permute-start.16
  133.1 5.9 %row_stats.3 = (f32[64,8192]{1,0:T(8,128)S(1)}, f32[64,8192]{1,0:T(8,128)S(1)}, f32[64,128]{1,0:T(8,128)S(1)}) custom-call(f32[128,8192]{1,0:T(8,128)S(1)} %copy-done.3, s16[64,8320]{1,0:T(8,128)(2,1)S(1)} %collective-permute-done.9.refs_1_, s16[64,8320]{1,0:T(8,128)(2,1)S(1)} %collective-permute-done.10.refs_2_, s32[128,16]{1,0:T(8,128)S(1)} %fusion.6.refs_5_.refs_3_), custom_call_target="tpu_custom_call" | custom-call | flops 1024 | bytes 1024 | tf_op jit(solution)/shard_map/row_stats/pallas_call | solution.py:211
  138.9 14.5 %all-gather.1 = f32[512,128]{1,0:T(8,128)S(1)} all-gather(f32[64,128]{1,0:T(8,128)S(1)} %get-tuple-element.56), channel_id=3, replica_groups=mesh['prompt'=4,'vocab'=8] {'vocab'}, dimensions={0}, use_global_device_ids=true | all-gather | bytes 294912 | tf_op jit(solution)/shard_map/all_gather | solution.py:481
  153.4 3.0 logit_grads.3
  156.5 1.7 collective-permute-start.13
  161.4 1.0 copy-done.4
  163.3 19.7 %collective-permute-done.13.refs_1_.refs_6_ = bf16[64,8320]{1,0:T(8,128)(2,1)S(1)} collective-permute-done((bf16[64,8320]{1,0:T(8,128)(2,1)}, bf16[64,8320]{1,0:T(8,128)(2,1)S(1)}, u32[]{:S(2)}, u32[]{:S(2)}) %collective-permute-start.13) | collective-permute-done | bytes 1064992 | tf_op jit(solution)/shard_map/ppermute | solution.py:431
  183.0 1.7 collective-permute-done.14.refs_2_.refs_7_
  184.7 9.2 %collective-permute-done.17.refs_3_.refs_8_ = bf16[32,8320]{1,0:T(8,128)(2,1)} collective-permute-done((bf16[32,8320]{1,0:T(8,128)(2,1)}, bf16[32,8320]{1,0:T(8,128)(2,1)}, u32[]{:S(2)}, u32[]{:S(2)}) %collective-permute-start.17) | collective-permute-done | bytes 532512 | tf_op jit(solution)/shard_map/ppermute | solution.py:431
  193.9 1.4 collective-permute-done.18.refs_4_.refs_9_
  195.3 1.2 copy-done.5
  196.6 1.2 copy-done.8
  197.8 13.5 %grad_rows.4 = s16[256,1152]{1,0:T(8,128)(2,1)} custom-call(s32[2]{0:T(128)S(1)} %pad_add_fusion.place_ref, bf16[64,8320]{1,0:T(8,128)(2,1)S(1)} %copy-done.8, bf16[64,8320]{1,0:T(8,128)(2,1)S(1)} %copy-done.5, bf16[64,8320]{1,0:T(8,128)(2,1)S(1)} %collective-permute-done.16.refs_2_.refs_7_, bf16[32,8320]{1,0:T(8,128)(2,1)} %collective-permute-done.17.refs_3_.refs_8_, ...), custom_call_target="tpu_custom_call" | custom-call | flops 1024 | bytes 1024 | tf_op jit(solution)/shard_map/grad_rows/pallas_call | solution.py:339
  213.4 1.2 collective-permute-start.20
  214.7 12.2 %collective-permute-done.19.refs_3_.refs_8_ = bf16[32,8320]{1,0:T(8,128)(2,1)} collective-permute-done((bf16[32,8320]{1,0:T(8,128)(2,1)}, bf16[32,8320]{1,0:T(8,128)(2,1)}, u32[]{:S(2)}, u32[]{:S(2)}) %collective-permute-start.19) | collective-permute-done | bytes 532512 | tf_op jit(solution)/shard_map/ppermute | solution.py:431
  227.0 0.9 collective-permute-done.20.refs_4_.refs_9_
  227.9 1.2 copy-done.6
  229.1 1.2 copy-done.9
  230.4 12.4 %grad_rows.5.keep_ref = f32[256,1152]{1,0:T(8,128)S(1)} custom-call(s32[2]{0:T(128)S(1)} %pad_add_fusion.1.place_ref, bf16[64,8320]{1,0:T(8,128)(2,1)S(1)} %copy-done.9, bf16[64,8320]{1,0:T(8,128)(2,1)S(1)} %copy-done.6, bf16[64,8320]{1,0:T(8,128)(2,1)S(1)} %collective-permute-done.16.refs_2_.refs_7_, ...), custom_call_target="tpu_custom_call" | custom-call | flops 1024 | bytes 1024 | tf_op jit(solution)/shard_map/grad_rows/pallas_call | solution.py:339
  242.8 2.3 group_sum.2
  245.1 12.6 %grad_rows.6 = s16[256,1152]{1,0:T(8,128)(2,1)S(1)} custom-call(s32[2]{0:T(128)S(1)} %pad_add_fusion.place_ref, bf16[64,8320]{1,0:T(8,128)(2,1)} %get-tuple-element.57.refs_0_.refs_5_, bf16[64,8320]{1,0:T(8,128)(2,1)S(1)} %collective-permute-done.13.refs_1_.refs_6_, bf16[64,8320]{1,0:T(8,128)(2,1)S(1)} %collective-permute-done.14.refs_2_.refs_7_, ...), custom_call_target="tpu_custom_call" | custom-call | flops 1024 | bytes 1024 | tf_op jit(solution)/shard_map/grad_rows/pallas_call | solution.py:339
  257.8 1.5 collective-permute-start.22
  259.3 2.4 collective-permute-start.23
  262.3 4.4 %collective-permute-done.22.refs_0_ = s16[64,1152]{1,0:T(8,128)(2,1)S(1)} collective-permute-done((s16[64,1152]{1,0:T(8,128)(2,1)}, s16[64,1152]{1,0:T(8,128)(2,1)S(1)}, u32[]{:S(2)}, u32[]{:S(2)}) %collective-permute-start.22) | collective-permute-done | bytes 147488 | tf_op jit(solution)/shard_map/ppermute | solution.py:502
  266.8 6.8 %collective-permute-done.23.refs_1_ = s16[64,1152]{1,0:T(8,128)(2,1)} collective-permute-done((s16[64,1152]{1,0:T(8,128)(2,1)}, s16[64,1152]{1,0:T(8,128)(2,1)}, u32[]{:S(2)}, u32[]{:S(2)}) %collective-permute-start.23) | collective-permute-done | bytes 147488 | tf_op jit(solution)/shard_map/ppermute | solution.py:502
  273.6 1.0 copy-done.13
  274.5 1.3 last_sum.2
  275.8 6.0 %collective-permute-start.25 = (s16[64,1152]{1,0:T(8,128)(2,1)S(1)}, s16[64,1152]{1,0:T(8,128)(2,1)S(1)}, u32[]{:S(2)}, u32[]{:S(2)}) collective-permute-start(s16[64,1152]{1,0:T(8,128)(2,1)S(1)} %last_sum.2), channel_id=1, source_target_pairs={{0,0},{1,1},{2,8},{3,9},{4,16},{5,17},{6,24},{7,25},{8,2},{9,3},{1... | collective-permute-start | bytes 442376 | tf_op jit(solution)/shard_map/ppermute | solution.py:505
  281.8 12.3 %grad_rows.7.keep_ref = f32[256,1152]{1,0:T(8,128)S(1)} custom-call(s32[2]{0:T(128)S(1)} %pad_add_fusion.1.place_ref, bf16[64,8320]{1,0:T(8,128)(2,1)} %get-tuple-element.57.refs_0_.refs_5_, bf16[64,8320]{1,0:T(8,128)(2,1)S(1)} %collective-permute-done.13.refs_1_.refs_6_, bf16[64,8320]{1,0:T(8,128)(2,1)S(1)} %collective-permute-done.14.refs_2_.refs_7_, ...), custom_call_target="tpu_custom_call" | custom-call | flops 1024 | bytes 1024 | tf_op jit(solution)/shard_map/grad_rows/pallas_call | solution.py:339
  294.1 1.1 group_sum.3
  295.3 2.5 collective-permute-start.28
  297.7 1.9 collective-permute-start.29
  300.3 1.8 collective-permute-done.27.refs_0_
  302.1 6.9 %collective-permute-done.28.refs_1_ = s16[64,1152]{1,0:T(8,128)(2,1)S(1)} collective-permute-done((s16[64,1152]{1,0:T(8,128)(2,1)S(1)}, s16[64,1152]{1,0:T(8,128)(2,1)S(1)}, u32[]{:S(2)}, u32[]{:S(2)}) %collective-permute-start.28) | collective-permute-done | bytes 147488 | tf_op jit(solution)/shard_map/ppermute | solution.py:502
  309.3 4.0 %collective-permute-start.30 = (s16[64,1152]{1,0:T(8,128)(2,1)S(1)}, s16[64,1152]{1,0:T(8,128)(2,1)S(1)}, u32[]{:S(2)}, u32[]{:S(2)}) collective-permute-start(s16[64,1152]{1,0:T(8,128)(2,1)S(1)} %last_sum.3), channel_id=1, source_target_pairs={{0,0},{1,1},{2,8},{3,9},{4,16},{5,17},{6,24},{7,25},{8,2},{9,3},{1... | collective-permute-start | bytes 442376 | tf_op jit(solution)/shard_map/ppermute | solution.py:505
  313.3 8.4 %collective-permute-done.30 = s16[64,1152]{1,0:T(8,128)(2,1)S(1)} collective-permute-done((s16[64,1152]{1,0:T(8,128)(2,1)S(1)}, s16[64,1152]{1,0:T(8,128)(2,1)S(1)}, u32[]{:S(2)}, u32[]{:S(2)}) %collective-permute-start.30) | collective-permute-done | bytes 147488 | tf_op jit(solution)/shard_map/ppermute | solution.py:505
  322.1 2.0 multiply_subtract_fusion
  (81 shorter events, 14.5 us)
Async XLA Ops:
  0.6 2.3 copy-start.14
  0.6 2.3 copy-start.15
  6.6 19.3 %collective-permute-start = (bf16[128,2048]{1,0:T(8,128)(2,1)S(1)}, bf16[128,2048]{1,0:T(8,128)(2,1)S(1)}, u32[]{:S(2)}, u32[]{:S(2)}) collective-permute-start(bf16[128,2048]{1,0:T(8,128)(2,1)S(1)} %get-tuple-element.74), channel_id=1, source_target_pairs={{0,8},{8,0},{16,24},{24,16},{1,9},{9,1},{17,25},{25,17},{2,10},{10... | collective-permute-start | bytes 1572872 | tf_op jit(solution)/shard_map/ppermute | solution.py:431
  6.7 24.2 %collective-permute-start.1 = (bf16[128,2048]{1,0:T(8,128)(2,1)S(1)}, bf16[128,2048]{1,0:T(8,128)(2,1)S(1)}, u32[]{:S(2)}, u32[]{:S(2)}) collective-permute-start(bf16[128,2048]{1,0:T(8,128)(2,1)S(1)} %get-tuple-element.73), channel_id=1, source_target_pairs={{0,16},{8,24},{16,0},{24,8},{1,17},{9,25},{17,1},{25,9},{2,18},{10... | collective-permute-start | bytes 1572872 | tf_op jit(solution)/shard_map/ppermute | solution.py:431
  8.7 23.8 %collective-permute-start.2 = (bf16[128,2048]{1,0:T(8,128)(2,1)S(1)}, bf16[128,2048]{1,0:T(8,128)(2,1)S(1)}, u32[]{:S(2)}, u32[]{:S(2)}) collective-permute-start(bf16[128,2048]{1,0:T(8,128)(2,1)S(1)} %get-tuple-element.72), channel_id=1, source_target_pairs={{0,24},{8,16},{16,8},{24,0},{1,25},{9,17},{17,9},{25,1},{2,26},{10... | collective-permute-start | bytes 1572872 | tf_op jit(solution)/shard_map/ppermute | solution.py:431
  23.9 2.0 copy-start.1
  32.5 10.5 %copy-start = (bf16[2048,8192]{1,0:T(8,128)(2,1)S(1)}, bf16[2048,8192]{1,0:T(8,128)(2,1)}, u32[]{:S(2)}) copy-start(bf16[2048,8192]{1,0:T(8,128)(2,1)} %refs_10_.7) | copy-start | bytes 100663296
  47.7 15.3 %collective-permute-start.5 = (s16[64,4224]{1,0:T(8,128)(2,1)S(1)}, s16[64,4224]{1,0:T(8,128)(2,1)S(1)}, u32[]{:S(2)}, u32[]{:S(2)}) collective-permute-start(s16[64,4224]{1,0:T(8,128)(2,1)S(1)} %get-tuple-element.41), channel_id=1, source_target_pairs={{0,8},{8,0},{16,24},{24,16},{1,9},{9,1},{17,25},{25,17},{2,10},{10... | collective-permute-start | bytes 1622024 | tf_op jit(solution)/shard_map/ppermute | solution.py:431
  48.5 15.2 %collective-permute-start.6 = (s16[64,4224]{1,0:T(8,128)(2,1)S(1)}, s16[64,4224]{1,0:T(8,128)(2,1)S(1)}, u32[]{:S(2)}, u32[]{:S(2)}) collective-permute-start(s16[64,4224]{1,0:T(8,128)(2,1)S(1)} %get-tuple-element.42), channel_id=1, source_target_pairs={{0,16},{8,24},{16,0},{24,8},{1,17},{9,25},{17,1},{25,9},{2,18},{10... | collective-permute-start | bytes 1622024 | tf_op jit(solution)/shard_map/ppermute | solution.py:431
  54.7 19.9 %collective-permute-start.3 = (s16[64,4224]{1,0:T(8,128)(2,1)S(1)}, s16[64,4224]{1,0:T(8,128)(2,1)S(1)}, u32[]{:S(2)}, u32[]{:S(2)}) collective-permute-start(s16[64,4224]{1,0:T(8,128)(2,1)S(1)} %get-tuple-element.38), channel_id=1, source_target_pairs={{0,8},{8,0},{16,24},{24,16},{1,9},{9,1},{17,25},{25,17},{2,10},{10... | collective-permute-start | bytes 1622024 | tf_op jit(solution)/shard_map/ppermute | solution.py:431
  55.3 19.8 %collective-permute-start.4 = (s16[64,4224]{1,0:T(8,128)(2,1)S(1)}, s16[64,4224]{1,0:T(8,128)(2,1)S(1)}, u32[]{:S(2)}, u32[]{:S(2)}) collective-permute-start(s16[64,4224]{1,0:T(8,128)(2,1)S(1)} %get-tuple-element.39), channel_id=1, source_target_pairs={{0,16},{8,24},{16,0},{24,8},{1,17},{9,25},{17,1},{25,9},{2,18},{10... | collective-permute-start | bytes 1622024 | tf_op jit(solution)/shard_map/ppermute | solution.py:431
  71.4 14.7 %collective-permute-start.7 = (s16[64,4224]{1,0:T(8,128)(2,1)S(1)}, s16[64,4224]{1,0:T(8,128)(2,1)S(1)}, u32[]{:S(2)}, u32[]{:S(2)}) collective-permute-start(s16[64,4224]{1,0:T(8,128)(2,1)S(1)} %get-tuple-element.43), channel_id=1, source_target_pairs={{0,8},{8,0},{16,24},{24,16},{1,9},{9,1},{17,25},{25,17},{2,10},{10... | collective-permute-start | bytes 1622024 | tf_op jit(solution)/shard_map/ppermute | solution.py:431
  72.7 13.4 %collective-permute-start.8 = (s16[64,4224]{1,0:T(8,128)(2,1)S(1)}, s16[64,4224]{1,0:T(8,128)(2,1)S(1)}, u32[]{:S(2)}, u32[]{:S(2)}) collective-permute-start(s16[64,4224]{1,0:T(8,128)(2,1)S(1)} %get-tuple-element.44), channel_id=1, source_target_pairs={{0,16},{8,24},{16,0},{24,8},{1,17},{9,25},{17,1},{25,9},{2,18},{10... | collective-permute-start | bytes 1622024 | tf_op jit(solution)/shard_map/ppermute | solution.py:431
  83.7 20.9 %collective-permute-start.11 = (s16[64,4224]{1,0:T(8,128)(2,1)}, s16[64,4224]{1,0:T(8,128)(2,1)}, u32[]{:S(2)}, u32[]{:S(2)}) collective-permute-start(s16[64,4224]{1,0:T(8,128)(2,1)} %get-tuple-element.40), channel_id=1, source_target_pairs={{0,8},{8,0},{16,24},{24,16},{1,9},{9,1},{17,25},{25,17},{2,10},{10... | collective-permute-start | bytes 1622024 | tf_op jit(solution)/shard_map/ppermute | solution.py:431
  85.3 19.0 %copy-start.16 = (s32[128,16]{0,1:T(8,128)S(1)}, s32[128,16]{0,1:T(8,128)}, u32[]{:S(2)}) copy-start(s32[128,16]{0,1:T(8,128)} %param.9) | copy-start | bytes 24580
  85.3 19.1 %copy-start.17 = (s32[128]{0:T(128)S(1)}, s32[128]{0:T(128)}, u32[]{:S(2)}) copy-start(s32[128]{0:T(128)} %param.10) | copy-start | bytes 1540
  85.3 19.2 %copy-start.18 = (f32[128]{0:T(128)S(1)}, f32[128]{0:T(128)}, u32[]{:S(2)}) copy-start(f32[128]{0:T(128)} %param.11) | copy-start | bytes 1540
  85.3 19.3 %collective-permute-start.12 = (s16[64,4224]{1,0:T(8,128)(2,1)}, s16[64,4224]{1,0:T(8,128)(2,1)}, u32[]{:S(2)}, u32[]{:S(2)}) collective-permute-start(s16[64,4224]{1,0:T(8,128)(2,1)} %get-tuple-element.48), channel_id=1, source_target_pairs={{0,16},{8,24},{16,0},{24,8},{1,17},{9,25},{17,1},{25,9},{2,18},{10... | collective-permute-start | bytes 1622024 | tf_op jit(solution)/shard_map/ppermute | solution.py:431
  86.1 15.7 %copy-start.10 = (s16[64,4224]{1,0:T(8,128)(2,1)}, s16[64,4224]{1,0:T(8,128)(2,1)S(1)}, u32[]{:S(2)}) copy-start(s16[64,4224]{1,0:T(8,128)(2,1)S(1)} %collective-permute-done.8.refs_3_) | copy-start | bytes 1622020
  101.8 31.2 %collective-permute-start.9 = (s16[64,8320]{1,0:T(8,128)(2,1)}, s16[64,8320]{1,0:T(8,128)(2,1)S(1)}, u32[]{:S(2)}, u32[]{:S(2)}) collective-permute-start(s16[64,8320]{1,0:T(8,128)(2,1)} %get-tuple-element.46), channel_id=1, source_target_pairs={{0,8},{8,0},{16,24},{24,16},{1,9},{9,1},{17,25},{25,17},{2,10},{10... | collective-permute-start | bytes 3194888 | tf_op jit(solution)/shard_map/ppermute | solution.py:431
  103.5 29.6 %collective-permute-start.10 = (s16[64,8320]{1,0:T(8,128)(2,1)}, s16[64,8320]{1,0:T(8,128)(2,1)S(1)}, u32[]{:S(2)}, u32[]{:S(2)}) collective-permute-start(s16[64,8320]{1,0:T(8,128)(2,1)} %get-tuple-element.47), channel_id=1, source_target_pairs={{0,16},{8,24},{16,0},{24,8},{1,17},{9,25},{17,1},{25,9},{2,18},{10... | collective-permute-start | bytes 3194888 | tf_op jit(solution)/shard_map/ppermute | solution.py:431
  104.6 2.2 copy-start.2
  106.8 1.0 copy-start.11
  129.2 3.8 %copy-start.3 = (f32[128,8192]{1,0:T(8,128)S(1)}, f32[128,8192]{1,0:T(8,128)}, u32[]{:S(2)}) copy-start(f32[128,8192]{1,0:T(8,128)} %copy-done.1) | copy-start | bytes 12582916
  131.4 7.5 %copy-start.7 = (bf16[64,8320]{1,0:T(8,128)(2,1)}, bf16[64,8320]{1,0:T(8,128)(2,1)S(1)}, u32[]{:S(2)}) copy-start(bf16[64,8320]{1,0:T(8,128)(2,1)S(1)} %get-tuple-element.59.refs_0_.refs_5_) | copy-start | bytes 3194884
  131.4 27.5 %collective-permute-start.16 = (bf16[64,8320]{1,0:T(8,128)(2,1)S(1)}, bf16[64,8320]{1,0:T(8,128)(2,1)S(1)}, u32[]{:S(2)}, u32[]{:S(2)}) collective-permute-start(bf16[64,8320]{1,0:T(8,128)(2,1)S(1)} %get-tuple-element.59.refs_0_.refs_5_), channel_id=1, source_target_pairs={{0,16},{8,24},{16,0},{24,8},{1,17},{9,25},{17,1},{25,9},{2,18},{10... | collective-permute-start | bytes 3194888 | tf_op jit(solution)/shard_map/ppermute | solution.py:431
  132.7 27.9 %collective-permute-start.15 = (bf16[64,8320]{1,0:T(8,128)(2,1)S(1)}, bf16[64,8320]{1,0:T(8,128)(2,1)S(1)}, u32[]{:S(2)}, u32[]{:S(2)}) collective-permute-start(bf16[64,8320]{1,0:T(8,128)(2,1)S(1)} %get-tuple-element.59.refs_0_.refs_5_), channel_id=1, source_target_pairs={{0,8},{8,0},{16,24},{24,16},{1,9},{9,1},{17,25},{25,17},{2,10},{10... | collective-permute-start | bytes 3194888 | tf_op jit(solution)/shard_map/ppermute | solution.py:431
  156.5 26.5 %collective-permute-start.13 = (bf16[64,8320]{1,0:T(8,128)(2,1)}, bf16[64,8320]{1,0:T(8,128)(2,1)S(1)}, u32[]{:S(2)}, u32[]{:S(2)}) collective-permute-start(bf16[64,8320]{1,0:T(8,128)(2,1)} %get-tuple-element.57.refs_0_.refs_5_), channel_id=1, source_target_pairs={{0,8},{8,0},{16,24},{24,16},{1,9},{9,1},{17,25},{25,17},{2,10},{10... | collective-permute-start | bytes 3194888 | tf_op jit(solution)/shard_map/ppermute | solution.py:431
  158.1 26.6 %collective-permute-start.14 = (bf16[64,8320]{1,0:T(8,128)(2,1)}, bf16[64,8320]{1,0:T(8,128)(2,1)S(1)}, u32[]{:S(2)}, u32[]{:S(2)}) collective-permute-start(bf16[64,8320]{1,0:T(8,128)(2,1)} %get-tuple-element.57.refs_0_.refs_5_), channel_id=1, source_target_pairs={{0,16},{8,24},{16,0},{24,8},{1,17},{9,25},{17,1},{25,9},{2,18},{10... | collective-permute-start | bytes 3194888 | tf_op jit(solution)/shard_map/ppermute | solution.py:431
  159.8 34.1 %collective-permute-start.17 = (bf16[32,8320]{1,0:T(8,128)(2,1)}, bf16[32,8320]{1,0:T(8,128)(2,1)}, u32[]{:S(2)}, u32[]{:S(2)}) collective-permute-start(bf16[32,8320]{1,0:T(8,128)(2,1)} %slice.44), channel_id=1, source_target_pairs={{0,8},{8,0},{16,24},{24,16},{1,9},{9,1},{17,25},{25,17},{2,10},{10... | collective-permute-start | bytes 1597448 | tf_op jit(solution)/shard_map/ppermute | solution.py:431
  161.4 1.0 copy-start.4
  162.4 33.0 %collective-permute-start.18 = (bf16[32,8320]{1,0:T(8,128)(2,1)}, bf16[32,8320]{1,0:T(8,128)(2,1)}, u32[]{:S(2)}, u32[]{:S(2)}) collective-permute-start(bf16[32,8320]{1,0:T(8,128)(2,1)} %slice.45), channel_id=1, source_target_pairs={{0,16},{8,24},{16,0},{24,8},{1,17},{9,25},{17,1},{25,9},{2,18},{10... | collective-permute-start | bytes 1597448 | tf_op jit(solution)/shard_map/ppermute | solution.py:431
  195.3 1.2 copy-start.5
  196.6 1.2 copy-start.8
  211.3 31.5 %collective-permute-start.21 = (s16[256,1152]{1,0:T(8,128)(2,1)}, s16[256,1152]{1,0:T(8,128)(2,1)}, u32[]{:S(2)}, u32[]{:S(2)}) collective-permute-start(s16[256,1152]{1,0:T(8,128)(2,1)} %grad_rows.4), channel_id=1, source_target_pairs={{0,1},{1,0},{2,3},{3,2},{4,5},{5,4},{6,7},{7,6},{8,9},{9,8},{10,11... | collective-permute-start | bytes 1769480 | tf_op jit(solution)/shard_map/ppermute | solution.py:498
  212.1 14.8 %collective-permute-start.19 = (bf16[32,8320]{1,0:T(8,128)(2,1)}, bf16[32,8320]{1,0:T(8,128)(2,1)}, u32[]{:S(2)}, u32[]{:S(2)}) collective-permute-start(bf16[32,8320]{1,0:T(8,128)(2,1)} %slice.46), channel_id=1, source_target_pairs={{0,8},{8,0},{16,24},{24,16},{1,9},{9,1},{17,25},{25,17},{2,10},{10... | collective-permute-start | bytes 1597448 | tf_op jit(solution)/shard_map/ppermute | solution.py:431
  213.4 14.5 %collective-permute-start.20 = (bf16[32,8320]{1,0:T(8,128)(2,1)}, bf16[32,8320]{1,0:T(8,128)(2,1)}, u32[]{:S(2)}, u32[]{:S(2)}) collective-permute-start(bf16[32,8320]{1,0:T(8,128)(2,1)} %slice.47), channel_id=1, source_target_pairs={{0,16},{8,24},{16,0},{24,8},{1,17},{9,25},{17,1},{25,9},{2,18},{10... | collective-permute-start | bytes 1597448 | tf_op jit(solution)/shard_map/ppermute | solution.py:431
  227.9 1.2 copy-start.6
  229.1 1.2 copy-start.9
  245.1 12.6 %copy-start.12 = (f32[64,1152]{1,0:T(8,128)}, f32[64,1152]{1,0:T(8,128)S(1)}, u32[]{:S(2)}) copy-start(f32[64,1152]{1,0:T(8,128)S(1)} %get-tuple-element.61.keep_ref) | copy-start | bytes 884740
  257.7 36.4 %collective-permute-start.26 = (s16[256,1152]{1,0:T(8,128)(2,1)S(1)}, s16[256,1152]{1,0:T(8,128)(2,1)S(1)}, u32[]{:S(2)}, u32[]{:S(2)}) collective-permute-start(s16[256,1152]{1,0:T(8,128)(2,1)S(1)} %grad_rows.6), channel_id=1, source_target_pairs={{0,1},{1,0},{2,3},{3,2},{4,5},{5,4},{6,7},{7,6},{8,9},{9,8},{10,11... | collective-permute-start | bytes 1769480 | tf_op jit(solution)/shard_map/ppermute | solution.py:498
  257.8 9.0 %collective-permute-start.22 = (s16[64,1152]{1,0:T(8,128)(2,1)}, s16[64,1152]{1,0:T(8,128)(2,1)S(1)}, u32[]{:S(2)}, u32[]{:S(2)}) collective-permute-start(s16[64,1152]{1,0:T(8,128)(2,1)} %get-tuple-element.62), channel_id=1, source_target_pairs={{0,2},{1,3},{2,0},{3,1},{4,6},{5,7},{6,4},{7,5},{8,10},{9,11},{10,... | collective-permute-start | bytes 442376 | tf_op jit(solution)/shard_map/ppermute | solution.py:502
  259.3 14.3 %collective-permute-start.23 = (s16[64,1152]{1,0:T(8,128)(2,1)}, s16[64,1152]{1,0:T(8,128)(2,1)}, u32[]{:S(2)}, u32[]{:S(2)}) collective-permute-start(s16[64,1152]{1,0:T(8,128)(2,1)} %get-tuple-element.63), channel_id=1, source_target_pairs={{0,4},{1,5},{2,6},{3,7},{4,0},{5,1},{6,2},{7,3},{8,12},{9,13},{10,... | collective-permute-start | bytes 442376 | tf_op jit(solution)/shard_map/ppermute | solution.py:502
  261.7 11.9 %collective-permute-start.24 = (s16[64,1152]{1,0:T(8,128)(2,1)}, s16[64,1152]{1,0:T(8,128)(2,1)}, u32[]{:S(2)}, u32[]{:S(2)}) collective-permute-start(s16[64,1152]{1,0:T(8,128)(2,1)} %get-tuple-element.64), channel_id=1, source_target_pairs={{0,6},{1,7},{2,4},{3,5},{4,2},{5,3},{6,0},{7,1},{8,14},{9,15},{10,... | collective-permute-start | bytes 442376 | tf_op jit(solution)/shard_map/ppermute | solution.py:502
  273.6 1.0 copy-start.13
  275.8 37.5 %collective-permute-start.25 = (s16[64,1152]{1,0:T(8,128)(2,1)S(1)}, s16[64,1152]{1,0:T(8,128)(2,1)S(1)}, u32[]{:S(2)}, u32[]{:S(2)}) collective-permute-start(s16[64,1152]{1,0:T(8,128)(2,1)S(1)} %last_sum.2), channel_id=1, source_target_pairs={{0,0},{1,1},{2,8},{3,9},{4,16},{5,17},{6,24},{7,25},{8,2},{9,3},{1... | collective-permute-start | bytes 442376 | tf_op jit(solution)/shard_map/ppermute | solution.py:505
  294.1 28.0 %dynamic-slice-start = ((f32[8192]{0:T(1024)}, s32[]{:T(128)}), f32[1024]{0:T(1024)S(1)}, s32[]{:S(2)}) async-start(f32[8192]{0:T(1024)} %param.8, s32[]{:T(128)} %select_n.37), calls=%async_computation | async-start | bytes 8704 | tf_op jit(solution)/shard_map/dynamic_slice | solution.py:515
  295.2 6.9 %collective-permute-start.27 = (s16[64,1152]{1,0:T(8,128)(2,1)S(1)}, s16[64,1152]{1,0:T(8,128)(2,1)S(1)}, u32[]{:S(2)}, u32[]{:S(2)}) collective-permute-start(s16[64,1152]{1,0:T(8,128)(2,1)S(1)} %get-tuple-element.68), channel_id=1, source_target_pairs={{0,2},{1,3},{2,0},{3,1},{4,6},{5,7},{6,4},{7,5},{8,10},{9,11},{10,... | collective-permute-start | bytes 442376 | tf_op jit(solution)/shard_map/ppermute | solution.py:502
  295.3 13.7 %collective-permute-start.28 = (s16[64,1152]{1,0:T(8,128)(2,1)S(1)}, s16[64,1152]{1,0:T(8,128)(2,1)S(1)}, u32[]{:S(2)}, u32[]{:S(2)}) collective-permute-start(s16[64,1152]{1,0:T(8,128)(2,1)S(1)} %get-tuple-element.69), channel_id=1, source_target_pairs={{0,4},{1,5},{2,6},{3,7},{4,0},{5,1},{6,2},{7,3},{8,12},{9,13},{10,... | collective-permute-start | bytes 442376 | tf_op jit(solution)/shard_map/ppermute | solution.py:502
  297.7 11.3 %collective-permute-start.29 = (s16[64,1152]{1,0:T(8,128)(2,1)S(1)}, s16[64,1152]{1,0:T(8,128)(2,1)S(1)}, u32[]{:S(2)}, u32[]{:S(2)}) collective-permute-start(s16[64,1152]{1,0:T(8,128)(2,1)S(1)} %get-tuple-element.70), channel_id=1, source_target_pairs={{0,6},{1,7},{2,4},{3,5},{4,2},{5,3},{6,0},{7,1},{8,14},{9,15},{10,... | collective-permute-start | bytes 442376 | tf_op jit(solution)/shard_map/ppermute | solution.py:502
  309.3 12.5 %collective-permute-start.30 = (s16[64,1152]{1,0:T(8,128)(2,1)S(1)}, s16[64,1152]{1,0:T(8,128)(2,1)S(1)}, u32[]{:S(2)}, u32[]{:S(2)}) collective-permute-start(s16[64,1152]{1,0:T(8,128)(2,1)S(1)} %last_sum.3), channel_id=1, source_target_pairs={{0,0},{1,1},{2,8},{3,9},{4,16},{5,17},{6,24},{7,25},{8,2},{9,3},{1... | collective-permute-start | bytes 442376 | tf_op jit(solution)/shard_map/ppermute | solution.py:505

commit v5 on v4

--- a/solution.py
+++ b/solution.py
@@ -49,21 +49,37 @@
 
 
 def compiler_params():
-    return pltpu.CompilerParams(vmem_limit_bytes=20 * megabyte)
+    return pltpu.CompilerParams(vmem_limit_bytes=28 * megabyte)
 
 
 def small_cost():
     return pl.CostEstimate(flops=1024, bytes_accessed=1024, transcendentals=0)
 
 
+streams = 4
+
+
+def head_specs(depth, width, skip=0):
+    block = (depth // streams, width)
+    return [pl.BlockSpec(block, lambda j, q=q: (q, j + skip)) for q in range(streams)]
+
+
+def dot_head(x, head_refs):
+    each = x.shape[1] // len(head_refs)
+    return functools.reduce(
+        jnp.add, [dot(x[:, q * each : (q + 1) * each], ref[...]) for q, ref in enumerate(head_refs)]
+    )
+
+
 def constant(*shape):
     return pl.BlockSpec(shape, lambda *_: (0,) * len(shape))
 
 
-def far_kernel(width, x_ref, head_ref, first_ref, second_ref, powers_ref):
+def far_kernel(width, x_ref, *refs):
+    head_refs, (first_ref, second_ref, powers_ref) = refs[:streams], refs[streams:]
     tile = pl.program_id(0)
     columns = first_ref.shape[1] - tail
-    value = dot(x_ref[...], head_ref[...])
+    value = dot_head(x_ref, head_refs)
     q = value.shape[0] // 4
     first = jnp.concatenate([value[:q], value[2 * q : 3 * q]], axis=0)
     second = jnp.concatenate([value[q : 2 * q], value[3 * q :]], axis=0)
@@ -77,17 +93,14 @@
     return pl.pallas_call(
         functools.partial(far_kernel, width),
         grid=(tiles,),
-        in_specs=[
-            constant(rows, depth),
-            pl.BlockSpec((depth, width), lambda j: (0, j + skip)),
-        ],
+        in_specs=[constant(rows, depth)] + head_specs(depth, width, skip),
         out_specs=[constant(rows // 2, columns + tail)] * 2,
         out_shape=[jax.ShapeDtypeStruct((rows // 2, columns + tail), jnp.int16)] * 2,
         scratch_shapes=[pltpu.VMEM((rows, tail), jnp.float32)],
         compiler_params=compiler_params(),
         cost_estimate=small_cost(),
         name="far_codes",
-    )(rows_in, head)
+    )(rows_in, *[head] * streams)
 
 
 def decode_any(refs, tile, width):
@@ -102,14 +115,15 @@
     return jnp.where(tile < each, low, high)
 
 
-def near_kernel(width, parts, x_ref, y_ref, head_ref, *refs):
+def near_kernel(width, parts, x_ref, y_ref, *refs):
+    head_refs, refs = refs[:streams], refs[streams:]
     by_x_refs, by_y_refs = refs[:parts], refs[parts : 2 * parts]
     to_x_ref, to_y_ref, powers_ref = refs[2 * parts :]
     tile = pl.program_id(0)
     rows = x_ref.shape[0]
     half = rows // 2
     columns = to_x_ref.shape[1] - tail
-    value = dot(jnp.concatenate([x_ref[...], y_ref[...]], axis=0), head_ref[...])
+    value = dot_head(jnp.concatenate([x_ref[...], y_ref[...]], axis=0), head_refs)
     more_x = decode_any(by_y_refs, tile, width)
     more_y = decode_any(by_x_refs, tile, width)
     for_x = jnp.concatenate([value[:half], value[half:rows] + more_x], axis=0)
@@ -127,7 +141,7 @@
         functools.partial(near_kernel, width, len(by_x)),
         grid=(tiles,),
         in_specs=[pl.BlockSpec((rows, depth), lambda j: (part, 0))] * 2
-        + [pl.BlockSpec((depth, width), lambda j: (0, j + skip))]
+        + head_specs(depth, width, skip)
         + [received] * (2 * len(by_x)),
         out_specs=[constant(rows, columns + tail)] * 2,
         out_shape=[jax.ShapeDtypeStruct((rows, columns + tail), jnp.int16)] * 2,
@@ -135,11 +149,11 @@
         compiler_params=compiler_params(),
         cost_estimate=small_cost(),
         name="near_codes",
-    )(rows_x, rows_y, head, *by_x, *by_y)
-
-
-def own_kernel(x_ref, head_ref, out_ref):
-    out_ref[...] = dot(x_ref[...], head_ref[...])
+    )(rows_x, rows_y, *[head] * streams, *by_x, *by_y)
+
+
+def own_kernel(x_ref, *refs):
+    refs[-1][...] = dot_head(x_ref, refs[:-1])
 
 
 def own_logits(rows_in, head, width):
@@ -148,16 +162,13 @@
     return pl.pallas_call(
         own_kernel,
         grid=(columns // width,),
-        in_specs=[
-            constant(rows, depth),
-            pl.BlockSpec((depth, width), lambda j: (0, j)),
-        ],
+        in_specs=[constant(rows, depth)] + head_specs(depth, width),
         out_specs=pl.BlockSpec((rows, width), lambda j: (0, j)),
         out_shape=jax.ShapeDtypeStruct((rows, columns), jnp.float32),
         compiler_params=compiler_params(),
         cost_estimate=small_cost(),
         name="own_logits",
-    )(rows_in, head)
+    )(rows_in, *[head] * streams)
 
 
 def members(ids, start, width):
@@ -302,17 +313,18 @@
 
 
 def back_kernel(tiles, keeps, place_ref, *refs):
-    grads, terms, head_ref, outs, total_ref = refs[:5], refs[5:10], refs[10], refs[11:-1], refs[-1]
+    grads, terms, refs = refs[:5], refs[5:10], refs[10:]
+    head_refs, outs, total_ref = refs[:streams], refs[streams:-1], refs[-1]
     tile = pl.program_id(0)
 
     @pl.when(tile == 0)
     def _():
         total_ref[...] = jnp.zeros_like(total_ref)
 
-    grad = jnp.concatenate([g[...] for g in grads], axis=0)
-    total_ref[...] += lax.dot_general(
-        grad, head_ref[...], (((1,), (1,)), ((), ())), preferred_element_type=jnp.float32
-    )
+    grad = jnp.concatenate([g[...] for g in grads], axis=0).T
+    each = total_ref.shape[0] // streams
+    for q, head_ref in enumerate(head_refs):
+        total_ref[q * each : (q + 1) * each, :] += dot(head_ref[...], grad)
 
     @pl.when(tile == tiles - 1)
     def _():
@@ -321,11 +333,12 @@
         width = outs[0].shape[1] - tail
         for k, out_ref in enumerate(outs):
             start = pl.multiple_of((place_ref[1] ^ k) * width, width)
+            value = total_ref[pl.ds(start, width), :].T
             if k == 0 and keeps:
-                out_ref[:, :width] = total_ref[:, pl.ds(start, width)]
+                out_ref[:, :width] = value
                 out_ref[:, width:] = term
             else:
-                put_row(out_ref, jnp.concatenate([total_ref[:, pl.ds(start, width)], term], axis=1))
+                put_row(out_ref, jnp.concatenate([value, term], axis=1))
 
 
 def back(grads, head, place, width, group, keeps):
@@ -336,6 +349,7 @@
     types = [jnp.float32 if keeps and k == 0 else jnp.int16 for k in range(blocks)]
     across = lambda g: pl.BlockSpec((g.shape[0], width), lambda j, place: (0, j))
     beside = lambda g: pl.BlockSpec((g.shape[0], tail), lambda j, place: (0, columns // tail))
+    block = (blocks * part // streams, width)
     return pl.pallas_call(
         functools.partial(back_kernel, columns // width, keeps),
         grid_spec=pltpu.PrefetchScalarGridSpec(
@@ -343,15 +357,15 @@
             grid=(columns // width,),
             in_specs=[across(g) for g in grads]
             + [beside(g) for g in grads]
-            + [pl.BlockSpec((blocks * part, width), lambda j, place: (place[0], j))],
+            + [pl.BlockSpec(block, lambda j, place, q=q: (place[0] * streams + q, j)) for q in range(streams)],
             out_specs=[constant(rows, part + tail)] * blocks,
-            scratch_shapes=[pltpu.VMEM((rows, blocks * part), jnp.float32)],
+            scratch_shapes=[pltpu.VMEM((blocks * part, rows), jnp.float32)],
         ),
         out_shape=[jax.ShapeDtypeStruct((rows, part + tail), t) for t in types],
         compiler_params=compiler_params(),
         cost_estimate=small_cost(),
         name="grad_rows",
-    )(place, *grads, *grads, head)
+    )(place, *grads, *grads, *[head] * streams)
 
 
 def group_kernel(place_ref, keep_ref, *refs):
@@ -475,33 +489,33 @@
             for i in range(group):
                 moves.append((p * vocab_size + r * group + i, r * vocab_size + p * group + i))
 
+    quarter = half // 2
     infos, grads = [], []
     for part, (sums_x, sums_y) in enumerate(halves):
         logits, listed, stats = row_stats(part, own, sums_x, sums_y, after(ids, *infos), width)
         stats = lax.all_gather(stats, "vocab", axis=0)
         grad, info = logit_grads(part, logits, listed, stats, loss_scale[:, None], width)
         infos.append(info)
-        grads.append((grad, send(grad, to_x), send(grad, to_y)))
+        grads.append(grad)
     log_refusal = jnp.concatenate([info[:, 0] for info in infos])
 
-    quarter = half // 2
-    gathered = []
-    for grad, grad_x, grad_y in grads:
-        far_0 = send(grad_y[:quarter], to_x)
-        far_1 = send(grad_x[quarter:], to_y)
-        gathered.append((grad, grad_x, grad_y, far_0, far_1))
-    (_, grad_x, grad_y, far_0, far_1) = gathered[1]
-    waits_other, waits_mine = [grad_x, grad_y], [far_0, far_1]
-    grad_cols = []
-    for parts in gathered:
+    gathering, waits_other, waits_mine, grad_cols = [], [], [], []
+    waits_send = [infos[-1]]
+    for grad in grads:
+        sent = after(grad, *gathering)
+        grad_x, grad_y = send(sent, to_x), send(sent, to_y)
+        passed_x, passed_y = after(grad_y, *waits_send)[:quarter], after(grad_x, *waits_send)[quarter:]
+        gathering = [send(passed_x, to_x), send(passed_y, to_y)]
+        parts = (grad, grad_x, grad_y, *gathering)
         others = back(parts, head, after(place_other, *waits_other), width, group, False)
         received = [lax.ppermute(c, "vocab", to) for c, to in zip(others, to_member[spread - 1 :])]
         keep, *codes = back(parts, head, after(place_mine, *others, *waits_mine), width, group, True)
         received += [lax.ppermute(c, "vocab", to) for c, to in zip(codes, to_member)]
+        waits_send = [keep]
         keep, *codes = group_sum(place_block, keep, received)
         received = [lax.ppermute(c, "vocab", to) for c, to in zip(codes, to_block)]
-        waits_other, waits_mine = [keep], received
         codes = last_sum(keep, received)
+        waits_other, waits_mine = received, [codes]
         grad_cols.append(lax.ppermute(codes, ("prompt", "vocab"), moves))
 
     slice_width = model_width // vocab_size

time: 325 us -> 286 us (0.88)
  waiting for transfers between devices: 89 us -> 53.3 us
  local copies, waits for them, and re-layouts: 28.3 us -> 18.8 us
  Pallas kernels: 129 us -> 135 us
    ppermute x21, waiting for transfers between devices: 60.7 us -> 24.3 us  [shards(): send = lambda value, pairs: lax.ppermute(value, 'prompt', pairs)]
    unnamed x39 -> x69, local copies, waits for them, and re-layouts: 22.7 us -> 16.5 us
    pallas_call x2, Pallas kernels: 9.18 us -> 15.2 us  [far_codes(): pl.pallas_call(functools.partial(far_kernel, width), grid=(tiles,), in_sp...]
  transfers between devices with their start and end apart: 31 -> 31, of which waited for: 17 -> 13; matrix products, arithmetic and copies ran while one was open for 1% -> 1% of each run, Pallas kernels for 30% -> 40%
where the time goes in v5:
time: 286 us; the launch traced here: 285 us
  Pallas kernels  135 us (47%)
  waiting for transfers between devices  53.3 us (19%)
  starting transfers between devices  41.2 us (14%)
  blocking collectives  29 us (10%)
  local copies, waits for them, and re-layouts  18.8 us (7%)
  other arithmetic  6.53 us (2%)
    pallas_call x4, Pallas kernels, back(): pl.pallas_call(functools.partial(back_kernel, columns // width, keeps), g...  52.5 us
    pallas_call x3, Pallas kernels, near_codes(): pl.pallas_call(functools.partial(near_kernel, width, len(by_x)), grid=(ti...  31.5 us
    all_gather x2, blocking collectives, shards(): stats = lax.all_gather(stats, 'vocab', axis=0)  29 us
    ppermute x21, waiting for transfers between devices, shards(): send = lambda value, pairs: lax.ppermute(value, 'prompt', pairs)  24.3 us
    ppermute x21, starting transfers between devices, shards(): send = lambda value, pairs: lax.ppermute(value, 'prompt', pairs)  22.7 us
    ppermute x6, waiting for transfers between devices, shards(): received = [lax.ppermute(c, 'vocab', to) for c, to in zip(codes, to_block)]  19.3 us
    unnamed x69, local copies, waits for them, and re-layouts  16.5 us
    pallas_call x2, Pallas kernels, far_codes(): pl.pallas_call(functools.partial(far_kernel, width), grid=(tiles,), in_sp...  15.2 us
  transfers between devices with their start and end apart: 31, of which 13 were waited for; matrix products, arithmetic and copies ran while one was open for 1% of the time, Pallas kernels for 40%

profile of v5, /device:TPU:2, one launch (start us, length us, event | category | flops | bytes accessed | tf_op | source)
XLA Modules:
  0.0 284.5 jit_solution(10881512760688342649)
XLA Ops:
  0.7 2.2 fusion
  4.3 2.0 collective-permute-start.1
  6.4 1.4 collective-permute-start.2
  7.8 13.6 %own_logits.1.refs_0_ = f32[128,8192]{1,0:T(8,128)S(1)} custom-call(bf16[128,2048]{1,0:T(8,128)(2,1)S(1)} %get-tuple-element.83.x_ref, bf16[2048,8192]{1,0:T(8,128)(2,1)} %refs_13_.7, bf16[2048,8192]{1,0:T(8,128)(2,1)} %refs_13_.7, bf16[2048,8192]{1,0:T(8,128)(2,1)} %refs_13_.7, bf16[2048,8192]{1,0:T(8,128)(2,1)} %refs_13_.7), custom_call_target="tpu_custom_call" | custom-call | flops 1024 | bytes 1024 | tf_op jit(solution)/shard_map/own_logits/pallas_call | solution.py:162
  21.4 2.0 copy-done
  23.4 5.1 %collective-permute-done.1.y_ref = bf16[128,2048]{1,0:T(8,128)(2,1)S(1)} collective-permute-done((bf16[128,2048]{1,0:T(8,128)(2,1)S(1)}, bf16[128,2048]{1,0:T(8,128)(2,1)S(1)}, u32[]{:S(2)}, u32[]{:S(2)}) %collective-permute-start.1) | collective-permute-done | bytes 524320 | tf_op jit(solution)/shard_map/ppermute | solution.py:445
  28.5 1.6 collective-permute-done.2.x_ref
  30.2 7.6 %far_codes.2 = (s16[64,4224]{1,0:T(8,128)(2,1)S(1)}, s16[64,4224]{1,0:T(8,128)(2,1)S(1)}) custom-call(bf16[128,2048]{1,0:T(8,128)(2,1)S(1)} %collective-permute-done.2.x_ref, bf16[2048,8192]{1,0:T(8,128)(2,1)} %refs_13_.7, bf16[2048,8192]{1,0:T(8,128)(2,1)} %refs_13_.7, bf16[2048,8192]{1,0:T(8,128)(2,1)} %refs_13_.7, bf16[2048,8192]{1,0:T(8,128)(2,1)} %refs_13_.7), custom_call_target="tpu_custom_call" | custom-call | flops 1024 | bytes 1024 | tf_op jit(solution)/shard_map/far_codes/pallas_call | solution.py:93
  37.7 0.9 collective-permute-start.3
  38.6 1.5 collective-permute-start.4
  40.1 7.6 %far_codes.3 = (s16[64,4224]{1,0:T(8,128)(2,1)S(1)}, s16[64,4224]{1,0:T(8,128)(2,1)S(1)}) custom-call(bf16[128,2048]{1,0:T(8,128)(2,1)S(1)} %collective-permute-done.2.x_ref, bf16[2048,8192]{1,0:T(8,128)(2,1)} %refs_13_.7, bf16[2048,8192]{1,0:T(8,128)(2,1)} %refs_13_.7, bf16[2048,8192]{1,0:T(8,128)(2,1)} %refs_13_.7, bf16[2048,8192]{1,0:T(8,128)(2,1)} %refs_13_.7), custom_call_target="tpu_custom_call" | custom-call | flops 1024 | bytes 1024 | tf_op jit(solution)/shard_map/far_codes/pallas_call | solution.py:93
  48.3 1.2 collective-permute-start.7
  49.5 3.5 %collective-permute-done.3.refs_4_ = s16[64,4224]{1,0:T(8,128)(2,1)S(1)} collective-permute-done((s16[64,4224]{1,0:T(8,128)(2,1)S(1)}, s16[64,4224]{1,0:T(8,128)(2,1)S(1)}, u32[]{:S(2)}, u32[]{:S(2)}) %collective-permute-start.3) | collective-permute-done | bytes 540704 | tf_op jit(solution)/shard_map/ppermute | solution.py:445
  53.7 8.5 %near_codes.3 = (s16[64,4224]{1,0:T(8,128)(2,1)}, s16[64,4224]{1,0:T(8,128)(2,1)}) custom-call(bf16[128,2048]{1,0:T(8,128)(2,1)S(1)} %collective-permute-done.x_ref, bf16[128,2048]{1,0:T(8,128)(2,1)S(1)} %collective-permute-done.1.y_ref, bf16[2048,8192]{1,0:T(8,128)(2,1)} %refs_13_.7, bf16[2048,8192]{1,0:T(8,128)(2,1)} %refs_13_.7, ...), custom_call_target="tpu_custom_call" | custom-call | flops 1024 | bytes 1024 | tf_op jit(solution)/shard_map/near_codes/pallas_call | solution.py:140
  62.2 1.4 collective-permute-start.5
  64.6 8.6 %near_codes.4 = (s16[64,4224]{1,0:T(8,128)(2,1)}, s16[64,4224]{1,0:T(8,128)(2,1)}) custom-call(bf16[128,2048]{1,0:T(8,128)(2,1)S(1)} %collective-permute-done.x_ref, bf16[128,2048]{1,0:T(8,128)(2,1)S(1)} %collective-permute-done.1.y_ref, bf16[2048,8192]{1,0:T(8,128)(2,1)} %refs_13_.7, bf16[2048,8192]{1,0:T(8,128)(2,1)} %refs_13_.7, ...), custom_call_target="tpu_custom_call" | custom-call | flops 1024 | bytes 1024 | tf_op jit(solution)/shard_map/near_codes/pallas_call | solution.py:140
  73.2 1.0 collective-permute-start.10
  74.3 1.6 collective-permute-start.8
  76.1 0.8 collective-permute-done.9.refs_3_
  76.9 14.4 %near_codes.5 = (s16[64,8320]{1,0:T(8,128)(2,1)S(1)}, s16[64,8320]{1,0:T(8,128)(2,1)S(1)}) custom-call(bf16[128,2048]{1,0:T(8,128)(2,1)S(1)} %collective-permute-done.x_ref, bf16[128,2048]{1,0:T(8,128)(2,1)S(1)} %collective-permute-done.1.y_ref, bf16[2048,8192]{1,0:T(8,128)(2,1)} %refs_13_.7, bf16[2048,8192]{1,0:T(8,128)(2,1)} %refs_13_.7, ...), custom_call_target="tpu_custom_call" | custom-call | flops 1024 | bytes 1024 | tf_op jit(solution)/shard_map/near_codes/pallas_call | solution.py:140
  91.3 1.5 collective-permute-start.13
  93.4 7.0 %row_stats.2 = (f32[64,8192]{1,0:T(8,128)S(1)}, f32[64,8192]{1,0:T(8,128)S(1)}, f32[64,128]{1,0:T(8,128)S(1)}) custom-call(f32[128,8192]{1,0:T(8,128)S(1)} %copy-done.1, s16[64,4224]{1,0:T(8,128)(2,1)} %collective-permute-done.5.refs_1_, s16[64,4224]{1,0:T(8,128)(2,1)} %collective-permute-done.8.refs_2_, s16[64,4224]{1,0:T(8,128)(2,1)} %collective-permute-done.9.refs_3_, ...), custom_call_target="tpu_custom_call" | custom-call | flops 1024 | bytes 1024 | tf_op jit(solution)/shard_map/row_stats/pallas_call | solution.py:222
  100.3 14.5 %all-gather = f32[512,128]{1,0:T(8,128)S(1)} all-gather(f32[64,128]{1,0:T(8,128)S(1)} %get-tuple-element.52), channel_id=2, replica_groups=mesh['prompt'=4,'vocab'=8] {'vocab'}, dimensions={0}, use_global_device_ids=true | all-gather | bytes 294912 | tf_op jit(solution)/shard_map/all_gather | solution.py:496
  114.9 2.2 logit_grads.2
  117.7 1.5 collective-permute-start.12
  119.2 5.8 %row_stats.3 = (f32[64,8192]{1,0:T(8,128)S(1)}, f32[64,8192]{1,0:T(8,128)S(1)}, f32[64,128]{1,0:T(8,128)S(1)}) custom-call(f32[128,8192]{1,0:T(8,128)S(1)} %copy-done.1, s16[64,8320]{1,0:T(8,128)(2,1)S(1)} %collective-permute-done.13.refs_1_, s16[64,8320]{1,0:T(8,128)(2,1)S(1)} %collective-permute-done.14.refs_2_, s32[128,16]{1,0:T(8,128)S(1)} %fusion.6.refs_5_.refs_3_), custom_call_target="tpu_custom_call" | custom-call | flops 1024 | bytes 1024 | tf_op jit(solution)/shard_map/row_stats/pallas_call | solution.py:222
  125.0 14.5 %all-gather.1 = f32[512,128]{1,0:T(8,128)S(1)} all-gather(f32[64,128]{1,0:T(8,128)S(1)} %get-tuple-element.61), channel_id=3, replica_groups=mesh['prompt'=4,'vocab'=8] {'vocab'}, dimensions={0}, use_global_device_ids=true | all-gather | bytes 294912 | tf_op jit(solution)/shard_map/all_gather | solution.py:496
  139.5 3.1 %logit_grads.3 = (bf16[64,8320]{1,0:T(8,128)(2,1)}, f32[64,128]{1,0:T(8,128)S(1)}) custom-call(f32[64,8192]{1,0:T(8,128)S(1)} %get-tuple-element.59.logits_ref, f32[64,8192]{1,0:T(8,128)S(1)} %get-tuple-element.60.listed_ref, f32[8,64,128]{2,1,0:T(8,128)S(1)} %bitcast.9, f32[128,1]{1,0:T(8,128)S(1)} %copy.17.scale_ref), custom_call_target="tpu_custom_call" | custom-call | flops 1024 | bytes 1024 | tf_op jit(solution)/shard_map/logit_grads/pallas_call | solution.py:274
  142.9 1.5 collective-permute-start.16
  145.2 11.9 %collective-permute-done.16.refs_4_.refs_9_ = bf16[32,8320]{1,0:T(8,128)(2,1)S(1)} collective-permute-done((bf16[32,8320]{1,0:T(8,128)(2,1)S(1)}, bf16[32,8320]{1,0:T(8,128)(2,1)S(1)}, u32[]{:S(2)}, u32[]{:S(2)}) %collective-permute-start.16) | collective-permute-done | bytes 532512 | tf_op jit(solution)/shard_map/ppermute | solution.py:445
  157.1 0.8 copy-done.7
  157.9 0.8 copy-done.10
  158.7 1.4 collective-permute-start.22
  160.1 1.0 collective-permute-start.23
  161.2 1.2 copy-done.3
  162.5 1.2 copy-done.6
  163.7 1.0 copy-done.8
  164.7 1.0 copy-done.11
  165.8 13.7 %grad_rows.4 = s16[256,1152]{1,0:T(8,128)(2,1)} custom-call(s32[2]{0:T(128)S(1)} %pad_add_fusion.place_ref, bf16[64,8320]{1,0:T(8,128)(2,1)S(1)} %copy-done.6, bf16[64,8320]{1,0:T(8,128)(2,1)S(1)} %collective-permute-done.11.refs_1_.refs_6_, bf16[64,8320]{1,0:T(8,128)(2,1)S(1)} %copy-done.3, bf16[32,8320]{1,0:T(8,128)(2,1)S(1)} %copy-done.11, ...), custom_call_target="tpu_custom_call" | custom-call | flops 1024 | bytes 1024 | tf_op jit(solution)/shard_map/grad_rows/pallas_call | solution.py:353
  179.6 12.7 %grad_rows.5.keep_ref = f32[256,1152]{1,0:T(8,128)S(1)} custom-call(s32[2]{0:T(128)S(1)} %pad_add_fusion.1.place_ref, bf16[64,8320]{1,0:T(8,128)(2,1)S(1)} %copy-done.6, bf16[64,8320]{1,0:T(8,128)(2,1)S(1)} %collective-permute-done.11.refs_1_.refs_6_, bf16[64,8320]{1,0:T(8,128)(2,1)S(1)} %copy-done.4, bf16[32,8320]{1,0:T(8,128)(2,1)S(1)} %copy-done.11, ...), custom_call_target="tpu_custom_call" | custom-call | flops 1024 | bytes 1024 | tf_op jit(solution)/shard_map/grad_rows/pallas_call | solution.py:353
  192.3 1.0 copy-done.12
  193.3 0.8 slice.36
  194.2 1.0 collective-permute-start.25
  195.2 0.8 slice.35
  196.7 1.3 copy-done.13
  197.9 1.6 group_sum.2
  199.5 1.5 collective-permute-start.18
  201.0 2.4 collective-permute-start.19
  204.0 3.5 %collective-permute-done.18.refs_0_ = s16[64,1152]{1,0:T(8,128)(2,1)S(1)} collective-permute-done((s16[64,1152]{1,0:T(8,128)(2,1)S(1)}, s16[64,1152]{1,0:T(8,128)(2,1)S(1)}, u32[]{:S(2)}, u32[]{:S(2)}) %collective-permute-start.18) | collective-permute-done | bytes 147488 | tf_op jit(solution)/shard_map/ppermute | solution.py:516
  208.2 6.8 %collective-permute-done.19.refs_1_ = s16[64,1152]{1,0:T(8,128)(2,1)S(1)} collective-permute-done((s16[64,1152]{1,0:T(8,128)(2,1)S(1)}, s16[64,1152]{1,0:T(8,128)(2,1)S(1)}, u32[]{:S(2)}, u32[]{:S(2)}) %collective-permute-start.19) | collective-permute-done | bytes 147488 | tf_op jit(solution)/shard_map/ppermute | solution.py:516
  217.0 13.6 %grad_rows.6 = s16[256,1152]{1,0:T(8,128)(2,1)} custom-call(s32[2]{0:T(128)S(1)} %copy-done.25, bf16[64,8320]{1,0:T(8,128)(2,1)} %get-tuple-element.72.refs_0_.refs_5_, bf16[64,8320]{1,0:T(8,128)(2,1)S(1)} %collective-permute-done.22.refs_1_.refs_6_, bf16[64,8320]{1,0:T(8,128)(2,1)S(1)} %collective-permute-done.23.refs_2_.refs_7_, ...), custom_call_target="tpu_custom_call" | custom-call | flops 1024 | bytes 1024 | tf_op jit(solution)/shard_map/grad_rows/pallas_call | solution.py:353
  230.7 0.9 copy-done.15
  231.6 0.9 copy-done.17
  232.5 0.9 copy-done.19
  233.7 4.6 %collective-permute-start.21 = (s16[64,1152]{1,0:T(8,128)(2,1)S(1)}, s16[64,1152]{1,0:T(8,128)(2,1)S(1)}, u32[]{:S(2)}, u32[]{:S(2)}) collective-permute-start(s16[64,1152]{1,0:T(8,128)(2,1)S(1)} %last_sum.2), channel_id=1, source_target_pairs={{0,0},{1,1},{2,8},{3,9},{4,16},{5,17},{6,24},{7,25},{8,2},{9,3},{1... | collective-permute-start | bytes 442376 | tf_op jit(solution)/shard_map/ppermute | solution.py:519
  238.9 12.6 %grad_rows.7.keep_ref = f32[256,1152]{1,0:T(8,128)S(1)} custom-call(s32[2]{0:T(128)S(1)} %copy-done.23, bf16[64,8320]{1,0:T(8,128)(2,1)} %get-tuple-element.72.refs_0_.refs_5_, bf16[64,8320]{1,0:T(8,128)(2,1)S(1)} %collective-permute-done.22.refs_1_.refs_6_, bf16[64,8320]{1,0:T(8,128)(2,1)S(1)} %collective-permute-done.23.refs_2_.refs_7_, ...), custom_call_target="tpu_custom_call" | custom-call | flops 1024 | bytes 1024 | tf_op jit(solution)/shard_map/grad_rows/pallas_call | solution.py:353
  251.6 1.6 group_sum.3
  253.2 2.5 collective-permute-start.28
  255.8 1.9 collective-permute-start.29
  258.3 3.9 %collective-permute-done.27.refs_0_ = s16[64,1152]{1,0:T(8,128)(2,1)S(1)} collective-permute-done((s16[64,1152]{1,0:T(8,128)(2,1)S(1)}, s16[64,1152]{1,0:T(8,128)(2,1)S(1)}, u32[]{:S(2)}, u32[]{:S(2)}) %collective-permute-start.27) | collective-permute-done | bytes 147488 | tf_op jit(solution)/shard_map/ppermute | solution.py:516
  262.2 5.0 %collective-permute-done.28.refs_1_ = s16[64,1152]{1,0:T(8,128)(2,1)S(1)} collective-permute-done((s16[64,1152]{1,0:T(8,128)(2,1)S(1)}, s16[64,1152]{1,0:T(8,128)(2,1)S(1)}, u32[]{:S(2)}, u32[]{:S(2)}) %collective-permute-start.28) | collective-permute-done | bytes 147488 | tf_op jit(solution)/shard_map/ppermute | solution.py:516
  267.6 5.0 %collective-permute-start.30 = (s16[64,1152]{1,0:T(8,128)(2,1)S(1)}, s16[64,1152]{1,0:T(8,128)(2,1)S(1)}, u32[]{:S(2)}, u32[]{:S(2)}) collective-permute-start(s16[64,1152]{1,0:T(8,128)(2,1)S(1)} %last_sum.3), channel_id=1, source_target_pairs={{0,0},{1,1},{2,8},{3,9},{4,16},{5,17},{6,24},{7,25},{8,2},{9,3},{1... | collective-permute-start | bytes 442376 | tf_op jit(solution)/shard_map/ppermute | solution.py:519
  272.6 9.6 %collective-permute-done.30 = s16[64,1152]{1,0:T(8,128)(2,1)S(1)} collective-permute-done((s16[64,1152]{1,0:T(8,128)(2,1)S(1)}, s16[64,1152]{1,0:T(8,128)(2,1)S(1)}, u32[]{:S(2)}, u32[]{:S(2)}) %collective-permute-start.30) | collective-permute-done | bytes 147488 | tf_op jit(solution)/shard_map/ppermute | solution.py:519
  282.6 2.0 multiply_subtract_fusion
  (111 shorter events, 12.7 us)
Async XLA Ops:
  0.6 2.8 copy-start.26
  0.6 2.8 copy-start.27
  3.4 0.7 copy-start.29
  4.2 19.2 %collective-permute-start = (bf16[128,2048]{1,0:T(8,128)(2,1)S(1)}, bf16[128,2048]{1,0:T(8,128)(2,1)S(1)}, u32[]{:S(2)}, u32[]{:S(2)}) collective-permute-start(bf16[128,2048]{1,0:T(8,128)(2,1)S(1)} %get-tuple-element.82), channel_id=1, source_target_pairs={{0,8},{8,0},{16,24},{24,16},{1,9},{9,1},{17,25},{25,17},{2,10},{10... | collective-permute-start | bytes 1572872 | tf_op jit(solution)/shard_map/ppermute | solution.py:445
  4.3 24.2 %collective-permute-start.1 = (bf16[128,2048]{1,0:T(8,128)(2,1)S(1)}, bf16[128,2048]{1,0:T(8,128)(2,1)S(1)}, u32[]{:S(2)}, u32[]{:S(2)}) collective-permute-start(bf16[128,2048]{1,0:T(8,128)(2,1)S(1)} %get-tuple-element.81), channel_id=1, source_target_pairs={{0,16},{8,24},{16,0},{24,8},{1,17},{9,25},{17,1},{25,9},{2,18},{10... | collective-permute-start | bytes 1572872 | tf_op jit(solution)/shard_map/ppermute | solution.py:445
  6.4 23.8 %collective-permute-start.2 = (bf16[128,2048]{1,0:T(8,128)(2,1)S(1)}, bf16[128,2048]{1,0:T(8,128)(2,1)S(1)}, u32[]{:S(2)}, u32[]{:S(2)}) collective-permute-start(bf16[128,2048]{1,0:T(8,128)(2,1)S(1)} %get-tuple-element.80), channel_id=1, source_target_pairs={{0,24},{8,16},{16,8},{24,0},{1,25},{9,17},{17,9},{25,1},{2,26},{10... | collective-permute-start | bytes 1572872 | tf_op jit(solution)/shard_map/ppermute | solution.py:445
  21.4 2.0 copy-start
  37.7 15.3 %collective-permute-start.3 = (s16[64,4224]{1,0:T(8,128)(2,1)S(1)}, s16[64,4224]{1,0:T(8,128)(2,1)S(1)}, u32[]{:S(2)}, u32[]{:S(2)}) collective-permute-start(s16[64,4224]{1,0:T(8,128)(2,1)S(1)} %get-tuple-element.42), channel_id=1, source_target_pairs={{0,8},{8,0},{16,24},{24,16},{1,9},{9,1},{17,25},{25,17},{2,10},{10... | collective-permute-start | bytes 1622024 | tf_op jit(solution)/shard_map/ppermute | solution.py:445
  38.6 15.1 %collective-permute-start.4 = (s16[64,4224]{1,0:T(8,128)(2,1)S(1)}, s16[64,4224]{1,0:T(8,128)(2,1)S(1)}, u32[]{:S(2)}, u32[]{:S(2)}) collective-permute-start(s16[64,4224]{1,0:T(8,128)(2,1)S(1)} %get-tuple-element.43), channel_id=1, source_target_pairs={{0,16},{8,24},{16,0},{24,8},{1,17},{9,25},{17,1},{25,9},{2,18},{10... | collective-permute-start | bytes 1622024 | tf_op jit(solution)/shard_map/ppermute | solution.py:445
  47.7 16.9 %collective-permute-start.6 = (s16[64,4224]{1,0:T(8,128)(2,1)S(1)}, s16[64,4224]{1,0:T(8,128)(2,1)S(1)}, u32[]{:S(2)}, u32[]{:S(2)}) collective-permute-start(s16[64,4224]{1,0:T(8,128)(2,1)S(1)} %get-tuple-element.45), channel_id=1, source_target_pairs={{0,8},{8,0},{16,24},{24,16},{1,9},{9,1},{17,25},{25,17},{2,10},{10... | collective-permute-start | bytes 1622024 | tf_op jit(solution)/shard_map/ppermute | solution.py:445
  48.3 16.3 %collective-permute-start.7 = (s16[64,4224]{1,0:T(8,128)(2,1)S(1)}, s16[64,4224]{1,0:T(8,128)(2,1)S(1)}, u32[]{:S(2)}, u32[]{:S(2)}) collective-permute-start(s16[64,4224]{1,0:T(8,128)(2,1)S(1)} %get-tuple-element.46), channel_id=1, source_target_pairs={{0,16},{8,24},{16,0},{24,8},{1,17},{9,25},{17,1},{25,9},{2,18},{10... | collective-permute-start | bytes 1622024 | tf_op jit(solution)/shard_map/ppermute | solution.py:445
  62.2 13.9 %collective-permute-start.5 = (s16[64,4224]{1,0:T(8,128)(2,1)}, s16[64,4224]{1,0:T(8,128)(2,1)}, u32[]{:S(2)}, u32[]{:S(2)}) collective-permute-start(s16[64,4224]{1,0:T(8,128)(2,1)} %get-tuple-element.44), channel_id=1, source_target_pairs={{0,8},{8,0},{16,24},{24,16},{1,9},{9,1},{17,25},{25,17},{2,10},{10... | collective-permute-start | bytes 1622024 | tf_op jit(solution)/shard_map/ppermute | solution.py:445
  63.6 12.2 %copy-start.28 = (s32[128,16]{0,1:T(8,128)S(1)}, s32[128,16]{0,1:T(8,128)}, u32[]{:S(2)}) copy-start(s32[128,16]{0,1:T(8,128)} %param.9) | copy-start | bytes 24580
  63.6 12.3 %copy-start.31 = (s32[128]{0:T(128)S(1)}, s32[128]{0:T(128)}, u32[]{:S(2)}) copy-start(s32[128]{0:T(128)} %param.10) | copy-start | bytes 1540
  63.6 12.4 %copy-start.32 = (f32[128]{0:T(128)S(1)}, f32[128]{0:T(128)}, u32[]{:S(2)}) copy-start(f32[128]{0:T(128)} %param.11) | copy-start | bytes 1540
  63.6 13.3 %collective-permute-start.9 = (s16[64,4224]{1,0:T(8,128)(2,1)}, s16[64,4224]{1,0:T(8,128)(2,1)}, u32[]{:S(2)}, u32[]{:S(2)}) collective-permute-start(s16[64,4224]{1,0:T(8,128)(2,1)} %get-tuple-element.48), channel_id=1, source_target_pairs={{0,16},{8,24},{16,0},{24,8},{1,17},{9,25},{17,1},{25,9},{2,18},{10... | collective-permute-start | bytes 1622024 | tf_op jit(solution)/shard_map/ppermute | solution.py:445
  73.2 20.1 %collective-permute-start.10 = (s16[64,4224]{1,0:T(8,128)(2,1)}, s16[64,4224]{1,0:T(8,128)(2,1)}, u32[]{:S(2)}, u32[]{:S(2)}) collective-permute-start(s16[64,4224]{1,0:T(8,128)(2,1)} %get-tuple-element.49), channel_id=1, source_target_pairs={{0,16},{8,24},{16,0},{24,8},{1,17},{9,25},{17,1},{25,9},{2,18},{10... | collective-permute-start | bytes 1622024 | tf_op jit(solution)/shard_map/ppermute | solution.py:445
  74.3 19.1 %collective-permute-start.8 = (s16[64,4224]{1,0:T(8,128)(2,1)}, s16[64,4224]{1,0:T(8,128)(2,1)}, u32[]{:S(2)}, u32[]{:S(2)}) collective-permute-start(s16[64,4224]{1,0:T(8,128)(2,1)} %get-tuple-element.47), channel_id=1, source_target_pairs={{0,8},{8,0},{16,24},{24,16},{1,9},{9,1},{17,25},{25,17},{2,10},{10... | collective-permute-start | bytes 1622024 | tf_op jit(solution)/shard_map/ppermute | solution.py:445
  76.9 16.5 %copy-start.1 = (f32[128,8192]{1,0:T(8,128)S(1)}, f32[128,8192]{1,0:T(8,128)}, u32[]{:S(2)}) copy-start(f32[128,8192]{1,0:T(8,128)} %copy-done) | copy-start | bytes 12582916
  91.3 27.9 %collective-permute-start.13 = (s16[64,8320]{1,0:T(8,128)(2,1)S(1)}, s16[64,8320]{1,0:T(8,128)(2,1)S(1)}, u32[]{:S(2)}, u32[]{:S(2)}) collective-permute-start(s16[64,8320]{1,0:T(8,128)(2,1)S(1)} %get-tuple-element.55), channel_id=1, source_target_pairs={{0,8},{8,0},{16,24},{24,16},{1,9},{9,1},{17,25},{25,17},{2,10},{10... | collective-permute-start | bytes 3194888 | tf_op jit(solution)/shard_map/ppermute | solution.py:445
  92.8 26.4 %collective-permute-start.14 = (s16[64,8320]{1,0:T(8,128)(2,1)S(1)}, s16[64,8320]{1,0:T(8,128)(2,1)S(1)}, u32[]{:S(2)}, u32[]{:S(2)}) collective-permute-start(s16[64,8320]{1,0:T(8,128)(2,1)S(1)} %get-tuple-element.56), channel_id=1, source_target_pairs={{0,16},{8,24},{16,0},{24,8},{1,17},{9,25},{17,1},{25,9},{2,18},{10... | collective-permute-start | bytes 3194888 | tf_op jit(solution)/shard_map/ppermute | solution.py:445
  117.1 8.0 %copy-start.5 = (bf16[64,8320]{1,0:T(8,128)(2,1)}, bf16[64,8320]{1,0:T(8,128)(2,1)S(1)}, u32[]{:S(2)}) copy-start(bf16[64,8320]{1,0:T(8,128)(2,1)S(1)} %get-tuple-element.53.refs_0_.refs_5_) | copy-start | bytes 3194884
  117.1 25.8 %collective-permute-start.11 = (bf16[64,8320]{1,0:T(8,128)(2,1)S(1)}, bf16[64,8320]{1,0:T(8,128)(2,1)S(1)}, u32[]{:S(2)}, u32[]{:S(2)}) collective-permute-start(bf16[64,8320]{1,0:T(8,128)(2,1)S(1)} %get-tuple-element.53.refs_0_.refs_5_), channel_id=1, source_target_pairs={{0,8},{8,0},{16,24},{24,16},{1,9},{9,1},{17,25},{25,17},{2,10},{10... | collective-permute-start | bytes 3194888 | tf_op jit(solution)/shard_map/ppermute | solution.py:445
  117.7 26.8 %collective-permute-start.12 = (bf16[64,8320]{1,0:T(8,128)(2,1)S(1)}, bf16[64,8320]{1,0:T(8,128)(2,1)S(1)}, u32[]{:S(2)}, u32[]{:S(2)}) collective-permute-start(bf16[64,8320]{1,0:T(8,128)(2,1)S(1)} %get-tuple-element.53.refs_0_.refs_5_), channel_id=1, source_target_pairs={{0,16},{8,24},{16,0},{24,8},{1,17},{9,25},{17,1},{25,9},{2,18},{10... | collective-permute-start | bytes 3194888 | tf_op jit(solution)/shard_map/ppermute | solution.py:445
  142.9 14.1 %collective-permute-start.16 = (bf16[32,8320]{1,0:T(8,128)(2,1)S(1)}, bf16[32,8320]{1,0:T(8,128)(2,1)S(1)}, u32[]{:S(2)}, u32[]{:S(2)}) collective-permute-start(bf16[32,8320]{1,0:T(8,128)(2,1)S(1)} %slice.34), channel_id=1, source_target_pairs={{0,16},{8,24},{16,0},{24,8},{1,17},{9,25},{17,1},{25,9},{2,18},{10... | collective-permute-start | bytes 1597448 | tf_op jit(solution)/shard_map/ppermute | solution.py:445
  144.5 14.2 %copy-start.2 = (bf16[64,8320]{1,0:T(8,128)(2,1)}, bf16[64,8320]{1,0:T(8,128)(2,1)S(1)}, u32[]{:S(2)}) copy-start(bf16[64,8320]{1,0:T(8,128)(2,1)S(1)} %collective-permute-done.12.refs_2_.refs_7_) | copy-start | bytes 3194884
  144.5 13.4 %collective-permute-start.15 = (bf16[32,8320]{1,0:T(8,128)(2,1)S(1)}, bf16[32,8320]{1,0:T(8,128)(2,1)S(1)}, u32[]{:S(2)}, u32[]{:S(2)}) collective-permute-start(bf16[32,8320]{1,0:T(8,128)(2,1)S(1)} %slice.33), channel_id=1, source_target_pairs={{0,8},{8,0},{16,24},{24,16},{1,9},{9,1},{17,25},{25,17},{2,10},{10... | collective-permute-start | bytes 1597448 | tf_op jit(solution)/shard_map/ppermute | solution.py:445
  157.1 0.8 copy-start.7
  157.9 0.8 copy-start.10
  158.7 34.7 %collective-permute-start.22 = (bf16[64,8320]{1,0:T(8,128)(2,1)}, bf16[64,8320]{1,0:T(8,128)(2,1)S(1)}, u32[]{:S(2)}, u32[]{:S(2)}) collective-permute-start(bf16[64,8320]{1,0:T(8,128)(2,1)} %get-tuple-element.72.refs_0_.refs_5_), channel_id=1, source_target_pairs={{0,8},{8,0},{16,24},{24,16},{1,9},{9,1},{17,25},{25,17},{2,10},{10... | collective-permute-start | bytes 3194888 | tf_op jit(solution)/shard_map/ppermute | solution.py:445
  160.1 35.1 %collective-permute-start.23 = (bf16[64,8320]{1,0:T(8,128)(2,1)}, bf16[64,8320]{1,0:T(8,128)(2,1)S(1)}, u32[]{:S(2)}, u32[]{:S(2)}) collective-permute-start(bf16[64,8320]{1,0:T(8,128)(2,1)} %get-tuple-element.72.refs_0_.refs_5_), channel_id=1, source_target_pairs={{0,16},{8,24},{16,0},{24,8},{1,17},{9,25},{17,1},{25,9},{2,18},{10... | collective-permute-start | bytes 3194888 | tf_op jit(solution)/shard_map/ppermute | solution.py:445
  161.2 1.2 copy-start.3
  162.5 1.2 copy-start.6
  163.7 1.0 copy-start.8
  164.7 1.0 copy-start.11
  165.8 13.7 %copy-start.24 = (s32[2]{0:T(128)}, s32[2]{0:T(128)S(1)}, u32[]{:S(2)}) copy-start(s32[2]{0:T(128)S(1)} %pad_add_fusion.place_ref) | copy-start | bytes 28
  165.8 13.8 %copy-start.4 = (bf16[64,8320]{1,0:T(8,128)(2,1)S(1)}, bf16[64,8320]{1,0:T(8,128)(2,1)}, u32[]{:S(2)}) copy-start(bf16[64,8320]{1,0:T(8,128)(2,1)} %copy-done.2) | copy-start | bytes 3194884
  165.8 13.8 %copy-start.9 = (bf16[32,8320]{1,0:T(8,128)(2,1)S(1)}, bf16[32,8320]{1,0:T(8,128)(2,1)}, u32[]{:S(2)}) copy-start(bf16[32,8320]{1,0:T(8,128)(2,1)} %copy-done.7) | copy-start | bytes 1597444
  179.5 17.2 %collective-permute-start.17 = (s16[256,1152]{1,0:T(8,128)(2,1)}, s16[256,1152]{1,0:T(8,128)(2,1)}, u32[]{:S(2)}, u32[]{:S(2)}) collective-permute-start(s16[256,1152]{1,0:T(8,128)(2,1)} %grad_rows.4), channel_id=1, source_target_pairs={{0,1},{1,0},{2,3},{3,2},{4,5},{5,4},{6,7},{7,6},{8,9},{9,8},{10,11... | collective-permute-start | bytes 1769480 | tf_op jit(solution)/shard_map/ppermute | solution.py:511
  179.6 12.7 %copy-start.22 = (s32[2]{0:T(128)}, s32[2]{0:T(128)S(1)}, u32[]{:S(2)}) copy-start(s32[2]{0:T(128)S(1)} %pad_add_fusion.1.place_ref) | copy-start | bytes 28
  192.3 1.1 copy-start.12
  194.2 22.2 %collective-permute-start.25 = (bf16[32,8320]{1,0:T(8,128)(2,1)}, bf16[32,8320]{1,0:T(8,128)(2,1)S(1)}, u32[]{:S(2)}, u32[]{:S(2)}) collective-permute-start(bf16[32,8320]{1,0:T(8,128)(2,1)} %slice.36), channel_id=1, source_target_pairs={{0,16},{8,24},{16,0},{24,8},{1,17},{9,25},{17,1},{25,9},{2,18},{10... | collective-permute-start | bytes 1597448 | tf_op jit(solution)/shard_map/ppermute | solution.py:445
  196.0 20.3 %collective-permute-start.24 = (bf16[32,8320]{1,0:T(8,128)(2,1)}, bf16[32,8320]{1,0:T(8,128)(2,1)S(1)}, u32[]{:S(2)}, u32[]{:S(2)}) collective-permute-start(bf16[32,8320]{1,0:T(8,128)(2,1)} %slice.35), channel_id=1, source_target_pairs={{0,8},{8,0},{16,24},{24,16},{1,9},{9,1},{17,25},{25,17},{2,10},{10... | collective-permute-start | bytes 1597448 | tf_op jit(solution)/shard_map/ppermute | solution.py:445
  196.7 33.9 %copy-start.20 = (s32[4]{0:T(128)}, s32[4]{0:T(128)S(1)}, u32[]{:S(2)}) copy-start(s32[4]{0:T(128)S(1)} %pad_add_fusion.2.place_ref) | copy-start | bytes 52
  196.7 1.3 copy-start.13
  199.5 8.0 %collective-permute-start.18 = (s16[64,1152]{1,0:T(8,128)(2,1)S(1)}, s16[64,1152]{1,0:T(8,128)(2,1)S(1)}, u32[]{:S(2)}, u32[]{:S(2)}) collective-permute-start(s16[64,1152]{1,0:T(8,128)(2,1)S(1)} %get-tuple-element.67), channel_id=1, source_target_pairs={{0,2},{1,3},{2,0},{3,1},{4,6},{5,7},{6,4},{7,5},{8,10},{9,11},{10,... | collective-permute-start | bytes 442376 | tf_op jit(solution)/shard_map/ppermute | solution.py:516
  201.0 14.0 %collective-permute-start.19 = (s16[64,1152]{1,0:T(8,128)(2,1)S(1)}, s16[64,1152]{1,0:T(8,128)(2,1)S(1)}, u32[]{:S(2)}, u32[]{:S(2)}) collective-permute-start(s16[64,1152]{1,0:T(8,128)(2,1)S(1)} %get-tuple-element.68), channel_id=1, source_target_pairs={{0,4},{1,5},{2,6},{3,7},{4,0},{5,1},{6,2},{7,3},{8,12},{9,13},{10,... | collective-permute-start | bytes 442376 | tf_op jit(solution)/shard_map/ppermute | solution.py:516
  203.5 12.2 %collective-permute-start.20 = (s16[64,1152]{1,0:T(8,128)(2,1)S(1)}, s16[64,1152]{1,0:T(8,128)(2,1)S(1)}, u32[]{:S(2)}, u32[]{:S(2)}) collective-permute-start(s16[64,1152]{1,0:T(8,128)(2,1)S(1)} %get-tuple-element.69), channel_id=1, source_target_pairs={{0,6},{1,7},{2,4},{3,5},{4,2},{5,3},{6,0},{7,1},{8,14},{9,15},{10,... | collective-permute-start | bytes 442376 | tf_op jit(solution)/shard_map/ppermute | solution.py:516
  207.5 0.7 copy-start.14
  215.0 0.7 copy-start.16
  230.6 21.0 %collective-permute-start.26 = (s16[256,1152]{1,0:T(8,128)(2,1)}, s16[256,1152]{1,0:T(8,128)(2,1)}, u32[]{:S(2)}, u32[]{:S(2)}) collective-permute-start(s16[256,1152]{1,0:T(8,128)(2,1)} %grad_rows.6), channel_id=1, source_target_pairs={{0,1},{1,0},{2,3},{3,2},{4,5},{5,4},{6,7},{7,6},{8,9},{9,8},{10,11... | collective-permute-start | bytes 1769480 | tf_op jit(solution)/shard_map/ppermute | solution.py:511
  230.7 0.9 copy-start.15
  231.6 0.9 copy-start.17
  232.5 0.9 copy-start.19
  233.7 17.8 %copy-start.21 = (s32[4]{0:T(128)S(1)}, s32[4]{0:T(128)}, u32[]{:S(2)}) copy-start(s32[4]{0:T(128)} %copy-done.20) | copy-start | bytes 52
  233.7 38.9 %collective-permute-start.21 = (s16[64,1152]{1,0:T(8,128)(2,1)S(1)}, s16[64,1152]{1,0:T(8,128)(2,1)S(1)}, u32[]{:S(2)}, u32[]{:S(2)}) collective-permute-start(s16[64,1152]{1,0:T(8,128)(2,1)S(1)} %last_sum.2), channel_id=1, source_target_pairs={{0,0},{1,1},{2,8},{3,9},{4,16},{5,17},{6,24},{7,25},{8,2},{9,3},{1... | collective-permute-start | bytes 442376 | tf_op jit(solution)/shard_map/ppermute | solution.py:519
  238.3 0.7 copy-start.23
  251.5 31.0 %dynamic-slice-start = ((f32[8192]{0:T(1024)}, s32[]{:T(128)}), f32[1024]{0:T(1024)S(1)}, s32[]{:S(2)}) async-start(f32[8192]{0:T(1024)} %param.8, s32[]{:T(128)} %select_n.37), calls=%async_computation | async-start | bytes 8704 | tf_op jit(solution)/shard_map/dynamic_slice | solution.py:529
  251.5 31.0 %copy-start.30 = (f32[128]{0:T(128)S(1)}, f32[128]{0:T(128)}, u32[]{:S(2)}) copy-start(f32[128]{0:T(128)} %copy-done.29) | copy-start | bytes 1540
  251.5 31.0 %copy-start.33 = (f32[128]{0:T(128)S(1)}, f32[128]{0:T(128)}, u32[]{:S(2)}) copy-start(f32[128]{0:T(128)} %get-tuple-element.84) | copy-start | bytes 1540
  253.2 9.1 %collective-permute-start.27 = (s16[64,1152]{1,0:T(8,128)(2,1)S(1)}, s16[64,1152]{1,0:T(8,128)(2,1)S(1)}, u32[]{:S(2)}, u32[]{:S(2)}) collective-permute-start(s16[64,1152]{1,0:T(8,128)(2,1)S(1)} %get-tuple-element.77), channel_id=1, source_target_pairs={{0,2},{1,3},{2,0},{3,1},{4,6},{5,7},{6,4},{7,5},{8,10},{9,11},{10,... | collective-permute-start | bytes 442376 | tf_op jit(solution)/shard_map/ppermute | solution.py:516
  253.2 14.0 %collective-permute-start.28 = (s16[64,1152]{1,0:T(8,128)(2,1)S(1)}, s16[64,1152]{1,0:T(8,128)(2,1)S(1)}, u32[]{:S(2)}, u32[]{:S(2)}) collective-permute-start(s16[64,1152]{1,0:T(8,128)(2,1)S(1)} %get-tuple-element.78), channel_id=1, source_target_pairs={{0,4},{1,5},{2,6},{3,7},{4,0},{5,1},{6,2},{7,3},{8,12},{9,13},{10,... | collective-permute-start | bytes 442376 | tf_op jit(solution)/shard_map/ppermute | solution.py:516
  255.8 11.5 %collective-permute-start.29 = (s16[64,1152]{1,0:T(8,128)(2,1)S(1)}, s16[64,1152]{1,0:T(8,128)(2,1)S(1)}, u32[]{:S(2)}, u32[]{:S(2)}) collective-permute-start(s16[64,1152]{1,0:T(8,128)(2,1)S(1)} %get-tuple-element.79), channel_id=1, source_target_pairs={{0,6},{1,7},{2,4},{3,5},{4,2},{5,3},{6,0},{7,1},{8,14},{9,15},{10,... | collective-permute-start | bytes 442376 | tf_op jit(solution)/shard_map/ppermute | solution.py:516
  267.6 14.7 %collective-permute-start.30 = (s16[64,1152]{1,0:T(8,128)(2,1)S(1)}, s16[64,1152]{1,0:T(8,128)(2,1)S(1)}, u32[]{:S(2)}, u32[]{:S(2)}) collective-permute-start(s16[64,1152]{1,0:T(8,128)(2,1)S(1)} %last_sum.3), channel_id=1, source_target_pairs={{0,0},{1,1},{2,8},{3,9},{4,16},{5,17},{6,24},{7,25},{8,2},{9,3},{1... | collective-permute-start | bytes 442376 | tf_op jit(solution)/shard_map/ppermute | solution.py:519
  (2 other events, 1.3 us)

commit v6 on v4

--- a/solution.py
+++ b/solution.py
@@ -49,7 +49,7 @@
 
 
 def compiler_params():
-    return pltpu.CompilerParams(vmem_limit_bytes=20 * megabyte)
+    return pltpu.CompilerParams(vmem_limit_bytes=28 * megabyte)
 
 
 def small_cost():
@@ -90,28 +90,14 @@
     )(rows_in, head)
 
 
-def decode_any(refs, tile, width):
-    columns = refs[0].shape[1] - tail
-    if len(refs) == 1:
-        return decode(refs[0], tile, width, columns)
-    each = columns // width
-    if isinstance(tile, int):
-        return decode(refs[tile // each], tile % each, width, columns)
-    low = decode(refs[0], jnp.minimum(tile, each - 1), width, columns)
-    high = decode(refs[1], jnp.maximum(tile - each, 0), width, columns)
-    return jnp.where(tile < each, low, high)
-
-
-def near_kernel(width, parts, x_ref, y_ref, head_ref, *refs):
-    by_x_refs, by_y_refs = refs[:parts], refs[parts : 2 * parts]
-    to_x_ref, to_y_ref, powers_ref = refs[2 * parts :]
+def near_kernel(width, x_ref, y_ref, head_ref, by_x_ref, by_y_ref, to_x_ref, to_y_ref, powers_ref):
     tile = pl.program_id(0)
     rows = x_ref.shape[0]
     half = rows // 2
     columns = to_x_ref.shape[1] - tail
     value = dot(jnp.concatenate([x_ref[...], y_ref[...]], axis=0), head_ref[...])
-    more_x = decode_any(by_y_refs, tile, width)
-    more_y = decode_any(by_x_refs, tile, width)
+    more_x = decode(by_y_ref, tile, width, columns)
+    more_y = decode(by_x_ref, tile, width, columns)
     for_x = jnp.concatenate([value[:half], value[half:rows] + more_x], axis=0)
     for_y = jnp.concatenate([value[rows : rows + half] + more_y, value[rows + half :]], axis=0)
     put(to_x_ref, powers_ref, slice(0, rows), tile, width, columns, for_x)
@@ -119,23 +105,22 @@
 
 
 def near_codes(part, rows_x, rows_y, head, by_x, by_y, width, skip, tiles):
-    depth = rows_x.shape[1]
+    depth = head.shape[0]
     rows = rows_x.shape[0] // 2
     columns = tiles * width
-    received = pl.BlockSpec((rows // 2, by_x[0].shape[1]), lambda j: (part, 0))
-    return pl.pallas_call(
-        functools.partial(near_kernel, width, len(by_x)),
+    return pl.pallas_call(
+        functools.partial(near_kernel, width),
         grid=(tiles,),
         in_specs=[pl.BlockSpec((rows, depth), lambda j: (part, 0))] * 2
         + [pl.BlockSpec((depth, width), lambda j: (0, j + skip))]
-        + [received] * (2 * len(by_x)),
+        + [pl.BlockSpec((rows // 2, columns + tail), lambda j: (part, 0))] * 2,
         out_specs=[constant(rows, columns + tail)] * 2,
         out_shape=[jax.ShapeDtypeStruct((rows, columns + tail), jnp.int16)] * 2,
         scratch_shapes=[pltpu.VMEM((2 * rows, tail), jnp.float32)],
         compiler_params=compiler_params(),
         cost_estimate=small_cost(),
         name="near_codes",
-    )(rows_x, rows_y, head, *by_x, *by_y)
+    )(rows_x, rows_y, head, by_x, by_y)
 
 
 def own_kernel(x_ref, head_ref, out_ref):
@@ -173,13 +158,15 @@
     own_ref, by_x_refs, by_y_refs = refs[0], refs[1 : 1 + parts], refs[1 + parts : 1 + 2 * parts]
     ids_ref, logits_ref, listed_ref, out_ref = refs[1 + 2 * parts :]
     rows, columns = logits_ref.shape
+    each = columns // parts
     ids = ids_ref[...]
     top_all = jnp.full((rows, width), lowest, jnp.float32)
     top_ref = jnp.full((rows, width), lowest, jnp.float32)
     for start in range(0, columns, width):
         at = slice(start, start + width)
-        piece = own_ref[:, at] + decode_any(by_x_refs, start // width, width)
-        piece = piece + decode_any(by_y_refs, start // width, width)
+        where, inner = start // each, start % each // width
+        piece = own_ref[:, at] + decode(by_x_refs[where], inner, width, each)
+        piece = piece + decode(by_y_refs[where], inner, width, each)
         listed = jnp.where(members(ids, start, width), piece, lowest)
         logits_ref[:, at] = piece
         listed_ref[:, at] = listed
@@ -301,49 +288,49 @@
     return value, jnp.broadcast_to(term, beside.shape)
 
 
-def back_kernel(tiles, keeps, place_ref, *refs):
-    grads, terms, head_ref, outs, total_ref = refs[:5], refs[5:10], refs[10], refs[11:-1], refs[-1]
+def back_kernel(tiles, keeps, place_ref, grad_ref, beside_ref, head_ref, *refs):
+    outs, total_ref = refs[:-1], refs[-1]
     tile = pl.program_id(0)
 
     @pl.when(tile == 0)
     def _():
         total_ref[...] = jnp.zeros_like(total_ref)
 
-    grad = jnp.concatenate([g[...] for g in grads], axis=0)
     total_ref[...] += lax.dot_general(
-        grad, head_ref[...], (((1,), (1,)), ((), ())), preferred_element_type=jnp.float32
+        grad_ref[...], head_ref[...], (((1,), (1,)), ((), ())), preferred_element_type=jnp.float32
     )
 
     @pl.when(tile == tiles - 1)
     def _():
-        term = jnp.concatenate([t[...].astype(jnp.float32) for t in terms], axis=0)
-        term = jnp.broadcast_to(term[:, 0:1] + term[:, 1:2] + term[:, 2:3], (term.shape[0], tail))
+        term = beside_ref[...].astype(jnp.float32)
+        term = jnp.broadcast_to(term[:, 0:1] + term[:, 1:2] + term[:, 2:3], term.shape)
         width = outs[0].shape[1] - tail
         for k, out_ref in enumerate(outs):
             start = pl.multiple_of((place_ref[1] ^ k) * width, width)
+            value = total_ref[:, pl.ds(start, width)]
             if k == 0 and keeps:
-                out_ref[:, :width] = total_ref[:, pl.ds(start, width)]
+                out_ref[:, :width] = value
                 out_ref[:, width:] = term
             else:
-                put_row(out_ref, jnp.concatenate([total_ref[:, pl.ds(start, width)], term], axis=1))
-
-
-def back(grads, head, place, width, group, keeps):
+                put_row(out_ref, jnp.concatenate([value, term], axis=1))
+
+
+def back(grad, head, place, width, group, keeps):
     depth, columns = head.shape
-    rows = sum(g.shape[0] for g in grads)
+    rows = grad.shape[0]
     blocks = max(group // 2, 1)
     part = depth // group
     types = [jnp.float32 if keeps and k == 0 else jnp.int16 for k in range(blocks)]
-    across = lambda g: pl.BlockSpec((g.shape[0], width), lambda j, place: (0, j))
-    beside = lambda g: pl.BlockSpec((g.shape[0], tail), lambda j, place: (0, columns // tail))
     return pl.pallas_call(
         functools.partial(back_kernel, columns // width, keeps),
         grid_spec=pltpu.PrefetchScalarGridSpec(
             num_scalar_prefetch=1,
             grid=(columns // width,),
-            in_specs=[across(g) for g in grads]
-            + [beside(g) for g in grads]
-            + [pl.BlockSpec((blocks * part, width), lambda j, place: (place[0], j))],
+            in_specs=[
+                pl.BlockSpec((rows, width), lambda j, place: (0, j)),
+                pl.BlockSpec((rows, tail), lambda j, place: (0, columns // tail)),
+                pl.BlockSpec((blocks * part, width), lambda j, place: (place[0], j)),
+            ],
             out_specs=[constant(rows, part + tail)] * blocks,
             scratch_shapes=[pltpu.VMEM((rows, blocks * part), jnp.float32)],
         ),
@@ -351,7 +338,7 @@
         compiler_params=compiler_params(),
         cost_estimate=small_cost(),
         name="grad_rows",
-    )(place, *grads, *grads, head)
+    )(place, grad, grad, head)
 
 
 def group_kernel(place_ref, keep_ref, *refs):
@@ -435,26 +422,26 @@
     normed = (hidden_f * inverse_rms * gain).astype(jnp.bfloat16)
     columns = lambda p: lax.dynamic_slice_in_dim(normed, p * depth, depth, 1)
     rows_far = send(columns(me ^ 3), to_far)
-    rows_x = send(columns(me ^ 1), to_x)
-    rows_y = send(columns(me ^ 2), to_y)
+    beside = ((0, 0), (0, tail))
+    rows_x = send(jnp.pad(columns(me ^ 1), beside), to_x)
+    rows_y = send(jnp.pad(columns(me ^ 2), beside), to_y)
     own = own_logits(columns(me), head, width)
-    rows_far = after(rows_far, rows_x, rows_y, own)
-
+    first_tiles = tiles // 2
+    column_parts = ((0, first_tiles), (first_tiles, tiles - first_tiles))
     by_x, by_y = [], []
-    for skip in (0, tiles // 2):
-        first, second = far_codes(rows_far, head, width, skip, tiles // 2)
+    for (skip, count), waits in zip(column_parts, ([own], [rows_x, rows_y])):
+        first, second = far_codes(after(rows_far, *waits), head, width, skip, count)
         by_x.append(send(first, to_x))
         by_y.append(send(second, to_y))
-    sums_x_a, sums_y_a = [], []
-    for c, skip in enumerate((0, tiles // 2)):
-        codes_x, codes_y = near_codes(
-            0, rows_x, rows_y, head, [by_x[c]], [by_y[c]], width, skip, tiles // 2
-        )
-        sums_x_a.append(send(codes_x, to_x))
-        sums_y_a.append(send(codes_y, to_y))
-    rows_x = after(rows_x, codes_x, sums_x_a[0], sums_y_a[0])
-    codes_x, codes_y = near_codes(1, rows_x, rows_y, head, by_x, by_y, width, 0, tiles)
-    halves = ((sums_x_a, sums_y_a), ([send(codes_x, to_x)], [send(codes_y, to_y)]))
+    halves = []
+    for part in range(2):
+        sums_x, sums_y = [], []
+        for c, (skip, count) in enumerate(column_parts):
+            codes_x, codes_y = near_codes(part, rows_x, rows_y, head, by_x[c], by_y[c], width, skip, count)
+            sums_x.append(send(codes_x, to_x))
+            sums_y.append(send(codes_y, to_y))
+        halves.append((sums_x, sums_y))
+        rows_x = after(rows_x, codes_x, sums_x[0], sums_y[0])
 
     in_list = jnp.arange(list_length)[None, :] < refusal_count[:, None]
     ids = jnp.where(in_list, refusal_ids - shard * vocab_local, -1)
@@ -475,34 +462,46 @@
             for i in range(group):
                 moves.append((p * vocab_size + r * group + i, r * vocab_size + p * group + i))
 
+    quarter = half // 2
     infos, grads = [], []
     for part, (sums_x, sums_y) in enumerate(halves):
         logits, listed, stats = row_stats(part, own, sums_x, sums_y, after(ids, *infos), width)
         stats = lax.all_gather(stats, "vocab", axis=0)
         grad, info = logit_grads(part, logits, listed, stats, loss_scale[:, None], width)
         infos.append(info)
-        grads.append((grad, send(grad, to_x), send(grad, to_y)))
+        grads.append(grad)
     log_refusal = jnp.concatenate([info[:, 0] for info in infos])
 
-    quarter = half // 2
-    gathered = []
-    for grad, grad_x, grad_y in grads:
-        far_0 = send(grad_y[:quarter], to_x)
-        far_1 = send(grad_x[quarter:], to_y)
-        gathered.append((grad, grad_x, grad_y, far_0, far_1))
-    (_, grad_x, grad_y, far_0, far_1) = gathered[1]
-    waits_other, waits_mine = [grad_x, grad_y], [far_0, far_1]
-    grad_cols = []
-    for parts in gathered:
-        others = back(parts, head, after(place_other, *waits_other), width, group, False)
+    def neighbours(grad, *waits):
+        sent = after(grad, *waits)
+        return grad, send(sent, to_x), send(sent, to_y)
+
+    def diagonal(grad_x, grad_y, *waits):
+        passed_x, passed_y = after(grad_y, *waits)[:quarter], after(grad_x, *waits)[quarter:]
+        return (passed_x, passed_y), [send(passed_x, to_x), send(passed_y, to_y)]
+
+    def gradient(rows, waits_other=(), waits_mine=()):
+        rows = jnp.concatenate(rows)
+        others = back(rows, head, after(place_other, *waits_other), width, group, False)
         received = [lax.ppermute(c, "vocab", to) for c, to in zip(others, to_member[spread - 1 :])]
-        keep, *codes = back(parts, head, after(place_mine, *others, *waits_mine), width, group, True)
+        keep, *codes = back(rows, head, after(place_mine, *others, *waits_mine), width, group, True)
         received += [lax.ppermute(c, "vocab", to) for c, to in zip(codes, to_member)]
-        keep, *codes = group_sum(place_block, keep, received)
-        received = [lax.ppermute(c, "vocab", to) for c, to in zip(codes, to_block)]
-        waits_other, waits_mine = [keep], received
-        codes = last_sum(keep, received)
-        grad_cols.append(lax.ppermute(codes, ("prompt", "vocab"), moves))
+        return keep, received
+
+    def blocks(keep, received, *waits):
+        keep, *codes = group_sum(after(place_block, *waits), keep, received)
+        return keep, [lax.ppermute(c, "vocab", to) for c, to in zip(codes, to_block)]
+
+    rows_a = neighbours(grads[0])
+    _, far_a = diagonal(*rows_a[1:], infos[1])
+    rows_b = neighbours(grads[1], *far_a)
+    keep_a, received_a = gradient((*rows_a, *far_a))
+    passed, far_b = diagonal(*rows_b[1:], keep_a)
+    keep_a, received_a = blocks(keep_a, received_a, *passed)
+    sum_a = last_sum(keep_a, received_a)
+    keep_b, received_b = gradient((*rows_b, *far_b), received_a, [sum_a])
+    sum_b = last_sum(*blocks(keep_b, received_b))
+    grad_cols = [lax.ppermute(total, ("prompt", "vocab"), moves) for total in (sum_a, sum_b)]
 
     slice_width = model_width // vocab_size
     col_start = shard * slice_width

time: 325 us -> 268 us (0.82)
  waiting for transfers between devices: 89 us -> 43.7 us
  local copies, waits for them, and re-layouts: 28.3 us -> 6.76 us
  starting transfers between devices: 40.8 us -> 46.6 us
    ppermute x21 -> x23, waiting for transfers between devices: 60.7 us -> 14.1 us  [shards(): send = lambda value, pairs: lax.ppermute(value, 'prompt', pairs)]
    unnamed x39 -> x27, local copies, waits for them, and re-layouts: 22.7 us -> 5.8 us
    pallas_call x2, Pallas kernels: 9.18 us -> 16.3 us  [far_codes(): pl.pallas_call(functools.partial(far_kernel, width), grid=(tiles,), in_sp...]
    ppermute x21 -> x23, starting transfers between devices: 21.9 us -> 27.7 us  [shards(): send = lambda value, pairs: lax.ppermute(value, 'prompt', pairs)]
    pallas_call x3 -> x4, Pallas kernels: 32.1 us -> 34.1 us  [near_codes(): pl.pallas_call(functools.partial(near_kernel, width), grid=(tiles,), in_s...]
  transfers between devices with their start and end apart: 31 -> 33, of which waited for: 17 -> 9; matrix products, arithmetic and copies ran while one was open for 1% -> 1% of each run, Pallas kernels for 30% -> 45%
where the time goes in v6:
time: 268 us; the launch traced here: 267 us
  Pallas kernels  132 us (49%)
  starting transfers between devices  46.6 us (17%)
  waiting for transfers between devices  43.7 us (16%)
  blocking collectives  29 us (11%)
  other arithmetic  7.42 us (3%)
  local copies, waits for them, and re-layouts  6.76 us (3%)
    pallas_call x4, Pallas kernels, back(): pl.pallas_call(functools.partial(back_kernel, columns // width, keeps), g...  48.4 us
    pallas_call x4, Pallas kernels, near_codes(): pl.pallas_call(functools.partial(near_kernel, width), grid=(tiles,), in_s...  34.1 us
    all_gather x2, blocking collectives, shards(): stats = lax.all_gather(stats, 'vocab', axis=0)  29 us
    ppermute x23, starting transfers between devices, shards(): send = lambda value, pairs: lax.ppermute(value, 'prompt', pairs)  27.7 us
    ppermute x6, waiting for transfers between devices, blocks(): lax.ppermute(c, 'vocab', to)  19.9 us
    pallas_call x2, Pallas kernels, far_codes(): pl.pallas_call(functools.partial(far_kernel, width), grid=(tiles,), in_sp...  16.3 us
    ppermute x23, waiting for transfers between devices, shards(): send = lambda value, pairs: lax.ppermute(value, 'prompt', pairs)  14.1 us
    pallas_call x1, Pallas kernels, own_logits(): pl.pallas_call(own_kernel, grid=(columns // width,), in_specs=[constant(r...  13.8 us
  transfers between devices with their start and end apart: 33, of which 9 were waited for; matrix products, arithmetic and copies ran while one was open for 1% of the time, Pallas kernels for 45%

profile of v6, /device:TPU:2, one launch (start us, length us, event | category | flops | bytes accessed | tf_op | source)
XLA Modules:
  0.0 267.0 jit_solution(9150818704770043711)
XLA Ops:
  0.6 2.1 fusion
  2.7 2.2 fusion.2
  5.1 1.6 collective-permute-start.2
  6.7 1.6 collective-permute-start
  8.3 0.6 collective-permute-start.1
  8.9 13.8 %own_logits.1.refs_0_ = f32[128,8192]{1,0:T(8,128)S(1)} custom-call(bf16[128,2048]{1,0:T(8,128)(2,1)S(1)} %get-tuple-element.91.x_ref, bf16[2048,8192]{1,0:T(8,128)(2,1)} %head_ref.21), custom_call_target="tpu_custom_call" | custom-call | flops 1024 | bytes 1024 | tf_op jit(solution)/shard_map/own_logits/pallas_call | solution.py:133
  22.7 2.0 copy-done.2
  24.7 7.7 %far_codes.3 = (s16[64,4224]{1,0:T(8,128)(2,1)S(1)}, s16[64,4224]{1,0:T(8,128)(2,1)S(1)}) custom-call(bf16[128,2048]{1,0:T(8,128)(2,1)S(1)} %collective-permute-done.2.x_ref, bf16[2048,8192]{1,0:T(8,128)(2,1)} %head_ref.21), custom_call_target="tpu_custom_call" | custom-call | flops 1024 | bytes 1024 | tf_op jit(solution)/shard_map/far_codes/pallas_call | solution.py:77
  32.5 2.0 collective-permute-start.6
  34.5 8.6 %far_codes.2 = (s16[64,4224]{1,0:T(8,128)(2,1)}, s16[64,4224]{1,0:T(8,128)(2,1)}) custom-call(bf16[128,2048]{1,0:T(8,128)(2,1)S(1)} %collective-permute-done.2.x_ref, bf16[2048,8192]{1,0:T(8,128)(2,1)} %head_ref.21), custom_call_target="tpu_custom_call" | custom-call | flops 1024 | bytes 1024 | tf_op jit(solution)/shard_map/far_codes/pallas_call | solution.py:77
  43.1 1.5 collective-permute-start.3
  44.6 0.5 collective-permute-start.4
  45.1 1.7 collective-permute-done.5.by_x_ref
  46.8 8.7 %near_codes.5 = (s16[64,4224]{1,0:T(8,128)(2,1)}, s16[64,4224]{1,0:T(8,128)(2,1)}) custom-call(bf16[128,2176]{1,0:T(8,128)(2,1)S(1)} %collective-permute-done.x_ref, bf16[128,2176]{1,0:T(8,128)(2,1)S(1)} %collective-permute-done.1.y_ref, bf16[2048,8192]{1,0:T(8,128)(2,1)} %head_ref.21, s16[64,4224]{1,0:T(8,128)(2,1)S(1)} %collective-permute-done.5.by_x_ref, ...), custom_call_target="tpu_custom_call" | custom-call | flops 1024 | bytes 1024 | tf_op jit(solution)/shard_map/near_codes/pallas_call | solution.py:111
  55.4 1.9 collective-permute-start.7
  57.4 2.5 collective-permute-start.8
  59.9 8.6 %near_codes.4 = (s16[64,4224]{1,0:T(8,128)(2,1)}, s16[64,4224]{1,0:T(8,128)(2,1)}) custom-call(bf16[128,2176]{1,0:T(8,128)(2,1)S(1)} %collective-permute-done.x_ref, bf16[128,2176]{1,0:T(8,128)(2,1)S(1)} %collective-permute-done.1.y_ref, bf16[2048,8192]{1,0:T(8,128)(2,1)} %head_ref.21, s16[64,4224]{1,0:T(8,128)(2,1)S(1)} %collective-permute-done.3.by_x_ref, ...), custom_call_target="tpu_custom_call" | custom-call | flops 1024 | bytes 1024 | tf_op jit(solution)/shard_map/near_codes/pallas_call | solution.py:111
  68.5 0.7 collective-permute-start.13
  69.2 1.8 collective-permute-start.14
  71.2 8.5 %near_codes.6 = (s16[64,4224]{1,0:T(8,128)(2,1)}, s16[64,4224]{1,0:T(8,128)(2,1)S(1)}) custom-call(bf16[128,2176]{1,0:T(8,128)(2,1)S(1)} %collective-permute-done.x_ref, bf16[128,2176]{1,0:T(8,128)(2,1)S(1)} %collective-permute-done.1.y_ref, bf16[2048,8192]{1,0:T(8,128)(2,1)} %head_ref.21, s16[64,4224]{1,0:T(8,128)(2,1)S(1)} %collective-permute-done.5.by_x_ref, ...), custom_call_target="tpu_custom_call" | custom-call | flops 1024 | bytes 1024 | tf_op jit(solution)/shard_map/near_codes/pallas_call | solution.py:111
  79.7 0.9 copy-done.4
  80.5 0.8 collective-permute-start.9
  81.7 8.3 %near_codes.7 = (s16[64,4224]{1,0:T(8,128)(2,1)S(1)}, s16[64,4224]{1,0:T(8,128)(2,1)S(1)}) custom-call(bf16[128,2176]{1,0:T(8,128)(2,1)S(1)} %collective-permute-done.x_ref, bf16[128,2176]{1,0:T(8,128)(2,1)S(1)} %collective-permute-done.1.y_ref, bf16[2048,8192]{1,0:T(8,128)(2,1)} %head_ref.21, s16[64,4224]{1,0:T(8,128)(2,1)S(1)} %collective-permute-done.3.by_x_ref, ...), custom_call_target="tpu_custom_call" | custom-call | flops 1024 | bytes 1024 | tf_op jit(solution)/shard_map/near_codes/pallas_call | solution.py:111
  90.0 1.3 collective-permute-start.10
  91.3 0.6 collective-permute-start.11
  91.9 1.5 collective-permute-start.12
  93.4 7.0 %row_stats.2 = (f32[64,8192]{1,0:T(8,128)S(1)}, f32[64,8192]{1,0:T(8,128)S(1)}, f32[64,128]{1,0:T(8,128)S(1)}) custom-call(f32[128,8192]{1,0:T(8,128)S(1)} %copy-done.3, s16[64,4224]{1,0:T(8,128)(2,1)} %collective-permute-done.7.refs_1_, s16[64,4224]{1,0:T(8,128)(2,1)} %collective-permute-done.13.refs_2_, s16[64,4224]{1,0:T(8,128)(2,1)} %collective-permute-done.8.refs_3_, ...), custom_call_target="tpu_custom_call" | custom-call | flops 1024 | bytes 1024 | tf_op jit(solution)/shard_map/row_stats/pallas_call | solution.py:198
  100.3 14.5 %all-gather = f32[512,128]{1,0:T(8,128)S(1)} all-gather(f32[64,128]{1,0:T(8,128)S(1)} %get-tuple-element.62), channel_id=2, replica_groups=mesh['prompt'=4,'vocab'=8] {'vocab'}, dimensions={0}, use_global_device_ids=true | all-gather | bytes 294912 | tf_op jit(solution)/shard_map/all_gather | solution.py:469
  114.9 2.2 logit_grads.2
  117.0 0.6 collective-permute-start.15
  117.6 1.7 collective-permute-start.17
  119.4 5.9 %row_stats.3 = (f32[64,8192]{1,0:T(8,128)S(1)}, f32[64,8192]{1,0:T(8,128)S(1)}, f32[64,128]{1,0:T(8,128)S(1)}) custom-call(f32[128,8192]{1,0:T(8,128)S(1)} %copy-done.3, s16[64,4224]{1,0:T(8,128)(2,1)S(1)} %collective-permute-done.9.refs_1_, s16[64,4224]{1,0:T(8,128)(2,1)S(1)} %collective-permute-done.10.refs_2_, ...), custom_call_target="tpu_custom_call" | custom-call | flops 1024 | bytes 1024 | tf_op jit(solution)/shard_map/row_stats/pallas_call | solution.py:198
  125.3 14.5 %all-gather.1 = f32[512,128]{1,0:T(8,128)S(1)} all-gather(f32[64,128]{1,0:T(8,128)S(1)} %get-tuple-element.67), channel_id=3, replica_groups=mesh['prompt'=4,'vocab'=8] {'vocab'}, dimensions={0}, use_global_device_ids=true | all-gather | bytes 294912 | tf_op jit(solution)/shard_map/all_gather | solution.py:469
  139.8 2.2 logit_grads.3
  141.9 0.9 collective-permute-done.15
  142.9 0.8 collective-permute-start.16
  143.8 1.5 collective-permute-start.18
  145.6 10.9 %collective-permute-done.16 = bf16[32,8320]{1,0:T(8,128)(2,1)S(1)} collective-permute-done((bf16[32,8320]{1,0:T(8,128)(2,1)S(1)}, bf16[32,8320]{1,0:T(8,128)(2,1)S(1)}, u32[]{:S(2)}, u32[]{:S(2)}) %collective-permute-start.16) | collective-permute-done | bytes 532512 | tf_op jit(solution)/shard_map/ppermute | solution.py:418
  156.5 0.6 collective-permute-done.18
  157.1 1.5 collective-permute-start.19
  158.6 0.3 collective-permute-start.20
  159.1 12.0 %grad_rows.4 = s16[256,1152]{1,0:T(8,128)(2,1)S(1)} custom-call(s32[2]{0:T(128)S(1)} %pad_add_fusion.place_ref, bf16[256,8320]{1,0:T(8,128)(2,1)S(1)} %constant_dynamic-update-slice_fusion.grad_ref.beside_ref, bf16[256,8320]{1,0:T(8,128)(2,1)S(1)} %constant_dynamic-update-slice_fusion.grad_ref.beside_ref, bf16[2048,8192]{1,0:T(8,128)(2,1)} %head_ref.21), custom_call_target="tpu_custom_call" | custom-call | flops 1024 | bytes 1024 | tf_op jit(solution)/shard_map/grad_rows/pallas_call | solution.py:324
  171.2 11.7 %grad_rows.5.keep_ref = f32[256,1152]{1,0:T(8,128)S(1)} custom-call(s32[2]{0:T(128)S(1)} %pad_add_fusion.1.place_ref, bf16[256,8320]{1,0:T(8,128)(2,1)S(1)} %constant_dynamic-update-slice_fusion.grad_ref.beside_ref, bf16[256,8320]{1,0:T(8,128)(2,1)S(1)} %constant_dynamic-update-slice_fusion.grad_ref.beside_ref, bf16[2048,8192]{1,0:T(8,128)(2,1)} %head_ref.21), custom_call_target="tpu_custom_call" | custom-call | flops 1024 | bytes 1024 | tf_op jit(solution)/shard_map/grad_rows/pallas_call | solution.py:324
  183.1 1.8 collective-permute-start.26
  184.9 0.5 collective-permute-start.27
  185.4 1.1 group_sum.2
  186.5 1.5 collective-permute-start.22
  188.0 2.4 collective-permute-start.23
  190.4 0.5 collective-permute-start.24
  191.2 3.2 %collective-permute-done.22.refs_0_ = s16[64,1152]{1,0:T(8,128)(2,1)S(1)} collective-permute-done((s16[64,1152]{1,0:T(8,128)(2,1)S(1)}, s16[64,1152]{1,0:T(8,128)(2,1)S(1)}, u32[]{:S(2)}, u32[]{:S(2)}) %collective-permute-start.22) | collective-permute-done | bytes 147488 | tf_op jit(solution)/shard_map/ppermute | solution.py:493
  194.4 7.6 %collective-permute-done.23.refs_1_ = s16[64,1152]{1,0:T(8,128)(2,1)S(1)} collective-permute-done((s16[64,1152]{1,0:T(8,128)(2,1)S(1)}, s16[64,1152]{1,0:T(8,128)(2,1)S(1)}, u32[]{:S(2)}, u32[]{:S(2)}) %collective-permute-start.23) | collective-permute-done | bytes 147488 | tf_op jit(solution)/shard_map/ppermute | solution.py:493
  202.1 12.9 %grad_rows.6 = s16[256,1152]{1,0:T(8,128)(2,1)S(1)} custom-call(s32[2]{0:T(128)S(1)} %pad_add_fusion.place_ref, bf16[256,8320]{1,0:T(8,128)(2,1)S(1)} %constant_dynamic-update-slice_fusion.5.grad_ref.beside_ref, bf16[256,8320]{1,0:T(8,128)(2,1)S(1)} %constant_dynamic-update-slice_fusion.5.grad_ref.beside_ref, bf16[2048,8192]{1,0:T(8,128)(2,1)} %head_ref.21), custom_call_target="tpu_custom_call" | custom-call | flops 1024 | bytes 1024 | tf_op jit(solution)/shard_map/grad_rows/pallas_call | solution.py:324
  215.5 5.0 %collective-permute-start.25 = (s16[64,1152]{1,0:T(8,128)(2,1)S(1)}, s16[64,1152]{1,0:T(8,128)(2,1)S(1)}, u32[]{:S(2)}, u32[]{:S(2)}) collective-permute-start(s16[64,1152]{1,0:T(8,128)(2,1)S(1)} %last_sum.2), channel_id=1, source_target_pairs={{0,0},{1,1},{2,8},{3,9},{4,16},{5,17},{6,24},{7,25},{8,2},{9,3},{1... | collective-permute-start | bytes 442376 | tf_op jit(solution)/shard_map/ppermute | solution.py:504
  220.6 2.2 copy-done.1
  222.8 11.8 %grad_rows.7.keep_ref = f32[256,1152]{1,0:T(8,128)S(1)} custom-call(s32[2]{0:T(128)S(1)} %pad_add_fusion.1.place_ref, bf16[256,8320]{1,0:T(8,128)(2,1)S(1)} %copy-done.1, bf16[256,8320]{1,0:T(8,128)(2,1)S(1)} %copy-done.1, bf16[2048,8192]{1,0:T(8,128)(2,1)} %head_ref.21), custom_call_target="tpu_custom_call" | custom-call | flops 1024 | bytes 1024 | tf_op jit(solution)/shard_map/grad_rows/pallas_call | solution.py:324
  234.6 1.1 group_sum.3
  235.7 3.1 %collective-permute-start.30 = (s16[64,1152]{1,0:T(8,128)(2,1)S(1)}, s16[64,1152]{1,0:T(8,128)(2,1)S(1)}, u32[]{:S(2)}, u32[]{:S(2)}) collective-permute-start(s16[64,1152]{1,0:T(8,128)(2,1)S(1)} %get-tuple-element.86), channel_id=1, source_target_pairs={{0,4},{1,5},{2,6},{3,7},{4,0},{5,1},{6,2},{7,3},{8,12},{9,13},{10,... | collective-permute-start | bytes 442376 | tf_op jit(solution)/shard_map/ppermute | solution.py:493
  238.8 1.2 collective-permute-start.31
  240.2 0.6 pad_maximum_fusion
  240.8 3.6 %collective-permute-done.29.refs_0_ = s16[64,1152]{1,0:T(8,128)(2,1)S(1)} collective-permute-done((s16[64,1152]{1,0:T(8,128)(2,1)S(1)}, s16[64,1152]{1,0:T(8,128)(2,1)S(1)}, u32[]{:S(2)}, u32[]{:S(2)}) %collective-permute-start.29) | collective-permute-done | bytes 147488 | tf_op jit(solution)/shard_map/ppermute | solution.py:493
  244.4 5.5 %collective-permute-done.30.refs_1_ = s16[64,1152]{1,0:T(8,128)(2,1)S(1)} collective-permute-done((s16[64,1152]{1,0:T(8,128)(2,1)S(1)}, s16[64,1152]{1,0:T(8,128)(2,1)S(1)}, u32[]{:S(2)}, u32[]{:S(2)}) %collective-permute-start.30) | collective-permute-done | bytes 147488 | tf_op jit(solution)/shard_map/ppermute | solution.py:493
  250.2 4.9 %collective-permute-start.32 = (s16[64,1152]{1,0:T(8,128)(2,1)S(1)}, s16[64,1152]{1,0:T(8,128)(2,1)S(1)}, u32[]{:S(2)}, u32[]{:S(2)}) collective-permute-start(s16[64,1152]{1,0:T(8,128)(2,1)S(1)} %last_sum.3), channel_id=1, source_target_pairs={{0,0},{1,1},{2,8},{3,9},{4,16},{5,17},{6,24},{7,25},{8,2},{9,3},{1... | collective-permute-start | bytes 442376 | tf_op jit(solution)/shard_map/ppermute | solution.py:504
  255.1 9.7 %collective-permute-done.32 = s16[64,1152]{1,0:T(8,128)(2,1)S(1)} collective-permute-done((s16[64,1152]{1,0:T(8,128)(2,1)S(1)}, s16[64,1152]{1,0:T(8,128)(2,1)S(1)}, u32[]{:S(2)}, u32[]{:S(2)}) %collective-permute-start.32) | collective-permute-done | bytes 147488 | tf_op jit(solution)/shard_map/ppermute | solution.py:504
  265.0 2.0 multiply_subtract_fusion
  (78 shorter events, 3.3 us)
Async XLA Ops:
  5.1 19.5 %collective-permute-start.2 = (bf16[128,2048]{1,0:T(8,128)(2,1)S(1)}, bf16[128,2048]{1,0:T(8,128)(2,1)S(1)}, u32[]{:S(2)}, u32[]{:S(2)}) collective-permute-start(bf16[128,2048]{1,0:T(8,128)(2,1)S(1)} %get-tuple-element.88), channel_id=1, source_target_pairs={{0,24},{8,16},{16,8},{24,0},{1,25},{9,17},{17,9},{25,1},{2,26},{10... | collective-permute-start | bytes 1572872 | tf_op jit(solution)/shard_map/ppermute | solution.py:418
  6.7 27.7 %collective-permute-start = (bf16[128,2176]{1,0:T(8,128)(2,1)S(1)}, bf16[128,2176]{1,0:T(8,128)(2,1)S(1)}, u32[]{:S(2)}, u32[]{:S(2)}) collective-permute-start(bf16[128,2176]{1,0:T(8,128)(2,1)S(1)} %pad.7), channel_id=1, source_target_pairs={{0,8},{8,0},{16,24},{24,16},{1,9},{9,1},{17,25},{25,17},{2,10},{10... | collective-permute-start | bytes 1671176 | tf_op jit(solution)/shard_map/ppermute | solution.py:418
  8.3 26.1 %collective-permute-start.1 = (bf16[128,2176]{1,0:T(8,128)(2,1)S(1)}, bf16[128,2176]{1,0:T(8,128)(2,1)S(1)}, u32[]{:S(2)}, u32[]{:S(2)}) collective-permute-start(bf16[128,2176]{1,0:T(8,128)(2,1)S(1)} %pad.8), channel_id=1, source_target_pairs={{0,16},{8,24},{16,0},{24,8},{1,17},{9,25},{17,1},{25,9},{2,18},{10... | collective-permute-start | bytes 1671176 | tf_op jit(solution)/shard_map/ppermute | solution.py:418
  22.7 2.0 copy-start.2
  32.3 14.4 %collective-permute-start.5 = (s16[64,4224]{1,0:T(8,128)(2,1)S(1)}, s16[64,4224]{1,0:T(8,128)(2,1)S(1)}, u32[]{:S(2)}, u32[]{:S(2)}) collective-permute-start(s16[64,4224]{1,0:T(8,128)(2,1)S(1)} %get-tuple-element.50), channel_id=1, source_target_pairs={{0,8},{8,0},{16,24},{24,16},{1,9},{9,1},{17,25},{25,17},{2,10},{10... | collective-permute-start | bytes 1622024 | tf_op jit(solution)/shard_map/ppermute | solution.py:418
  32.5 14.3 %collective-permute-start.6 = (s16[64,4224]{1,0:T(8,128)(2,1)S(1)}, s16[64,4224]{1,0:T(8,128)(2,1)S(1)}, u32[]{:S(2)}, u32[]{:S(2)}) collective-permute-start(s16[64,4224]{1,0:T(8,128)(2,1)S(1)} %get-tuple-element.51), channel_id=1, source_target_pairs={{0,16},{8,24},{16,0},{24,8},{1,17},{9,25},{17,1},{25,9},{2,18},{10... | collective-permute-start | bytes 1622024 | tf_op jit(solution)/shard_map/ppermute | solution.py:418
  43.1 16.7 %collective-permute-start.3 = (s16[64,4224]{1,0:T(8,128)(2,1)}, s16[64,4224]{1,0:T(8,128)(2,1)S(1)}, u32[]{:S(2)}, u32[]{:S(2)}) collective-permute-start(s16[64,4224]{1,0:T(8,128)(2,1)} %get-tuple-element.46), channel_id=1, source_target_pairs={{0,8},{8,0},{16,24},{24,16},{1,9},{9,1},{17,25},{25,17},{2,10},{10... | collective-permute-start | bytes 1622024 | tf_op jit(solution)/shard_map/ppermute | solution.py:418
  44.6 15.3 %collective-permute-start.4 = (s16[64,4224]{1,0:T(8,128)(2,1)}, s16[64,4224]{1,0:T(8,128)(2,1)S(1)}, u32[]{:S(2)}, u32[]{:S(2)}) collective-permute-start(s16[64,4224]{1,0:T(8,128)(2,1)} %get-tuple-element.47), channel_id=1, source_target_pairs={{0,16},{8,24},{16,0},{24,8},{1,17},{9,25},{17,1},{25,9},{2,18},{10... | collective-permute-start | bytes 1622024 | tf_op jit(solution)/shard_map/ppermute | solution.py:418
  55.4 15.7 %collective-permute-start.7 = (s16[64,4224]{1,0:T(8,128)(2,1)}, s16[64,4224]{1,0:T(8,128)(2,1)}, u32[]{:S(2)}, u32[]{:S(2)}) collective-permute-start(s16[64,4224]{1,0:T(8,128)(2,1)} %get-tuple-element.52), channel_id=1, source_target_pairs={{0,8},{8,0},{16,24},{24,16},{1,9},{9,1},{17,25},{25,17},{2,10},{10... | collective-permute-start | bytes 1622024 | tf_op jit(solution)/shard_map/ppermute | solution.py:418
  57.4 13.8 %collective-permute-start.8 = (s16[64,4224]{1,0:T(8,128)(2,1)}, s16[64,4224]{1,0:T(8,128)(2,1)}, u32[]{:S(2)}, u32[]{:S(2)}) collective-permute-start(s16[64,4224]{1,0:T(8,128)(2,1)} %get-tuple-element.53), channel_id=1, source_target_pairs={{0,16},{8,24},{16,0},{24,8},{1,17},{9,25},{17,1},{25,9},{2,18},{10... | collective-permute-start | bytes 1622024 | tf_op jit(solution)/shard_map/ppermute | solution.py:418
  59.8 11.2 %copy-start.6 = (s32[128,16]{0,1:T(8,128)S(1)}, s32[128,16]{0,1:T(8,128)}, u32[]{:S(2)}) copy-start(s32[128,16]{0,1:T(8,128)} %param.9) | copy-start | bytes 24580
  68.5 23.4 %collective-permute-start.13 = (s16[64,4224]{1,0:T(8,128)(2,1)}, s16[64,4224]{1,0:T(8,128)(2,1)}, u32[]{:S(2)}, u32[]{:S(2)}) collective-permute-start(s16[64,4224]{1,0:T(8,128)(2,1)} %get-tuple-element.48), channel_id=1, source_target_pairs={{0,8},{8,0},{16,24},{24,16},{1,9},{9,1},{17,25},{25,17},{2,10},{10... | collective-permute-start | bytes 1622024 | tf_op jit(solution)/shard_map/ppermute | solution.py:418
  69.2 24.2 %collective-permute-start.14 = (s16[64,4224]{1,0:T(8,128)(2,1)}, s16[64,4224]{1,0:T(8,128)(2,1)}, u32[]{:S(2)}, u32[]{:S(2)}) collective-permute-start(s16[64,4224]{1,0:T(8,128)(2,1)} %get-tuple-element.59), channel_id=1, source_target_pairs={{0,16},{8,24},{16,0},{24,8},{1,17},{9,25},{17,1},{25,9},{2,18},{10... | collective-permute-start | bytes 1622024 | tf_op jit(solution)/shard_map/ppermute | solution.py:418
  71.1 10.2 %copy-start.7 = (s32[128]{0:T(128)S(1)}, s32[128]{0:T(128)}, u32[]{:S(2)}) copy-start(s32[128]{0:T(128)} %param.10) | copy-start | bytes 1540
  71.2 10.2 %copy-start.8 = (f32[128]{0:T(128)S(1)}, f32[128]{0:T(128)}, u32[]{:S(2)}) copy-start(f32[128]{0:T(128)} %param.11) | copy-start | bytes 1540
  79.7 0.9 copy-start.4
  80.5 37.0 %collective-permute-start.9 = (s16[64,4224]{1,0:T(8,128)(2,1)}, s16[64,4224]{1,0:T(8,128)(2,1)S(1)}, u32[]{:S(2)}, u32[]{:S(2)}) collective-permute-start(s16[64,4224]{1,0:T(8,128)(2,1)} %get-tuple-element.55), channel_id=1, source_target_pairs={{0,8},{8,0},{16,24},{24,16},{1,9},{9,1},{17,25},{25,17},{2,10},{10... | collective-permute-start | bytes 1622024 | tf_op jit(solution)/shard_map/ppermute | solution.py:418
  81.7 9.7 %copy-start.5 = (s16[64,4224]{1,0:T(8,128)(2,1)S(1)}, s16[64,4224]{1,0:T(8,128)(2,1)}, u32[]{:S(2)}) copy-start(s16[64,4224]{1,0:T(8,128)(2,1)} %copy-done.4) | copy-start | bytes 1622020
  81.7 11.7 %copy-start.3 = (f32[128,8192]{1,0:T(8,128)S(1)}, f32[128,8192]{1,0:T(8,128)}, u32[]{:S(2)}) copy-start(f32[128,8192]{1,0:T(8,128)} %copy-done.2) | copy-start | bytes 12582916
  90.0 29.4 %collective-permute-start.10 = (s16[64,4224]{1,0:T(8,128)(2,1)S(1)}, s16[64,4224]{1,0:T(8,128)(2,1)S(1)}, u32[]{:S(2)}, u32[]{:S(2)}) collective-permute-start(s16[64,4224]{1,0:T(8,128)(2,1)S(1)} %get-tuple-element.56), channel_id=1, source_target_pairs={{0,8},{8,0},{16,24},{24,16},{1,9},{9,1},{17,25},{25,17},{2,10},{10... | collective-permute-start | bytes 1622024 | tf_op jit(solution)/shard_map/ppermute | solution.py:418
  91.3 28.1 %collective-permute-start.11 = (s16[64,4224]{1,0:T(8,128)(2,1)S(1)}, s16[64,4224]{1,0:T(8,128)(2,1)S(1)}, u32[]{:S(2)}, u32[]{:S(2)}) collective-permute-start(s16[64,4224]{1,0:T(8,128)(2,1)S(1)} %copy-done.5), channel_id=1, source_target_pairs={{0,16},{8,24},{16,0},{24,8},{1,17},{9,25},{17,1},{25,9},{2,18},{10... | collective-permute-start | bytes 1622024 | tf_op jit(solution)/shard_map/ppermute | solution.py:418
  91.9 27.5 %collective-permute-start.12 = (s16[64,4224]{1,0:T(8,128)(2,1)S(1)}, s16[64,4224]{1,0:T(8,128)(2,1)S(1)}, u32[]{:S(2)}, u32[]{:S(2)}) collective-permute-start(s16[64,4224]{1,0:T(8,128)(2,1)S(1)} %get-tuple-element.58), channel_id=1, source_target_pairs={{0,16},{8,24},{16,0},{24,8},{1,17},{9,25},{17,1},{25,9},{2,18},{10... | collective-permute-start | bytes 1622024 | tf_op jit(solution)/shard_map/ppermute | solution.py:418
  117.0 25.8 %collective-permute-start.15 = (bf16[64,8320]{1,0:T(8,128)(2,1)S(1)}, bf16[64,8320]{1,0:T(8,128)(2,1)S(1)}, u32[]{:S(2)}, u32[]{:S(2)}) collective-permute-start(bf16[64,8320]{1,0:T(8,128)(2,1)S(1)} %get-tuple-element.69), channel_id=1, source_target_pairs={{0,16},{8,24},{16,0},{24,8},{1,17},{9,25},{17,1},{25,9},{2,18},{10... | collective-permute-start | bytes 3194888 | tf_op jit(solution)/shard_map/ppermute | solution.py:418
  117.6 26.1 %collective-permute-start.17 = (bf16[64,8320]{1,0:T(8,128)(2,1)S(1)}, bf16[64,8320]{1,0:T(8,128)(2,1)S(1)}, u32[]{:S(2)}, u32[]{:S(2)}) collective-permute-start(bf16[64,8320]{1,0:T(8,128)(2,1)S(1)} %get-tuple-element.69), channel_id=1, source_target_pairs={{0,8},{8,0},{16,24},{24,16},{1,9},{9,1},{17,25},{25,17},{2,10},{10... | collective-permute-start | bytes 3194888 | tf_op jit(solution)/shard_map/ppermute | solution.py:418
  142.9 13.6 %collective-permute-start.16 = (bf16[32,8320]{1,0:T(8,128)(2,1)S(1)}, bf16[32,8320]{1,0:T(8,128)(2,1)S(1)}, u32[]{:S(2)}, u32[]{:S(2)}) collective-permute-start(bf16[32,8320]{1,0:T(8,128)(2,1)S(1)} %slice.33), channel_id=1, source_target_pairs={{0,8},{8,0},{16,24},{24,16},{1,9},{9,1},{17,25},{25,17},{2,10},{10... | collective-permute-start | bytes 1597448 | tf_op jit(solution)/shard_map/ppermute | solution.py:418
  143.8 13.3 %collective-permute-start.18 = (bf16[32,8320]{1,0:T(8,128)(2,1)S(1)}, bf16[32,8320]{1,0:T(8,128)(2,1)S(1)}, u32[]{:S(2)}, u32[]{:S(2)}) collective-permute-start(bf16[32,8320]{1,0:T(8,128)(2,1)S(1)} %slice.34), channel_id=1, source_target_pairs={{0,16},{8,24},{16,0},{24,8},{1,17},{9,25},{17,1},{25,9},{2,18},{10... | collective-permute-start | bytes 1597448 | tf_op jit(solution)/shard_map/ppermute | solution.py:418
  157.1 25.9 %collective-permute-start.19 = (bf16[64,8320]{1,0:T(8,128)(2,1)S(1)}, bf16[64,8320]{1,0:T(8,128)(2,1)S(1)}, u32[]{:S(2)}, u32[]{:S(2)}) collective-permute-start(bf16[64,8320]{1,0:T(8,128)(2,1)S(1)} %get-tuple-element.73), channel_id=1, source_target_pairs={{0,16},{8,24},{16,0},{24,8},{1,17},{9,25},{17,1},{25,9},{2,18},{10... | collective-permute-start | bytes 3194888 | tf_op jit(solution)/shard_map/ppermute | solution.py:418
  158.6 24.5 %collective-permute-start.20 = (bf16[64,8320]{1,0:T(8,128)(2,1)S(1)}, bf16[64,8320]{1,0:T(8,128)(2,1)S(1)}, u32[]{:S(2)}, u32[]{:S(2)}) collective-permute-start(bf16[64,8320]{1,0:T(8,128)(2,1)S(1)} %get-tuple-element.73), channel_id=1, source_target_pairs={{0,8},{8,0},{16,24},{24,16},{1,9},{9,1},{17,25},{25,17},{2,10},{10... | collective-permute-start | bytes 3194888 | tf_op jit(solution)/shard_map/ppermute | solution.py:418
  171.1 14.4 %collective-permute-start.21 = (s16[256,1152]{1,0:T(8,128)(2,1)S(1)}, s16[256,1152]{1,0:T(8,128)(2,1)S(1)}, u32[]{:S(2)}, u32[]{:S(2)}) collective-permute-start(s16[256,1152]{1,0:T(8,128)(2,1)S(1)} %grad_rows.4), channel_id=1, source_target_pairs={{0,1},{1,0},{2,3},{3,2},{4,5},{5,4},{6,7},{7,6},{8,9},{9,8},{10,11... | collective-permute-start | bytes 1769480 | tf_op jit(solution)/shard_map/ppermute | solution.py:486
  183.1 18.9 %collective-permute-start.26 = (bf16[32,8320]{1,0:T(8,128)(2,1)S(1)}, bf16[32,8320]{1,0:T(8,128)(2,1)S(1)}, u32[]{:S(2)}, u32[]{:S(2)}) collective-permute-start(bf16[32,8320]{1,0:T(8,128)(2,1)S(1)} %slice.35), channel_id=1, source_target_pairs={{0,8},{8,0},{16,24},{24,16},{1,9},{9,1},{17,25},{25,17},{2,10},{10... | collective-permute-start | bytes 1597448 | tf_op jit(solution)/shard_map/ppermute | solution.py:418
  184.9 17.2 %collective-permute-start.27 = (bf16[32,8320]{1,0:T(8,128)(2,1)S(1)}, bf16[32,8320]{1,0:T(8,128)(2,1)S(1)}, u32[]{:S(2)}, u32[]{:S(2)}) collective-permute-start(bf16[32,8320]{1,0:T(8,128)(2,1)S(1)} %slice.36), channel_id=1, source_target_pairs={{0,16},{8,24},{16,0},{24,8},{1,17},{9,25},{17,1},{25,9},{2,18},{10... | collective-permute-start | bytes 1597448 | tf_op jit(solution)/shard_map/ppermute | solution.py:418
  186.5 8.0 %collective-permute-start.22 = (s16[64,1152]{1,0:T(8,128)(2,1)S(1)}, s16[64,1152]{1,0:T(8,128)(2,1)S(1)}, u32[]{:S(2)}, u32[]{:S(2)}) collective-permute-start(s16[64,1152]{1,0:T(8,128)(2,1)S(1)} %get-tuple-element.79), channel_id=1, source_target_pairs={{0,2},{1,3},{2,0},{3,1},{4,6},{5,7},{6,4},{7,5},{8,10},{9,11},{10,... | collective-permute-start | bytes 442376 | tf_op jit(solution)/shard_map/ppermute | solution.py:493
  188.0 14.0 %collective-permute-start.23 = (s16[64,1152]{1,0:T(8,128)(2,1)S(1)}, s16[64,1152]{1,0:T(8,128)(2,1)S(1)}, u32[]{:S(2)}, u32[]{:S(2)}) collective-permute-start(s16[64,1152]{1,0:T(8,128)(2,1)S(1)} %get-tuple-element.80), channel_id=1, source_target_pairs={{0,4},{1,5},{2,6},{3,7},{4,0},{5,1},{6,2},{7,3},{8,12},{9,13},{10,... | collective-permute-start | bytes 442376 | tf_op jit(solution)/shard_map/ppermute | solution.py:493
  190.4 11.6 %collective-permute-start.24 = (s16[64,1152]{1,0:T(8,128)(2,1)S(1)}, s16[64,1152]{1,0:T(8,128)(2,1)S(1)}, u32[]{:S(2)}, u32[]{:S(2)}) collective-permute-start(s16[64,1152]{1,0:T(8,128)(2,1)S(1)} %get-tuple-element.81), channel_id=1, source_target_pairs={{0,6},{1,7},{2,4},{3,5},{4,2},{5,3},{6,0},{7,1},{8,14},{9,15},{10,... | collective-permute-start | bytes 442376 | tf_op jit(solution)/shard_map/ppermute | solution.py:493
  202.1 12.9 %copy-start = (bf16[256,8320]{1,0:T(8,128)(2,1)}, bf16[256,8320]{1,0:T(8,128)(2,1)S(1)}, u32[]{:S(2)}) copy-start(bf16[256,8320]{1,0:T(8,128)(2,1)S(1)} %constant_dynamic-update-slice_fusion.5.grad_ref.beside_ref) | copy-start | bytes 12779524
  215.0 19.5 %collective-permute-start.28 = (s16[256,1152]{1,0:T(8,128)(2,1)S(1)}, s16[256,1152]{1,0:T(8,128)(2,1)S(1)}, u32[]{:S(2)}, u32[]{:S(2)}) collective-permute-start(s16[256,1152]{1,0:T(8,128)(2,1)S(1)} %grad_rows.6), channel_id=1, source_target_pairs={{0,1},{1,0},{2,3},{3,2},{4,5},{5,4},{6,7},{7,6},{8,9},{9,8},{10,11... | collective-permute-start | bytes 1769480 | tf_op jit(solution)/shard_map/ppermute | solution.py:486
  215.5 39.5 %collective-permute-start.25 = (s16[64,1152]{1,0:T(8,128)(2,1)S(1)}, s16[64,1152]{1,0:T(8,128)(2,1)S(1)}, u32[]{:S(2)}, u32[]{:S(2)}) collective-permute-start(s16[64,1152]{1,0:T(8,128)(2,1)S(1)} %last_sum.2), channel_id=1, source_target_pairs={{0,0},{1,1},{2,8},{3,9},{4,16},{5,17},{6,24},{7,25},{8,2},{9,3},{1... | collective-permute-start | bytes 442376 | tf_op jit(solution)/shard_map/ppermute | solution.py:504
  220.6 2.2 copy-start.1
  222.8 42.2 %dynamic-slice-start = ((f32[8192]{0:T(1024)}, s32[]{:T(128)}), f32[1024]{0:T(1024)S(1)}, s32[]{:S(2)}) async-start(f32[8192]{0:T(1024)} %param.8, s32[]{:T(128)} %select_n.37), calls=%async_computation | async-start | bytes 8704 | tf_op jit(solution)/shard_map/dynamic_slice | solution.py:514
  235.6 8.7 %collective-permute-start.29 = (s16[64,1152]{1,0:T(8,128)(2,1)S(1)}, s16[64,1152]{1,0:T(8,128)(2,1)S(1)}, u32[]{:S(2)}, u32[]{:S(2)}) collective-permute-start(s16[64,1152]{1,0:T(8,128)(2,1)S(1)} %get-tuple-element.85), channel_id=1, source_target_pairs={{0,2},{1,3},{2,0},{3,1},{4,6},{5,7},{6,4},{7,5},{8,10},{9,11},{10,... | collective-permute-start | bytes 442376 | tf_op jit(solution)/shard_map/ppermute | solution.py:493
  235.7 14.1 %collective-permute-start.30 = (s16[64,1152]{1,0:T(8,128)(2,1)S(1)}, s16[64,1152]{1,0:T(8,128)(2,1)S(1)}, u32[]{:S(2)}, u32[]{:S(2)}) collective-permute-start(s16[64,1152]{1,0:T(8,128)(2,1)S(1)} %get-tuple-element.86), channel_id=1, source_target_pairs={{0,4},{1,5},{2,6},{3,7},{4,0},{5,1},{6,2},{7,3},{8,12},{9,13},{10,... | collective-permute-start | bytes 442376 | tf_op jit(solution)/shard_map/ppermute | solution.py:493
  238.8 11.0 %collective-permute-start.31 = (s16[64,1152]{1,0:T(8,128)(2,1)S(1)}, s16[64,1152]{1,0:T(8,128)(2,1)S(1)}, u32[]{:S(2)}, u32[]{:S(2)}) collective-permute-start(s16[64,1152]{1,0:T(8,128)(2,1)S(1)} %get-tuple-element.87), channel_id=1, source_target_pairs={{0,6},{1,7},{2,4},{3,5},{4,2},{5,3},{6,0},{7,1},{8,14},{9,15},{10,... | collective-permute-start | bytes 442376 | tf_op jit(solution)/shard_map/ppermute | solution.py:493
  250.2 14.6 %collective-permute-start.32 = (s16[64,1152]{1,0:T(8,128)(2,1)S(1)}, s16[64,1152]{1,0:T(8,128)(2,1)S(1)}, u32[]{:S(2)}, u32[]{:S(2)}) collective-permute-start(s16[64,1152]{1,0:T(8,128)(2,1)S(1)} %last_sum.3), channel_id=1, source_target_pairs={{0,0},{1,1},{2,8},{3,9},{4,16},{5,17},{6,24},{7,25},{8,2},{9,3},{1... | collective-permute-start | bytes 442376 | tf_op jit(solution)/shard_map/ppermute | solution.py:504

commit v7 on v6

--- a/solution.py
+++ b/solution.py
@@ -56,14 +56,54 @@
     return pl.CostEstimate(flops=1024, bytes_accessed=1024, transcendentals=0)
 
 
+head_spec = pl.BlockSpec(memory_space=pl.ANY)
+
+
+def head_scratch(rows, width, tiles):
+    slots = min(tiles, 16 * megabyte // (2 * rows * width))
+    return [pltpu.VMEM((slots, rows, width), jnp.bfloat16), pltpu.SemaphoreType.DMA((slots,))]
+
+
+class Tiles:
+    def __init__(self, head_ref, slots_ref, sems_ref, first_row, skip, tiles):
+        self.slots, rows, width = slots_ref.shape
+        self.tiles, self.slots_ref = tiles, slots_ref
+
+        def copy(tile):
+            slot = lax.rem(tile, self.slots)
+            column = pl.multiple_of((tile + skip) * width, width)
+            source = head_ref.at[pl.ds(first_row, rows), pl.ds(column, width)]
+            return pltpu.make_async_copy(source, slots_ref.at[slot], sems_ref.at[slot])
+
+        self.copy = copy
+
+    def get(self, tile):
+        @pl.when(tile == 0)
+        def _():
+            for first in range(self.slots):
+                self.copy(first).start()
+
+        self.copy(tile).wait()
+        return self.slots_ref[lax.rem(tile, self.slots)]
+
+    def release(self, tile):
+        if self.slots < self.tiles:
+
+            @pl.when(tile + self.slots < self.tiles)
+            def _():
+                self.copy(tile + self.slots).start()
+
+
 def constant(*shape):
     return pl.BlockSpec(shape, lambda *_: (0,) * len(shape))
 
 
-def far_kernel(width, x_ref, head_ref, first_ref, second_ref, powers_ref):
+def far_kernel(width, skip, tiles, x_ref, head_ref, first_ref, second_ref, powers_ref, slots_ref, sems_ref):
     tile = pl.program_id(0)
+    head = Tiles(head_ref, slots_ref, sems_ref, 0, skip, tiles)
     columns = first_ref.shape[1] - tail
-    value = dot(x_ref[...], head_ref[...])
+    value = dot(x_ref[...], head.get(tile))
+    head.release(tile)
     q = value.shape[0] // 4
     first = jnp.concatenate([value[:q], value[2 * q : 3 * q]], axis=0)
     second = jnp.concatenate([value[q : 2 * q], value[3 * q :]], axis=0)
@@ -75,27 +115,27 @@
     rows, depth = rows_in.shape
     columns = tiles * width
     return pl.pallas_call(
-        functools.partial(far_kernel, width),
+        functools.partial(far_kernel, width, skip, tiles),
         grid=(tiles,),
-        in_specs=[
-            constant(rows, depth),
-            pl.BlockSpec((depth, width), lambda j: (0, j + skip)),
-        ],
+        in_specs=[constant(rows, depth), head_spec],
         out_specs=[constant(rows // 2, columns + tail)] * 2,
         out_shape=[jax.ShapeDtypeStruct((rows // 2, columns + tail), jnp.int16)] * 2,
-        scratch_shapes=[pltpu.VMEM((rows, tail), jnp.float32)],
+        scratch_shapes=[pltpu.VMEM((rows, tail), jnp.float32)] + head_scratch(depth, width, tiles),
         compiler_params=compiler_params(),
         cost_estimate=small_cost(),
         name="far_codes",
     )(rows_in, head)
 
 
-def near_kernel(width, x_ref, y_ref, head_ref, by_x_ref, by_y_ref, to_x_ref, to_y_ref, powers_ref):
+def near_kernel(width, skip, tiles, x_ref, y_ref, head_ref, by_x_ref, by_y_ref, to_x_ref, to_y_ref, *refs):
+    powers_ref, slots_ref, sems_ref = refs
     tile = pl.program_id(0)
+    head = Tiles(head_ref, slots_ref, sems_ref, 0, skip, tiles)
     rows = x_ref.shape[0]
     half = rows // 2
     columns = to_x_ref.shape[1] - tail
-    value = dot(jnp.concatenate([x_ref[...], y_ref[...]], axis=0), head_ref[...])
+    value = dot(jnp.concatenate([x_ref[...], y_ref[...]], axis=0), head.get(tile))
+    head.release(tile)
     more_x = decode(by_y_ref, tile, width, columns)
     more_y = decode(by_x_ref, tile, width, columns)
     for_x = jnp.concatenate([value[:half], value[half:rows] + more_x], axis=0)
@@ -109,36 +149,37 @@
     rows = rows_x.shape[0] // 2
     columns = tiles * width
     return pl.pallas_call(
-        functools.partial(near_kernel, width),
+        functools.partial(near_kernel, width, skip, tiles),
         grid=(tiles,),
         in_specs=[pl.BlockSpec((rows, depth), lambda j: (part, 0))] * 2
-        + [pl.BlockSpec((depth, width), lambda j: (0, j + skip))]
+        + [head_spec]
         + [pl.BlockSpec((rows // 2, columns + tail), lambda j: (part, 0))] * 2,
         out_specs=[constant(rows, columns + tail)] * 2,
         out_shape=[jax.ShapeDtypeStruct((rows, columns + tail), jnp.int16)] * 2,
-        scratch_shapes=[pltpu.VMEM((2 * rows, tail), jnp.float32)],
+        scratch_shapes=[pltpu.VMEM((2 * rows, tail), jnp.float32)] + head_scratch(depth, width, tiles),
         compiler_params=compiler_params(),
         cost_estimate=small_cost(),
         name="near_codes",
     )(rows_x, rows_y, head, by_x, by_y)
 
 
-def own_kernel(x_ref, head_ref, out_ref):
-    out_ref[...] = dot(x_ref[...], head_ref[...])
+def own_kernel(tiles, x_ref, head_ref, out_ref, slots_ref, sems_ref):
+    tile = pl.program_id(0)
+    head = Tiles(head_ref, slots_ref, sems_ref, 0, 0, tiles)
+    out_ref[...] = dot(x_ref[...], head.get(tile))
+    head.release(tile)
 
 
 def own_logits(rows_in, head, width):
     rows, depth = rows_in.shape
     columns = head.shape[1]
     return pl.pallas_call(
-        own_kernel,
+        functools.partial(own_kernel, columns // width),
         grid=(columns // width,),
-        in_specs=[
-            constant(rows, depth),
-            pl.BlockSpec((depth, width), lambda j: (0, j)),
-        ],
+        in_specs=[constant(rows, depth), head_spec],
         out_specs=pl.BlockSpec((rows, width), lambda j: (0, j)),
         out_shape=jax.ShapeDtypeStruct((rows, columns), jnp.float32),
+        scratch_shapes=head_scratch(depth, width, columns // width),
         compiler_params=compiler_params(),
         cost_estimate=small_cost(),
         name="own_logits",
@@ -289,16 +330,19 @@
 
 
 def back_kernel(tiles, keeps, place_ref, grad_ref, beside_ref, head_ref, *refs):
-    outs, total_ref = refs[:-1], refs[-1]
+    outs, (total_ref, slots_ref, sems_ref) = refs[:-3], refs[-3:]
     tile = pl.program_id(0)
+    rows = slots_ref.shape[1]
+    head = Tiles(head_ref, slots_ref, sems_ref, pl.multiple_of(place_ref[0] * rows, rows), 0, tiles)
 
     @pl.when(tile == 0)
     def _():
         total_ref[...] = jnp.zeros_like(total_ref)
 
     total_ref[...] += lax.dot_general(
-        grad_ref[...], head_ref[...], (((1,), (1,)), ((), ())), preferred_element_type=jnp.float32
+        grad_ref[...], head.get(tile), (((1,), (1,)), ((), ())), preferred_element_type=jnp.float32
     )
+    head.release(tile)
 
     @pl.when(tile == tiles - 1)
     def _():
@@ -329,10 +373,11 @@
             in_specs=[
                 pl.BlockSpec((rows, width), lambda j, place: (0, j)),
                 pl.BlockSpec((rows, tail), lambda j, place: (0, columns // tail)),
-                pl.BlockSpec((blocks * part, width), lambda j, place: (place[0], j)),
+                head_spec,
             ],
             out_specs=[constant(rows, part + tail)] * blocks,
-            scratch_shapes=[pltpu.VMEM((rows, blocks * part), jnp.float32)],
+            scratch_shapes=[pltpu.VMEM((rows, blocks * part), jnp.float32)]
+            + head_scratch(blocks * part, width, columns // width),
         ),
         out_shape=[jax.ShapeDtypeStruct((rows, part + tail), t) for t in types],
         compiler_params=compiler_params(),

time: 268 us -> 254 us (0.948)
  Pallas kernels: 132 us -> 117 us
  waiting for transfers between devices: 43.7 us -> 49.3 us
  starting transfers between devices: 46.6 us -> 43.4 us
    pallas_call x4, Pallas kernels: 48.4 us -> 40.2 us  [back(): pl.pallas_call(functools.partial(back_kernel, columns // width, keeps), g...]
    ppermute x23, waiting for transfers between devices: 14.1 us -> 21.8 us  [shards(): send = lambda value, pairs: lax.ppermute(value, 'prompt', pairs)]
    pallas_call x7, Pallas kernels: 64.2 us -> 56.6 us  [the longest x4 30.3 us: near_codes(): pl.pallas_call(functools.partial(near_kernel, width, skip, tiles), grid=(...]
    ppermute x23, starting transfers between devices: 27.7 us -> 24.7 us  [shards(): send = lambda value, pairs: lax.ppermute(value, 'prompt', pairs)]
  transfers between devices with their start and end apart: 33 -> 33, of which waited for: 9 -> 15; matrix products, arithmetic and copies ran while one was open for 1% -> 1% of each run, Pallas kernels for 45% -> 42%
where the time goes in v7:
time: 254 us
  Pallas kernels  117 us (46%)
  waiting for transfers between devices  49.3 us (19%)
  starting transfers between devices  43.4 us (17%)
  blocking collectives  29.1 us (11%)
  other arithmetic  7.42 us (3%)
  local copies, waits for them, and re-layouts  6.75 us (3%)
    pallas_call x4, Pallas kernels, back(): pl.pallas_call(functools.partial(back_kernel, columns // width, keeps), g...  40.2 us
    pallas_call x4, Pallas kernels, near_codes(): pl.pallas_call(functools.partial(near_kernel, width, skip, tiles), grid=(...  30.3 us
    all_gather x2, blocking collectives, shards(): stats = lax.all_gather(stats, 'vocab', axis=0)  29.1 us
    ppermute x23, starting transfers between devices, shards(): send = lambda value, pairs: lax.ppermute(value, 'prompt', pairs)  24.7 us
    ppermute x23, waiting for transfers between devices, shards(): send = lambda value, pairs: lax.ppermute(value, 'prompt', pairs)  21.8 us
    ppermute x6, waiting for transfers between devices, blocks(): lax.ppermute(c, 'vocab', to)  17.8 us
    pallas_call x2, Pallas kernels, far_codes(): pl.pallas_call(functools.partial(far_kernel, width, skip, tiles), grid=(t...  14.6 us
    pallas_call x2, Pallas kernels, row_stats(): pl.pallas_call(functools.partial(stats_kernel, width, parts), grid=(rows...  12.8 us
  transfers between devices with their start and end apart: 33, of which 15 were waited for; matrix products, arithmetic and copies ran while one was open for 1% of the time, Pallas kernels for 42%

profile of v7, /device:TPU:2, one launch (start us, length us, event | category | flops | bytes accessed | tf_op | source)
XLA Modules:
  0.0 253.7 jit_solution(3658468968201765939)
XLA Ops:
  0.6 2.1 fusion
  2.7 2.2 fusion.2
  5.1 1.6 collective-permute-start.2
  6.7 1.6 collective-permute-start
  8.9 11.8 %own_logits.1.refs_0_ = f32[128,8192]{1,0:T(8,128)S(1)} custom-call(bf16[128,2048]{1,0:T(8,128)(2,1)S(1)} %get-tuple-element.91.x_ref, bf16[2048,8192]{1,0:T(8,128)(2,1)} %head_ref.21), custom_call_target="tpu_custom_call" | custom-call | flops 1024 | bytes 1024 | tf_op jit(solution)/shard_map/own_logits/pallas_call | solution.py:176
  20.7 2.0 copy-done.2
  22.7 6.8 %far_codes.3 = (s16[64,4224]{1,0:T(8,128)(2,1)S(1)}, s16[64,4224]{1,0:T(8,128)(2,1)S(1)}) custom-call(bf16[128,2048]{1,0:T(8,128)(2,1)S(1)} %collective-permute-done.2.x_ref, bf16[2048,8192]{1,0:T(8,128)(2,1)} %head_ref.21), custom_call_target="tpu_custom_call" | custom-call | flops 1024 | bytes 1024 | tf_op jit(solution)/shard_map/far_codes/pallas_call | solution.py:117
  29.7 2.0 collective-permute-start.6
  31.6 0.8 collective-permute-done.x_ref
  32.4 7.8 %far_codes.2 = (s16[64,4224]{1,0:T(8,128)(2,1)}, s16[64,4224]{1,0:T(8,128)(2,1)}) custom-call(bf16[128,2048]{1,0:T(8,128)(2,1)S(1)} %collective-permute-done.2.x_ref, bf16[2048,8192]{1,0:T(8,128)(2,1)} %head_ref.21), custom_call_target="tpu_custom_call" | custom-call | flops 1024 | bytes 1024 | tf_op jit(solution)/shard_map/far_codes/pallas_call | solution.py:117
  40.2 0.8 collective-permute-start.3
  41.6 2.7 %collective-permute-done.5.by_x_ref = s16[64,4224]{1,0:T(8,128)(2,1)S(1)} collective-permute-done((s16[64,4224]{1,0:T(8,128)(2,1)S(1)}, s16[64,4224]{1,0:T(8,128)(2,1)S(1)}, u32[]{:S(2)}, u32[]{:S(2)}) %collective-permute-start.5) | collective-permute-done | bytes 540704 | tf_op jit(solution)/shard_map/ppermute | solution.py:463
  44.3 7.8 %near_codes.5 = (s16[64,4224]{1,0:T(8,128)(2,1)}, s16[64,4224]{1,0:T(8,128)(2,1)}) custom-call(bf16[128,2176]{1,0:T(8,128)(2,1)S(1)} %collective-permute-done.x_ref, bf16[128,2176]{1,0:T(8,128)(2,1)S(1)} %collective-permute-done.1.y_ref, bf16[2048,8192]{1,0:T(8,128)(2,1)} %head_ref.21, s16[64,4224]{1,0:T(8,128)(2,1)S(1)} %collective-permute-done.5.by_x_ref, ...), custom_call_target="tpu_custom_call" | custom-call | flops 1024 | bytes 1024 | tf_op jit(solution)/shard_map/near_codes/pallas_call | solution.py:151
  52.8 1.4 collective-permute-start.8
  54.2 1.7 collective-permute-done.3.by_x_ref
  56.1 7.8 %near_codes.4 = (s16[64,4224]{1,0:T(8,128)(2,1)}, s16[64,4224]{1,0:T(8,128)(2,1)}) custom-call(bf16[128,2176]{1,0:T(8,128)(2,1)S(1)} %collective-permute-done.x_ref, bf16[128,2176]{1,0:T(8,128)(2,1)S(1)} %collective-permute-done.1.y_ref, bf16[2048,8192]{1,0:T(8,128)(2,1)} %head_ref.21, s16[64,4224]{1,0:T(8,128)(2,1)S(1)} %collective-permute-done.3.by_x_ref, ...), custom_call_target="tpu_custom_call" | custom-call | flops 1024 | bytes 1024 | tf_op jit(solution)/shard_map/near_codes/pallas_call | solution.py:151
  63.9 1.5 collective-permute-start.13
  65.4 1.1 collective-permute-start.14
  66.6 1.2 collective-permute-done.7.refs_1_
  67.8 7.6 %near_codes.6 = (s16[64,4224]{1,0:T(8,128)(2,1)}, s16[64,4224]{1,0:T(8,128)(2,1)S(1)}) custom-call(bf16[128,2176]{1,0:T(8,128)(2,1)S(1)} %collective-permute-done.x_ref, bf16[128,2176]{1,0:T(8,128)(2,1)S(1)} %collective-permute-done.1.y_ref, bf16[2048,8192]{1,0:T(8,128)(2,1)} %head_ref.21, s16[64,4224]{1,0:T(8,128)(2,1)S(1)} %collective-permute-done.5.by_x_ref, ...), custom_call_target="tpu_custom_call" | custom-call | flops 1024 | bytes 1024 | tf_op jit(solution)/shard_map/near_codes/pallas_call | solution.py:151
  75.5 0.9 copy-done.4
  76.3 1.0 collective-permute-start.9
  77.7 7.0 %near_codes.7 = (s16[64,4224]{1,0:T(8,128)(2,1)S(1)}, s16[64,4224]{1,0:T(8,128)(2,1)S(1)}) custom-call(bf16[128,2176]{1,0:T(8,128)(2,1)S(1)} %collective-permute-done.x_ref, bf16[128,2176]{1,0:T(8,128)(2,1)S(1)} %collective-permute-done.1.y_ref, bf16[2048,8192]{1,0:T(8,128)(2,1)} %head_ref.21, s16[64,4224]{1,0:T(8,128)(2,1)S(1)} %collective-permute-done.3.by_x_ref, ...), custom_call_target="tpu_custom_call" | custom-call | flops 1024 | bytes 1024 | tf_op jit(solution)/shard_map/near_codes/pallas_call | solution.py:151
  84.7 1.1 collective-permute-start.10
  85.8 1.1 collective-permute-start.11
  86.9 0.9 collective-permute-start.12
  87.8 7.0 %row_stats.2 = (f32[64,8192]{1,0:T(8,128)S(1)}, f32[64,8192]{1,0:T(8,128)S(1)}, f32[64,128]{1,0:T(8,128)S(1)}) custom-call(f32[128,8192]{1,0:T(8,128)S(1)} %copy-done.3, s16[64,4224]{1,0:T(8,128)(2,1)} %collective-permute-done.7.refs_1_, s16[64,4224]{1,0:T(8,128)(2,1)} %collective-permute-done.13.refs_2_, s16[64,4224]{1,0:T(8,128)(2,1)} %collective-permute-done.8.refs_3_, ...), custom_call_target="tpu_custom_call" | custom-call | flops 1024 | bytes 1024 | tf_op jit(solution)/shard_map/row_stats/pallas_call | solution.py:239
  94.8 14.7 %all-gather = f32[512,128]{1,0:T(8,128)S(1)} all-gather(f32[64,128]{1,0:T(8,128)S(1)} %get-tuple-element.62), channel_id=2, replica_groups=mesh['prompt'=4,'vocab'=8] {'vocab'}, dimensions={0}, use_global_device_ids=true | all-gather | bytes 294912 | tf_op jit(solution)/shard_map/all_gather | solution.py:514
  109.5 2.2 logit_grads.2
  111.7 1.2 collective-permute-start.15
  112.8 1.2 collective-permute-start.17
  114.1 5.9 %row_stats.3 = (f32[64,8192]{1,0:T(8,128)S(1)}, f32[64,8192]{1,0:T(8,128)S(1)}, f32[64,128]{1,0:T(8,128)S(1)}) custom-call(f32[128,8192]{1,0:T(8,128)S(1)} %copy-done.3, s16[64,4224]{1,0:T(8,128)(2,1)S(1)} %collective-permute-done.9.refs_1_, s16[64,4224]{1,0:T(8,128)(2,1)S(1)} %collective-permute-done.10.refs_2_, ...), custom_call_target="tpu_custom_call" | custom-call | flops 1024 | bytes 1024 | tf_op jit(solution)/shard_map/row_stats/pallas_call | solution.py:239
  120.0 14.3 %all-gather.1 = f32[512,128]{1,0:T(8,128)S(1)} all-gather(f32[64,128]{1,0:T(8,128)S(1)} %get-tuple-element.67), channel_id=3, replica_groups=mesh['prompt'=4,'vocab'=8] {'vocab'}, dimensions={0}, use_global_device_ids=true | all-gather | bytes 294912 | tf_op jit(solution)/shard_map/all_gather | solution.py:514
  134.3 2.2 logit_grads.3
  136.5 1.0 collective-permute-done.15
  137.5 1.1 collective-permute-start.16
  138.6 1.4 collective-permute-start.18
  140.3 10.9 %collective-permute-done.16 = bf16[32,8320]{1,0:T(8,128)(2,1)S(1)} collective-permute-done((bf16[32,8320]{1,0:T(8,128)(2,1)S(1)}, bf16[32,8320]{1,0:T(8,128)(2,1)S(1)}, u32[]{:S(2)}, u32[]{:S(2)}) %collective-permute-start.16) | collective-permute-done | bytes 532512 | tf_op jit(solution)/shard_map/ppermute | solution.py:463
  151.1 0.8 collective-permute-done.18
  152.0 1.3 collective-permute-start.19
  153.3 0.8 collective-permute-start.20
  154.3 10.0 %grad_rows.4 = s16[256,1152]{1,0:T(8,128)(2,1)S(1)} custom-call(s32[2]{0:T(128)S(1)} %pad_add_fusion.place_ref, bf16[256,8320]{1,0:T(8,128)(2,1)S(1)} %constant_dynamic-update-slice_fusion.grad_ref.beside_ref, bf16[256,8320]{1,0:T(8,128)(2,1)S(1)} %constant_dynamic-update-slice_fusion.grad_ref.beside_ref, bf16[2048,8192]{1,0:T(8,128)(2,1)} %head_ref.21), custom_call_target="tpu_custom_call" | custom-call | flops 1024 | bytes 1024 | tf_op jit(solution)/shard_map/grad_rows/pallas_call | solution.py:368
  164.4 9.7 %grad_rows.5.keep_ref = f32[256,1152]{1,0:T(8,128)S(1)} custom-call(s32[2]{0:T(128)S(1)} %pad_add_fusion.1.place_ref, bf16[256,8320]{1,0:T(8,128)(2,1)S(1)} %constant_dynamic-update-slice_fusion.grad_ref.beside_ref, bf16[256,8320]{1,0:T(8,128)(2,1)S(1)} %constant_dynamic-update-slice_fusion.grad_ref.beside_ref, bf16[2048,8192]{1,0:T(8,128)(2,1)} %head_ref.21), custom_call_target="tpu_custom_call" | custom-call | flops 1024 | bytes 1024 | tf_op jit(solution)/shard_map/grad_rows/pallas_call | solution.py:368
  174.2 1.5 collective-permute-done.19
  175.7 1.0 collective-permute-done.20
  176.8 0.9 collective-permute-start.26
  177.7 0.9 collective-permute-start.27
  178.6 1.1 group_sum.2
  179.7 1.5 collective-permute-start.22
  181.2 2.4 collective-permute-start.23
  184.4 1.1 collective-permute-done.22.refs_0_
  185.5 7.6 %collective-permute-done.23.refs_1_ = s16[64,1152]{1,0:T(8,128)(2,1)S(1)} collective-permute-done((s16[64,1152]{1,0:T(8,128)(2,1)S(1)}, s16[64,1152]{1,0:T(8,128)(2,1)S(1)}, u32[]{:S(2)}, u32[]{:S(2)}) %collective-permute-start.23) | collective-permute-done | bytes 147488 | tf_op jit(solution)/shard_map/ppermute | solution.py:538
  193.2 10.7 %grad_rows.6 = s16[256,1152]{1,0:T(8,128)(2,1)S(1)} custom-call(s32[2]{0:T(128)S(1)} %pad_add_fusion.place_ref, bf16[256,8320]{1,0:T(8,128)(2,1)S(1)} %constant_dynamic-update-slice_fusion.5.grad_ref.beside_ref, bf16[256,8320]{1,0:T(8,128)(2,1)S(1)} %constant_dynamic-update-slice_fusion.5.grad_ref.beside_ref, bf16[2048,8192]{1,0:T(8,128)(2,1)} %head_ref.21), custom_call_target="tpu_custom_call" | custom-call | flops 1024 | bytes 1024 | tf_op jit(solution)/shard_map/grad_rows/pallas_call | solution.py:368
  204.4 4.5 %collective-permute-start.25 = (s16[64,1152]{1,0:T(8,128)(2,1)S(1)}, s16[64,1152]{1,0:T(8,128)(2,1)S(1)}, u32[]{:S(2)}, u32[]{:S(2)}) collective-permute-start(s16[64,1152]{1,0:T(8,128)(2,1)S(1)} %last_sum.2), channel_id=1, source_target_pairs={{0,0},{1,1},{2,8},{3,9},{4,16},{5,17},{6,24},{7,25},{8,2},{9,3},{1... | collective-permute-start | bytes 442376 | tf_op jit(solution)/shard_map/ppermute | solution.py:549
  209.0 2.2 copy-done.1
  211.2 9.7 %grad_rows.7.keep_ref = f32[256,1152]{1,0:T(8,128)S(1)} custom-call(s32[2]{0:T(128)S(1)} %pad_add_fusion.1.place_ref, bf16[256,8320]{1,0:T(8,128)(2,1)S(1)} %copy-done.1, bf16[256,8320]{1,0:T(8,128)(2,1)S(1)} %copy-done.1, bf16[2048,8192]{1,0:T(8,128)(2,1)} %head_ref.21), custom_call_target="tpu_custom_call" | custom-call | flops 1024 | bytes 1024 | tf_op jit(solution)/shard_map/grad_rows/pallas_call | solution.py:368
  221.0 1.1 group_sum.3
  222.1 3.2 %collective-permute-start.30 = (s16[64,1152]{1,0:T(8,128)(2,1)S(1)}, s16[64,1152]{1,0:T(8,128)(2,1)S(1)}, u32[]{:S(2)}, u32[]{:S(2)}) collective-permute-start(s16[64,1152]{1,0:T(8,128)(2,1)S(1)} %get-tuple-element.86), channel_id=1, source_target_pairs={{0,4},{1,5},{2,6},{3,7},{4,0},{5,1},{6,2},{7,3},{8,12},{9,13},{10,... | collective-permute-start | bytes 442376 | tf_op jit(solution)/shard_map/ppermute | solution.py:538
  225.3 1.2 collective-permute-start.31
  227.2 3.8 %collective-permute-done.29.refs_0_ = s16[64,1152]{1,0:T(8,128)(2,1)S(1)} collective-permute-done((s16[64,1152]{1,0:T(8,128)(2,1)S(1)}, s16[64,1152]{1,0:T(8,128)(2,1)S(1)}, u32[]{:S(2)}, u32[]{:S(2)}) %collective-permute-start.29) | collective-permute-done | bytes 147488 | tf_op jit(solution)/shard_map/ppermute | solution.py:538
  231.0 5.3 %collective-permute-done.30.refs_1_ = s16[64,1152]{1,0:T(8,128)(2,1)S(1)} collective-permute-done((s16[64,1152]{1,0:T(8,128)(2,1)S(1)}, s16[64,1152]{1,0:T(8,128)(2,1)S(1)}, u32[]{:S(2)}, u32[]{:S(2)}) %collective-permute-start.30) | collective-permute-done | bytes 147488 | tf_op jit(solution)/shard_map/ppermute | solution.py:538
  236.6 5.1 %collective-permute-start.32 = (s16[64,1152]{1,0:T(8,128)(2,1)S(1)}, s16[64,1152]{1,0:T(8,128)(2,1)S(1)}, u32[]{:S(2)}, u32[]{:S(2)}) collective-permute-start(s16[64,1152]{1,0:T(8,128)(2,1)S(1)} %last_sum.3), channel_id=1, source_target_pairs={{0,0},{1,1},{2,8},{3,9},{4,16},{5,17},{6,24},{7,25},{8,2},{9,3},{1... | collective-permute-start | bytes 442376 | tf_op jit(solution)/shard_map/ppermute | solution.py:549
  241.8 9.7 %collective-permute-done.32 = s16[64,1152]{1,0:T(8,128)(2,1)S(1)} collective-permute-done((s16[64,1152]{1,0:T(8,128)(2,1)S(1)}, s16[64,1152]{1,0:T(8,128)(2,1)S(1)}, u32[]{:S(2)}, u32[]{:S(2)}) %collective-permute-start.32) | collective-permute-done | bytes 147488 | tf_op jit(solution)/shard_map/ppermute | solution.py:549
  251.7 2.0 multiply_subtract_fusion
  (78 shorter events, 6.4 us)
Async XLA Ops:
  5.1 17.5 %collective-permute-start.2 = (bf16[128,2048]{1,0:T(8,128)(2,1)S(1)}, bf16[128,2048]{1,0:T(8,128)(2,1)S(1)}, u32[]{:S(2)}, u32[]{:S(2)}) collective-permute-start(bf16[128,2048]{1,0:T(8,128)(2,1)S(1)} %get-tuple-element.88), channel_id=1, source_target_pairs={{0,24},{8,16},{16,8},{24,0},{1,25},{9,17},{17,9},{25,1},{2,26},{10... | collective-permute-start | bytes 1572872 | tf_op jit(solution)/shard_map/ppermute | solution.py:463
  6.7 25.6 %collective-permute-start = (bf16[128,2176]{1,0:T(8,128)(2,1)S(1)}, bf16[128,2176]{1,0:T(8,128)(2,1)S(1)}, u32[]{:S(2)}, u32[]{:S(2)}) collective-permute-start(bf16[128,2176]{1,0:T(8,128)(2,1)S(1)} %pad.7), channel_id=1, source_target_pairs={{0,8},{8,0},{16,24},{24,16},{1,9},{9,1},{17,25},{25,17},{2,10},{10... | collective-permute-start | bytes 1671176 | tf_op jit(solution)/shard_map/ppermute | solution.py:463
  8.3 24.0 %collective-permute-start.1 = (bf16[128,2176]{1,0:T(8,128)(2,1)S(1)}, bf16[128,2176]{1,0:T(8,128)(2,1)S(1)}, u32[]{:S(2)}, u32[]{:S(2)}) collective-permute-start(bf16[128,2176]{1,0:T(8,128)(2,1)S(1)} %pad.8), channel_id=1, source_target_pairs={{0,16},{8,24},{16,0},{24,8},{1,17},{9,25},{17,1},{25,9},{2,18},{10... | collective-permute-start | bytes 1671176 | tf_op jit(solution)/shard_map/ppermute | solution.py:463
  20.7 2.0 copy-start.2
  29.5 14.8 %collective-permute-start.5 = (s16[64,4224]{1,0:T(8,128)(2,1)S(1)}, s16[64,4224]{1,0:T(8,128)(2,1)S(1)}, u32[]{:S(2)}, u32[]{:S(2)}) collective-permute-start(s16[64,4224]{1,0:T(8,128)(2,1)S(1)} %get-tuple-element.50), channel_id=1, source_target_pairs={{0,8},{8,0},{16,24},{24,16},{1,9},{9,1},{17,25},{25,17},{2,10},{10... | collective-permute-start | bytes 1622024 | tf_op jit(solution)/shard_map/ppermute | solution.py:463
  29.7 14.7 %collective-permute-start.6 = (s16[64,4224]{1,0:T(8,128)(2,1)S(1)}, s16[64,4224]{1,0:T(8,128)(2,1)S(1)}, u32[]{:S(2)}, u32[]{:S(2)}) collective-permute-start(s16[64,4224]{1,0:T(8,128)(2,1)S(1)} %get-tuple-element.51), channel_id=1, source_target_pairs={{0,16},{8,24},{16,0},{24,8},{1,17},{9,25},{17,1},{25,9},{2,18},{10... | collective-permute-start | bytes 1622024 | tf_op jit(solution)/shard_map/ppermute | solution.py:463
  40.2 15.8 %collective-permute-start.3 = (s16[64,4224]{1,0:T(8,128)(2,1)}, s16[64,4224]{1,0:T(8,128)(2,1)S(1)}, u32[]{:S(2)}, u32[]{:S(2)}) collective-permute-start(s16[64,4224]{1,0:T(8,128)(2,1)} %get-tuple-element.46), channel_id=1, source_target_pairs={{0,8},{8,0},{16,24},{24,16},{1,9},{9,1},{17,25},{25,17},{2,10},{10... | collective-permute-start | bytes 1622024 | tf_op jit(solution)/shard_map/ppermute | solution.py:463
  41.0 15.1 %collective-permute-start.4 = (s16[64,4224]{1,0:T(8,128)(2,1)}, s16[64,4224]{1,0:T(8,128)(2,1)S(1)}, u32[]{:S(2)}, u32[]{:S(2)}) collective-permute-start(s16[64,4224]{1,0:T(8,128)(2,1)} %get-tuple-element.47), channel_id=1, source_target_pairs={{0,16},{8,24},{16,0},{24,8},{1,17},{9,25},{17,1},{25,9},{2,18},{10... | collective-permute-start | bytes 1622024 | tf_op jit(solution)/shard_map/ppermute | solution.py:463
  52.2 15.6 %collective-permute-start.7 = (s16[64,4224]{1,0:T(8,128)(2,1)}, s16[64,4224]{1,0:T(8,128)(2,1)}, u32[]{:S(2)}, u32[]{:S(2)}) collective-permute-start(s16[64,4224]{1,0:T(8,128)(2,1)} %get-tuple-element.52), channel_id=1, source_target_pairs={{0,8},{8,0},{16,24},{24,16},{1,9},{9,1},{17,25},{25,17},{2,10},{10... | collective-permute-start | bytes 1622024 | tf_op jit(solution)/shard_map/ppermute | solution.py:463
  52.8 15.0 %collective-permute-start.8 = (s16[64,4224]{1,0:T(8,128)(2,1)}, s16[64,4224]{1,0:T(8,128)(2,1)}, u32[]{:S(2)}, u32[]{:S(2)}) collective-permute-start(s16[64,4224]{1,0:T(8,128)(2,1)} %get-tuple-element.53), channel_id=1, source_target_pairs={{0,16},{8,24},{16,0},{24,8},{1,17},{9,25},{17,1},{25,9},{2,18},{10... | collective-permute-start | bytes 1622024 | tf_op jit(solution)/shard_map/ppermute | solution.py:463
  54.2 12.2 %copy-start.6 = (s32[128,16]{0,1:T(8,128)S(1)}, s32[128,16]{0,1:T(8,128)}, u32[]{:S(2)}) copy-start(s32[128,16]{0,1:T(8,128)} %param.9) | copy-start | bytes 24580
  63.9 23.0 %collective-permute-start.13 = (s16[64,4224]{1,0:T(8,128)(2,1)}, s16[64,4224]{1,0:T(8,128)(2,1)}, u32[]{:S(2)}, u32[]{:S(2)}) collective-permute-start(s16[64,4224]{1,0:T(8,128)(2,1)} %get-tuple-element.48), channel_id=1, source_target_pairs={{0,8},{8,0},{16,24},{24,16},{1,9},{9,1},{17,25},{25,17},{2,10},{10... | collective-permute-start | bytes 1622024 | tf_op jit(solution)/shard_map/ppermute | solution.py:463
  65.4 22.4 %collective-permute-start.14 = (s16[64,4224]{1,0:T(8,128)(2,1)}, s16[64,4224]{1,0:T(8,128)(2,1)}, u32[]{:S(2)}, u32[]{:S(2)}) collective-permute-start(s16[64,4224]{1,0:T(8,128)(2,1)} %get-tuple-element.59), channel_id=1, source_target_pairs={{0,16},{8,24},{16,0},{24,8},{1,17},{9,25},{17,1},{25,9},{2,18},{10... | collective-permute-start | bytes 1622024 | tf_op jit(solution)/shard_map/ppermute | solution.py:463
  66.6 10.7 %copy-start.7 = (s32[128]{0:T(128)S(1)}, s32[128]{0:T(128)}, u32[]{:S(2)}) copy-start(s32[128]{0:T(128)} %param.10) | copy-start | bytes 1540
  66.6 10.8 %copy-start.8 = (f32[128]{0:T(128)S(1)}, f32[128]{0:T(128)}, u32[]{:S(2)}) copy-start(f32[128]{0:T(128)} %param.11) | copy-start | bytes 1540
  75.4 0.9 copy-start.4
  76.3 36.5 %collective-permute-start.9 = (s16[64,4224]{1,0:T(8,128)(2,1)}, s16[64,4224]{1,0:T(8,128)(2,1)S(1)}, u32[]{:S(2)}, u32[]{:S(2)}) collective-permute-start(s16[64,4224]{1,0:T(8,128)(2,1)} %get-tuple-element.55), channel_id=1, source_target_pairs={{0,8},{8,0},{16,24},{24,16},{1,9},{9,1},{17,25},{25,17},{2,10},{10... | collective-permute-start | bytes 1622024 | tf_op jit(solution)/shard_map/ppermute | solution.py:463
  77.7 8.1 %copy-start.5 = (s16[64,4224]{1,0:T(8,128)(2,1)S(1)}, s16[64,4224]{1,0:T(8,128)(2,1)}, u32[]{:S(2)}) copy-start(s16[64,4224]{1,0:T(8,128)(2,1)} %copy-done.4) | copy-start | bytes 1622020
  77.7 10.1 %copy-start.3 = (f32[128,8192]{1,0:T(8,128)S(1)}, f32[128,8192]{1,0:T(8,128)}, u32[]{:S(2)}) copy-start(f32[128,8192]{1,0:T(8,128)} %copy-done.2) | copy-start | bytes 12582916
  84.7 29.4 %collective-permute-start.10 = (s16[64,4224]{1,0:T(8,128)(2,1)S(1)}, s16[64,4224]{1,0:T(8,128)(2,1)S(1)}, u32[]{:S(2)}, u32[]{:S(2)}) collective-permute-start(s16[64,4224]{1,0:T(8,128)(2,1)S(1)} %get-tuple-element.56), channel_id=1, source_target_pairs={{0,8},{8,0},{16,24},{24,16},{1,9},{9,1},{17,25},{25,17},{2,10},{10... | collective-permute-start | bytes 1622024 | tf_op jit(solution)/shard_map/ppermute | solution.py:463
  85.8 28.3 %collective-permute-start.11 = (s16[64,4224]{1,0:T(8,128)(2,1)S(1)}, s16[64,4224]{1,0:T(8,128)(2,1)S(1)}, u32[]{:S(2)}, u32[]{:S(2)}) collective-permute-start(s16[64,4224]{1,0:T(8,128)(2,1)S(1)} %copy-done.5), channel_id=1, source_target_pairs={{0,16},{8,24},{16,0},{24,8},{1,17},{9,25},{17,1},{25,9},{2,18},{10... | collective-permute-start | bytes 1622024 | tf_op jit(solution)/shard_map/ppermute | solution.py:463
  86.9 27.2 %collective-permute-start.12 = (s16[64,4224]{1,0:T(8,128)(2,1)S(1)}, s16[64,4224]{1,0:T(8,128)(2,1)S(1)}, u32[]{:S(2)}, u32[]{:S(2)}) collective-permute-start(s16[64,4224]{1,0:T(8,128)(2,1)S(1)} %get-tuple-element.58), channel_id=1, source_target_pairs={{0,16},{8,24},{16,0},{24,8},{1,17},{9,25},{17,1},{25,9},{2,18},{10... | collective-permute-start | bytes 1622024 | tf_op jit(solution)/shard_map/ppermute | solution.py:463
  111.7 25.8 %collective-permute-start.15 = (bf16[64,8320]{1,0:T(8,128)(2,1)S(1)}, bf16[64,8320]{1,0:T(8,128)(2,1)S(1)}, u32[]{:S(2)}, u32[]{:S(2)}) collective-permute-start(bf16[64,8320]{1,0:T(8,128)(2,1)S(1)} %get-tuple-element.69), channel_id=1, source_target_pairs={{0,16},{8,24},{16,0},{24,8},{1,17},{9,25},{17,1},{25,9},{2,18},{10... | collective-permute-start | bytes 3194888 | tf_op jit(solution)/shard_map/ppermute | solution.py:463
  112.8 25.8 %collective-permute-start.17 = (bf16[64,8320]{1,0:T(8,128)(2,1)S(1)}, bf16[64,8320]{1,0:T(8,128)(2,1)S(1)}, u32[]{:S(2)}, u32[]{:S(2)}) collective-permute-start(bf16[64,8320]{1,0:T(8,128)(2,1)S(1)} %get-tuple-element.69), channel_id=1, source_target_pairs={{0,8},{8,0},{16,24},{24,16},{1,9},{9,1},{17,25},{25,17},{2,10},{10... | collective-permute-start | bytes 3194888 | tf_op jit(solution)/shard_map/ppermute | solution.py:463
  137.5 13.6 %collective-permute-start.16 = (bf16[32,8320]{1,0:T(8,128)(2,1)S(1)}, bf16[32,8320]{1,0:T(8,128)(2,1)S(1)}, u32[]{:S(2)}, u32[]{:S(2)}) collective-permute-start(bf16[32,8320]{1,0:T(8,128)(2,1)S(1)} %slice.33), channel_id=1, source_target_pairs={{0,8},{8,0},{16,24},{24,16},{1,9},{9,1},{17,25},{25,17},{2,10},{10... | collective-permute-start | bytes 1597448 | tf_op jit(solution)/shard_map/ppermute | solution.py:463
  138.6 13.3 %collective-permute-start.18 = (bf16[32,8320]{1,0:T(8,128)(2,1)S(1)}, bf16[32,8320]{1,0:T(8,128)(2,1)S(1)}, u32[]{:S(2)}, u32[]{:S(2)}) collective-permute-start(bf16[32,8320]{1,0:T(8,128)(2,1)S(1)} %slice.34), channel_id=1, source_target_pairs={{0,16},{8,24},{16,0},{24,8},{1,17},{9,25},{17,1},{25,9},{2,18},{10... | collective-permute-start | bytes 1597448 | tf_op jit(solution)/shard_map/ppermute | solution.py:463
  152.0 23.8 %collective-permute-start.19 = (bf16[64,8320]{1,0:T(8,128)(2,1)S(1)}, bf16[64,8320]{1,0:T(8,128)(2,1)S(1)}, u32[]{:S(2)}, u32[]{:S(2)}) collective-permute-start(bf16[64,8320]{1,0:T(8,128)(2,1)S(1)} %get-tuple-element.73), channel_id=1, source_target_pairs={{0,16},{8,24},{16,0},{24,8},{1,17},{9,25},{17,1},{25,9},{2,18},{10... | collective-permute-start | bytes 3194888 | tf_op jit(solution)/shard_map/ppermute | solution.py:463
  153.3 23.5 %collective-permute-start.20 = (bf16[64,8320]{1,0:T(8,128)(2,1)S(1)}, bf16[64,8320]{1,0:T(8,128)(2,1)S(1)}, u32[]{:S(2)}, u32[]{:S(2)}) collective-permute-start(bf16[64,8320]{1,0:T(8,128)(2,1)S(1)} %get-tuple-element.73), channel_id=1, source_target_pairs={{0,8},{8,0},{16,24},{24,16},{1,9},{9,1},{17,25},{25,17},{2,10},{10... | collective-permute-start | bytes 3194888 | tf_op jit(solution)/shard_map/ppermute | solution.py:463
  164.3 14.3 %collective-permute-start.21 = (s16[256,1152]{1,0:T(8,128)(2,1)S(1)}, s16[256,1152]{1,0:T(8,128)(2,1)S(1)}, u32[]{:S(2)}, u32[]{:S(2)}) collective-permute-start(s16[256,1152]{1,0:T(8,128)(2,1)S(1)} %grad_rows.4), channel_id=1, source_target_pairs={{0,1},{1,0},{2,3},{3,2},{4,5},{5,4},{6,7},{7,6},{8,9},{9,8},{10,11... | collective-permute-start | bytes 1769480 | tf_op jit(solution)/shard_map/ppermute | solution.py:531
  176.8 16.3 %collective-permute-start.26 = (bf16[32,8320]{1,0:T(8,128)(2,1)S(1)}, bf16[32,8320]{1,0:T(8,128)(2,1)S(1)}, u32[]{:S(2)}, u32[]{:S(2)}) collective-permute-start(bf16[32,8320]{1,0:T(8,128)(2,1)S(1)} %slice.35), channel_id=1, source_target_pairs={{0,8},{8,0},{16,24},{24,16},{1,9},{9,1},{17,25},{25,17},{2,10},{10... | collective-permute-start | bytes 1597448 | tf_op jit(solution)/shard_map/ppermute | solution.py:463
  177.7 15.5 %collective-permute-start.27 = (bf16[32,8320]{1,0:T(8,128)(2,1)S(1)}, bf16[32,8320]{1,0:T(8,128)(2,1)S(1)}, u32[]{:S(2)}, u32[]{:S(2)}) collective-permute-start(bf16[32,8320]{1,0:T(8,128)(2,1)S(1)} %slice.36), channel_id=1, source_target_pairs={{0,16},{8,24},{16,0},{24,8},{1,17},{9,25},{17,1},{25,9},{2,18},{10... | collective-permute-start | bytes 1597448 | tf_op jit(solution)/shard_map/ppermute | solution.py:463
  179.7 5.8 %collective-permute-start.22 = (s16[64,1152]{1,0:T(8,128)(2,1)S(1)}, s16[64,1152]{1,0:T(8,128)(2,1)S(1)}, u32[]{:S(2)}, u32[]{:S(2)}) collective-permute-start(s16[64,1152]{1,0:T(8,128)(2,1)S(1)} %get-tuple-element.79), channel_id=1, source_target_pairs={{0,2},{1,3},{2,0},{3,1},{4,6},{5,7},{6,4},{7,5},{8,10},{9,11},{10,... | collective-permute-start | bytes 442376 | tf_op jit(solution)/shard_map/ppermute | solution.py:538
  181.2 11.9 %collective-permute-start.23 = (s16[64,1152]{1,0:T(8,128)(2,1)S(1)}, s16[64,1152]{1,0:T(8,128)(2,1)S(1)}, u32[]{:S(2)}, u32[]{:S(2)}) collective-permute-start(s16[64,1152]{1,0:T(8,128)(2,1)S(1)} %get-tuple-element.80), channel_id=1, source_target_pairs={{0,4},{1,5},{2,6},{3,7},{4,0},{5,1},{6,2},{7,3},{8,12},{9,13},{10,... | collective-permute-start | bytes 442376 | tf_op jit(solution)/shard_map/ppermute | solution.py:538
  183.6 9.5 %collective-permute-start.24 = (s16[64,1152]{1,0:T(8,128)(2,1)S(1)}, s16[64,1152]{1,0:T(8,128)(2,1)S(1)}, u32[]{:S(2)}, u32[]{:S(2)}) collective-permute-start(s16[64,1152]{1,0:T(8,128)(2,1)S(1)} %get-tuple-element.81), channel_id=1, source_target_pairs={{0,6},{1,7},{2,4},{3,5},{4,2},{5,3},{6,0},{7,1},{8,14},{9,15},{10,... | collective-permute-start | bytes 442376 | tf_op jit(solution)/shard_map/ppermute | solution.py:538
  193.2 10.7 %copy-start = (bf16[256,8320]{1,0:T(8,128)(2,1)}, bf16[256,8320]{1,0:T(8,128)(2,1)S(1)}, u32[]{:S(2)}) copy-start(bf16[256,8320]{1,0:T(8,128)(2,1)S(1)} %constant_dynamic-update-slice_fusion.5.grad_ref.beside_ref) | copy-start | bytes 12779524
  203.9 17.0 %collective-permute-start.28 = (s16[256,1152]{1,0:T(8,128)(2,1)S(1)}, s16[256,1152]{1,0:T(8,128)(2,1)S(1)}, u32[]{:S(2)}, u32[]{:S(2)}) collective-permute-start(s16[256,1152]{1,0:T(8,128)(2,1)S(1)} %grad_rows.6), channel_id=1, source_target_pairs={{0,1},{1,0},{2,3},{3,2},{4,5},{5,4},{6,7},{7,6},{8,9},{9,8},{10,11... | collective-permute-start | bytes 1769480 | tf_op jit(solution)/shard_map/ppermute | solution.py:531
  204.4 37.3 %collective-permute-start.25 = (s16[64,1152]{1,0:T(8,128)(2,1)S(1)}, s16[64,1152]{1,0:T(8,128)(2,1)S(1)}, u32[]{:S(2)}, u32[]{:S(2)}) collective-permute-start(s16[64,1152]{1,0:T(8,128)(2,1)S(1)} %last_sum.2), channel_id=1, source_target_pairs={{0,0},{1,1},{2,8},{3,9},{4,16},{5,17},{6,24},{7,25},{8,2},{9,3},{1... | collective-permute-start | bytes 442376 | tf_op jit(solution)/shard_map/ppermute | solution.py:549
  209.0 2.2 copy-start.1
  211.2 40.5 %dynamic-slice-start = ((f32[8192]{0:T(1024)}, s32[]{:T(128)}), f32[1024]{0:T(1024)S(1)}, s32[]{:S(2)}) async-start(f32[8192]{0:T(1024)} %param.8, s32[]{:T(128)} %select_n.37), calls=%async_computation | async-start | bytes 8704 | tf_op jit(solution)/shard_map/dynamic_slice | solution.py:559
  222.0 9.0 %collective-permute-start.29 = (s16[64,1152]{1,0:T(8,128)(2,1)S(1)}, s16[64,1152]{1,0:T(8,128)(2,1)S(1)}, u32[]{:S(2)}, u32[]{:S(2)}) collective-permute-start(s16[64,1152]{1,0:T(8,128)(2,1)S(1)} %get-tuple-element.85), channel_id=1, source_target_pairs={{0,2},{1,3},{2,0},{3,1},{4,6},{5,7},{6,4},{7,5},{8,10},{9,11},{10,... | collective-permute-start | bytes 442376 | tf_op jit(solution)/shard_map/ppermute | solution.py:538
  222.1 14.2 %collective-permute-start.30 = (s16[64,1152]{1,0:T(8,128)(2,1)S(1)}, s16[64,1152]{1,0:T(8,128)(2,1)S(1)}, u32[]{:S(2)}, u32[]{:S(2)}) collective-permute-start(s16[64,1152]{1,0:T(8,128)(2,1)S(1)} %get-tuple-element.86), channel_id=1, source_target_pairs={{0,4},{1,5},{2,6},{3,7},{4,0},{5,1},{6,2},{7,3},{8,12},{9,13},{10,... | collective-permute-start | bytes 442376 | tf_op jit(solution)/shard_map/ppermute | solution.py:538
  225.3 11.0 %collective-permute-start.31 = (s16[64,1152]{1,0:T(8,128)(2,1)S(1)}, s16[64,1152]{1,0:T(8,128)(2,1)S(1)}, u32[]{:S(2)}, u32[]{:S(2)}) collective-permute-start(s16[64,1152]{1,0:T(8,128)(2,1)S(1)} %get-tuple-element.87), channel_id=1, source_target_pairs={{0,6},{1,7},{2,4},{3,5},{4,2},{5,3},{6,0},{7,1},{8,14},{9,15},{10,... | collective-permute-start | bytes 442376 | tf_op jit(solution)/shard_map/ppermute | solution.py:538
  236.6 14.8 %collective-permute-start.32 = (s16[64,1152]{1,0:T(8,128)(2,1)S(1)}, s16[64,1152]{1,0:T(8,128)(2,1)S(1)}, u32[]{:S(2)}, u32[]{:S(2)}) collective-permute-start(s16[64,1152]{1,0:T(8,128)(2,1)S(1)} %last_sum.3), channel_id=1, source_target_pairs={{0,0},{1,1},{2,8},{3,9},{4,16},{5,17},{6,24},{7,25},{8,2},{9,3},{1... | collective-permute-start | bytes 442376 | tf_op jit(solution)/shard_map/ppermute | solution.py:549

commit v8 on v7

--- a/solution.py
+++ b/solution.py
@@ -339,9 +339,7 @@
     def _():
         total_ref[...] = jnp.zeros_like(total_ref)
 
-    total_ref[...] += lax.dot_general(
-        grad_ref[...], head.get(tile), (((1,), (1,)), ((), ())), preferred_element_type=jnp.float32
-    )
+    total_ref[...] += dot(head.get(tile), grad_ref[...].T)
     head.release(tile)
 
     @pl.when(tile == tiles - 1)
@@ -351,7 +349,7 @@
         width = outs[0].shape[1] - tail
         for k, out_ref in enumerate(outs):
             start = pl.multiple_of((place_ref[1] ^ k) * width, width)
-            value = total_ref[:, pl.ds(start, width)]
+            value = total_ref[pl.ds(start, width), :].T
             if k == 0 and keeps:
                 out_ref[:, :width] = value
                 out_ref[:, width:] = term
@@ -376,7 +374,7 @@
                 head_spec,
             ],
             out_specs=[constant(rows, part + tail)] * blocks,
-            scratch_shapes=[pltpu.VMEM((rows, blocks * part), jnp.float32)]
+            scratch_shapes=[pltpu.VMEM((blocks * part, rows), jnp.float32)]
             + head_scratch(blocks * part, width, columns // width),
         ),
         out_shape=[jax.ShapeDtypeStruct((rows, part + tail), t) for t in types],
@@ -546,11 +544,10 @@
     sum_a = last_sum(keep_a, received_a)
     keep_b, received_b = gradient((*rows_b, *far_b), received_a, [sum_a])
     sum_b = last_sum(*blocks(keep_b, received_b))
-    grad_cols = [lax.ppermute(total, ("prompt", "vocab"), moves) for total in (sum_a, sum_b)]
+    codes = lax.ppermute(jnp.concatenate([sum_a, sum_b]), ("prompt", "vocab"), moves)
 
     slice_width = model_width // vocab_size
     col_start = shard * slice_width
-    codes = jnp.concatenate(grad_cols)
     power = codes[:, slice_width : slice_width + 1].astype(jnp.float32)
     grad_cols = codes[:, :slice_width].astype(jnp.float32) * jnp.exp(power * per_step)
     term = codes[:, slice_width + 1 : slice_width + 3].astype(jnp.float32)

time: 254 us -> 258 us (1.016)
  waiting for transfers between devices: 49.3 us -> 59.5 us
  starting transfers between devices: 43.4 us -> 39.4 us
    ppermute x2 -> x1, waiting for transfers between devices: 9.67 us -> 18.4 us  [shards(): lax.ppermute(jnp.concatenate([sum_a, sum_b]), ('prompt', 'vocab'), moves)]
    ppermute x2 -> x1, starting transfers between devices: 9.64 us -> 5.37 us  [shards(): lax.ppermute(jnp.concatenate([sum_a, sum_b]), ('prompt', 'vocab'), moves)]
    unnamed x27 -> x22, local copies, waits for them, and re-layouts: 5.79 us -> 3.57 us
  transfers between devices with their start and end apart: 33 -> 32, of which waited for: 15 -> 15; matrix products, arithmetic and copies ran while one was open for 1% -> 1% of each run, Pallas kernels for 42% -> 41%
where the time goes in v8:
time: 258 us
  Pallas kernels  116 us (45%)
  waiting for transfers between devices  59.5 us (23%)
  starting transfers between devices  39.4 us (15%)
  blocking collectives  29.1 us (11%)
  other arithmetic  7.44 us (3%)
  local copies, waits for them, and re-layouts  5.2 us (2%)
    pallas_call x4, Pallas kernels, back(): pl.pallas_call(functools.partial(back_kernel, columns // width, keeps), g...  39.9 us
    pallas_call x4, Pallas kernels, near_codes(): pl.pallas_call(functools.partial(near_kernel, width, skip, tiles), grid=(...  30.3 us
    all_gather x2, blocking collectives, shards(): stats = lax.all_gather(stats, 'vocab', axis=0)  29.1 us
    ppermute x23, starting transfers between devices, shards(): send = lambda value, pairs: lax.ppermute(value, 'prompt', pairs)  24.8 us
    ppermute x23, waiting for transfers between devices, shards(): send = lambda value, pairs: lax.ppermute(value, 'prompt', pairs)  21.3 us
    ppermute x6, waiting for transfers between devices, blocks(): lax.ppermute(c, 'vocab', to)  19.8 us
    ppermute x1, waiting for transfers between devices, shards(): lax.ppermute(jnp.concatenate([sum_a, sum_b]), ('prompt', 'vocab'), moves)  18.4 us
    pallas_call x2, Pallas kernels, far_codes(): pl.pallas_call(functools.partial(far_kernel, width, skip, tiles), grid=(t...  14.6 us
  transfers between devices with their start and end apart: 32, of which 15 were waited for; matrix products, arithmetic and copies ran while one was open for 1% of the time, Pallas kernels for 41%

profile of v8, /device:TPU:2, one launch (start us, length us, event | category | flops | bytes accessed | tf_op | source)
XLA Modules:
  0.0 258.2 jit_solution(1315525898675718378)
XLA Ops:
  0.6 2.1 fusion
  2.7 2.2 fusion.2
  5.1 1.6 collective-permute-start.2
  6.7 1.6 collective-permute-start
  8.9 11.8 %own_logits.1.refs_0_ = f32[128,8192]{1,0:T(8,128)S(1)} custom-call(bf16[128,2048]{1,0:T(8,128)(2,1)S(1)} %get-tuple-element.91.x_ref, bf16[2048,8192]{1,0:T(8,128)(2,1)} %head_ref.21), custom_call_target="tpu_custom_call" | custom-call | flops 1024 | bytes 1024 | tf_op jit(solution)/shard_map/own_logits/pallas_call | solution.py:176
  20.7 2.0 copy-done
  22.7 6.8 %far_codes.3 = (s16[64,4224]{1,0:T(8,128)(2,1)S(1)}, s16[64,4224]{1,0:T(8,128)(2,1)S(1)}) custom-call(bf16[128,2048]{1,0:T(8,128)(2,1)S(1)} %collective-permute-done.2.x_ref, bf16[2048,8192]{1,0:T(8,128)(2,1)} %head_ref.21), custom_call_target="tpu_custom_call" | custom-call | flops 1024 | bytes 1024 | tf_op jit(solution)/shard_map/far_codes/pallas_call | solution.py:117
  29.7 2.0 collective-permute-start.6
  31.6 0.7 collective-permute-done.x_ref
  32.4 7.8 %far_codes.2 = (s16[64,4224]{1,0:T(8,128)(2,1)}, s16[64,4224]{1,0:T(8,128)(2,1)}) custom-call(bf16[128,2048]{1,0:T(8,128)(2,1)S(1)} %collective-permute-done.2.x_ref, bf16[2048,8192]{1,0:T(8,128)(2,1)} %head_ref.21), custom_call_target="tpu_custom_call" | custom-call | flops 1024 | bytes 1024 | tf_op jit(solution)/shard_map/far_codes/pallas_call | solution.py:117
  40.2 0.8 collective-permute-start.3
  41.6 2.7 %collective-permute-done.5.by_x_ref = s16[64,4224]{1,0:T(8,128)(2,1)S(1)} collective-permute-done((s16[64,4224]{1,0:T(8,128)(2,1)S(1)}, s16[64,4224]{1,0:T(8,128)(2,1)S(1)}, u32[]{:S(2)}, u32[]{:S(2)}) %collective-permute-start.5) | collective-permute-done | bytes 540704 | tf_op jit(solution)/shard_map/ppermute | solution.py:461
  44.3 7.9 %near_codes.5 = (s16[64,4224]{1,0:T(8,128)(2,1)}, s16[64,4224]{1,0:T(8,128)(2,1)}) custom-call(bf16[128,2176]{1,0:T(8,128)(2,1)S(1)} %collective-permute-done.x_ref, bf16[128,2176]{1,0:T(8,128)(2,1)S(1)} %collective-permute-done.1.y_ref, bf16[2048,8192]{1,0:T(8,128)(2,1)} %head_ref.21, s16[64,4224]{1,0:T(8,128)(2,1)S(1)} %collective-permute-done.5.by_x_ref, ...), custom_call_target="tpu_custom_call" | custom-call | flops 1024 | bytes 1024 | tf_op jit(solution)/shard_map/near_codes/pallas_call | solution.py:151
  52.8 1.4 collective-permute-start.8
  54.3 1.6 collective-permute-done.3.by_x_ref
  56.1 7.8 %near_codes.4 = (s16[64,4224]{1,0:T(8,128)(2,1)}, s16[64,4224]{1,0:T(8,128)(2,1)}) custom-call(bf16[128,2176]{1,0:T(8,128)(2,1)S(1)} %collective-permute-done.x_ref, bf16[128,2176]{1,0:T(8,128)(2,1)S(1)} %collective-permute-done.1.y_ref, bf16[2048,8192]{1,0:T(8,128)(2,1)} %head_ref.21, s16[64,4224]{1,0:T(8,128)(2,1)S(1)} %collective-permute-done.3.by_x_ref, ...), custom_call_target="tpu_custom_call" | custom-call | flops 1024 | bytes 1024 | tf_op jit(solution)/shard_map/near_codes/pallas_call | solution.py:151
  63.9 1.5 collective-permute-start.13
  65.4 1.1 collective-permute-start.14
  66.6 1.1 collective-permute-done.7.refs_1_
  67.8 7.6 %near_codes.6 = (s16[64,4224]{1,0:T(8,128)(2,1)}, s16[64,4224]{1,0:T(8,128)(2,1)S(1)}) custom-call(bf16[128,2176]{1,0:T(8,128)(2,1)S(1)} %collective-permute-done.x_ref, bf16[128,2176]{1,0:T(8,128)(2,1)S(1)} %collective-permute-done.1.y_ref, bf16[2048,8192]{1,0:T(8,128)(2,1)} %head_ref.21, s16[64,4224]{1,0:T(8,128)(2,1)S(1)} %collective-permute-done.5.by_x_ref, ...), custom_call_target="tpu_custom_call" | custom-call | flops 1024 | bytes 1024 | tf_op jit(solution)/shard_map/near_codes/pallas_call | solution.py:151
  75.4 0.8 copy-done.2
  76.3 1.0 collective-permute-start.9
  77.7 7.0 %near_codes.7 = (s16[64,4224]{1,0:T(8,128)(2,1)S(1)}, s16[64,4224]{1,0:T(8,128)(2,1)S(1)}) custom-call(bf16[128,2176]{1,0:T(8,128)(2,1)S(1)} %collective-permute-done.x_ref, bf16[128,2176]{1,0:T(8,128)(2,1)S(1)} %collective-permute-done.1.y_ref, bf16[2048,8192]{1,0:T(8,128)(2,1)} %head_ref.21, s16[64,4224]{1,0:T(8,128)(2,1)S(1)} %collective-permute-done.3.by_x_ref, ...), custom_call_target="tpu_custom_call" | custom-call | flops 1024 | bytes 1024 | tf_op jit(solution)/shard_map/near_codes/pallas_call | solution.py:151
  84.6 1.1 collective-permute-start.10
  85.7 1.1 collective-permute-start.11
  86.8 0.9 collective-permute-start.12
  87.7 7.0 %row_stats.2 = (f32[64,8192]{1,0:T(8,128)S(1)}, f32[64,8192]{1,0:T(8,128)S(1)}, f32[64,128]{1,0:T(8,128)S(1)}) custom-call(f32[128,8192]{1,0:T(8,128)S(1)} %copy-done.1, s16[64,4224]{1,0:T(8,128)(2,1)} %collective-permute-done.7.refs_1_, s16[64,4224]{1,0:T(8,128)(2,1)} %collective-permute-done.13.refs_2_, s16[64,4224]{1,0:T(8,128)(2,1)} %collective-permute-done.8.refs_3_, ...), custom_call_target="tpu_custom_call" | custom-call | flops 1024 | bytes 1024 | tf_op jit(solution)/shard_map/row_stats/pallas_call | solution.py:239
  94.7 14.7 %all-gather = f32[512,128]{1,0:T(8,128)S(1)} all-gather(f32[64,128]{1,0:T(8,128)S(1)} %get-tuple-element.62), channel_id=2, replica_groups=mesh['prompt'=4,'vocab'=8] {'vocab'}, dimensions={0}, use_global_device_ids=true | all-gather | bytes 294912 | tf_op jit(solution)/shard_map/all_gather | solution.py:512
  109.4 2.2 logit_grads.2
  111.6 1.2 collective-permute-start.15
  112.8 1.2 collective-permute-start.17
  114.1 5.9 %row_stats.3 = (f32[64,8192]{1,0:T(8,128)S(1)}, f32[64,8192]{1,0:T(8,128)S(1)}, f32[64,128]{1,0:T(8,128)S(1)}) custom-call(f32[128,8192]{1,0:T(8,128)S(1)} %copy-done.1, s16[64,4224]{1,0:T(8,128)(2,1)S(1)} %collective-permute-done.9.refs_1_, s16[64,4224]{1,0:T(8,128)(2,1)S(1)} %collective-permute-done.10.refs_2_, ...), custom_call_target="tpu_custom_call" | custom-call | flops 1024 | bytes 1024 | tf_op jit(solution)/shard_map/row_stats/pallas_call | solution.py:239
  120.0 14.3 %all-gather.1 = f32[512,128]{1,0:T(8,128)S(1)} all-gather(f32[64,128]{1,0:T(8,128)S(1)} %get-tuple-element.67), channel_id=3, replica_groups=mesh['prompt'=4,'vocab'=8] {'vocab'}, dimensions={0}, use_global_device_ids=true | all-gather | bytes 294912 | tf_op jit(solution)/shard_map/all_gather | solution.py:512
  134.3 2.2 logit_grads.3
  136.5 0.9 collective-permute-done.15
  137.5 1.1 collective-permute-start.16
  138.6 1.4 collective-permute-start.18
  140.3 10.8 %collective-permute-done.16 = bf16[32,8320]{1,0:T(8,128)(2,1)S(1)} collective-permute-done((bf16[32,8320]{1,0:T(8,128)(2,1)S(1)}, bf16[32,8320]{1,0:T(8,128)(2,1)S(1)}, u32[]{:S(2)}, u32[]{:S(2)}) %collective-permute-start.16) | collective-permute-done | bytes 532512 | tf_op jit(solution)/shard_map/ppermute | solution.py:461
  151.1 0.9 collective-permute-done.18
  151.9 1.3 collective-permute-start.19
  153.3 0.8 collective-permute-start.20
  154.3 10.1 %grad_rows.4 = s16[256,1152]{1,0:T(8,128)(2,1)S(1)} custom-call(s32[2]{0:T(128)S(1)} %pad_add_fusion.1.place_ref, bf16[256,8320]{1,0:T(8,128)(2,1)S(1)} %constant_dynamic-update-slice_fusion.grad_ref.beside_ref, bf16[256,8320]{1,0:T(8,128)(2,1)S(1)} %constant_dynamic-update-slice_fusion.grad_ref.beside_ref, bf16[2048,8192]{1,0:T(8,128)(2,1)} %head_ref.21), custom_call_target="tpu_custom_call" | custom-call | flops 1024 | bytes 1024 | tf_op jit(solution)/shard_map/grad_rows/pallas_call | solution.py:366
  164.5 9.8 %grad_rows.5.keep_ref = f32[256,1152]{1,0:T(8,128)S(1)} custom-call(s32[2]{0:T(128)S(1)} %pad_add_fusion.2.place_ref, bf16[256,8320]{1,0:T(8,128)(2,1)S(1)} %constant_dynamic-update-slice_fusion.grad_ref.beside_ref, bf16[256,8320]{1,0:T(8,128)(2,1)S(1)} %constant_dynamic-update-slice_fusion.grad_ref.beside_ref, bf16[2048,8192]{1,0:T(8,128)(2,1)} %head_ref.21), custom_call_target="tpu_custom_call" | custom-call | flops 1024 | bytes 1024 | tf_op jit(solution)/shard_map/grad_rows/pallas_call | solution.py:366
  174.4 1.3 collective-permute-done.19
  175.7 1.0 collective-permute-done.20
  176.8 0.9 collective-permute-start.25
  177.6 0.9 collective-permute-start.26
  178.5 1.1 group_sum.2
  179.6 1.5 collective-permute-start.22
  181.1 2.4 collective-permute-start.23
  184.3 1.1 collective-permute-done.22.refs_0_
  185.4 7.9 %collective-permute-done.23.refs_1_ = s16[64,1152]{1,0:T(8,128)(2,1)S(1)} collective-permute-done((s16[64,1152]{1,0:T(8,128)(2,1)S(1)}, s16[64,1152]{1,0:T(8,128)(2,1)S(1)}, u32[]{:S(2)}, u32[]{:S(2)}) %collective-permute-start.23) | collective-permute-done | bytes 147488 | tf_op jit(solution)/shard_map/ppermute | solution.py:536
  193.4 10.1 %grad_rows.6 = s16[256,1152]{1,0:T(8,128)(2,1)S(1)} custom-call(s32[2]{0:T(128)S(1)} %pad_add_fusion.1.place_ref, bf16[256,8320]{1,0:T(8,128)(2,1)S(1)} %constant_dynamic-update-slice_fusion.5.grad_ref.beside_ref, bf16[256,8320]{1,0:T(8,128)(2,1)S(1)} %constant_dynamic-update-slice_fusion.5.grad_ref.beside_ref, bf16[2048,8192]{1,0:T(8,128)(2,1)} %head_ref.21), custom_call_target="tpu_custom_call" | custom-call | flops 1024 | bytes 1024 | tf_op jit(solution)/shard_map/grad_rows/pallas_call | solution.py:366
  203.9 9.8 %grad_rows.7.keep_ref = f32[256,1152]{1,0:T(8,128)S(1)} custom-call(s32[2]{0:T(128)S(1)} %pad_add_fusion.2.place_ref, bf16[256,8320]{1,0:T(8,128)(2,1)S(1)} %constant_dynamic-update-slice_fusion.5.grad_ref.beside_ref, bf16[256,8320]{1,0:T(8,128)(2,1)S(1)} %constant_dynamic-update-slice_fusion.5.grad_ref.beside_ref, bf16[2048,8192]{1,0:T(8,128)(2,1)} %head_ref.21), custom_call_target="tpu_custom_call" | custom-call | flops 1024 | bytes 1024 | tf_op jit(solution)/shard_map/grad_rows/pallas_call | solution.py:366
  213.8 1.1 group_sum.3
  214.8 2.2 collective-permute-start.28
  217.0 0.9 collective-permute-start.29
  217.9 1.6 collective-permute-start.30
  219.5 0.7 dynamic_slice.18
  220.2 4.0 %collective-permute-done.28.refs_0_ = s16[64,1152]{1,0:T(8,128)(2,1)S(1)} collective-permute-done((s16[64,1152]{1,0:T(8,128)(2,1)S(1)}, s16[64,1152]{1,0:T(8,128)(2,1)S(1)}, u32[]{:S(2)}, u32[]{:S(2)}) %collective-permute-start.28) | collective-permute-done | bytes 147488 | tf_op jit(solution)/shard_map/ppermute | solution.py:536
  224.2 6.8 %collective-permute-done.29.refs_1_ = s16[64,1152]{1,0:T(8,128)(2,1)S(1)} collective-permute-done((s16[64,1152]{1,0:T(8,128)(2,1)S(1)}, s16[64,1152]{1,0:T(8,128)(2,1)S(1)}, u32[]{:S(2)}, u32[]{:S(2)}) %collective-permute-start.29) | collective-permute-done | bytes 147488 | tf_op jit(solution)/shard_map/ppermute | solution.py:536
  231.3 5.4 %collective-permute-start.31 = (s16[128,1152]{1,0:T(8,128)(2,1)S(1)}, s16[128,1152]{1,0:T(8,128)(2,1)S(1)}, u32[]{:S(2)}, u32[]{:S(2)}) collective-permute-start(s16[128,1152]{1,0:T(8,128)(2,1)S(1)} %pad_add_fusion), channel_id=1, source_target_pairs={{0,0},{1,1},{2,8},{3,9},{4,16},{5,17},{6,24},{7,25},{8,2},{9,3},{1... | collective-permute-start | bytes 884744 | tf_op jit(solution)/shard_map/ppermute | solution.py:547
  237.5 18.4 %collective-permute-done.31 = s16[128,1152]{1,0:T(8,128)(2,1)S(1)} collective-permute-done((s16[128,1152]{1,0:T(8,128)(2,1)S(1)}, s16[128,1152]{1,0:T(8,128)(2,1)S(1)}, u32[]{:S(2)}, u32[]{:S(2)}) %collective-permute-start.31) | collective-permute-done | bytes 294944 | tf_op jit(solution)/shard_map/ppermute | solution.py:547
  256.2 2.0 multiply_subtract_fusion
  (70 shorter events, 6.4 us)
Async XLA Ops:
  5.1 17.5 %collective-permute-start.2 = (bf16[128,2048]{1,0:T(8,128)(2,1)S(1)}, bf16[128,2048]{1,0:T(8,128)(2,1)S(1)}, u32[]{:S(2)}, u32[]{:S(2)}) collective-permute-start(bf16[128,2048]{1,0:T(8,128)(2,1)S(1)} %get-tuple-element.88), channel_id=1, source_target_pairs={{0,24},{8,16},{16,8},{24,0},{1,25},{9,17},{17,9},{25,1},{2,26},{10... | collective-permute-start | bytes 1572872 | tf_op jit(solution)/shard_map/ppermute | solution.py:461
  6.7 25.6 %collective-permute-start = (bf16[128,2176]{1,0:T(8,128)(2,1)S(1)}, bf16[128,2176]{1,0:T(8,128)(2,1)S(1)}, u32[]{:S(2)}, u32[]{:S(2)}) collective-permute-start(bf16[128,2176]{1,0:T(8,128)(2,1)S(1)} %pad.7), channel_id=1, source_target_pairs={{0,8},{8,0},{16,24},{24,16},{1,9},{9,1},{17,25},{25,17},{2,10},{10... | collective-permute-start | bytes 1671176 | tf_op jit(solution)/shard_map/ppermute | solution.py:461
  8.3 24.0 %collective-permute-start.1 = (bf16[128,2176]{1,0:T(8,128)(2,1)S(1)}, bf16[128,2176]{1,0:T(8,128)(2,1)S(1)}, u32[]{:S(2)}, u32[]{:S(2)}) collective-permute-start(bf16[128,2176]{1,0:T(8,128)(2,1)S(1)} %pad.8), channel_id=1, source_target_pairs={{0,16},{8,24},{16,0},{24,8},{1,17},{9,25},{17,1},{25,9},{2,18},{10... | collective-permute-start | bytes 1671176 | tf_op jit(solution)/shard_map/ppermute | solution.py:461
  20.7 2.0 copy-start
  29.5 14.8 %collective-permute-start.5 = (s16[64,4224]{1,0:T(8,128)(2,1)S(1)}, s16[64,4224]{1,0:T(8,128)(2,1)S(1)}, u32[]{:S(2)}, u32[]{:S(2)}) collective-permute-start(s16[64,4224]{1,0:T(8,128)(2,1)S(1)} %get-tuple-element.50), channel_id=1, source_target_pairs={{0,8},{8,0},{16,24},{24,16},{1,9},{9,1},{17,25},{25,17},{2,10},{10... | collective-permute-start | bytes 1622024 | tf_op jit(solution)/shard_map/ppermute | solution.py:461
  29.7 14.6 %collective-permute-start.6 = (s16[64,4224]{1,0:T(8,128)(2,1)S(1)}, s16[64,4224]{1,0:T(8,128)(2,1)S(1)}, u32[]{:S(2)}, u32[]{:S(2)}) collective-permute-start(s16[64,4224]{1,0:T(8,128)(2,1)S(1)} %get-tuple-element.51), channel_id=1, source_target_pairs={{0,16},{8,24},{16,0},{24,8},{1,17},{9,25},{17,1},{25,9},{2,18},{10... | collective-permute-start | bytes 1622024 | tf_op jit(solution)/shard_map/ppermute | solution.py:461
  40.2 15.7 %collective-permute-start.3 = (s16[64,4224]{1,0:T(8,128)(2,1)}, s16[64,4224]{1,0:T(8,128)(2,1)S(1)}, u32[]{:S(2)}, u32[]{:S(2)}) collective-permute-start(s16[64,4224]{1,0:T(8,128)(2,1)} %get-tuple-element.46), channel_id=1, source_target_pairs={{0,8},{8,0},{16,24},{24,16},{1,9},{9,1},{17,25},{25,17},{2,10},{10... | collective-permute-start | bytes 1622024 | tf_op jit(solution)/shard_map/ppermute | solution.py:461
  41.0 15.1 %collective-permute-start.4 = (s16[64,4224]{1,0:T(8,128)(2,1)}, s16[64,4224]{1,0:T(8,128)(2,1)S(1)}, u32[]{:S(2)}, u32[]{:S(2)}) collective-permute-start(s16[64,4224]{1,0:T(8,128)(2,1)} %get-tuple-element.47), channel_id=1, source_target_pairs={{0,16},{8,24},{16,0},{24,8},{1,17},{9,25},{17,1},{25,9},{2,18},{10... | collective-permute-start | bytes 1622024 | tf_op jit(solution)/shard_map/ppermute | solution.py:461
  52.2 15.6 %collective-permute-start.7 = (s16[64,4224]{1,0:T(8,128)(2,1)}, s16[64,4224]{1,0:T(8,128)(2,1)}, u32[]{:S(2)}, u32[]{:S(2)}) collective-permute-start(s16[64,4224]{1,0:T(8,128)(2,1)} %get-tuple-element.52), channel_id=1, source_target_pairs={{0,8},{8,0},{16,24},{24,16},{1,9},{9,1},{17,25},{25,17},{2,10},{10... | collective-permute-start | bytes 1622024 | tf_op jit(solution)/shard_map/ppermute | solution.py:461
  52.8 14.9 %collective-permute-start.8 = (s16[64,4224]{1,0:T(8,128)(2,1)}, s16[64,4224]{1,0:T(8,128)(2,1)}, u32[]{:S(2)}, u32[]{:S(2)}) collective-permute-start(s16[64,4224]{1,0:T(8,128)(2,1)} %get-tuple-element.53), channel_id=1, source_target_pairs={{0,16},{8,24},{16,0},{24,8},{1,17},{9,25},{17,1},{25,9},{2,18},{10... | collective-permute-start | bytes 1622024 | tf_op jit(solution)/shard_map/ppermute | solution.py:461
  54.3 12.2 %copy-start.4 = (s32[128,16]{0,1:T(8,128)S(1)}, s32[128,16]{0,1:T(8,128)}, u32[]{:S(2)}) copy-start(s32[128,16]{0,1:T(8,128)} %param.9) | copy-start | bytes 24580
  63.9 22.9 %collective-permute-start.13 = (s16[64,4224]{1,0:T(8,128)(2,1)}, s16[64,4224]{1,0:T(8,128)(2,1)}, u32[]{:S(2)}, u32[]{:S(2)}) collective-permute-start(s16[64,4224]{1,0:T(8,128)(2,1)} %get-tuple-element.48), channel_id=1, source_target_pairs={{0,8},{8,0},{16,24},{24,16},{1,9},{9,1},{17,25},{25,17},{2,10},{10... | collective-permute-start | bytes 1622024 | tf_op jit(solution)/shard_map/ppermute | solution.py:461
  65.4 22.3 %collective-permute-start.14 = (s16[64,4224]{1,0:T(8,128)(2,1)}, s16[64,4224]{1,0:T(8,128)(2,1)}, u32[]{:S(2)}, u32[]{:S(2)}) collective-permute-start(s16[64,4224]{1,0:T(8,128)(2,1)} %get-tuple-element.59), channel_id=1, source_target_pairs={{0,16},{8,24},{16,0},{24,8},{1,17},{9,25},{17,1},{25,9},{2,18},{10... | collective-permute-start | bytes 1622024 | tf_op jit(solution)/shard_map/ppermute | solution.py:461
  66.6 10.7 %copy-start.5 = (s32[128]{0:T(128)S(1)}, s32[128]{0:T(128)}, u32[]{:S(2)}) copy-start(s32[128]{0:T(128)} %param.10) | copy-start | bytes 1540
  66.6 10.8 %copy-start.6 = (f32[128]{0:T(128)S(1)}, f32[128]{0:T(128)}, u32[]{:S(2)}) copy-start(f32[128]{0:T(128)} %param.11) | copy-start | bytes 1540
  75.4 0.8 copy-start.2
  76.3 36.6 %collective-permute-start.9 = (s16[64,4224]{1,0:T(8,128)(2,1)}, s16[64,4224]{1,0:T(8,128)(2,1)S(1)}, u32[]{:S(2)}, u32[]{:S(2)}) collective-permute-start(s16[64,4224]{1,0:T(8,128)(2,1)} %get-tuple-element.55), channel_id=1, source_target_pairs={{0,8},{8,0},{16,24},{24,16},{1,9},{9,1},{17,25},{25,17},{2,10},{10... | collective-permute-start | bytes 1622024 | tf_op jit(solution)/shard_map/ppermute | solution.py:461
  77.6 8.1 %copy-start.3 = (s16[64,4224]{1,0:T(8,128)(2,1)S(1)}, s16[64,4224]{1,0:T(8,128)(2,1)}, u32[]{:S(2)}) copy-start(s16[64,4224]{1,0:T(8,128)(2,1)} %copy-done.2) | copy-start | bytes 1622020
  77.7 10.1 %copy-start.1 = (f32[128,8192]{1,0:T(8,128)S(1)}, f32[128,8192]{1,0:T(8,128)}, u32[]{:S(2)}) copy-start(f32[128,8192]{1,0:T(8,128)} %copy-done) | copy-start | bytes 12582916
  84.6 29.5 %collective-permute-start.10 = (s16[64,4224]{1,0:T(8,128)(2,1)S(1)}, s16[64,4224]{1,0:T(8,128)(2,1)S(1)}, u32[]{:S(2)}, u32[]{:S(2)}) collective-permute-start(s16[64,4224]{1,0:T(8,128)(2,1)S(1)} %get-tuple-element.56), channel_id=1, source_target_pairs={{0,8},{8,0},{16,24},{24,16},{1,9},{9,1},{17,25},{25,17},{2,10},{10... | collective-permute-start | bytes 1622024 | tf_op jit(solution)/shard_map/ppermute | solution.py:461
  85.7 28.4 %collective-permute-start.11 = (s16[64,4224]{1,0:T(8,128)(2,1)S(1)}, s16[64,4224]{1,0:T(8,128)(2,1)S(1)}, u32[]{:S(2)}, u32[]{:S(2)}) collective-permute-start(s16[64,4224]{1,0:T(8,128)(2,1)S(1)} %copy-done.3), channel_id=1, source_target_pairs={{0,16},{8,24},{16,0},{24,8},{1,17},{9,25},{17,1},{25,9},{2,18},{10... | collective-permute-start | bytes 1622024 | tf_op jit(solution)/shard_map/ppermute | solution.py:461
  86.8 27.3 %collective-permute-start.12 = (s16[64,4224]{1,0:T(8,128)(2,1)S(1)}, s16[64,4224]{1,0:T(8,128)(2,1)S(1)}, u32[]{:S(2)}, u32[]{:S(2)}) collective-permute-start(s16[64,4224]{1,0:T(8,128)(2,1)S(1)} %get-tuple-element.58), channel_id=1, source_target_pairs={{0,16},{8,24},{16,0},{24,8},{1,17},{9,25},{17,1},{25,9},{2,18},{10... | collective-permute-start | bytes 1622024 | tf_op jit(solution)/shard_map/ppermute | solution.py:461
  111.6 25.8 %collective-permute-start.15 = (bf16[64,8320]{1,0:T(8,128)(2,1)S(1)}, bf16[64,8320]{1,0:T(8,128)(2,1)S(1)}, u32[]{:S(2)}, u32[]{:S(2)}) collective-permute-start(bf16[64,8320]{1,0:T(8,128)(2,1)S(1)} %get-tuple-element.69), channel_id=1, source_target_pairs={{0,16},{8,24},{16,0},{24,8},{1,17},{9,25},{17,1},{25,9},{2,18},{10... | collective-permute-start | bytes 3194888 | tf_op jit(solution)/shard_map/ppermute | solution.py:461
  112.8 25.7 %collective-permute-start.17 = (bf16[64,8320]{1,0:T(8,128)(2,1)S(1)}, bf16[64,8320]{1,0:T(8,128)(2,1)S(1)}, u32[]{:S(2)}, u32[]{:S(2)}) collective-permute-start(bf16[64,8320]{1,0:T(8,128)(2,1)S(1)} %get-tuple-element.69), channel_id=1, source_target_pairs={{0,8},{8,0},{16,24},{24,16},{1,9},{9,1},{17,25},{25,17},{2,10},{10... | collective-permute-start | bytes 3194888 | tf_op jit(solution)/shard_map/ppermute | solution.py:461
  137.5 13.6 %collective-permute-start.16 = (bf16[32,8320]{1,0:T(8,128)(2,1)S(1)}, bf16[32,8320]{1,0:T(8,128)(2,1)S(1)}, u32[]{:S(2)}, u32[]{:S(2)}) collective-permute-start(bf16[32,8320]{1,0:T(8,128)(2,1)S(1)} %slice.33), channel_id=1, source_target_pairs={{0,8},{8,0},{16,24},{24,16},{1,9},{9,1},{17,25},{25,17},{2,10},{10... | collective-permute-start | bytes 1597448 | tf_op jit(solution)/shard_map/ppermute | solution.py:461
  138.6 13.3 %collective-permute-start.18 = (bf16[32,8320]{1,0:T(8,128)(2,1)S(1)}, bf16[32,8320]{1,0:T(8,128)(2,1)S(1)}, u32[]{:S(2)}, u32[]{:S(2)}) collective-permute-start(bf16[32,8320]{1,0:T(8,128)(2,1)S(1)} %slice.34), channel_id=1, source_target_pairs={{0,16},{8,24},{16,0},{24,8},{1,17},{9,25},{17,1},{25,9},{2,18},{10... | collective-permute-start | bytes 1597448 | tf_op jit(solution)/shard_map/ppermute | solution.py:461
  151.9 23.8 %collective-permute-start.19 = (bf16[64,8320]{1,0:T(8,128)(2,1)S(1)}, bf16[64,8320]{1,0:T(8,128)(2,1)S(1)}, u32[]{:S(2)}, u32[]{:S(2)}) collective-permute-start(bf16[64,8320]{1,0:T(8,128)(2,1)S(1)} %get-tuple-element.73), channel_id=1, source_target_pairs={{0,16},{8,24},{16,0},{24,8},{1,17},{9,25},{17,1},{25,9},{2,18},{10... | collective-permute-start | bytes 3194888 | tf_op jit(solution)/shard_map/ppermute | solution.py:461
  153.3 23.5 %collective-permute-start.20 = (bf16[64,8320]{1,0:T(8,128)(2,1)S(1)}, bf16[64,8320]{1,0:T(8,128)(2,1)S(1)}, u32[]{:S(2)}, u32[]{:S(2)}) collective-permute-start(bf16[64,8320]{1,0:T(8,128)(2,1)S(1)} %get-tuple-element.73), channel_id=1, source_target_pairs={{0,8},{8,0},{16,24},{24,16},{1,9},{9,1},{17,25},{25,17},{2,10},{10... | collective-permute-start | bytes 3194888 | tf_op jit(solution)/shard_map/ppermute | solution.py:461
  164.4 14.2 %collective-permute-start.21 = (s16[256,1152]{1,0:T(8,128)(2,1)S(1)}, s16[256,1152]{1,0:T(8,128)(2,1)S(1)}, u32[]{:S(2)}, u32[]{:S(2)}) collective-permute-start(s16[256,1152]{1,0:T(8,128)(2,1)S(1)} %grad_rows.4), channel_id=1, source_target_pairs={{0,1},{1,0},{2,3},{3,2},{4,5},{5,4},{6,7},{7,6},{8,9},{9,8},{10,11... | collective-permute-start | bytes 1769480 | tf_op jit(solution)/shard_map/ppermute | solution.py:529
  176.8 16.5 %collective-permute-start.25 = (bf16[32,8320]{1,0:T(8,128)(2,1)S(1)}, bf16[32,8320]{1,0:T(8,128)(2,1)S(1)}, u32[]{:S(2)}, u32[]{:S(2)}) collective-permute-start(bf16[32,8320]{1,0:T(8,128)(2,1)S(1)} %slice.35), channel_id=1, source_target_pairs={{0,8},{8,0},{16,24},{24,16},{1,9},{9,1},{17,25},{25,17},{2,10},{10... | collective-permute-start | bytes 1597448 | tf_op jit(solution)/shard_map/ppermute | solution.py:461
  177.6 15.7 %collective-permute-start.26 = (bf16[32,8320]{1,0:T(8,128)(2,1)S(1)}, bf16[32,8320]{1,0:T(8,128)(2,1)S(1)}, u32[]{:S(2)}, u32[]{:S(2)}) collective-permute-start(bf16[32,8320]{1,0:T(8,128)(2,1)S(1)} %slice.36), channel_id=1, source_target_pairs={{0,16},{8,24},{16,0},{24,8},{1,17},{9,25},{17,1},{25,9},{2,18},{10... | collective-permute-start | bytes 1597448 | tf_op jit(solution)/shard_map/ppermute | solution.py:461
  179.6 5.8 %collective-permute-start.22 = (s16[64,1152]{1,0:T(8,128)(2,1)S(1)}, s16[64,1152]{1,0:T(8,128)(2,1)S(1)}, u32[]{:S(2)}, u32[]{:S(2)}) collective-permute-start(s16[64,1152]{1,0:T(8,128)(2,1)S(1)} %get-tuple-element.79), channel_id=1, source_target_pairs={{0,2},{1,3},{2,0},{3,1},{4,6},{5,7},{6,4},{7,5},{8,10},{9,11},{10,... | collective-permute-start | bytes 442376 | tf_op jit(solution)/shard_map/ppermute | solution.py:536
  181.1 12.2 %collective-permute-start.23 = (s16[64,1152]{1,0:T(8,128)(2,1)S(1)}, s16[64,1152]{1,0:T(8,128)(2,1)S(1)}, u32[]{:S(2)}, u32[]{:S(2)}) collective-permute-start(s16[64,1152]{1,0:T(8,128)(2,1)S(1)} %get-tuple-element.80), channel_id=1, source_target_pairs={{0,4},{1,5},{2,6},{3,7},{4,0},{5,1},{6,2},{7,3},{8,12},{9,13},{10,... | collective-permute-start | bytes 442376 | tf_op jit(solution)/shard_map/ppermute | solution.py:536
  183.5 9.8 %collective-permute-start.24 = (s16[64,1152]{1,0:T(8,128)(2,1)S(1)}, s16[64,1152]{1,0:T(8,128)(2,1)S(1)}, u32[]{:S(2)}, u32[]{:S(2)}) collective-permute-start(s16[64,1152]{1,0:T(8,128)(2,1)S(1)} %get-tuple-element.81), channel_id=1, source_target_pairs={{0,6},{1,7},{2,4},{3,5},{4,2},{5,3},{6,0},{7,1},{8,14},{9,15},{10,... | collective-permute-start | bytes 442376 | tf_op jit(solution)/shard_map/ppermute | solution.py:536
  203.5 10.2 %collective-permute-start.27 = (s16[256,1152]{1,0:T(8,128)(2,1)S(1)}, s16[256,1152]{1,0:T(8,128)(2,1)S(1)}, u32[]{:S(2)}, u32[]{:S(2)}) collective-permute-start(s16[256,1152]{1,0:T(8,128)(2,1)S(1)} %grad_rows.6), channel_id=1, source_target_pairs={{0,1},{1,0},{2,3},{3,2},{4,5},{5,4},{6,7},{7,6},{8,9},{9,8},{10,11... | collective-permute-start | bytes 1769480 | tf_op jit(solution)/shard_map/ppermute | solution.py:529
  214.8 9.3 %collective-permute-start.28 = (s16[64,1152]{1,0:T(8,128)(2,1)S(1)}, s16[64,1152]{1,0:T(8,128)(2,1)S(1)}, u32[]{:S(2)}, u32[]{:S(2)}) collective-permute-start(s16[64,1152]{1,0:T(8,128)(2,1)S(1)} %get-tuple-element.85), channel_id=1, source_target_pairs={{0,2},{1,3},{2,0},{3,1},{4,6},{5,7},{6,4},{7,5},{8,10},{9,11},{10,... | collective-permute-start | bytes 442376 | tf_op jit(solution)/shard_map/ppermute | solution.py:536
  217.0 13.9 %collective-permute-start.29 = (s16[64,1152]{1,0:T(8,128)(2,1)S(1)}, s16[64,1152]{1,0:T(8,128)(2,1)S(1)}, u32[]{:S(2)}, u32[]{:S(2)}) collective-permute-start(s16[64,1152]{1,0:T(8,128)(2,1)S(1)} %get-tuple-element.86), channel_id=1, source_target_pairs={{0,4},{1,5},{2,6},{3,7},{4,0},{5,1},{6,2},{7,3},{8,12},{9,13},{10,... | collective-permute-start | bytes 442376 | tf_op jit(solution)/shard_map/ppermute | solution.py:536
  217.9 13.1 %collective-permute-start.30 = (s16[64,1152]{1,0:T(8,128)(2,1)S(1)}, s16[64,1152]{1,0:T(8,128)(2,1)S(1)}, u32[]{:S(2)}, u32[]{:S(2)}) collective-permute-start(s16[64,1152]{1,0:T(8,128)(2,1)S(1)} %get-tuple-element.87), channel_id=1, source_target_pairs={{0,6},{1,7},{2,4},{3,5},{4,2},{5,3},{6,0},{7,1},{8,14},{9,15},{10,... | collective-permute-start | bytes 442376 | tf_op jit(solution)/shard_map/ppermute | solution.py:536
  231.3 24.6 %collective-permute-start.31 = (s16[128,1152]{1,0:T(8,128)(2,1)S(1)}, s16[128,1152]{1,0:T(8,128)(2,1)S(1)}, u32[]{:S(2)}, u32[]{:S(2)}) collective-permute-start(s16[128,1152]{1,0:T(8,128)(2,1)S(1)} %pad_add_fusion), channel_id=1, source_target_pairs={{0,0},{1,1},{2,8},{3,9},{4,16},{5,17},{6,24},{7,25},{8,2},{9,3},{1... | collective-permute-start | bytes 884744 | tf_op jit(solution)/shard_map/ppermute | solution.py:547

commit v9 on v7

--- a/solution.py
+++ b/solution.py
@@ -127,35 +127,37 @@
     )(rows_in, head)
 
 
-def near_kernel(width, skip, tiles, x_ref, y_ref, head_ref, by_x_ref, by_y_ref, to_x_ref, to_y_ref, *refs):
-    powers_ref, slots_ref, sems_ref = refs
+def near_kernel(width, skip, tiles, x_ref, y_ref, head_ref, by_x_ref, by_y_ref, *refs):
+    to_x_refs, to_y_refs, (powers_ref, slots_ref, sems_ref) = refs[:2], refs[2:4], refs[4:]
     tile = pl.program_id(0)
     head = Tiles(head_ref, slots_ref, sems_ref, 0, skip, tiles)
     rows = x_ref.shape[0]
-    half = rows // 2
-    columns = to_x_ref.shape[1] - tail
+    columns = tiles * width
     value = dot(jnp.concatenate([x_ref[...], y_ref[...]], axis=0), head.get(tile))
     head.release(tile)
     more_x = decode(by_y_ref, tile, width, columns)
     more_y = decode(by_x_ref, tile, width, columns)
-    for_x = jnp.concatenate([value[:half], value[half:rows] + more_x], axis=0)
-    for_y = jnp.concatenate([value[rows : rows + half] + more_y, value[rows + half :]], axis=0)
-    put(to_x_ref, powers_ref, slice(0, rows), tile, width, columns, for_x)
-    put(to_y_ref, powers_ref, slice(rows, 2 * rows), tile, width, columns, for_y)
-
-
-def near_codes(part, rows_x, rows_y, head, by_x, by_y, width, skip, tiles):
-    depth = head.shape[0]
-    rows = rows_x.shape[0] // 2
+    part, half = rows // 2, rows // 4
+    for p in range(2):
+        for_x, for_y = value[p * part : (p + 1) * part], value[rows + p * part : rows + (p + 1) * part]
+        add = slice(p * half, (p + 1) * half)
+        for_x = jnp.concatenate([for_x[:half], for_x[half:] + more_x[add]], axis=0)
+        for_y = jnp.concatenate([for_y[:half] + more_y[add], for_y[half:]], axis=0)
+        for q, out_ref, out in ((0, to_x_refs[p], for_x), (2, to_y_refs[p], for_y)):
+            kept = slice((p + q) * part, (p + q + 1) * part)
+            put(out_ref, powers_ref, kept, tile, width, columns, out)
+
+
+def near_codes(rows_x, rows_y, head, by_x, by_y, width, skip, tiles):
+    rows, depth = rows_x.shape[0], head.shape[0]
     columns = tiles * width
+    shape = (rows // 2, columns + tail)
     return pl.pallas_call(
         functools.partial(near_kernel, width, skip, tiles),
         grid=(tiles,),
-        in_specs=[pl.BlockSpec((rows, depth), lambda j: (part, 0))] * 2
-        + [head_spec]
-        + [pl.BlockSpec((rows // 2, columns + tail), lambda j: (part, 0))] * 2,
-        out_specs=[constant(rows, columns + tail)] * 2,
-        out_shape=[jax.ShapeDtypeStruct((rows, columns + tail), jnp.int16)] * 2,
+        in_specs=[constant(rows, depth)] * 2 + [head_spec] + [constant(*shape)] * 2,
+        out_specs=[constant(*shape)] * 4,
+        out_shape=[jax.ShapeDtypeStruct(shape, jnp.int16)] * 4,
         scratch_shapes=[pltpu.VMEM((2 * rows, tail), jnp.float32)] + head_scratch(depth, width, tiles),
         compiler_params=compiler_params(),
         cost_estimate=small_cost(),
@@ -478,15 +480,16 @@
         first, second = far_codes(after(rows_far, *waits), head, width, skip, count)
         by_x.append(send(first, to_x))
         by_y.append(send(second, to_y))
+    codes = [
+        near_codes(rows_x, rows_y, head, by_x[c], by_y[c], width, skip, count)
+        for c, (skip, count) in enumerate(column_parts)
+    ]
     halves = []
     for part in range(2):
-        sums_x, sums_y = [], []
-        for c, (skip, count) in enumerate(column_parts):
-            codes_x, codes_y = near_codes(part, rows_x, rows_y, head, by_x[c], by_y[c], width, skip, count)
-            sums_x.append(send(codes_x, to_x))
-            sums_y.append(send(codes_y, to_y))
+        waits = codes[1][:1] if part else []
+        sums_x = [send(after(c[part], *waits), to_x) for c in codes]
+        sums_y = [send(after(c[2 + part], *waits), to_y) for c in codes]
         halves.append((sums_x, sums_y))
-        rows_x = after(rows_x, codes_x, sums_x[0], sums_y[0])
 
     in_list = jnp.arange(list_length)[None, :] < refusal_count[:, None]
     ids = jnp.where(in_list, refusal_ids - shard * vocab_local, -1)

time: 254 us -> 262 us (1.031)
  waiting for transfers between devices: 49.3 us -> 68.2 us
  Pallas kernels: 117 us -> 104 us
  local copies, waits for them, and re-layouts: 6.75 us -> 9.66 us
    ppermute x23, waiting for transfers between devices: 21.8 us -> 41 us  [shards(): send = lambda value, pairs: lax.ppermute(value, 'prompt', pairs)]
    pallas_call x4 -> x2, Pallas kernels: 30.3 us -> 18.3 us  [near_codes(): pl.pallas_call(functools.partial(near_kernel, width, skip, tiles), grid=(...]
    unnamed x27 -> x31, local copies, waits for them, and re-layouts: 5.79 us -> 8.75 us
  transfers between devices with their start and end apart: 33 -> 33, of which waited for: 15 -> 14; matrix products, arithmetic and copies ran while one was open for 1% -> 1% of each run, Pallas kernels for 42% -> 36%
where the time goes in v9:
time: 262 us; the launch traced here: 261 us
  Pallas kernels  104 us (40%)
  waiting for transfers between devices  68.2 us (26%)
  starting transfers between devices  42.2 us (16%)
  blocking collectives  29.1 us (11%)
  local copies, waits for them, and re-layouts  9.66 us (4%)
  other arithmetic  7.42 us (3%)
    ppermute x23, waiting for transfers between devices, shards(): send = lambda value, pairs: lax.ppermute(value, 'prompt', pairs)  41 us
    pallas_call x4, Pallas kernels, back(): pl.pallas_call(functools.partial(back_kernel, columns // width, keeps), g...  40.2 us
    all_gather x2, blocking collectives, shards(): stats = lax.all_gather(stats, 'vocab', axis=0)  29.1 us
    ppermute x23, starting transfers between devices, shards(): send = lambda value, pairs: lax.ppermute(value, 'prompt', pairs)  23.3 us
    pallas_call x2, Pallas kernels, near_codes(): pl.pallas_call(functools.partial(near_kernel, width, skip, tiles), grid=(...  18.3 us
    ppermute x6, waiting for transfers between devices, blocks(): lax.ppermute(c, 'vocab', to)  17.6 us
    pallas_call x2, Pallas kernels, far_codes(): pl.pallas_call(functools.partial(far_kernel, width, skip, tiles), grid=(t...  13.7 us
    pallas_call x2, Pallas kernels, row_stats(): pl.pallas_call(functools.partial(stats_kernel, width, parts), grid=(rows...  12.7 us
  transfers between devices with their start and end apart: 33, of which 14 were waited for; matrix products, arithmetic and copies ran while one was open for 1% of the time, Pallas kernels for 36%

profile of v9, /device:TPU:2, one launch (start us, length us, event | category | flops | bytes accessed | tf_op | source)
XLA Modules:
  0.0 261.5 jit_solution(11708395462851253579)
XLA Ops:
  0.6 2.1 fusion
  2.7 2.2 fusion.2
  5.3 2.1 collective-permute-start.1
  7.4 1.4 collective-permute-start.2
  8.8 11.8 %own_logits.1.refs_0_ = f32[128,8192]{1,0:T(8,128)S(1)} custom-call(bf16[128,2048]{1,0:T(8,128)(2,1)S(1)} %get-tuple-element.97.x_ref, bf16[2048,8192]{1,0:T(8,128)(2,1)} %head_ref.17), custom_call_target="tpu_custom_call" | custom-call | flops 1024 | bytes 1024 | tf_op jit(solution)/shard_map/own_logits/pallas_call | solution.py:178
  20.6 2.0 copy-done.2
  22.6 9.2 %collective-permute-done.2.x_ref = bf16[128,2048]{1,0:T(8,128)(2,1)S(1)} collective-permute-done((bf16[128,2048]{1,0:T(8,128)(2,1)S(1)}, bf16[128,2048]{1,0:T(8,128)(2,1)S(1)}, u32[]{:S(2)}, u32[]{:S(2)}) %collective-permute-start.2) | collective-permute-done | bytes 524320 | tf_op jit(solution)/shard_map/ppermute | solution.py:465
  31.8 6.8 %far_codes.2 = (s16[64,4224]{1,0:T(8,128)(2,1)S(1)}, s16[64,4224]{1,0:T(8,128)(2,1)S(1)}) custom-call(bf16[128,2048]{1,0:T(8,128)(2,1)S(1)} %collective-permute-done.2.x_ref, bf16[2048,8192]{1,0:T(8,128)(2,1)} %head_ref.17), custom_call_target="tpu_custom_call" | custom-call | flops 1024 | bytes 1024 | tf_op jit(solution)/shard_map/far_codes/pallas_call | solution.py:117
  38.6 0.7 collective-permute-start.3
  39.6 6.8 %far_codes.3 = (s16[64,4224]{1,0:T(8,128)(2,1)S(1)}, s16[64,4224]{1,0:T(8,128)(2,1)S(1)}) custom-call(bf16[128,2048]{1,0:T(8,128)(2,1)S(1)} %collective-permute-done.2.x_ref, bf16[2048,8192]{1,0:T(8,128)(2,1)} %head_ref.17), custom_call_target="tpu_custom_call" | custom-call | flops 1024 | bytes 1024 | tf_op jit(solution)/shard_map/far_codes/pallas_call | solution.py:117
  46.4 1.8 collective-permute-start.5
  48.2 1.4 collective-permute-start.6
  49.6 4.3 %collective-permute-done.3.by_x_ref = s16[64,4224]{1,0:T(8,128)(2,1)S(1)} collective-permute-done((s16[64,4224]{1,0:T(8,128)(2,1)S(1)}, s16[64,4224]{1,0:T(8,128)(2,1)S(1)}, u32[]{:S(2)}, u32[]{:S(2)}) %collective-permute-start.3) | collective-permute-done | bytes 540704 | tf_op jit(solution)/shard_map/ppermute | solution.py:465
  53.9 0.6 collective-permute-done.4.by_y_ref
  54.5 9.2 %near_codes.2 = (s16[64,4224]{1,0:T(8,128)(2,1)S(1)}, s16[64,4224]{1,0:T(8,128)(2,1)}, s16[64,4224]{1,0:T(8,128)(2,1)}, s16[64,4224]{1,0:T(8,128)(2,1)S(1)}) custom-call(bf16[128,2176]{1,0:T(8,128)(2,1)S(1)} %collective-permute-done.x_ref, bf16[128,2176]{1,0:T(8,128)(2,1)S(1)} %collective-permute-done.1.y_ref, bf16[2048,8192]{1,0:T(8,128)(2,1)} %head_ref.17, ...), custom_call_target="tpu_custom_call" | custom-call | flops 1024 | bytes 1024 | tf_op jit(solution)/shard_map/near_codes/pallas_call | solution.py:155
  63.7 1.4 collective-permute-start.11
  65.2 0.6 collective-permute-start.13
  65.8 9.1 %near_codes.3 = (s16[64,4224]{1,0:T(8,128)(2,1)}, s16[64,4224]{1,0:T(8,128)(2,1)S(1)}, s16[64,4224]{1,0:T(8,128)(2,1)}, s16[64,4224]{1,0:T(8,128)(2,1)S(1)}) custom-call(bf16[128,2176]{1,0:T(8,128)(2,1)S(1)} %collective-permute-done.x_ref, bf16[128,2176]{1,0:T(8,128)(2,1)S(1)} %collective-permute-done.1.y_ref, bf16[2048,8192]{1,0:T(8,128)(2,1)} %head_ref.17, ...), custom_call_target="tpu_custom_call" | custom-call | flops 1024 | bytes 1024 | tf_op jit(solution)/shard_map/near_codes/pallas_call | solution.py:155
  75.0 0.8 copy-done.6
  75.8 0.8 copy-done.7
  76.6 0.7 collective-permute-start.12
  77.3 1.3 collective-permute-start.14
  78.7 1.4 collective-permute-start.7
  80.2 0.6 collective-permute-start.8
  80.8 0.7 collective-permute-start.9
  81.5 10.5 %collective-permute-done.12.refs_2_ = s16[64,4224]{1,0:T(8,128)(2,1)S(1)} collective-permute-done((s16[64,4224]{1,0:T(8,128)(2,1)}, s16[64,4224]{1,0:T(8,128)(2,1)S(1)}, u32[]{:S(2)}, u32[]{:S(2)}) %collective-permute-start.12) | collective-permute-done | bytes 540704 | tf_op jit(solution)/shard_map/ppermute | solution.py:465
  92.0 1.4 collective-permute-start.10
  93.8 2.2 copy-done.3
  96.0 5.9 %row_stats.2 = (f32[64,8192]{1,0:T(8,128)S(1)}, f32[64,8192]{1,0:T(8,128)S(1)}, f32[64,128]{1,0:T(8,128)S(1)}) custom-call(f32[128,8192]{1,0:T(8,128)S(1)} %copy-done.3, s16[64,4224]{1,0:T(8,128)(2,1)S(1)} %collective-permute-done.11.refs_1_, s16[64,4224]{1,0:T(8,128)(2,1)S(1)} %collective-permute-done.12.refs_2_, ...), custom_call_target="tpu_custom_call" | custom-call | flops 1024 | bytes 1024 | tf_op jit(solution)/shard_map/row_stats/pallas_call | solution.py:241
  101.8 14.6 %all-gather = f32[512,128]{1,0:T(8,128)S(1)} all-gather(f32[64,128]{1,0:T(8,128)S(1)} %get-tuple-element.68), channel_id=2, replica_groups=mesh['prompt'=4,'vocab'=8] {'vocab'}, dimensions={0}, use_global_device_ids=true | all-gather | bytes 294912 | tf_op jit(solution)/shard_map/all_gather | solution.py:517
  116.4 2.2 logit_grads.2
  118.6 0.7 collective-permute-start.15
  119.3 1.0 collective-permute-start.17
  120.3 6.9 %row_stats.3 = (f32[64,8192]{1,0:T(8,128)S(1)}, f32[64,8192]{1,0:T(8,128)S(1)}, f32[64,128]{1,0:T(8,128)S(1)}) custom-call(f32[128,8192]{1,0:T(8,128)S(1)} %copy-done.4, s16[64,4224]{1,0:T(8,128)(2,1)S(1)} %collective-permute-done.7.refs_1_, s16[64,4224]{1,0:T(8,128)(2,1)S(1)} %collective-permute-done.8.refs_2_, ...), custom_call_target="tpu_custom_call" | custom-call | flops 1024 | bytes 1024 | tf_op jit(solution)/shard_map/row_stats/pallas_call | solution.py:241
  127.2 14.5 %all-gather.1 = f32[512,128]{1,0:T(8,128)S(1)} all-gather(f32[64,128]{1,0:T(8,128)S(1)} %get-tuple-element.73), channel_id=3, replica_groups=mesh['prompt'=4,'vocab'=8] {'vocab'}, dimensions={0}, use_global_device_ids=true | all-gather | bytes 294912 | tf_op jit(solution)/shard_map/all_gather | solution.py:517
  141.7 2.2 logit_grads.3
  144.5 0.7 collective-permute-start.16
  145.2 1.5 collective-permute-start.18
  146.9 11.6 %collective-permute-done.16 = bf16[32,8320]{1,0:T(8,128)(2,1)S(1)} collective-permute-done((bf16[32,8320]{1,0:T(8,128)(2,1)S(1)}, bf16[32,8320]{1,0:T(8,128)(2,1)S(1)}, u32[]{:S(2)}, u32[]{:S(2)}) %collective-permute-start.16) | collective-permute-done | bytes 532512 | tf_op jit(solution)/shard_map/ppermute | solution.py:465
  158.5 0.8 collective-permute-done.18
  159.3 1.4 collective-permute-start.19
  160.7 0.6 collective-permute-start.20
  161.6 10.0 %grad_rows.4 = s16[256,1152]{1,0:T(8,128)(2,1)S(1)} custom-call(s32[2]{0:T(128)S(1)} %pad_add_fusion.place_ref, bf16[256,8320]{1,0:T(8,128)(2,1)S(1)} %constant_dynamic-update-slice_fusion.grad_ref.beside_ref, bf16[256,8320]{1,0:T(8,128)(2,1)S(1)} %constant_dynamic-update-slice_fusion.grad_ref.beside_ref, bf16[2048,8192]{1,0:T(8,128)(2,1)} %head_ref.17), custom_call_target="tpu_custom_call" | custom-call | flops 1024 | bytes 1024 | tf_op jit(solution)/shard_map/grad_rows/pallas_call | solution.py:370
  171.7 9.8 %grad_rows.5.keep_ref = f32[256,1152]{1,0:T(8,128)S(1)} custom-call(s32[2]{0:T(128)S(1)} %pad_add_fusion.1.place_ref, bf16[256,8320]{1,0:T(8,128)(2,1)S(1)} %constant_dynamic-update-slice_fusion.grad_ref.beside_ref, bf16[256,8320]{1,0:T(8,128)(2,1)S(1)} %constant_dynamic-update-slice_fusion.grad_ref.beside_ref, bf16[2048,8192]{1,0:T(8,128)(2,1)} %head_ref.17), custom_call_target="tpu_custom_call" | custom-call | flops 1024 | bytes 1024 | tf_op jit(solution)/shard_map/grad_rows/pallas_call | solution.py:370
  181.5 2.5 collective-permute-done.19
  184.0 1.1 collective-permute-done.20
  185.1 0.7 collective-permute-start.26
  186.4 1.1 group_sum.2
  187.5 1.5 collective-permute-start.22
  189.0 2.4 collective-permute-start.23
  192.2 1.3 collective-permute-done.22.refs_0_
  193.5 7.3 %collective-permute-done.23.refs_1_ = s16[64,1152]{1,0:T(8,128)(2,1)S(1)} collective-permute-done((s16[64,1152]{1,0:T(8,128)(2,1)S(1)}, s16[64,1152]{1,0:T(8,128)(2,1)S(1)}, u32[]{:S(2)}, u32[]{:S(2)}) %collective-permute-start.23) | collective-permute-done | bytes 147488 | tf_op jit(solution)/shard_map/ppermute | solution.py:541
  200.9 10.7 %grad_rows.6 = s16[256,1152]{1,0:T(8,128)(2,1)S(1)} custom-call(s32[2]{0:T(128)S(1)} %pad_add_fusion.place_ref, bf16[256,8320]{1,0:T(8,128)(2,1)S(1)} %constant_dynamic-update-slice_fusion.5.grad_ref.beside_ref, bf16[256,8320]{1,0:T(8,128)(2,1)S(1)} %constant_dynamic-update-slice_fusion.5.grad_ref.beside_ref, bf16[2048,8192]{1,0:T(8,128)(2,1)} %head_ref.17), custom_call_target="tpu_custom_call" | custom-call | flops 1024 | bytes 1024 | tf_op jit(solution)/shard_map/grad_rows/pallas_call | solution.py:370
  212.1 4.9 %collective-permute-start.25 = (s16[64,1152]{1,0:T(8,128)(2,1)S(1)}, s16[64,1152]{1,0:T(8,128)(2,1)S(1)}, u32[]{:S(2)}, u32[]{:S(2)}) collective-permute-start(s16[64,1152]{1,0:T(8,128)(2,1)S(1)} %last_sum.2), channel_id=1, source_target_pairs={{0,0},{1,1},{2,8},{3,9},{4,16},{5,17},{6,24},{7,25},{8,2},{9,3},{1... | collective-permute-start | bytes 442376 | tf_op jit(solution)/shard_map/ppermute | solution.py:552
  217.0 2.2 copy-done.1
  219.2 9.7 %grad_rows.7.keep_ref = f32[256,1152]{1,0:T(8,128)S(1)} custom-call(s32[2]{0:T(128)S(1)} %pad_add_fusion.1.place_ref, bf16[256,8320]{1,0:T(8,128)(2,1)S(1)} %copy-done.1, bf16[256,8320]{1,0:T(8,128)(2,1)S(1)} %copy-done.1, bf16[2048,8192]{1,0:T(8,128)(2,1)} %head_ref.17), custom_call_target="tpu_custom_call" | custom-call | flops 1024 | bytes 1024 | tf_op jit(solution)/shard_map/grad_rows/pallas_call | solution.py:370
  229.0 1.0 group_sum.3
  230.1 3.0 %collective-permute-start.30 = (s16[64,1152]{1,0:T(8,128)(2,1)S(1)}, s16[64,1152]{1,0:T(8,128)(2,1)S(1)}, u32[]{:S(2)}, u32[]{:S(2)}) collective-permute-start(s16[64,1152]{1,0:T(8,128)(2,1)S(1)} %get-tuple-element.92), channel_id=1, source_target_pairs={{0,4},{1,5},{2,6},{3,7},{4,0},{5,1},{6,2},{7,3},{8,12},{9,13},{10,... | collective-permute-start | bytes 442376 | tf_op jit(solution)/shard_map/ppermute | solution.py:541
  233.0 1.4 collective-permute-start.31
  235.2 4.0 %collective-permute-done.29.refs_0_ = s16[64,1152]{1,0:T(8,128)(2,1)S(1)} collective-permute-done((s16[64,1152]{1,0:T(8,128)(2,1)S(1)}, s16[64,1152]{1,0:T(8,128)(2,1)S(1)}, u32[]{:S(2)}, u32[]{:S(2)}) %collective-permute-start.29) | collective-permute-done | bytes 147488 | tf_op jit(solution)/shard_map/ppermute | solution.py:541
  239.2 5.0 %collective-permute-done.31.refs_2_ = s16[64,1152]{1,0:T(8,128)(2,1)S(1)} collective-permute-done((s16[64,1152]{1,0:T(8,128)(2,1)S(1)}, s16[64,1152]{1,0:T(8,128)(2,1)S(1)}, u32[]{:S(2)}, u32[]{:S(2)}) %collective-permute-start.31) | collective-permute-done | bytes 147488 | tf_op jit(solution)/shard_map/ppermute | solution.py:541
  244.5 5.0 %collective-permute-start.32 = (s16[64,1152]{1,0:T(8,128)(2,1)S(1)}, s16[64,1152]{1,0:T(8,128)(2,1)S(1)}, u32[]{:S(2)}, u32[]{:S(2)}) collective-permute-start(s16[64,1152]{1,0:T(8,128)(2,1)S(1)} %last_sum.3), channel_id=1, source_target_pairs={{0,0},{1,1},{2,8},{3,9},{4,16},{5,17},{6,24},{7,25},{8,2},{9,3},{1... | collective-permute-start | bytes 442376 | tf_op jit(solution)/shard_map/ppermute | solution.py:552
  249.5 9.7 %collective-permute-done.32 = s16[64,1152]{1,0:T(8,128)(2,1)S(1)} collective-permute-done((s16[64,1152]{1,0:T(8,128)(2,1)S(1)}, s16[64,1152]{1,0:T(8,128)(2,1)S(1)}, u32[]{:S(2)}, u32[]{:S(2)}) %collective-permute-start.32) | collective-permute-done | bytes 147488 | tf_op jit(solution)/shard_map/ppermute | solution.py:552
  259.5 2.0 multiply_subtract_fusion
  (80 shorter events, 5.7 us)
Async XLA Ops:
  5.1 34.4 %collective-permute-start = (bf16[128,2176]{1,0:T(8,128)(2,1)S(1)}, bf16[128,2176]{1,0:T(8,128)(2,1)S(1)}, u32[]{:S(2)}, u32[]{:S(2)}) collective-permute-start(bf16[128,2176]{1,0:T(8,128)(2,1)S(1)} %pad.7), channel_id=1, source_target_pairs={{0,8},{8,0},{16,24},{24,16},{1,9},{9,1},{17,25},{25,17},{2,10},{10... | collective-permute-start | bytes 1671176 | tf_op jit(solution)/shard_map/ppermute | solution.py:465
  5.3 34.3 %collective-permute-start.1 = (bf16[128,2176]{1,0:T(8,128)(2,1)S(1)}, bf16[128,2176]{1,0:T(8,128)(2,1)S(1)}, u32[]{:S(2)}, u32[]{:S(2)}) collective-permute-start(bf16[128,2176]{1,0:T(8,128)(2,1)S(1)} %pad.8), channel_id=1, source_target_pairs={{0,16},{8,24},{16,0},{24,8},{1,17},{9,25},{17,1},{25,9},{2,18},{10... | collective-permute-start | bytes 1671176 | tf_op jit(solution)/shard_map/ppermute | solution.py:465
  7.4 24.4 %collective-permute-start.2 = (bf16[128,2048]{1,0:T(8,128)(2,1)S(1)}, bf16[128,2048]{1,0:T(8,128)(2,1)S(1)}, u32[]{:S(2)}, u32[]{:S(2)}) collective-permute-start(bf16[128,2048]{1,0:T(8,128)(2,1)S(1)} %get-tuple-element.94), channel_id=1, source_target_pairs={{0,24},{8,16},{16,8},{24,0},{1,25},{9,17},{17,9},{25,1},{2,26},{10... | collective-permute-start | bytes 1572872 | tf_op jit(solution)/shard_map/ppermute | solution.py:465
  20.6 2.0 copy-start.2
  38.6 15.3 %collective-permute-start.3 = (s16[64,4224]{1,0:T(8,128)(2,1)S(1)}, s16[64,4224]{1,0:T(8,128)(2,1)S(1)}, u32[]{:S(2)}, u32[]{:S(2)}) collective-permute-start(s16[64,4224]{1,0:T(8,128)(2,1)S(1)} %get-tuple-element.49), channel_id=1, source_target_pairs={{0,8},{8,0},{16,24},{24,16},{1,9},{9,1},{17,25},{25,17},{2,10},{10... | collective-permute-start | bytes 1622024 | tf_op jit(solution)/shard_map/ppermute | solution.py:465
  39.3 15.2 %collective-permute-start.4 = (s16[64,4224]{1,0:T(8,128)(2,1)S(1)}, s16[64,4224]{1,0:T(8,128)(2,1)S(1)}, u32[]{:S(2)}, u32[]{:S(2)}) collective-permute-start(s16[64,4224]{1,0:T(8,128)(2,1)S(1)} %get-tuple-element.50), channel_id=1, source_target_pairs={{0,16},{8,24},{16,0},{24,8},{1,17},{9,25},{17,1},{25,9},{2,18},{10... | collective-permute-start | bytes 1622024 | tf_op jit(solution)/shard_map/ppermute | solution.py:465
  46.4 19.4 %collective-permute-start.5 = (s16[64,4224]{1,0:T(8,128)(2,1)S(1)}, s16[64,4224]{1,0:T(8,128)(2,1)S(1)}, u32[]{:S(2)}, u32[]{:S(2)}) collective-permute-start(s16[64,4224]{1,0:T(8,128)(2,1)S(1)} %get-tuple-element.53), channel_id=1, source_target_pairs={{0,8},{8,0},{16,24},{24,16},{1,9},{9,1},{17,25},{25,17},{2,10},{10... | collective-permute-start | bytes 1622024 | tf_op jit(solution)/shard_map/ppermute | solution.py:465
  48.2 17.6 %collective-permute-start.6 = (s16[64,4224]{1,0:T(8,128)(2,1)S(1)}, s16[64,4224]{1,0:T(8,128)(2,1)S(1)}, u32[]{:S(2)}, u32[]{:S(2)}) collective-permute-start(s16[64,4224]{1,0:T(8,128)(2,1)S(1)} %get-tuple-element.54), channel_id=1, source_target_pairs={{0,16},{8,24},{16,0},{24,8},{1,17},{9,25},{17,1},{25,9},{2,18},{10... | collective-permute-start | bytes 1622024 | tf_op jit(solution)/shard_map/ppermute | solution.py:465
  63.7 11.2 %copy-start.5 = (s16[64,4224]{1,0:T(8,128)(2,1)}, s16[64,4224]{1,0:T(8,128)(2,1)S(1)}, u32[]{:S(2)}) copy-start(s16[64,4224]{1,0:T(8,128)(2,1)S(1)} %get-tuple-element.60) | copy-start | bytes 1622020
  63.7 16.4 %collective-permute-start.11 = (s16[64,4224]{1,0:T(8,128)(2,1)S(1)}, s16[64,4224]{1,0:T(8,128)(2,1)S(1)}, u32[]{:S(2)}, u32[]{:S(2)}) collective-permute-start(s16[64,4224]{1,0:T(8,128)(2,1)S(1)} %get-tuple-element.63), channel_id=1, source_target_pairs={{0,8},{8,0},{16,24},{24,16},{1,9},{9,1},{17,25},{25,17},{2,10},{10... | collective-permute-start | bytes 1622024 | tf_op jit(solution)/shard_map/ppermute | solution.py:465
  65.2 13.5 %copy-start.8 = (s32[128,16]{0,1:T(8,128)S(1)}, s32[128,16]{0,1:T(8,128)}, u32[]{:S(2)}) copy-start(s32[128,16]{0,1:T(8,128)} %param.9) | copy-start | bytes 24580
  65.2 28.2 %copy-start.9 = (s32[128]{0:T(128)S(1)}, s32[128]{0:T(128)}, u32[]{:S(2)}) copy-start(s32[128]{0:T(128)} %param.10) | copy-start | bytes 1540
  65.2 28.3 %copy-start.10 = (f32[128]{0:T(128)S(1)}, f32[128]{0:T(128)}, u32[]{:S(2)}) copy-start(f32[128]{0:T(128)} %param.11) | copy-start | bytes 1540
  65.2 15.6 %collective-permute-start.13 = (s16[64,4224]{1,0:T(8,128)(2,1)}, s16[64,4224]{1,0:T(8,128)(2,1)S(1)}, u32[]{:S(2)}, u32[]{:S(2)}) collective-permute-start(s16[64,4224]{1,0:T(8,128)(2,1)} %get-tuple-element.64), channel_id=1, source_target_pairs={{0,16},{8,24},{16,0},{24,8},{1,17},{9,25},{17,1},{25,9},{2,18},{10... | collective-permute-start | bytes 1622024 | tf_op jit(solution)/shard_map/ppermute | solution.py:465
  75.0 0.8 copy-start.6
  75.8 0.8 copy-start.7
  76.6 15.4 %collective-permute-start.12 = (s16[64,4224]{1,0:T(8,128)(2,1)}, s16[64,4224]{1,0:T(8,128)(2,1)S(1)}, u32[]{:S(2)}, u32[]{:S(2)}) collective-permute-start(s16[64,4224]{1,0:T(8,128)(2,1)} %get-tuple-element.55), channel_id=1, source_target_pairs={{0,8},{8,0},{16,24},{24,16},{1,9},{9,1},{17,25},{25,17},{2,10},{10... | collective-permute-start | bytes 1622024 | tf_op jit(solution)/shard_map/ppermute | solution.py:465
  77.3 16.5 %collective-permute-start.14 = (s16[64,4224]{1,0:T(8,128)(2,1)}, s16[64,4224]{1,0:T(8,128)(2,1)S(1)}, u32[]{:S(2)}, u32[]{:S(2)}) collective-permute-start(s16[64,4224]{1,0:T(8,128)(2,1)} %get-tuple-element.65), channel_id=1, source_target_pairs={{0,16},{8,24},{16,0},{24,8},{1,17},{9,25},{17,1},{25,9},{2,18},{10... | collective-permute-start | bytes 1622024 | tf_op jit(solution)/shard_map/ppermute | solution.py:465
  78.7 40.5 %collective-permute-start.7 = (s16[64,4224]{1,0:T(8,128)(2,1)}, s16[64,4224]{1,0:T(8,128)(2,1)S(1)}, u32[]{:S(2)}, u32[]{:S(2)}) collective-permute-start(s16[64,4224]{1,0:T(8,128)(2,1)} %get-tuple-element.56), channel_id=1, source_target_pairs={{0,8},{8,0},{16,24},{24,16},{1,9},{9,1},{17,25},{25,17},{2,10},{10... | collective-permute-start | bytes 1622024 | tf_op jit(solution)/shard_map/ppermute | solution.py:465
  80.2 40.1 %collective-permute-start.8 = (s16[64,4224]{1,0:T(8,128)(2,1)}, s16[64,4224]{1,0:T(8,128)(2,1)S(1)}, u32[]{:S(2)}, u32[]{:S(2)}) collective-permute-start(s16[64,4224]{1,0:T(8,128)(2,1)} %copy-done.7), channel_id=1, source_target_pairs={{0,8},{8,0},{16,24},{24,16},{1,9},{9,1},{17,25},{25,17},{2,10},{10... | collective-permute-start | bytes 1622024 | tf_op jit(solution)/shard_map/ppermute | solution.py:465
  80.8 39.5 %collective-permute-start.9 = (s16[64,4224]{1,0:T(8,128)(2,1)}, s16[64,4224]{1,0:T(8,128)(2,1)}, u32[]{:S(2)}, u32[]{:S(2)}) collective-permute-start(s16[64,4224]{1,0:T(8,128)(2,1)} %copy-done.5), channel_id=1, source_target_pairs={{0,16},{8,24},{16,0},{24,8},{1,17},{9,25},{17,1},{25,9},{2,18},{10... | collective-permute-start | bytes 1622024 | tf_op jit(solution)/shard_map/ppermute | solution.py:465
  92.0 28.3 %collective-permute-start.10 = (s16[64,4224]{1,0:T(8,128)(2,1)}, s16[64,4224]{1,0:T(8,128)(2,1)}, u32[]{:S(2)}, u32[]{:S(2)}) collective-permute-start(s16[64,4224]{1,0:T(8,128)(2,1)} %copy-done.6), channel_id=1, source_target_pairs={{0,16},{8,24},{16,0},{24,8},{1,17},{9,25},{17,1},{25,9},{2,18},{10... | collective-permute-start | bytes 1622024 | tf_op jit(solution)/shard_map/ppermute | solution.py:465
  93.8 2.2 copy-start.3
  96.0 24.4 %copy-start.4 = (f32[128,8192]{1,0:T(8,128)S(1)}, f32[128,8192]{1,0:T(8,128)}, u32[]{:S(2)}) copy-start(f32[128,8192]{1,0:T(8,128)} %copy-done.2) | copy-start | bytes 12582916
  118.6 25.8 %collective-permute-start.15 = (bf16[64,8320]{1,0:T(8,128)(2,1)S(1)}, bf16[64,8320]{1,0:T(8,128)(2,1)S(1)}, u32[]{:S(2)}, u32[]{:S(2)}) collective-permute-start(bf16[64,8320]{1,0:T(8,128)(2,1)S(1)} %get-tuple-element.75), channel_id=1, source_target_pairs={{0,16},{8,24},{16,0},{24,8},{1,17},{9,25},{17,1},{25,9},{2,18},{10... | collective-permute-start | bytes 3194888 | tf_op jit(solution)/shard_map/ppermute | solution.py:465
  119.3 25.9 %collective-permute-start.17 = (bf16[64,8320]{1,0:T(8,128)(2,1)S(1)}, bf16[64,8320]{1,0:T(8,128)(2,1)S(1)}, u32[]{:S(2)}, u32[]{:S(2)}) collective-permute-start(bf16[64,8320]{1,0:T(8,128)(2,1)S(1)} %get-tuple-element.75), channel_id=1, source_target_pairs={{0,8},{8,0},{16,24},{24,16},{1,9},{9,1},{17,25},{25,17},{2,10},{10... | collective-permute-start | bytes 3194888 | tf_op jit(solution)/shard_map/ppermute | solution.py:465
  144.5 14.0 %collective-permute-start.16 = (bf16[32,8320]{1,0:T(8,128)(2,1)S(1)}, bf16[32,8320]{1,0:T(8,128)(2,1)S(1)}, u32[]{:S(2)}, u32[]{:S(2)}) collective-permute-start(bf16[32,8320]{1,0:T(8,128)(2,1)S(1)} %slice.33), channel_id=1, source_target_pairs={{0,8},{8,0},{16,24},{24,16},{1,9},{9,1},{17,25},{25,17},{2,10},{10... | collective-permute-start | bytes 1597448 | tf_op jit(solution)/shard_map/ppermute | solution.py:465
  145.2 14.1 %collective-permute-start.18 = (bf16[32,8320]{1,0:T(8,128)(2,1)S(1)}, bf16[32,8320]{1,0:T(8,128)(2,1)S(1)}, u32[]{:S(2)}, u32[]{:S(2)}) collective-permute-start(bf16[32,8320]{1,0:T(8,128)(2,1)S(1)} %slice.34), channel_id=1, source_target_pairs={{0,16},{8,24},{16,0},{24,8},{1,17},{9,25},{17,1},{25,9},{2,18},{10... | collective-permute-start | bytes 1597448 | tf_op jit(solution)/shard_map/ppermute | solution.py:465
  159.3 24.6 %collective-permute-start.19 = (bf16[64,8320]{1,0:T(8,128)(2,1)S(1)}, bf16[64,8320]{1,0:T(8,128)(2,1)S(1)}, u32[]{:S(2)}, u32[]{:S(2)}) collective-permute-start(bf16[64,8320]{1,0:T(8,128)(2,1)S(1)} %get-tuple-element.79), channel_id=1, source_target_pairs={{0,16},{8,24},{16,0},{24,8},{1,17},{9,25},{17,1},{25,9},{2,18},{10... | collective-permute-start | bytes 3194888 | tf_op jit(solution)/shard_map/ppermute | solution.py:465
  160.7 24.4 %collective-permute-start.20 = (bf16[64,8320]{1,0:T(8,128)(2,1)S(1)}, bf16[64,8320]{1,0:T(8,128)(2,1)S(1)}, u32[]{:S(2)}, u32[]{:S(2)}) collective-permute-start(bf16[64,8320]{1,0:T(8,128)(2,1)S(1)} %get-tuple-element.79), channel_id=1, source_target_pairs={{0,8},{8,0},{16,24},{24,16},{1,9},{9,1},{17,25},{25,17},{2,10},{10... | collective-permute-start | bytes 3194888 | tf_op jit(solution)/shard_map/ppermute | solution.py:465
  171.6 14.9 %collective-permute-start.21 = (s16[256,1152]{1,0:T(8,128)(2,1)S(1)}, s16[256,1152]{1,0:T(8,128)(2,1)S(1)}, u32[]{:S(2)}, u32[]{:S(2)}) collective-permute-start(s16[256,1152]{1,0:T(8,128)(2,1)S(1)} %grad_rows.4), channel_id=1, source_target_pairs={{0,1},{1,0},{2,3},{3,2},{4,5},{5,4},{6,7},{7,6},{8,9},{9,8},{10,11... | collective-permute-start | bytes 1769480 | tf_op jit(solution)/shard_map/ppermute | solution.py:534
  185.1 15.6 %collective-permute-start.26 = (bf16[32,8320]{1,0:T(8,128)(2,1)S(1)}, bf16[32,8320]{1,0:T(8,128)(2,1)S(1)}, u32[]{:S(2)}, u32[]{:S(2)}) collective-permute-start(bf16[32,8320]{1,0:T(8,128)(2,1)S(1)} %slice.35), channel_id=1, source_target_pairs={{0,8},{8,0},{16,24},{24,16},{1,9},{9,1},{17,25},{25,17},{2,10},{10... | collective-permute-start | bytes 1597448 | tf_op jit(solution)/shard_map/ppermute | solution.py:465
  185.8 15.0 %collective-permute-start.27 = (bf16[32,8320]{1,0:T(8,128)(2,1)S(1)}, bf16[32,8320]{1,0:T(8,128)(2,1)S(1)}, u32[]{:S(2)}, u32[]{:S(2)}) collective-permute-start(bf16[32,8320]{1,0:T(8,128)(2,1)S(1)} %slice.36), channel_id=1, source_target_pairs={{0,16},{8,24},{16,0},{24,8},{1,17},{9,25},{17,1},{25,9},{2,18},{10... | collective-permute-start | bytes 1597448 | tf_op jit(solution)/shard_map/ppermute | solution.py:465
  187.5 6.0 %collective-permute-start.22 = (s16[64,1152]{1,0:T(8,128)(2,1)S(1)}, s16[64,1152]{1,0:T(8,128)(2,1)S(1)}, u32[]{:S(2)}, u32[]{:S(2)}) collective-permute-start(s16[64,1152]{1,0:T(8,128)(2,1)S(1)} %get-tuple-element.85), channel_id=1, source_target_pairs={{0,2},{1,3},{2,0},{3,1},{4,6},{5,7},{6,4},{7,5},{8,10},{9,11},{10,... | collective-permute-start | bytes 442376 | tf_op jit(solution)/shard_map/ppermute | solution.py:541
  189.0 11.8 %collective-permute-start.23 = (s16[64,1152]{1,0:T(8,128)(2,1)S(1)}, s16[64,1152]{1,0:T(8,128)(2,1)S(1)}, u32[]{:S(2)}, u32[]{:S(2)}) collective-permute-start(s16[64,1152]{1,0:T(8,128)(2,1)S(1)} %get-tuple-element.86), channel_id=1, source_target_pairs={{0,4},{1,5},{2,6},{3,7},{4,0},{5,1},{6,2},{7,3},{8,12},{9,13},{10,... | collective-permute-start | bytes 442376 | tf_op jit(solution)/shard_map/ppermute | solution.py:541
  191.4 9.4 %collective-permute-start.24 = (s16[64,1152]{1,0:T(8,128)(2,1)S(1)}, s16[64,1152]{1,0:T(8,128)(2,1)S(1)}, u32[]{:S(2)}, u32[]{:S(2)}) collective-permute-start(s16[64,1152]{1,0:T(8,128)(2,1)S(1)} %get-tuple-element.87), channel_id=1, source_target_pairs={{0,6},{1,7},{2,4},{3,5},{4,2},{5,3},{6,0},{7,1},{8,14},{9,15},{10,... | collective-permute-start | bytes 442376 | tf_op jit(solution)/shard_map/ppermute | solution.py:541
  200.9 10.7 %copy-start = (bf16[256,8320]{1,0:T(8,128)(2,1)}, bf16[256,8320]{1,0:T(8,128)(2,1)S(1)}, u32[]{:S(2)}) copy-start(bf16[256,8320]{1,0:T(8,128)(2,1)S(1)} %constant_dynamic-update-slice_fusion.5.grad_ref.beside_ref) | copy-start | bytes 12779524
  211.6 17.3 %collective-permute-start.28 = (s16[256,1152]{1,0:T(8,128)(2,1)S(1)}, s16[256,1152]{1,0:T(8,128)(2,1)S(1)}, u32[]{:S(2)}, u32[]{:S(2)}) collective-permute-start(s16[256,1152]{1,0:T(8,128)(2,1)S(1)} %grad_rows.6), channel_id=1, source_target_pairs={{0,1},{1,0},{2,3},{3,2},{4,5},{5,4},{6,7},{7,6},{8,9},{9,8},{10,11... | collective-permute-start | bytes 1769480 | tf_op jit(solution)/shard_map/ppermute | solution.py:534
  212.1 37.4 %collective-permute-start.25 = (s16[64,1152]{1,0:T(8,128)(2,1)S(1)}, s16[64,1152]{1,0:T(8,128)(2,1)S(1)}, u32[]{:S(2)}, u32[]{:S(2)}) collective-permute-start(s16[64,1152]{1,0:T(8,128)(2,1)S(1)} %last_sum.2), channel_id=1, source_target_pairs={{0,0},{1,1},{2,8},{3,9},{4,16},{5,17},{6,24},{7,25},{8,2},{9,3},{1... | collective-permute-start | bytes 442376 | tf_op jit(solution)/shard_map/ppermute | solution.py:552
  217.0 2.2 copy-start.1
  219.2 40.3 %dynamic-slice-start = ((f32[8192]{0:T(1024)}, s32[]{:T(128)}), f32[1024]{0:T(1024)S(1)}, s32[]{:S(2)}) async-start(f32[8192]{0:T(1024)} %param.8, s32[]{:T(128)} %select_n.37), calls=%async_computation | async-start | bytes 8704 | tf_op jit(solution)/shard_map/dynamic_slice | solution.py:562
  230.0 9.2 %collective-permute-start.29 = (s16[64,1152]{1,0:T(8,128)(2,1)S(1)}, s16[64,1152]{1,0:T(8,128)(2,1)S(1)}, u32[]{:S(2)}, u32[]{:S(2)}) collective-permute-start(s16[64,1152]{1,0:T(8,128)(2,1)S(1)} %get-tuple-element.91), channel_id=1, source_target_pairs={{0,2},{1,3},{2,0},{3,1},{4,6},{5,7},{6,4},{7,5},{8,10},{9,11},{10,... | collective-permute-start | bytes 442376 | tf_op jit(solution)/shard_map/ppermute | solution.py:541
  230.1 9.1 %collective-permute-start.30 = (s16[64,1152]{1,0:T(8,128)(2,1)S(1)}, s16[64,1152]{1,0:T(8,128)(2,1)S(1)}, u32[]{:S(2)}, u32[]{:S(2)}) collective-permute-start(s16[64,1152]{1,0:T(8,128)(2,1)S(1)} %get-tuple-element.92), channel_id=1, source_target_pairs={{0,4},{1,5},{2,6},{3,7},{4,0},{5,1},{6,2},{7,3},{8,12},{9,13},{10,... | collective-permute-start | bytes 442376 | tf_op jit(solution)/shard_map/ppermute | solution.py:541
  233.0 11.2 %collective-permute-start.31 = (s16[64,1152]{1,0:T(8,128)(2,1)S(1)}, s16[64,1152]{1,0:T(8,128)(2,1)S(1)}, u32[]{:S(2)}, u32[]{:S(2)}) collective-permute-start(s16[64,1152]{1,0:T(8,128)(2,1)S(1)} %get-tuple-element.93), channel_id=1, source_target_pairs={{0,6},{1,7},{2,4},{3,5},{4,2},{5,3},{6,0},{7,1},{8,14},{9,15},{10,... | collective-permute-start | bytes 442376 | tf_op jit(solution)/shard_map/ppermute | solution.py:541
  244.5 14.7 %collective-permute-start.32 = (s16[64,1152]{1,0:T(8,128)(2,1)S(1)}, s16[64,1152]{1,0:T(8,128)(2,1)S(1)}, u32[]{:S(2)}, u32[]{:S(2)}) collective-permute-start(s16[64,1152]{1,0:T(8,128)(2,1)S(1)} %last_sum.3), channel_id=1, source_target_pairs={{0,0},{1,1},{2,8},{3,9},{4,16},{5,17},{6,24},{7,25},{8,2},{9,3},{1... | collective-permute-start | bytes 442376 | tf_op jit(solution)/shard_map/ppermute | solution.py:552

commit v10 on v9

--- a/solution.py
+++ b/solution.py
@@ -49,7 +49,7 @@
 
 
 def compiler_params():
-    return pltpu.CompilerParams(vmem_limit_bytes=28 * megabyte)
+    return pltpu.CompilerParams(vmem_limit_bytes=24 * megabyte)
 
 
 def small_cost():
@@ -60,7 +60,7 @@
 
 
 def head_scratch(rows, width, tiles):
-    slots = min(tiles, 16 * megabyte // (2 * rows * width))
+    slots = min(tiles, 12 * megabyte // (2 * rows * width))
     return [pltpu.VMEM((slots, rows, width), jnp.bfloat16), pltpu.SemaphoreType.DMA((slots,))]
 
 
@@ -112,7 +112,7 @@
 
 
 def far_codes(rows_in, head, width, skip, tiles):
-    rows, depth = rows_in.shape
+    rows, depth = rows_in.shape[0], head.shape[0]
     columns = tiles * width
     return pl.pallas_call(
         functools.partial(far_kernel, width, skip, tiles),
@@ -468,10 +468,10 @@
     inverse_rms = lax.rsqrt(jnp.mean(hidden_f * hidden_f, axis=1, keepdims=True) + epsilon)
     normed = (hidden_f * inverse_rms * gain).astype(jnp.bfloat16)
     columns = lambda p: lax.dynamic_slice_in_dim(normed, p * depth, depth, 1)
-    rows_far = send(columns(me ^ 3), to_far)
-    beside = ((0, 0), (0, tail))
-    rows_x = send(jnp.pad(columns(me ^ 1), beside), to_x)
-    rows_y = send(jnp.pad(columns(me ^ 2), beside), to_y)
+    wider = lambda p, more: jnp.pad(columns(p), ((0, 0), (0, more)))
+    rows_far = send(wider(me ^ 3, 2 * tail), to_far)
+    rows_x = send(wider(me ^ 1, tail), to_x)
+    rows_y = send(wider(me ^ 2, tail), to_y)
     own = own_logits(columns(me), head, width)
     first_tiles = tiles // 2
     column_parts = ((0, first_tiles), (first_tiles, tiles - first_tiles))
@@ -486,7 +486,7 @@
     ]
     halves = []
     for part in range(2):
-        waits = codes[1][:1] if part else []
+        waits = [codes[1][0], sums_x[0], sums_y[0]] if part else []
         sums_x = [send(after(c[part], *waits), to_x) for c in codes]
         sums_y = [send(after(c[2 + part], *waits), to_y) for c in codes]
         halves.append((sums_x, sums_y))

time: 262 us -> 299 us (1.14)
  waiting for transfers between devices: 68.2 us -> 103 us
    ppermute x23, waiting for transfers between devices: 41 us -> 76.1 us  [shards(): send = lambda value, pairs: lax.ppermute(value, 'prompt', pairs)]
    unnamed x31 -> x39, local copies, waits for them, and re-layouts: 8.75 us -> 10.4 us
  transfers between devices with their start and end apart: 33 -> 33, of which waited for: 14 -> 14; matrix products, arithmetic and copies ran while one was open for 1% -> 1% of each run, Pallas kernels for 36% -> 31%
where the time goes in v10:
time: 299 us
  Pallas kernels  104 us (35%)
  waiting for transfers between devices  103 us (34%)
  starting transfers between devices  41.8 us (14%)
  blocking collectives  29.1 us (10%)
  local copies, waits for them, and re-layouts  11.5 us (4%)
  other arithmetic  7.42 us (2%)
    ppermute x23, waiting for transfers between devices, shards(): send = lambda value, pairs: lax.ppermute(value, 'prompt', pairs)  76.1 us
    pallas_call x4, Pallas kernels, back(): pl.pallas_call(functools.partial(back_kernel, columns // width, keeps), g...  40.1 us
    all_gather x2, blocking collectives, shards(): stats = lax.all_gather(stats, 'vocab', axis=0)  29.1 us
    ppermute x23, starting transfers between devices, shards(): send = lambda value, pairs: lax.ppermute(value, 'prompt', pairs)  23.1 us
    pallas_call x2, Pallas kernels, near_codes(): pl.pallas_call(functools.partial(near_kernel, width, skip, tiles), grid=(...  18.3 us
    ppermute x6, waiting for transfers between devices, blocks(): lax.ppermute(c, 'vocab', to)  17.7 us
    pallas_call x2, Pallas kernels, far_codes(): pl.pallas_call(functools.partial(far_kernel, width, skip, tiles), grid=(t...  15.1 us
    pallas_call x1, Pallas kernels, own_logits(): pl.pallas_call(functools.partial(own_kernel, columns // width), grid=(col...  11.8 us
  transfers between devices with their start and end apart: 33, of which 14 were waited for; matrix products, arithmetic and copies ran while one was open for 1% of the time, Pallas kernels for 31%

profile of v10, /device:TPU:2, one launch (start us, length us, event | category | flops | bytes accessed | tf_op | source)
XLA Modules:
  0.0 298.5 jit_solution(8041336551189744173)
XLA Ops:
  0.6 2.1 fusion
  2.7 2.2 fusion.2
  5.2 1.6 collective-permute-start.2
  6.8 1.6 collective-permute-start
  9.0 11.8 %own_logits.1.refs_0_ = f32[128,8192]{1,0:T(8,128)S(1)} custom-call(bf16[128,2048]{1,0:T(8,128)(2,1)S(1)} %get-tuple-element.97.x_ref, bf16[2048,8192]{1,0:T(8,128)(2,1)} %head_ref.17), custom_call_target="tpu_custom_call" | custom-call | flops 1024 | bytes 1024 | tf_op jit(solution)/shard_map/own_logits/pallas_call | solution.py:178
  20.8 2.0 copy-done.2
  22.7 7.1 %far_codes.2 = (s16[64,4224]{1,0:T(8,128)(2,1)S(1)}, s16[64,4224]{1,0:T(8,128)(2,1)S(1)}) custom-call(bf16[128,2304]{1,0:T(8,128)(2,1)S(1)} %collective-permute-done.2.x_ref, bf16[2048,8192]{1,0:T(8,128)(2,1)} %head_ref.17), custom_call_target="tpu_custom_call" | custom-call | flops 1024 | bytes 1024 | tf_op jit(solution)/shard_map/far_codes/pallas_call | solution.py:117
  30.0 2.0 collective-permute-start.4
  31.9 2.5 collective-permute-done.x_ref
  34.4 8.0 %far_codes.3 = (s16[64,4224]{1,0:T(8,128)(2,1)}, s16[64,4224]{1,0:T(8,128)(2,1)}) custom-call(bf16[128,2304]{1,0:T(8,128)(2,1)S(1)} %collective-permute-done.2.x_ref, bf16[2048,8192]{1,0:T(8,128)(2,1)} %head_ref.17), custom_call_target="tpu_custom_call" | custom-call | flops 1024 | bytes 1024 | tf_op jit(solution)/shard_map/far_codes/pallas_call | solution.py:117
  42.4 0.6 collective-permute-start.5
  43.4 2.2 collective-permute-done.3.by_x_ref
  45.6 9.1 %near_codes.2 = (s16[64,4224]{1,0:T(8,128)(2,1)}, s16[64,4224]{1,0:T(8,128)(2,1)S(1)}, s16[64,4224]{1,0:T(8,128)(2,1)}, s16[64,4224]{1,0:T(8,128)(2,1)S(1)}) custom-call(bf16[128,2176]{1,0:T(8,128)(2,1)S(1)} %collective-permute-done.x_ref, bf16[128,2176]{1,0:T(8,128)(2,1)S(1)} %collective-permute-done.1.y_ref, bf16[2048,8192]{1,0:T(8,128)(2,1)} %head_ref.17, ...), custom_call_target="tpu_custom_call" | custom-call | flops 1024 | bytes 1024 | tf_op jit(solution)/shard_map/near_codes/pallas_call | solution.py:155
  54.7 0.8 copy-done.5
  55.5 0.8 copy-done.7
  56.4 0.7 collective-permute-start.7
  57.6 9.2 %near_codes.3 = (s16[64,4224]{1,0:T(8,128)(2,1)}, s16[64,4224]{1,0:T(8,128)(2,1)S(1)}, s16[64,4224]{1,0:T(8,128)(2,1)}, s16[64,4224]{1,0:T(8,128)(2,1)S(1)}) custom-call(bf16[128,2176]{1,0:T(8,128)(2,1)S(1)} %collective-permute-done.x_ref, bf16[128,2176]{1,0:T(8,128)(2,1)S(1)} %collective-permute-done.1.y_ref, bf16[2048,8192]{1,0:T(8,128)(2,1)} %head_ref.17, ...), custom_call_target="tpu_custom_call" | custom-call | flops 1024 | bytes 1024 | tf_op jit(solution)/shard_map/near_codes/pallas_call | solution.py:155
  66.9 0.8 copy-done.8
  67.7 0.9 copy-done.10
  68.5 1.9 collective-permute-start.13
  70.4 1.0 collective-permute-start.14
  71.5 0.8 collective-permute-start.9
  72.6 11.3 %collective-permute-done.13.refs_2_ = s16[64,4224]{1,0:T(8,128)(2,1)S(1)} collective-permute-done((s16[64,4224]{1,0:T(8,128)(2,1)}, s16[64,4224]{1,0:T(8,128)(2,1)S(1)}, u32[]{:S(2)}, u32[]{:S(2)}) %collective-permute-start.13) | collective-permute-done | bytes 540704 | tf_op jit(solution)/shard_map/ppermute | solution.py:465
  84.0 2.2 copy-done.3
  86.2 5.9 %row_stats.2 = (f32[64,8192]{1,0:T(8,128)S(1)}, f32[64,8192]{1,0:T(8,128)S(1)}, f32[64,128]{1,0:T(8,128)S(1)}) custom-call(f32[128,8192]{1,0:T(8,128)S(1)} %copy-done.3, s16[64,4224]{1,0:T(8,128)(2,1)S(1)} %collective-permute-done.7.refs_1_, s16[64,4224]{1,0:T(8,128)(2,1)S(1)} %collective-permute-done.13.refs_2_, ...), custom_call_target="tpu_custom_call" | custom-call | flops 1024 | bytes 1024 | tf_op jit(solution)/shard_map/row_stats/pallas_call | solution.py:241
  92.0 14.6 %all-gather = f32[512,128]{1,0:T(8,128)S(1)} all-gather(f32[64,128]{1,0:T(8,128)S(1)} %get-tuple-element.68), channel_id=2, replica_groups=mesh['prompt'=4,'vocab'=8] {'vocab'}, dimensions={0}, use_global_device_ids=true | all-gather | bytes 294912 | tf_op jit(solution)/shard_map/all_gather | solution.py:517
  106.6 2.2 logit_grads.2
  108.8 1.4 collective-permute-start.15
  110.2 1.5 collective-permute-start.17
  112.2 0.7 collective-permute-start.11
  112.9 1.3 collective-permute-start.12
  114.3 32.9 %collective-permute-done.10.refs_2_ = s16[64,4224]{1,0:T(8,128)(2,1)S(1)} collective-permute-done((s16[64,4224]{1,0:T(8,128)(2,1)S(1)}, s16[64,4224]{1,0:T(8,128)(2,1)S(1)}, u32[]{:S(2)}, u32[]{:S(2)}) %collective-permute-start.10) | collective-permute-done | bytes 540704 | tf_op jit(solution)/shard_map/ppermute | solution.py:465
  147.3 10.5 %collective-permute-done.12.refs_4_ = s16[64,4224]{1,0:T(8,128)(2,1)S(1)} collective-permute-done((s16[64,4224]{1,0:T(8,128)(2,1)S(1)}, s16[64,4224]{1,0:T(8,128)(2,1)S(1)}, u32[]{:S(2)}, u32[]{:S(2)}) %collective-permute-start.12) | collective-permute-done | bytes 540704 | tf_op jit(solution)/shard_map/ppermute | solution.py:465
  157.8 5.9 %row_stats.3 = (f32[64,8192]{1,0:T(8,128)S(1)}, f32[64,8192]{1,0:T(8,128)S(1)}, f32[64,128]{1,0:T(8,128)S(1)}) custom-call(f32[128,8192]{1,0:T(8,128)S(1)} %copy-done.4, s16[64,4224]{1,0:T(8,128)(2,1)S(1)} %collective-permute-done.9.refs_1_, s16[64,4224]{1,0:T(8,128)(2,1)S(1)} %collective-permute-done.10.refs_2_, ...), custom_call_target="tpu_custom_call" | custom-call | flops 1024 | bytes 1024 | tf_op jit(solution)/shard_map/row_stats/pallas_call | solution.py:241
  163.7 14.5 %all-gather.1 = f32[512,128]{1,0:T(8,128)S(1)} all-gather(f32[64,128]{1,0:T(8,128)S(1)} %get-tuple-element.73), channel_id=3, replica_groups=mesh['prompt'=4,'vocab'=8] {'vocab'}, dimensions={0}, use_global_device_ids=true | all-gather | bytes 294912 | tf_op jit(solution)/shard_map/all_gather | solution.py:517
  178.2 2.2 logit_grads.3
  180.5 1.9 collective-permute-start.16
  182.4 1.0 collective-permute-start.18
  183.7 11.3 %collective-permute-done.16 = bf16[32,8320]{1,0:T(8,128)(2,1)S(1)} collective-permute-done((bf16[32,8320]{1,0:T(8,128)(2,1)S(1)}, bf16[32,8320]{1,0:T(8,128)(2,1)S(1)}, u32[]{:S(2)}, u32[]{:S(2)}) %collective-permute-start.16) | collective-permute-done | bytes 532512 | tf_op jit(solution)/shard_map/ppermute | solution.py:465
  195.0 1.6 collective-permute-done.18
  196.6 1.0 collective-permute-start.19
  198.2 10.0 %grad_rows.4 = s16[256,1152]{1,0:T(8,128)(2,1)S(1)} custom-call(s32[2]{0:T(128)S(1)} %pad_add_fusion.place_ref, bf16[256,8320]{1,0:T(8,128)(2,1)S(1)} %constant_dynamic-update-slice_fusion.grad_ref.beside_ref, bf16[256,8320]{1,0:T(8,128)(2,1)S(1)} %constant_dynamic-update-slice_fusion.grad_ref.beside_ref, bf16[2048,8192]{1,0:T(8,128)(2,1)} %head_ref.17), custom_call_target="tpu_custom_call" | custom-call | flops 1024 | bytes 1024 | tf_op jit(solution)/shard_map/grad_rows/pallas_call | solution.py:370
  208.4 9.7 %grad_rows.5.keep_ref = f32[256,1152]{1,0:T(8,128)S(1)} custom-call(s32[2]{0:T(128)S(1)} %pad_add_fusion.1.place_ref, bf16[256,8320]{1,0:T(8,128)(2,1)S(1)} %constant_dynamic-update-slice_fusion.grad_ref.beside_ref, bf16[256,8320]{1,0:T(8,128)(2,1)S(1)} %constant_dynamic-update-slice_fusion.grad_ref.beside_ref, bf16[2048,8192]{1,0:T(8,128)(2,1)} %head_ref.17), custom_call_target="tpu_custom_call" | custom-call | flops 1024 | bytes 1024 | tf_op jit(solution)/shard_map/grad_rows/pallas_call | solution.py:370
  218.1 3.1 %collective-permute-done.19 = bf16[64,8320]{1,0:T(8,128)(2,1)S(1)} collective-permute-done((bf16[64,8320]{1,0:T(8,128)(2,1)S(1)}, bf16[64,8320]{1,0:T(8,128)(2,1)S(1)}, u32[]{:S(2)}, u32[]{:S(2)}) %collective-permute-start.19) | collective-permute-done | bytes 1064992 | tf_op jit(solution)/shard_map/ppermute | solution.py:465
  221.2 0.6 collective-permute-done.20
  221.9 0.6 collective-permute-start.26
  222.5 1.0 collective-permute-start.27
  223.5 1.1 group_sum.2
  224.6 1.6 collective-permute-start.22
  226.2 2.4 collective-permute-start.23
  229.3 1.1 collective-permute-done.22.refs_0_
  230.5 7.7 %collective-permute-done.23.refs_1_ = s16[64,1152]{1,0:T(8,128)(2,1)S(1)} collective-permute-done((s16[64,1152]{1,0:T(8,128)(2,1)S(1)}, s16[64,1152]{1,0:T(8,128)(2,1)S(1)}, u32[]{:S(2)}, u32[]{:S(2)}) %collective-permute-start.23) | collective-permute-done | bytes 147488 | tf_op jit(solution)/shard_map/ppermute | solution.py:541
  238.3 10.7 %grad_rows.6 = s16[256,1152]{1,0:T(8,128)(2,1)S(1)} custom-call(s32[2]{0:T(128)S(1)} %pad_add_fusion.place_ref, bf16[256,8320]{1,0:T(8,128)(2,1)S(1)} %constant_dynamic-update-slice_fusion.5.grad_ref.beside_ref, bf16[256,8320]{1,0:T(8,128)(2,1)S(1)} %constant_dynamic-update-slice_fusion.5.grad_ref.beside_ref, bf16[2048,8192]{1,0:T(8,128)(2,1)} %head_ref.17), custom_call_target="tpu_custom_call" | custom-call | flops 1024 | bytes 1024 | tf_op jit(solution)/shard_map/grad_rows/pallas_call | solution.py:370
  249.5 4.8 %collective-permute-start.25 = (s16[64,1152]{1,0:T(8,128)(2,1)S(1)}, s16[64,1152]{1,0:T(8,128)(2,1)S(1)}, u32[]{:S(2)}, u32[]{:S(2)}) collective-permute-start(s16[64,1152]{1,0:T(8,128)(2,1)S(1)} %last_sum.2), channel_id=1, source_target_pairs={{0,0},{1,1},{2,8},{3,9},{4,16},{5,17},{6,24},{7,25},{8,2},{9,3},{1... | collective-permute-start | bytes 442376 | tf_op jit(solution)/shard_map/ppermute | solution.py:552
  254.3 2.2 copy-done.1
  256.5 9.7 %grad_rows.7.keep_ref = f32[256,1152]{1,0:T(8,128)S(1)} custom-call(s32[2]{0:T(128)S(1)} %pad_add_fusion.1.place_ref, bf16[256,8320]{1,0:T(8,128)(2,1)S(1)} %copy-done.1, bf16[256,8320]{1,0:T(8,128)(2,1)S(1)} %copy-done.1, bf16[2048,8192]{1,0:T(8,128)(2,1)} %head_ref.17), custom_call_target="tpu_custom_call" | custom-call | flops 1024 | bytes 1024 | tf_op jit(solution)/shard_map/grad_rows/pallas_call | solution.py:370
  266.3 1.0 group_sum.3
  267.4 2.4 collective-permute-start.30
  269.8 2.0 collective-permute-start.31
  272.5 3.8 %collective-permute-done.29.refs_0_ = s16[64,1152]{1,0:T(8,128)(2,1)S(1)} collective-permute-done((s16[64,1152]{1,0:T(8,128)(2,1)S(1)}, s16[64,1152]{1,0:T(8,128)(2,1)S(1)}, u32[]{:S(2)}, u32[]{:S(2)}) %collective-permute-start.29) | collective-permute-done | bytes 147488 | tf_op jit(solution)/shard_map/ppermute | solution.py:541
  276.3 5.1 %collective-permute-done.30.refs_1_ = s16[64,1152]{1,0:T(8,128)(2,1)S(1)} collective-permute-done((s16[64,1152]{1,0:T(8,128)(2,1)S(1)}, s16[64,1152]{1,0:T(8,128)(2,1)S(1)}, u32[]{:S(2)}, u32[]{:S(2)}) %collective-permute-start.30) | collective-permute-done | bytes 147488 | tf_op jit(solution)/shard_map/ppermute | solution.py:541
  281.7 4.8 %collective-permute-start.32 = (s16[64,1152]{1,0:T(8,128)(2,1)S(1)}, s16[64,1152]{1,0:T(8,128)(2,1)S(1)}, u32[]{:S(2)}, u32[]{:S(2)}) collective-permute-start(s16[64,1152]{1,0:T(8,128)(2,1)S(1)} %last_sum.3), channel_id=1, source_target_pairs={{0,0},{1,1},{2,8},{3,9},{4,16},{5,17},{6,24},{7,25},{8,2},{9,3},{1... | collective-permute-start | bytes 442376 | tf_op jit(solution)/shard_map/ppermute | solution.py:552
  286.6 9.7 %collective-permute-done.32 = s16[64,1152]{1,0:T(8,128)(2,1)S(1)} collective-permute-done((s16[64,1152]{1,0:T(8,128)(2,1)S(1)}, s16[64,1152]{1,0:T(8,128)(2,1)S(1)}, u32[]{:S(2)}, u32[]{:S(2)}) %collective-permute-start.32) | collective-permute-done | bytes 147488 | tf_op jit(solution)/shard_map/ppermute | solution.py:552
  296.6 2.0 multiply_subtract_fusion
  (89 shorter events, 7.0 us)
Async XLA Ops:
  5.2 17.5 %collective-permute-start.2 = (bf16[128,2304]{1,0:T(8,128)(2,1)S(1)}, bf16[128,2304]{1,0:T(8,128)(2,1)S(1)}, u32[]{:S(2)}, u32[]{:S(2)}) collective-permute-start(bf16[128,2304]{1,0:T(8,128)(2,1)S(1)} %pad.13), channel_id=1, source_target_pairs={{0,24},{8,16},{16,8},{24,0},{1,25},{9,17},{17,9},{25,1},{2,26},{10... | collective-permute-start | bytes 1769480 | tf_op jit(solution)/shard_map/ppermute | solution.py:465
  6.8 27.6 %collective-permute-start = (bf16[128,2176]{1,0:T(8,128)(2,1)S(1)}, bf16[128,2176]{1,0:T(8,128)(2,1)S(1)}, u32[]{:S(2)}, u32[]{:S(2)}) collective-permute-start(bf16[128,2176]{1,0:T(8,128)(2,1)S(1)} %pad.11), channel_id=1, source_target_pairs={{0,8},{8,0},{16,24},{24,16},{1,9},{9,1},{17,25},{25,17},{2,10},{10... | collective-permute-start | bytes 1671176 | tf_op jit(solution)/shard_map/ppermute | solution.py:465
  8.4 26.0 %collective-permute-start.1 = (bf16[128,2176]{1,0:T(8,128)(2,1)S(1)}, bf16[128,2176]{1,0:T(8,128)(2,1)S(1)}, u32[]{:S(2)}, u32[]{:S(2)}) collective-permute-start(bf16[128,2176]{1,0:T(8,128)(2,1)S(1)} %pad.12), channel_id=1, source_target_pairs={{0,16},{8,24},{16,0},{24,8},{1,17},{9,25},{17,1},{25,9},{2,18},{10... | collective-permute-start | bytes 1671176 | tf_op jit(solution)/shard_map/ppermute | solution.py:465
  20.8 2.0 copy-start.2
  29.8 15.8 %collective-permute-start.3 = (s16[64,4224]{1,0:T(8,128)(2,1)S(1)}, s16[64,4224]{1,0:T(8,128)(2,1)S(1)}, u32[]{:S(2)}, u32[]{:S(2)}) collective-permute-start(s16[64,4224]{1,0:T(8,128)(2,1)S(1)} %get-tuple-element.49), channel_id=1, source_target_pairs={{0,8},{8,0},{16,24},{24,16},{1,9},{9,1},{17,25},{25,17},{2,10},{10... | collective-permute-start | bytes 1622024 | tf_op jit(solution)/shard_map/ppermute | solution.py:465
  30.0 15.6 %collective-permute-start.4 = (s16[64,4224]{1,0:T(8,128)(2,1)S(1)}, s16[64,4224]{1,0:T(8,128)(2,1)S(1)}, u32[]{:S(2)}, u32[]{:S(2)}) collective-permute-start(s16[64,4224]{1,0:T(8,128)(2,1)S(1)} %get-tuple-element.50), channel_id=1, source_target_pairs={{0,16},{8,24},{16,0},{24,8},{1,17},{9,25},{17,1},{25,9},{2,18},{10... | collective-permute-start | bytes 1622024 | tf_op jit(solution)/shard_map/ppermute | solution.py:465
  42.4 15.2 %collective-permute-start.5 = (s16[64,4224]{1,0:T(8,128)(2,1)}, s16[64,4224]{1,0:T(8,128)(2,1)S(1)}, u32[]{:S(2)}, u32[]{:S(2)}) collective-permute-start(s16[64,4224]{1,0:T(8,128)(2,1)} %get-tuple-element.53), channel_id=1, source_target_pairs={{0,8},{8,0},{16,24},{24,16},{1,9},{9,1},{17,25},{25,17},{2,10},{10... | collective-permute-start | bytes 1622024 | tf_op jit(solution)/shard_map/ppermute | solution.py:465
  43.0 14.6 %collective-permute-start.6 = (s16[64,4224]{1,0:T(8,128)(2,1)}, s16[64,4224]{1,0:T(8,128)(2,1)S(1)}, u32[]{:S(2)}, u32[]{:S(2)}) collective-permute-start(s16[64,4224]{1,0:T(8,128)(2,1)} %get-tuple-element.54), channel_id=1, source_target_pairs={{0,16},{8,24},{16,0},{24,8},{1,17},{9,25},{17,1},{25,9},{2,18},{10... | collective-permute-start | bytes 1622024 | tf_op jit(solution)/shard_map/ppermute | solution.py:465
  54.7 0.8 copy-start.5
  55.5 0.8 copy-start.7
  56.4 15.1 %collective-permute-start.7 = (s16[64,4224]{1,0:T(8,128)(2,1)}, s16[64,4224]{1,0:T(8,128)(2,1)S(1)}, u32[]{:S(2)}, u32[]{:S(2)}) collective-permute-start(s16[64,4224]{1,0:T(8,128)(2,1)} %get-tuple-element.56), channel_id=1, source_target_pairs={{0,8},{8,0},{16,24},{24,16},{1,9},{9,1},{17,25},{25,17},{2,10},{10... | collective-permute-start | bytes 1622024 | tf_op jit(solution)/shard_map/ppermute | solution.py:465
  57.1 14.4 %collective-permute-start.8 = (s16[64,4224]{1,0:T(8,128)(2,1)}, s16[64,4224]{1,0:T(8,128)(2,1)S(1)}, u32[]{:S(2)}, u32[]{:S(2)}) collective-permute-start(s16[64,4224]{1,0:T(8,128)(2,1)} %get-tuple-element.57), channel_id=1, source_target_pairs={{0,16},{8,24},{16,0},{24,8},{1,17},{9,25},{17,1},{25,9},{2,18},{10... | collective-permute-start | bytes 1622024 | tf_op jit(solution)/shard_map/ppermute | solution.py:465
  57.6 13.8 %copy-start.12 = (s32[128,16]{0,1:T(8,128)S(1)}, s32[128,16]{0,1:T(8,128)}, u32[]{:S(2)}) copy-start(s32[128,16]{0,1:T(8,128)} %param.9) | copy-start | bytes 24580
  57.6 14.7 %copy-start.13 = (s32[128]{0:T(128)S(1)}, s32[128]{0:T(128)}, u32[]{:S(2)}) copy-start(s32[128]{0:T(128)} %param.10) | copy-start | bytes 1540
  57.6 14.8 %copy-start.14 = (f32[128]{0:T(128)S(1)}, f32[128]{0:T(128)}, u32[]{:S(2)}) copy-start(f32[128]{0:T(128)} %param.11) | copy-start | bytes 1540
  66.8 0.8 copy-start.8
  67.7 0.9 copy-start.10
  68.5 15.4 %collective-permute-start.13 = (s16[64,4224]{1,0:T(8,128)(2,1)}, s16[64,4224]{1,0:T(8,128)(2,1)S(1)}, u32[]{:S(2)}, u32[]{:S(2)}) collective-permute-start(s16[64,4224]{1,0:T(8,128)(2,1)} %get-tuple-element.55), channel_id=1, source_target_pairs={{0,8},{8,0},{16,24},{24,16},{1,9},{9,1},{17,25},{25,17},{2,10},{10... | collective-permute-start | bytes 1622024 | tf_op jit(solution)/shard_map/ppermute | solution.py:465
  70.4 13.6 %collective-permute-start.14 = (s16[64,4224]{1,0:T(8,128)(2,1)}, s16[64,4224]{1,0:T(8,128)(2,1)S(1)}, u32[]{:S(2)}, u32[]{:S(2)}) collective-permute-start(s16[64,4224]{1,0:T(8,128)(2,1)} %get-tuple-element.65), channel_id=1, source_target_pairs={{0,16},{8,24},{16,0},{24,8},{1,17},{9,25},{17,1},{25,9},{2,18},{10... | collective-permute-start | bytes 1622024 | tf_op jit(solution)/shard_map/ppermute | solution.py:465
  71.5 41.5 %collective-permute-start.9 = (s16[64,4224]{1,0:T(8,128)(2,1)}, s16[64,4224]{1,0:T(8,128)(2,1)S(1)}, u32[]{:S(2)}, u32[]{:S(2)}) collective-permute-start(s16[64,4224]{1,0:T(8,128)(2,1)} %copy-done.7), channel_id=1, source_target_pairs={{0,8},{8,0},{16,24},{24,16},{1,9},{9,1},{17,25},{25,17},{2,10},{10... | collective-permute-start | bytes 1622024 | tf_op jit(solution)/shard_map/ppermute | solution.py:465
  84.0 2.2 copy-start.3
  86.1 25.6 %copy-start.11 = (s16[64,4224]{1,0:T(8,128)(2,1)S(1)}, s16[64,4224]{1,0:T(8,128)(2,1)}, u32[]{:S(2)}) copy-start(s16[64,4224]{1,0:T(8,128)(2,1)} %copy-done.10) | copy-start | bytes 1622020
  86.1 26.1 %copy-start.6 = (s16[64,4224]{1,0:T(8,128)(2,1)S(1)}, s16[64,4224]{1,0:T(8,128)(2,1)}, u32[]{:S(2)}) copy-start(s16[64,4224]{1,0:T(8,128)(2,1)} %copy-done.5) | copy-start | bytes 1622020
  86.1 26.8 %copy-start.9 = (s16[64,4224]{1,0:T(8,128)(2,1)S(1)}, s16[64,4224]{1,0:T(8,128)(2,1)}, u32[]{:S(2)}) copy-start(s16[64,4224]{1,0:T(8,128)(2,1)} %copy-done.8) | copy-start | bytes 1622020
  92.0 65.8 %copy-start.4 = (f32[128,8192]{1,0:T(8,128)S(1)}, f32[128,8192]{1,0:T(8,128)}, u32[]{:S(2)}) copy-start(f32[128,8192]{1,0:T(8,128)} %copy-done.2) | copy-start | bytes 12582916
  108.8 71.6 %collective-permute-start.15 = (bf16[64,8320]{1,0:T(8,128)(2,1)S(1)}, bf16[64,8320]{1,0:T(8,128)(2,1)S(1)}, u32[]{:S(2)}, u32[]{:S(2)}) collective-permute-start(bf16[64,8320]{1,0:T(8,128)(2,1)S(1)} %get-tuple-element.75), channel_id=1, source_target_pairs={{0,16},{8,24},{16,0},{24,8},{1,17},{9,25},{17,1},{25,9},{2,18},{10... | collective-permute-start | bytes 3194888 | tf_op jit(solution)/shard_map/ppermute | solution.py:465
  110.2 72.2 %collective-permute-start.17 = (bf16[64,8320]{1,0:T(8,128)(2,1)S(1)}, bf16[64,8320]{1,0:T(8,128)(2,1)S(1)}, u32[]{:S(2)}, u32[]{:S(2)}) collective-permute-start(bf16[64,8320]{1,0:T(8,128)(2,1)S(1)} %get-tuple-element.75), channel_id=1, source_target_pairs={{0,8},{8,0},{16,24},{24,16},{1,9},{9,1},{17,25},{25,17},{2,10},{10... | collective-permute-start | bytes 3194888 | tf_op jit(solution)/shard_map/ppermute | solution.py:465
  111.7 35.6 %collective-permute-start.10 = (s16[64,4224]{1,0:T(8,128)(2,1)S(1)}, s16[64,4224]{1,0:T(8,128)(2,1)S(1)}, u32[]{:S(2)}, u32[]{:S(2)}) collective-permute-start(s16[64,4224]{1,0:T(8,128)(2,1)S(1)} %copy-done.11), channel_id=1, source_target_pairs={{0,8},{8,0},{16,24},{24,16},{1,9},{9,1},{17,25},{25,17},{2,10},{10... | collective-permute-start | bytes 1622024 | tf_op jit(solution)/shard_map/ppermute | solution.py:465
  112.2 35.0 %collective-permute-start.11 = (s16[64,4224]{1,0:T(8,128)(2,1)S(1)}, s16[64,4224]{1,0:T(8,128)(2,1)S(1)}, u32[]{:S(2)}, u32[]{:S(2)}) collective-permute-start(s16[64,4224]{1,0:T(8,128)(2,1)S(1)} %copy-done.6), channel_id=1, source_target_pairs={{0,16},{8,24},{16,0},{24,8},{1,17},{9,25},{17,1},{25,9},{2,18},{10... | collective-permute-start | bytes 1622024 | tf_op jit(solution)/shard_map/ppermute | solution.py:465
  112.9 44.9 %collective-permute-start.12 = (s16[64,4224]{1,0:T(8,128)(2,1)S(1)}, s16[64,4224]{1,0:T(8,128)(2,1)S(1)}, u32[]{:S(2)}, u32[]{:S(2)}) collective-permute-start(s16[64,4224]{1,0:T(8,128)(2,1)S(1)} %copy-done.9), channel_id=1, source_target_pairs={{0,16},{8,24},{16,0},{24,8},{1,17},{9,25},{17,1},{25,9},{2,18},{10... | collective-permute-start | bytes 1622024 | tf_op jit(solution)/shard_map/ppermute | solution.py:465
  180.5 14.5 %collective-permute-start.16 = (bf16[32,8320]{1,0:T(8,128)(2,1)S(1)}, bf16[32,8320]{1,0:T(8,128)(2,1)S(1)}, u32[]{:S(2)}, u32[]{:S(2)}) collective-permute-start(bf16[32,8320]{1,0:T(8,128)(2,1)S(1)} %slice.33), channel_id=1, source_target_pairs={{0,8},{8,0},{16,24},{24,16},{1,9},{9,1},{17,25},{25,17},{2,10},{10... | collective-permute-start | bytes 1597448 | tf_op jit(solution)/shard_map/ppermute | solution.py:465
  182.4 14.1 %collective-permute-start.18 = (bf16[32,8320]{1,0:T(8,128)(2,1)S(1)}, bf16[32,8320]{1,0:T(8,128)(2,1)S(1)}, u32[]{:S(2)}, u32[]{:S(2)}) collective-permute-start(bf16[32,8320]{1,0:T(8,128)(2,1)S(1)} %slice.34), channel_id=1, source_target_pairs={{0,16},{8,24},{16,0},{24,8},{1,17},{9,25},{17,1},{25,9},{2,18},{10... | collective-permute-start | bytes 1597448 | tf_op jit(solution)/shard_map/ppermute | solution.py:465
  196.6 24.6 %collective-permute-start.19 = (bf16[64,8320]{1,0:T(8,128)(2,1)S(1)}, bf16[64,8320]{1,0:T(8,128)(2,1)S(1)}, u32[]{:S(2)}, u32[]{:S(2)}) collective-permute-start(bf16[64,8320]{1,0:T(8,128)(2,1)S(1)} %get-tuple-element.79), channel_id=1, source_target_pairs={{0,16},{8,24},{16,0},{24,8},{1,17},{9,25},{17,1},{25,9},{2,18},{10... | collective-permute-start | bytes 3194888 | tf_op jit(solution)/shard_map/ppermute | solution.py:465
  197.5 24.4 %collective-permute-start.20 = (bf16[64,8320]{1,0:T(8,128)(2,1)S(1)}, bf16[64,8320]{1,0:T(8,128)(2,1)S(1)}, u32[]{:S(2)}, u32[]{:S(2)}) collective-permute-start(bf16[64,8320]{1,0:T(8,128)(2,1)S(1)} %get-tuple-element.79), channel_id=1, source_target_pairs={{0,8},{8,0},{16,24},{24,16},{1,9},{9,1},{17,25},{25,17},{2,10},{10... | collective-permute-start | bytes 3194888 | tf_op jit(solution)/shard_map/ppermute | solution.py:465
  208.2 15.3 %collective-permute-start.21 = (s16[256,1152]{1,0:T(8,128)(2,1)S(1)}, s16[256,1152]{1,0:T(8,128)(2,1)S(1)}, u32[]{:S(2)}, u32[]{:S(2)}) collective-permute-start(s16[256,1152]{1,0:T(8,128)(2,1)S(1)} %grad_rows.4), channel_id=1, source_target_pairs={{0,1},{1,0},{2,3},{3,2},{4,5},{5,4},{6,7},{7,6},{8,9},{9,8},{10,11... | collective-permute-start | bytes 1769480 | tf_op jit(solution)/shard_map/ppermute | solution.py:534
  221.9 16.2 %collective-permute-start.26 = (bf16[32,8320]{1,0:T(8,128)(2,1)S(1)}, bf16[32,8320]{1,0:T(8,128)(2,1)S(1)}, u32[]{:S(2)}, u32[]{:S(2)}) collective-permute-start(bf16[32,8320]{1,0:T(8,128)(2,1)S(1)} %slice.35), channel_id=1, source_target_pairs={{0,8},{8,0},{16,24},{24,16},{1,9},{9,1},{17,25},{25,17},{2,10},{10... | collective-permute-start | bytes 1597448 | tf_op jit(solution)/shard_map/ppermute | solution.py:465
  222.5 15.7 %collective-permute-start.27 = (bf16[32,8320]{1,0:T(8,128)(2,1)S(1)}, bf16[32,8320]{1,0:T(8,128)(2,1)S(1)}, u32[]{:S(2)}, u32[]{:S(2)}) collective-permute-start(bf16[32,8320]{1,0:T(8,128)(2,1)S(1)} %slice.36), channel_id=1, source_target_pairs={{0,16},{8,24},{16,0},{24,8},{1,17},{9,25},{17,1},{25,9},{2,18},{10... | collective-permute-start | bytes 1597448 | tf_op jit(solution)/shard_map/ppermute | solution.py:465
  224.6 5.9 %collective-permute-start.22 = (s16[64,1152]{1,0:T(8,128)(2,1)S(1)}, s16[64,1152]{1,0:T(8,128)(2,1)S(1)}, u32[]{:S(2)}, u32[]{:S(2)}) collective-permute-start(s16[64,1152]{1,0:T(8,128)(2,1)S(1)} %get-tuple-element.85), channel_id=1, source_target_pairs={{0,2},{1,3},{2,0},{3,1},{4,6},{5,7},{6,4},{7,5},{8,10},{9,11},{10,... | collective-permute-start | bytes 442376 | tf_op jit(solution)/shard_map/ppermute | solution.py:541
  226.2 11.9 %collective-permute-start.23 = (s16[64,1152]{1,0:T(8,128)(2,1)S(1)}, s16[64,1152]{1,0:T(8,128)(2,1)S(1)}, u32[]{:S(2)}, u32[]{:S(2)}) collective-permute-start(s16[64,1152]{1,0:T(8,128)(2,1)S(1)} %get-tuple-element.86), channel_id=1, source_target_pairs={{0,4},{1,5},{2,6},{3,7},{4,0},{5,1},{6,2},{7,3},{8,12},{9,13},{10,... | collective-permute-start | bytes 442376 | tf_op jit(solution)/shard_map/ppermute | solution.py:541
  228.6 9.5 %collective-permute-start.24 = (s16[64,1152]{1,0:T(8,128)(2,1)S(1)}, s16[64,1152]{1,0:T(8,128)(2,1)S(1)}, u32[]{:S(2)}, u32[]{:S(2)}) collective-permute-start(s16[64,1152]{1,0:T(8,128)(2,1)S(1)} %get-tuple-element.87), channel_id=1, source_target_pairs={{0,6},{1,7},{2,4},{3,5},{4,2},{5,3},{6,0},{7,1},{8,14},{9,15},{10,... | collective-permute-start | bytes 442376 | tf_op jit(solution)/shard_map/ppermute | solution.py:541
  238.2 10.7 %copy-start = (bf16[256,8320]{1,0:T(8,128)(2,1)}, bf16[256,8320]{1,0:T(8,128)(2,1)S(1)}, u32[]{:S(2)}) copy-start(bf16[256,8320]{1,0:T(8,128)(2,1)S(1)} %constant_dynamic-update-slice_fusion.5.grad_ref.beside_ref) | copy-start | bytes 12779524
  249.0 17.3 %collective-permute-start.28 = (s16[256,1152]{1,0:T(8,128)(2,1)S(1)}, s16[256,1152]{1,0:T(8,128)(2,1)S(1)}, u32[]{:S(2)}, u32[]{:S(2)}) collective-permute-start(s16[256,1152]{1,0:T(8,128)(2,1)S(1)} %grad_rows.6), channel_id=1, source_target_pairs={{0,1},{1,0},{2,3},{3,2},{4,5},{5,4},{6,7},{7,6},{8,9},{9,8},{10,11... | collective-permute-start | bytes 1769480 | tf_op jit(solution)/shard_map/ppermute | solution.py:534
  249.5 37.1 %collective-permute-start.25 = (s16[64,1152]{1,0:T(8,128)(2,1)S(1)}, s16[64,1152]{1,0:T(8,128)(2,1)S(1)}, u32[]{:S(2)}, u32[]{:S(2)}) collective-permute-start(s16[64,1152]{1,0:T(8,128)(2,1)S(1)} %last_sum.2), channel_id=1, source_target_pairs={{0,0},{1,1},{2,8},{3,9},{4,16},{5,17},{6,24},{7,25},{8,2},{9,3},{1... | collective-permute-start | bytes 442376 | tf_op jit(solution)/shard_map/ppermute | solution.py:552
  254.3 2.2 copy-start.1
  256.5 40.0 %dynamic-slice-start = ((f32[8192]{0:T(1024)}, s32[]{:T(128)}), f32[1024]{0:T(1024)S(1)}, s32[]{:S(2)}) async-start(f32[8192]{0:T(1024)} %param.8, s32[]{:T(128)} %select_n.37), calls=%async_computation | async-start | bytes 8704 | tf_op jit(solution)/shard_map/dynamic_slice | solution.py:562
  267.3 9.0 %collective-permute-start.29 = (s16[64,1152]{1,0:T(8,128)(2,1)S(1)}, s16[64,1152]{1,0:T(8,128)(2,1)S(1)}, u32[]{:S(2)}, u32[]{:S(2)}) collective-permute-start(s16[64,1152]{1,0:T(8,128)(2,1)S(1)} %get-tuple-element.91), channel_id=1, source_target_pairs={{0,2},{1,3},{2,0},{3,1},{4,6},{5,7},{6,4},{7,5},{8,10},{9,11},{10,... | collective-permute-start | bytes 442376 | tf_op jit(solution)/shard_map/ppermute | solution.py:541
  267.4 14.0 %collective-permute-start.30 = (s16[64,1152]{1,0:T(8,128)(2,1)S(1)}, s16[64,1152]{1,0:T(8,128)(2,1)S(1)}, u32[]{:S(2)}, u32[]{:S(2)}) collective-permute-start(s16[64,1152]{1,0:T(8,128)(2,1)S(1)} %get-tuple-element.92), channel_id=1, source_target_pairs={{0,4},{1,5},{2,6},{3,7},{4,0},{5,1},{6,2},{7,3},{8,12},{9,13},{10,... | collective-permute-start | bytes 442376 | tf_op jit(solution)/shard_map/ppermute | solution.py:541
  269.8 11.7 %collective-permute-start.31 = (s16[64,1152]{1,0:T(8,128)(2,1)S(1)}, s16[64,1152]{1,0:T(8,128)(2,1)S(1)}, u32[]{:S(2)}, u32[]{:S(2)}) collective-permute-start(s16[64,1152]{1,0:T(8,128)(2,1)S(1)} %get-tuple-element.93), channel_id=1, source_target_pairs={{0,6},{1,7},{2,4},{3,5},{4,2},{5,3},{6,0},{7,1},{8,14},{9,15},{10,... | collective-permute-start | bytes 442376 | tf_op jit(solution)/shard_map/ppermute | solution.py:541
  281.7 14.5 %collective-permute-start.32 = (s16[64,1152]{1,0:T(8,128)(2,1)S(1)}, s16[64,1152]{1,0:T(8,128)(2,1)S(1)}, u32[]{:S(2)}, u32[]{:S(2)}) collective-permute-start(s16[64,1152]{1,0:T(8,128)(2,1)S(1)} %last_sum.3), channel_id=1, source_target_pairs={{0,0},{1,1},{2,8},{3,9},{4,16},{5,17},{6,24},{7,25},{8,2},{9,3},{1... | collective-permute-start | bytes 442376 | tf_op jit(solution)/shard_map/ppermute | solution.py:552

commit v11 on v7

--- a/solution.py
+++ b/solution.py
@@ -178,7 +178,7 @@
         grid=(columns // width,),
         in_specs=[constant(rows, depth), head_spec],
         out_specs=pl.BlockSpec((rows, width), lambda j: (0, j)),
-        out_shape=jax.ShapeDtypeStruct((rows, columns), jnp.float32),
+        out_shape=pltpu.HBM((rows, columns), jnp.float32),
         scratch_shapes=head_scratch(depth, width, columns // width),
         compiler_params=compiler_params(),
         cost_estimate=small_cost(),

time: 254 us -> 254 us (level)
    unnamed x27 -> x25, local copies, waits for them, and re-layouts: 5.79 us -> 3.82 us
  transfers between devices with their start and end apart: 33 -> 33, of which waited for: 15 -> 15; matrix products, arithmetic and copies ran while one was open for 1% -> 1% of each run, Pallas kernels for 42% -> 43%
where the time goes in v11:
time: 254 us
  Pallas kernels  119 us (47%)
  waiting for transfers between devices  49.2 us (19%)
  starting transfers between devices  43.4 us (17%)
  blocking collectives  29.1 us (11%)
  other arithmetic  7.42 us (3%)
  local copies, waits for them, and re-layouts  4.77 us (2%)
    pallas_call x4, Pallas kernels, back(): pl.pallas_call(functools.partial(back_kernel, columns // width, keeps), g...  40.2 us
    pallas_call x4, Pallas kernels, near_codes(): pl.pallas_call(functools.partial(near_kernel, width, skip, tiles), grid=(...  30.2 us
    all_gather x2, blocking collectives, shards(): stats = lax.all_gather(stats, 'vocab', axis=0)  29.1 us
    ppermute x23, starting transfers between devices, shards(): send = lambda value, pairs: lax.ppermute(value, 'prompt', pairs)  24.7 us
    ppermute x23, waiting for transfers between devices, shards(): send = lambda value, pairs: lax.ppermute(value, 'prompt', pairs)  21.8 us
    ppermute x6, waiting for transfers between devices, blocks(): lax.ppermute(c, 'vocab', to)  17.7 us
    pallas_call x2, Pallas kernels, far_codes(): pl.pallas_call(functools.partial(far_kernel, width, skip, tiles), grid=(t...  14.6 us
    pallas_call x1, Pallas kernels, own_logits(): pl.pallas_call(functools.partial(own_kernel, columns // width), grid=(col...  13.7 us
  transfers between devices with their start and end apart: 33, of which 15 were waited for; matrix products, arithmetic and copies ran while one was open for 1% of the time, Pallas kernels for 43%

profile of v11, /device:TPU:2, one launch (start us, length us, event | category | flops | bytes accessed | tf_op | source)
XLA Modules:
  0.0 253.6 jit_solution(10564647342208452284)
XLA Ops:
  0.6 2.1 fusion
  2.7 2.2 fusion.2
  5.1 1.6 collective-permute-start.2
  6.7 1.6 collective-permute-start
  8.9 13.7 %own_logits.1.refs_0_ = f32[128,8192]{1,0:T(8,128)} custom-call(bf16[128,2048]{1,0:T(8,128)(2,1)S(1)} %get-tuple-element.91.x_ref, bf16[2048,8192]{1,0:T(8,128)(2,1)} %head_ref.21), custom_call_target="tpu_custom_call" | custom-call | flops 1024 | bytes 1024 | tf_op jit(solution)/shard_map/own_logits/pallas_call | solution.py:176
  22.6 6.8 %far_codes.3 = (s16[64,4224]{1,0:T(8,128)(2,1)S(1)}, s16[64,4224]{1,0:T(8,128)(2,1)S(1)}) custom-call(bf16[128,2048]{1,0:T(8,128)(2,1)S(1)} %collective-permute-done.2.x_ref, bf16[2048,8192]{1,0:T(8,128)(2,1)} %head_ref.21), custom_call_target="tpu_custom_call" | custom-call | flops 1024 | bytes 1024 | tf_op jit(solution)/shard_map/far_codes/pallas_call | solution.py:117
  29.6 2.0 collective-permute-start.6
  31.6 0.8 collective-permute-done.x_ref
  32.4 7.8 %far_codes.2 = (s16[64,4224]{1,0:T(8,128)(2,1)}, s16[64,4224]{1,0:T(8,128)(2,1)}) custom-call(bf16[128,2048]{1,0:T(8,128)(2,1)S(1)} %collective-permute-done.2.x_ref, bf16[2048,8192]{1,0:T(8,128)(2,1)} %head_ref.21), custom_call_target="tpu_custom_call" | custom-call | flops 1024 | bytes 1024 | tf_op jit(solution)/shard_map/far_codes/pallas_call | solution.py:117
  40.2 0.8 collective-permute-start.3
  41.0 0.6 collective-permute-start.4
  41.6 2.7 %collective-permute-done.5.by_x_ref = s16[64,4224]{1,0:T(8,128)(2,1)S(1)} collective-permute-done((s16[64,4224]{1,0:T(8,128)(2,1)S(1)}, s16[64,4224]{1,0:T(8,128)(2,1)S(1)}, u32[]{:S(2)}, u32[]{:S(2)}) %collective-permute-start.5) | collective-permute-done | bytes 540704 | tf_op jit(solution)/shard_map/ppermute | solution.py:463
  44.3 7.8 %near_codes.5 = (s16[64,4224]{1,0:T(8,128)(2,1)}, s16[64,4224]{1,0:T(8,128)(2,1)}) custom-call(bf16[128,2176]{1,0:T(8,128)(2,1)S(1)} %collective-permute-done.x_ref, bf16[128,2176]{1,0:T(8,128)(2,1)S(1)} %collective-permute-done.1.y_ref, bf16[2048,8192]{1,0:T(8,128)(2,1)} %head_ref.21, s16[64,4224]{1,0:T(8,128)(2,1)S(1)} %collective-permute-done.5.by_x_ref, ...), custom_call_target="tpu_custom_call" | custom-call | flops 1024 | bytes 1024 | tf_op jit(solution)/shard_map/near_codes/pallas_call | solution.py:151
  52.7 1.4 collective-permute-start.8
  54.2 1.8 collective-permute-done.3.by_x_ref
  56.1 7.8 %near_codes.4 = (s16[64,4224]{1,0:T(8,128)(2,1)}, s16[64,4224]{1,0:T(8,128)(2,1)}) custom-call(bf16[128,2176]{1,0:T(8,128)(2,1)S(1)} %collective-permute-done.x_ref, bf16[128,2176]{1,0:T(8,128)(2,1)S(1)} %collective-permute-done.1.y_ref, bf16[2048,8192]{1,0:T(8,128)(2,1)} %head_ref.21, s16[64,4224]{1,0:T(8,128)(2,1)S(1)} %collective-permute-done.3.by_x_ref, ...), custom_call_target="tpu_custom_call" | custom-call | flops 1024 | bytes 1024 | tf_op jit(solution)/shard_map/near_codes/pallas_call | solution.py:151
  63.9 1.4 collective-permute-start.13
  65.3 1.2 collective-permute-start.14
  66.6 1.2 collective-permute-done.7.refs_1_
  67.8 7.6 %near_codes.6 = (s16[64,4224]{1,0:T(8,128)(2,1)}, s16[64,4224]{1,0:T(8,128)(2,1)S(1)}) custom-call(bf16[128,2176]{1,0:T(8,128)(2,1)S(1)} %collective-permute-done.x_ref, bf16[128,2176]{1,0:T(8,128)(2,1)S(1)} %collective-permute-done.1.y_ref, bf16[2048,8192]{1,0:T(8,128)(2,1)} %head_ref.21, s16[64,4224]{1,0:T(8,128)(2,1)S(1)} %collective-permute-done.5.by_x_ref, ...), custom_call_target="tpu_custom_call" | custom-call | flops 1024 | bytes 1024 | tf_op jit(solution)/shard_map/near_codes/pallas_call | solution.py:151
  75.4 0.8 copy-done.3
  76.3 0.9 collective-permute-start.9
  77.6 7.0 %near_codes.7 = (s16[64,4224]{1,0:T(8,128)(2,1)S(1)}, s16[64,4224]{1,0:T(8,128)(2,1)S(1)}) custom-call(bf16[128,2176]{1,0:T(8,128)(2,1)S(1)} %collective-permute-done.x_ref, bf16[128,2176]{1,0:T(8,128)(2,1)S(1)} %collective-permute-done.1.y_ref, bf16[2048,8192]{1,0:T(8,128)(2,1)} %head_ref.21, s16[64,4224]{1,0:T(8,128)(2,1)S(1)} %collective-permute-done.3.by_x_ref, ...), custom_call_target="tpu_custom_call" | custom-call | flops 1024 | bytes 1024 | tf_op jit(solution)/shard_map/near_codes/pallas_call | solution.py:151
  84.6 1.2 collective-permute-start.10
  85.7 1.2 collective-permute-start.11
  87.0 0.8 collective-permute-start.12
  87.8 7.0 %row_stats.2 = (f32[64,8192]{1,0:T(8,128)S(1)}, f32[64,8192]{1,0:T(8,128)S(1)}, f32[64,128]{1,0:T(8,128)S(1)}) custom-call(f32[128,8192]{1,0:T(8,128)S(1)} %copy-done.2, s16[64,4224]{1,0:T(8,128)(2,1)} %collective-permute-done.7.refs_1_, s16[64,4224]{1,0:T(8,128)(2,1)} %collective-permute-done.13.refs_2_, s16[64,4224]{1,0:T(8,128)(2,1)} %collective-permute-done.8.refs_3_, ...), custom_call_target="tpu_custom_call" | custom-call | flops 1024 | bytes 1024 | tf_op jit(solution)/shard_map/row_stats/pallas_call | solution.py:239
  94.7 14.7 %all-gather = f32[512,128]{1,0:T(8,128)S(1)} all-gather(f32[64,128]{1,0:T(8,128)S(1)} %get-tuple-element.62), channel_id=2, replica_groups=mesh['prompt'=4,'vocab'=8] {'vocab'}, dimensions={0}, use_global_device_ids=true | all-gather | bytes 294912 | tf_op jit(solution)/shard_map/all_gather | solution.py:514
  109.5 2.2 logit_grads.2
  111.6 1.3 collective-permute-start.15
  112.9 1.0 collective-permute-start.17
  114.0 5.9 %row_stats.3 = (f32[64,8192]{1,0:T(8,128)S(1)}, f32[64,8192]{1,0:T(8,128)S(1)}, f32[64,128]{1,0:T(8,128)S(1)}) custom-call(f32[128,8192]{1,0:T(8,128)S(1)} %copy-done.2, s16[64,4224]{1,0:T(8,128)(2,1)S(1)} %collective-permute-done.9.refs_1_, s16[64,4224]{1,0:T(8,128)(2,1)S(1)} %collective-permute-done.10.refs_2_, ...), custom_call_target="tpu_custom_call" | custom-call | flops 1024 | bytes 1024 | tf_op jit(solution)/shard_map/row_stats/pallas_call | solution.py:239
  119.9 14.3 %all-gather.1 = f32[512,128]{1,0:T(8,128)S(1)} all-gather(f32[64,128]{1,0:T(8,128)S(1)} %get-tuple-element.67), channel_id=3, replica_groups=mesh['prompt'=4,'vocab'=8] {'vocab'}, dimensions={0}, use_global_device_ids=true | all-gather | bytes 294912 | tf_op jit(solution)/shard_map/all_gather | solution.py:514
  134.2 2.2 logit_grads.3
  136.4 1.1 collective-permute-done.15
  137.5 1.0 collective-permute-start.16
  138.5 1.4 collective-permute-start.18
  140.2 10.9 %collective-permute-done.16 = bf16[32,8320]{1,0:T(8,128)(2,1)S(1)} collective-permute-done((bf16[32,8320]{1,0:T(8,128)(2,1)S(1)}, bf16[32,8320]{1,0:T(8,128)(2,1)S(1)}, u32[]{:S(2)}, u32[]{:S(2)}) %collective-permute-start.16) | collective-permute-done | bytes 532512 | tf_op jit(solution)/shard_map/ppermute | solution.py:463
  151.1 0.8 collective-permute-done.18
  151.9 1.3 collective-permute-start.19
  153.2 1.0 collective-permute-start.20
  154.4 10.0 %grad_rows.4 = s16[256,1152]{1,0:T(8,128)(2,1)S(1)} custom-call(s32[2]{0:T(128)S(1)} %pad_add_fusion.place_ref, bf16[256,8320]{1,0:T(8,128)(2,1)S(1)} %constant_dynamic-update-slice_fusion.grad_ref.beside_ref, bf16[256,8320]{1,0:T(8,128)(2,1)S(1)} %constant_dynamic-update-slice_fusion.grad_ref.beside_ref, bf16[2048,8192]{1,0:T(8,128)(2,1)} %head_ref.21), custom_call_target="tpu_custom_call" | custom-call | flops 1024 | bytes 1024 | tf_op jit(solution)/shard_map/grad_rows/pallas_call | solution.py:368
  164.5 9.8 %grad_rows.5.keep_ref = f32[256,1152]{1,0:T(8,128)S(1)} custom-call(s32[2]{0:T(128)S(1)} %pad_add_fusion.1.place_ref, bf16[256,8320]{1,0:T(8,128)(2,1)S(1)} %constant_dynamic-update-slice_fusion.grad_ref.beside_ref, bf16[256,8320]{1,0:T(8,128)(2,1)S(1)} %constant_dynamic-update-slice_fusion.grad_ref.beside_ref, bf16[2048,8192]{1,0:T(8,128)(2,1)} %head_ref.21), custom_call_target="tpu_custom_call" | custom-call | flops 1024 | bytes 1024 | tf_op jit(solution)/shard_map/grad_rows/pallas_call | solution.py:368
  174.3 1.3 collective-permute-done.19
  175.7 1.0 collective-permute-done.20
  176.7 1.1 collective-permute-start.26
  177.8 0.8 collective-permute-start.27
  178.6 1.1 group_sum.2
  179.6 1.5 collective-permute-start.22
  181.2 2.4 collective-permute-start.23
  184.3 1.1 collective-permute-done.22.refs_0_
  185.5 7.5 %collective-permute-done.23.refs_1_ = s16[64,1152]{1,0:T(8,128)(2,1)S(1)} collective-permute-done((s16[64,1152]{1,0:T(8,128)(2,1)S(1)}, s16[64,1152]{1,0:T(8,128)(2,1)S(1)}, u32[]{:S(2)}, u32[]{:S(2)}) %collective-permute-start.23) | collective-permute-done | bytes 147488 | tf_op jit(solution)/shard_map/ppermute | solution.py:538
  193.1 10.7 %grad_rows.6 = s16[256,1152]{1,0:T(8,128)(2,1)S(1)} custom-call(s32[2]{0:T(128)S(1)} %pad_add_fusion.place_ref, bf16[256,8320]{1,0:T(8,128)(2,1)S(1)} %constant_dynamic-update-slice_fusion.5.grad_ref.beside_ref, bf16[256,8320]{1,0:T(8,128)(2,1)S(1)} %constant_dynamic-update-slice_fusion.5.grad_ref.beside_ref, bf16[2048,8192]{1,0:T(8,128)(2,1)} %head_ref.21), custom_call_target="tpu_custom_call" | custom-call | flops 1024 | bytes 1024 | tf_op jit(solution)/shard_map/grad_rows/pallas_call | solution.py:368
  204.4 4.6 %collective-permute-start.25 = (s16[64,1152]{1,0:T(8,128)(2,1)S(1)}, s16[64,1152]{1,0:T(8,128)(2,1)S(1)}, u32[]{:S(2)}, u32[]{:S(2)}) collective-permute-start(s16[64,1152]{1,0:T(8,128)(2,1)S(1)} %last_sum.2), channel_id=1, source_target_pairs={{0,0},{1,1},{2,8},{3,9},{4,16},{5,17},{6,24},{7,25},{8,2},{9,3},{1... | collective-permute-start | bytes 442376 | tf_op jit(solution)/shard_map/ppermute | solution.py:549
  209.0 2.2 copy-done.1
  211.2 9.7 %grad_rows.7.keep_ref = f32[256,1152]{1,0:T(8,128)S(1)} custom-call(s32[2]{0:T(128)S(1)} %pad_add_fusion.1.place_ref, bf16[256,8320]{1,0:T(8,128)(2,1)S(1)} %copy-done.1, bf16[256,8320]{1,0:T(8,128)(2,1)S(1)} %copy-done.1, bf16[2048,8192]{1,0:T(8,128)(2,1)} %head_ref.21), custom_call_target="tpu_custom_call" | custom-call | flops 1024 | bytes 1024 | tf_op jit(solution)/shard_map/grad_rows/pallas_call | solution.py:368
  220.9 1.1 group_sum.3
  222.1 3.1 %collective-permute-start.30 = (s16[64,1152]{1,0:T(8,128)(2,1)S(1)}, s16[64,1152]{1,0:T(8,128)(2,1)S(1)}, u32[]{:S(2)}, u32[]{:S(2)}) collective-permute-start(s16[64,1152]{1,0:T(8,128)(2,1)S(1)} %get-tuple-element.86), channel_id=1, source_target_pairs={{0,4},{1,5},{2,6},{3,7},{4,0},{5,1},{6,2},{7,3},{8,12},{9,13},{10,... | collective-permute-start | bytes 442376 | tf_op jit(solution)/shard_map/ppermute | solution.py:538
  225.2 1.2 collective-permute-start.31
  227.1 3.9 %collective-permute-done.29.refs_0_ = s16[64,1152]{1,0:T(8,128)(2,1)S(1)} collective-permute-done((s16[64,1152]{1,0:T(8,128)(2,1)S(1)}, s16[64,1152]{1,0:T(8,128)(2,1)S(1)}, u32[]{:S(2)}, u32[]{:S(2)}) %collective-permute-start.29) | collective-permute-done | bytes 147488 | tf_op jit(solution)/shard_map/ppermute | solution.py:538
  231.1 5.2 %collective-permute-done.30.refs_1_ = s16[64,1152]{1,0:T(8,128)(2,1)S(1)} collective-permute-done((s16[64,1152]{1,0:T(8,128)(2,1)S(1)}, s16[64,1152]{1,0:T(8,128)(2,1)S(1)}, u32[]{:S(2)}, u32[]{:S(2)}) %collective-permute-start.30) | collective-permute-done | bytes 147488 | tf_op jit(solution)/shard_map/ppermute | solution.py:538
  236.5 5.1 %collective-permute-start.32 = (s16[64,1152]{1,0:T(8,128)(2,1)S(1)}, s16[64,1152]{1,0:T(8,128)(2,1)S(1)}, u32[]{:S(2)}, u32[]{:S(2)}) collective-permute-start(s16[64,1152]{1,0:T(8,128)(2,1)S(1)} %last_sum.3), channel_id=1, source_target_pairs={{0,0},{1,1},{2,8},{3,9},{4,16},{5,17},{6,24},{7,25},{8,2},{9,3},{1... | collective-permute-start | bytes 442376 | tf_op jit(solution)/shard_map/ppermute | solution.py:549
  241.7 9.7 %collective-permute-done.32 = s16[64,1152]{1,0:T(8,128)(2,1)S(1)} collective-permute-done((s16[64,1152]{1,0:T(8,128)(2,1)S(1)}, s16[64,1152]{1,0:T(8,128)(2,1)S(1)}, u32[]{:S(2)}, u32[]{:S(2)}) %collective-permute-start.32) | collective-permute-done | bytes 147488 | tf_op jit(solution)/shard_map/ppermute | solution.py:549
  251.7 2.0 multiply_subtract_fusion
  (76 shorter events, 5.8 us)
Async XLA Ops:
  5.1 17.5 %collective-permute-start.2 = (bf16[128,2048]{1,0:T(8,128)(2,1)S(1)}, bf16[128,2048]{1,0:T(8,128)(2,1)S(1)}, u32[]{:S(2)}, u32[]{:S(2)}) collective-permute-start(bf16[128,2048]{1,0:T(8,128)(2,1)S(1)} %get-tuple-element.88), channel_id=1, source_target_pairs={{0,24},{8,16},{16,8},{24,0},{1,25},{9,17},{17,9},{25,1},{2,26},{10... | collective-permute-start | bytes 1572872 | tf_op jit(solution)/shard_map/ppermute | solution.py:463
  6.7 25.7 %collective-permute-start = (bf16[128,2176]{1,0:T(8,128)(2,1)S(1)}, bf16[128,2176]{1,0:T(8,128)(2,1)S(1)}, u32[]{:S(2)}, u32[]{:S(2)}) collective-permute-start(bf16[128,2176]{1,0:T(8,128)(2,1)S(1)} %pad.7), channel_id=1, source_target_pairs={{0,8},{8,0},{16,24},{24,16},{1,9},{9,1},{17,25},{25,17},{2,10},{10... | collective-permute-start | bytes 1671176 | tf_op jit(solution)/shard_map/ppermute | solution.py:463
  8.3 24.1 %collective-permute-start.1 = (bf16[128,2176]{1,0:T(8,128)(2,1)S(1)}, bf16[128,2176]{1,0:T(8,128)(2,1)S(1)}, u32[]{:S(2)}, u32[]{:S(2)}) collective-permute-start(bf16[128,2176]{1,0:T(8,128)(2,1)S(1)} %pad.8), channel_id=1, source_target_pairs={{0,16},{8,24},{16,0},{24,8},{1,17},{9,25},{17,1},{25,9},{2,18},{10... | collective-permute-start | bytes 1671176 | tf_op jit(solution)/shard_map/ppermute | solution.py:463
  29.5 14.9 %collective-permute-start.5 = (s16[64,4224]{1,0:T(8,128)(2,1)S(1)}, s16[64,4224]{1,0:T(8,128)(2,1)S(1)}, u32[]{:S(2)}, u32[]{:S(2)}) collective-permute-start(s16[64,4224]{1,0:T(8,128)(2,1)S(1)} %get-tuple-element.50), channel_id=1, source_target_pairs={{0,8},{8,0},{16,24},{24,16},{1,9},{9,1},{17,25},{25,17},{2,10},{10... | collective-permute-start | bytes 1622024 | tf_op jit(solution)/shard_map/ppermute | solution.py:463
  29.6 14.7 %collective-permute-start.6 = (s16[64,4224]{1,0:T(8,128)(2,1)S(1)}, s16[64,4224]{1,0:T(8,128)(2,1)S(1)}, u32[]{:S(2)}, u32[]{:S(2)}) collective-permute-start(s16[64,4224]{1,0:T(8,128)(2,1)S(1)} %get-tuple-element.51), channel_id=1, source_target_pairs={{0,16},{8,24},{16,0},{24,8},{1,17},{9,25},{17,1},{25,9},{2,18},{10... | collective-permute-start | bytes 1622024 | tf_op jit(solution)/shard_map/ppermute | solution.py:463
  40.2 15.7 %collective-permute-start.3 = (s16[64,4224]{1,0:T(8,128)(2,1)}, s16[64,4224]{1,0:T(8,128)(2,1)S(1)}, u32[]{:S(2)}, u32[]{:S(2)}) collective-permute-start(s16[64,4224]{1,0:T(8,128)(2,1)} %get-tuple-element.46), channel_id=1, source_target_pairs={{0,8},{8,0},{16,24},{24,16},{1,9},{9,1},{17,25},{25,17},{2,10},{10... | collective-permute-start | bytes 1622024 | tf_op jit(solution)/shard_map/ppermute | solution.py:463
  41.0 15.1 %collective-permute-start.4 = (s16[64,4224]{1,0:T(8,128)(2,1)}, s16[64,4224]{1,0:T(8,128)(2,1)S(1)}, u32[]{:S(2)}, u32[]{:S(2)}) collective-permute-start(s16[64,4224]{1,0:T(8,128)(2,1)} %get-tuple-element.47), channel_id=1, source_target_pairs={{0,16},{8,24},{16,0},{24,8},{1,17},{9,25},{17,1},{25,9},{2,18},{10... | collective-permute-start | bytes 1622024 | tf_op jit(solution)/shard_map/ppermute | solution.py:463
  52.2 15.6 %collective-permute-start.7 = (s16[64,4224]{1,0:T(8,128)(2,1)}, s16[64,4224]{1,0:T(8,128)(2,1)}, u32[]{:S(2)}, u32[]{:S(2)}) collective-permute-start(s16[64,4224]{1,0:T(8,128)(2,1)} %get-tuple-element.52), channel_id=1, source_target_pairs={{0,8},{8,0},{16,24},{24,16},{1,9},{9,1},{17,25},{25,17},{2,10},{10... | collective-permute-start | bytes 1622024 | tf_op jit(solution)/shard_map/ppermute | solution.py:463
  52.7 15.0 %collective-permute-start.8 = (s16[64,4224]{1,0:T(8,128)(2,1)}, s16[64,4224]{1,0:T(8,128)(2,1)}, u32[]{:S(2)}, u32[]{:S(2)}) collective-permute-start(s16[64,4224]{1,0:T(8,128)(2,1)} %get-tuple-element.53), channel_id=1, source_target_pairs={{0,16},{8,24},{16,0},{24,8},{1,17},{9,25},{17,1},{25,9},{2,18},{10... | collective-permute-start | bytes 1622024 | tf_op jit(solution)/shard_map/ppermute | solution.py:463
  54.2 12.3 %copy-start.5 = (s32[128,16]{0,1:T(8,128)S(1)}, s32[128,16]{0,1:T(8,128)}, u32[]{:S(2)}) copy-start(s32[128,16]{0,1:T(8,128)} %param.9) | copy-start | bytes 24580
  63.9 23.1 %collective-permute-start.13 = (s16[64,4224]{1,0:T(8,128)(2,1)}, s16[64,4224]{1,0:T(8,128)(2,1)}, u32[]{:S(2)}, u32[]{:S(2)}) collective-permute-start(s16[64,4224]{1,0:T(8,128)(2,1)} %get-tuple-element.48), channel_id=1, source_target_pairs={{0,8},{8,0},{16,24},{24,16},{1,9},{9,1},{17,25},{25,17},{2,10},{10... | collective-permute-start | bytes 1622024 | tf_op jit(solution)/shard_map/ppermute | solution.py:463
  65.3 22.5 %collective-permute-start.14 = (s16[64,4224]{1,0:T(8,128)(2,1)}, s16[64,4224]{1,0:T(8,128)(2,1)}, u32[]{:S(2)}, u32[]{:S(2)}) collective-permute-start(s16[64,4224]{1,0:T(8,128)(2,1)} %get-tuple-element.59), channel_id=1, source_target_pairs={{0,16},{8,24},{16,0},{24,8},{1,17},{9,25},{17,1},{25,9},{2,18},{10... | collective-permute-start | bytes 1622024 | tf_op jit(solution)/shard_map/ppermute | solution.py:463
  66.6 10.7 %copy-start.6 = (s32[128]{0:T(128)S(1)}, s32[128]{0:T(128)}, u32[]{:S(2)}) copy-start(s32[128]{0:T(128)} %param.10) | copy-start | bytes 1540
  66.6 10.7 %copy-start.7 = (f32[128]{0:T(128)S(1)}, f32[128]{0:T(128)}, u32[]{:S(2)}) copy-start(f32[128]{0:T(128)} %param.11) | copy-start | bytes 1540
  75.4 0.8 copy-start.3
  76.3 36.6 %collective-permute-start.9 = (s16[64,4224]{1,0:T(8,128)(2,1)}, s16[64,4224]{1,0:T(8,128)(2,1)S(1)}, u32[]{:S(2)}, u32[]{:S(2)}) collective-permute-start(s16[64,4224]{1,0:T(8,128)(2,1)} %get-tuple-element.55), channel_id=1, source_target_pairs={{0,8},{8,0},{16,24},{24,16},{1,9},{9,1},{17,25},{25,17},{2,10},{10... | collective-permute-start | bytes 1622024 | tf_op jit(solution)/shard_map/ppermute | solution.py:463
  77.6 8.1 %copy-start.4 = (s16[64,4224]{1,0:T(8,128)(2,1)S(1)}, s16[64,4224]{1,0:T(8,128)(2,1)}, u32[]{:S(2)}) copy-start(s16[64,4224]{1,0:T(8,128)(2,1)} %copy-done.3) | copy-start | bytes 1622020
  77.6 10.2 %copy-start.2 = (f32[128,8192]{1,0:T(8,128)S(1)}, f32[128,8192]{1,0:T(8,128)}, u32[]{:S(2)}) copy-start(f32[128,8192]{1,0:T(8,128)} %own_logits.1.refs_0_) | copy-start | bytes 12582916
  84.6 29.4 %collective-permute-start.10 = (s16[64,4224]{1,0:T(8,128)(2,1)S(1)}, s16[64,4224]{1,0:T(8,128)(2,1)S(1)}, u32[]{:S(2)}, u32[]{:S(2)}) collective-permute-start(s16[64,4224]{1,0:T(8,128)(2,1)S(1)} %get-tuple-element.56), channel_id=1, source_target_pairs={{0,8},{8,0},{16,24},{24,16},{1,9},{9,1},{17,25},{25,17},{2,10},{10... | collective-permute-start | bytes 1622024 | tf_op jit(solution)/shard_map/ppermute | solution.py:463
  85.7 28.3 %collective-permute-start.11 = (s16[64,4224]{1,0:T(8,128)(2,1)S(1)}, s16[64,4224]{1,0:T(8,128)(2,1)S(1)}, u32[]{:S(2)}, u32[]{:S(2)}) collective-permute-start(s16[64,4224]{1,0:T(8,128)(2,1)S(1)} %copy-done.4), channel_id=1, source_target_pairs={{0,16},{8,24},{16,0},{24,8},{1,17},{9,25},{17,1},{25,9},{2,18},{10... | collective-permute-start | bytes 1622024 | tf_op jit(solution)/shard_map/ppermute | solution.py:463
  87.0 27.1 %collective-permute-start.12 = (s16[64,4224]{1,0:T(8,128)(2,1)S(1)}, s16[64,4224]{1,0:T(8,128)(2,1)S(1)}, u32[]{:S(2)}, u32[]{:S(2)}) collective-permute-start(s16[64,4224]{1,0:T(8,128)(2,1)S(1)} %get-tuple-element.58), channel_id=1, source_target_pairs={{0,16},{8,24},{16,0},{24,8},{1,17},{9,25},{17,1},{25,9},{2,18},{10... | collective-permute-start | bytes 1622024 | tf_op jit(solution)/shard_map/ppermute | solution.py:463
  111.6 25.8 %collective-permute-start.15 = (bf16[64,8320]{1,0:T(8,128)(2,1)S(1)}, bf16[64,8320]{1,0:T(8,128)(2,1)S(1)}, u32[]{:S(2)}, u32[]{:S(2)}) collective-permute-start(bf16[64,8320]{1,0:T(8,128)(2,1)S(1)} %get-tuple-element.69), channel_id=1, source_target_pairs={{0,16},{8,24},{16,0},{24,8},{1,17},{9,25},{17,1},{25,9},{2,18},{10... | collective-permute-start | bytes 3194888 | tf_op jit(solution)/shard_map/ppermute | solution.py:463
  112.9 25.6 %collective-permute-start.17 = (bf16[64,8320]{1,0:T(8,128)(2,1)S(1)}, bf16[64,8320]{1,0:T(8,128)(2,1)S(1)}, u32[]{:S(2)}, u32[]{:S(2)}) collective-permute-start(bf16[64,8320]{1,0:T(8,128)(2,1)S(1)} %get-tuple-element.69), channel_id=1, source_target_pairs={{0,8},{8,0},{16,24},{24,16},{1,9},{9,1},{17,25},{25,17},{2,10},{10... | collective-permute-start | bytes 3194888 | tf_op jit(solution)/shard_map/ppermute | solution.py:463
  137.5 13.6 %collective-permute-start.16 = (bf16[32,8320]{1,0:T(8,128)(2,1)S(1)}, bf16[32,8320]{1,0:T(8,128)(2,1)S(1)}, u32[]{:S(2)}, u32[]{:S(2)}) collective-permute-start(bf16[32,8320]{1,0:T(8,128)(2,1)S(1)} %slice.33), channel_id=1, source_target_pairs={{0,8},{8,0},{16,24},{24,16},{1,9},{9,1},{17,25},{25,17},{2,10},{10... | collective-permute-start | bytes 1597448 | tf_op jit(solution)/shard_map/ppermute | solution.py:463
  138.5 13.3 %collective-permute-start.18 = (bf16[32,8320]{1,0:T(8,128)(2,1)S(1)}, bf16[32,8320]{1,0:T(8,128)(2,1)S(1)}, u32[]{:S(2)}, u32[]{:S(2)}) collective-permute-start(bf16[32,8320]{1,0:T(8,128)(2,1)S(1)} %slice.34), channel_id=1, source_target_pairs={{0,16},{8,24},{16,0},{24,8},{1,17},{9,25},{17,1},{25,9},{2,18},{10... | collective-permute-start | bytes 1597448 | tf_op jit(solution)/shard_map/ppermute | solution.py:463
  151.9 23.8 %collective-permute-start.19 = (bf16[64,8320]{1,0:T(8,128)(2,1)S(1)}, bf16[64,8320]{1,0:T(8,128)(2,1)S(1)}, u32[]{:S(2)}, u32[]{:S(2)}) collective-permute-start(bf16[64,8320]{1,0:T(8,128)(2,1)S(1)} %get-tuple-element.73), channel_id=1, source_target_pairs={{0,16},{8,24},{16,0},{24,8},{1,17},{9,25},{17,1},{25,9},{2,18},{10... | collective-permute-start | bytes 3194888 | tf_op jit(solution)/shard_map/ppermute | solution.py:463
  153.2 23.5 %collective-permute-start.20 = (bf16[64,8320]{1,0:T(8,128)(2,1)S(1)}, bf16[64,8320]{1,0:T(8,128)(2,1)S(1)}, u32[]{:S(2)}, u32[]{:S(2)}) collective-permute-start(bf16[64,8320]{1,0:T(8,128)(2,1)S(1)} %get-tuple-element.73), channel_id=1, source_target_pairs={{0,8},{8,0},{16,24},{24,16},{1,9},{9,1},{17,25},{25,17},{2,10},{10... | collective-permute-start | bytes 3194888 | tf_op jit(solution)/shard_map/ppermute | solution.py:463
  164.4 14.2 %collective-permute-start.21 = (s16[256,1152]{1,0:T(8,128)(2,1)S(1)}, s16[256,1152]{1,0:T(8,128)(2,1)S(1)}, u32[]{:S(2)}, u32[]{:S(2)}) collective-permute-start(s16[256,1152]{1,0:T(8,128)(2,1)S(1)} %grad_rows.4), channel_id=1, source_target_pairs={{0,1},{1,0},{2,3},{3,2},{4,5},{5,4},{6,7},{7,6},{8,9},{9,8},{10,11... | collective-permute-start | bytes 1769480 | tf_op jit(solution)/shard_map/ppermute | solution.py:531
  176.7 16.3 %collective-permute-start.26 = (bf16[32,8320]{1,0:T(8,128)(2,1)S(1)}, bf16[32,8320]{1,0:T(8,128)(2,1)S(1)}, u32[]{:S(2)}, u32[]{:S(2)}) collective-permute-start(bf16[32,8320]{1,0:T(8,128)(2,1)S(1)} %slice.35), channel_id=1, source_target_pairs={{0,8},{8,0},{16,24},{24,16},{1,9},{9,1},{17,25},{25,17},{2,10},{10... | collective-permute-start | bytes 1597448 | tf_op jit(solution)/shard_map/ppermute | solution.py:463
  177.8 15.3 %collective-permute-start.27 = (bf16[32,8320]{1,0:T(8,128)(2,1)S(1)}, bf16[32,8320]{1,0:T(8,128)(2,1)S(1)}, u32[]{:S(2)}, u32[]{:S(2)}) collective-permute-start(bf16[32,8320]{1,0:T(8,128)(2,1)S(1)} %slice.36), channel_id=1, source_target_pairs={{0,16},{8,24},{16,0},{24,8},{1,17},{9,25},{17,1},{25,9},{2,18},{10... | collective-permute-start | bytes 1597448 | tf_op jit(solution)/shard_map/ppermute | solution.py:463
  179.6 5.9 %collective-permute-start.22 = (s16[64,1152]{1,0:T(8,128)(2,1)S(1)}, s16[64,1152]{1,0:T(8,128)(2,1)S(1)}, u32[]{:S(2)}, u32[]{:S(2)}) collective-permute-start(s16[64,1152]{1,0:T(8,128)(2,1)S(1)} %get-tuple-element.79), channel_id=1, source_target_pairs={{0,2},{1,3},{2,0},{3,1},{4,6},{5,7},{6,4},{7,5},{8,10},{9,11},{10,... | collective-permute-start | bytes 442376 | tf_op jit(solution)/shard_map/ppermute | solution.py:538
  181.2 11.9 %collective-permute-start.23 = (s16[64,1152]{1,0:T(8,128)(2,1)S(1)}, s16[64,1152]{1,0:T(8,128)(2,1)S(1)}, u32[]{:S(2)}, u32[]{:S(2)}) collective-permute-start(s16[64,1152]{1,0:T(8,128)(2,1)S(1)} %get-tuple-element.80), channel_id=1, source_target_pairs={{0,4},{1,5},{2,6},{3,7},{4,0},{5,1},{6,2},{7,3},{8,12},{9,13},{10,... | collective-permute-start | bytes 442376 | tf_op jit(solution)/shard_map/ppermute | solution.py:538
  183.6 9.5 %collective-permute-start.24 = (s16[64,1152]{1,0:T(8,128)(2,1)S(1)}, s16[64,1152]{1,0:T(8,128)(2,1)S(1)}, u32[]{:S(2)}, u32[]{:S(2)}) collective-permute-start(s16[64,1152]{1,0:T(8,128)(2,1)S(1)} %get-tuple-element.81), channel_id=1, source_target_pairs={{0,6},{1,7},{2,4},{3,5},{4,2},{5,3},{6,0},{7,1},{8,14},{9,15},{10,... | collective-permute-start | bytes 442376 | tf_op jit(solution)/shard_map/ppermute | solution.py:538
  193.1 10.7 %copy-start = (bf16[256,8320]{1,0:T(8,128)(2,1)}, bf16[256,8320]{1,0:T(8,128)(2,1)S(1)}, u32[]{:S(2)}) copy-start(bf16[256,8320]{1,0:T(8,128)(2,1)S(1)} %constant_dynamic-update-slice_fusion.5.grad_ref.beside_ref) | copy-start | bytes 12779524
  203.9 17.0 %collective-permute-start.28 = (s16[256,1152]{1,0:T(8,128)(2,1)S(1)}, s16[256,1152]{1,0:T(8,128)(2,1)S(1)}, u32[]{:S(2)}, u32[]{:S(2)}) collective-permute-start(s16[256,1152]{1,0:T(8,128)(2,1)S(1)} %grad_rows.6), channel_id=1, source_target_pairs={{0,1},{1,0},{2,3},{3,2},{4,5},{5,4},{6,7},{7,6},{8,9},{9,8},{10,11... | collective-permute-start | bytes 1769480 | tf_op jit(solution)/shard_map/ppermute | solution.py:531
  204.4 37.3 %collective-permute-start.25 = (s16[64,1152]{1,0:T(8,128)(2,1)S(1)}, s16[64,1152]{1,0:T(8,128)(2,1)S(1)}, u32[]{:S(2)}, u32[]{:S(2)}) collective-permute-start(s16[64,1152]{1,0:T(8,128)(2,1)S(1)} %last_sum.2), channel_id=1, source_target_pairs={{0,0},{1,1},{2,8},{3,9},{4,16},{5,17},{6,24},{7,25},{8,2},{9,3},{1... | collective-permute-start | bytes 442376 | tf_op jit(solution)/shard_map/ppermute | solution.py:549
  208.9 2.2 copy-start.1
  211.2 40.5 %dynamic-slice-start = ((f32[8192]{0:T(1024)}, s32[]{:T(128)}), f32[1024]{0:T(1024)S(1)}, s32[]{:S(2)}) async-start(f32[8192]{0:T(1024)} %param.8, s32[]{:T(128)} %select_n.37), calls=%async_computation | async-start | bytes 8704 | tf_op jit(solution)/shard_map/dynamic_slice | solution.py:559
  222.0 9.1 %collective-permute-start.29 = (s16[64,1152]{1,0:T(8,128)(2,1)S(1)}, s16[64,1152]{1,0:T(8,128)(2,1)S(1)}, u32[]{:S(2)}, u32[]{:S(2)}) collective-permute-start(s16[64,1152]{1,0:T(8,128)(2,1)S(1)} %get-tuple-element.85), channel_id=1, source_target_pairs={{0,2},{1,3},{2,0},{3,1},{4,6},{5,7},{6,4},{7,5},{8,10},{9,11},{10,... | collective-permute-start | bytes 442376 | tf_op jit(solution)/shard_map/ppermute | solution.py:538
  222.1 14.2 %collective-permute-start.30 = (s16[64,1152]{1,0:T(8,128)(2,1)S(1)}, s16[64,1152]{1,0:T(8,128)(2,1)S(1)}, u32[]{:S(2)}, u32[]{:S(2)}) collective-permute-start(s16[64,1152]{1,0:T(8,128)(2,1)S(1)} %get-tuple-element.86), channel_id=1, source_target_pairs={{0,4},{1,5},{2,6},{3,7},{4,0},{5,1},{6,2},{7,3},{8,12},{9,13},{10,... | collective-permute-start | bytes 442376 | tf_op jit(solution)/shard_map/ppermute | solution.py:538
  225.2 11.0 %collective-permute-start.31 = (s16[64,1152]{1,0:T(8,128)(2,1)S(1)}, s16[64,1152]{1,0:T(8,128)(2,1)S(1)}, u32[]{:S(2)}, u32[]{:S(2)}) collective-permute-start(s16[64,1152]{1,0:T(8,128)(2,1)S(1)} %get-tuple-element.87), channel_id=1, source_target_pairs={{0,6},{1,7},{2,4},{3,5},{4,2},{5,3},{6,0},{7,1},{8,14},{9,15},{10,... | collective-permute-start | bytes 442376 | tf_op jit(solution)/shard_map/ppermute | solution.py:538
  236.5 14.8 %collective-permute-start.32 = (s16[64,1152]{1,0:T(8,128)(2,1)S(1)}, s16[64,1152]{1,0:T(8,128)(2,1)S(1)}, u32[]{:S(2)}, u32[]{:S(2)}) collective-permute-start(s16[64,1152]{1,0:T(8,128)(2,1)S(1)} %last_sum.3), channel_id=1, source_target_pairs={{0,0},{1,1},{2,8},{3,9},{4,16},{5,17},{6,24},{7,25},{8,2},{9,3},{1... | collective-permute-start | bytes 442376 | tf_op jit(solution)/shard_map/ppermute | solution.py:549

commit v12 on v10

--- a/solution.py
+++ b/solution.py
@@ -49,7 +49,7 @@
 
 
 def compiler_params():
-    return pltpu.CompilerParams(vmem_limit_bytes=24 * megabyte)
+    return pltpu.CompilerParams(vmem_limit_bytes=28 * megabyte)
 
 
 def small_cost():
@@ -60,7 +60,7 @@
 
 
 def head_scratch(rows, width, tiles):
-    slots = min(tiles, 12 * megabyte // (2 * rows * width))
+    slots = min(tiles, 16 * megabyte // (2 * rows * width))
     return [pltpu.VMEM((slots, rows, width), jnp.bfloat16), pltpu.SemaphoreType.DMA((slots,))]
 
 
@@ -486,7 +486,7 @@
     ]
     halves = []
     for part in range(2):
-        waits = [codes[1][0], sums_x[0], sums_y[0]] if part else []
+        waits = codes[1][:1] if part else []
         sums_x = [send(after(c[part], *waits), to_x) for c in codes]
         sums_y = [send(after(c[2 + part], *waits), to_y) for c in codes]
         halves.append((sums_x, sums_y))

time: 299 us -> 264 us (0.88)
  waiting for transfers between devices: 103 us -> 69.5 us
    ppermute x23, waiting for transfers between devices: 76.1 us -> 42.4 us  [shards(): send = lambda value, pairs: lax.ppermute(value, 'prompt', pairs)]
    unnamed x39 -> x31, local copies, waits for them, and re-layouts: 10.4 us -> 8.76 us
  transfers between devices with their start and end apart: 33 -> 33, of which waited for: 14 -> 14; matrix products, arithmetic and copies ran while one was open for 1% -> 1% of each run, Pallas kernels for 31% -> 35%
where the time goes in v12:
time: 264 us; the launch traced here: 263 us
  Pallas kernels  104 us (39%)
  waiting for transfers between devices  69.5 us (26%)
  starting transfers between devices  42.4 us (16%)
  blocking collectives  29.1 us (11%)
  local copies, waits for them, and re-layouts  9.75 us (4%)
  other arithmetic  7.42 us (3%)
    ppermute x23, waiting for transfers between devices, shards(): send = lambda value, pairs: lax.ppermute(value, 'prompt', pairs)  42.4 us
    pallas_call x4, Pallas kernels, back(): pl.pallas_call(functools.partial(back_kernel, columns // width, keeps), g...  40.2 us
    all_gather x2, blocking collectives, shards(): stats = lax.all_gather(stats, 'vocab', axis=0)  29.1 us
    ppermute x23, starting transfers between devices, shards(): send = lambda value, pairs: lax.ppermute(value, 'prompt', pairs)  24.3 us
    pallas_call x2, Pallas kernels, near_codes(): pl.pallas_call(functools.partial(near_kernel, width, skip, tiles), grid=(...  18.4 us
    ppermute x6, waiting for transfers between devices, blocks(): lax.ppermute(c, 'vocab', to)  17.7 us
    pallas_call x2, Pallas kernels, far_codes(): pl.pallas_call(functools.partial(far_kernel, width, skip, tiles), grid=(t...  13.7 us
    pallas_call x2, Pallas kernels, row_stats(): pl.pallas_call(functools.partial(stats_kernel, width, parts), grid=(rows...  12.7 us
  transfers between devices with their start and end apart: 33, of which 14 were waited for; matrix products, arithmetic and copies ran while one was open for 1% of the time, Pallas kernels for 35%

profile of v12, /device:TPU:2, one launch (start us, length us, event | category | flops | bytes accessed | tf_op | source)
XLA Modules:
  0.0 263.2 jit_solution(400069541583271530)
XLA Ops:
  0.6 2.1 fusion
  2.7 2.2 fusion.2
  5.2 1.6 collective-permute-start.2
  6.8 1.6 collective-permute-start
  8.4 0.6 collective-permute-start.1
  9.0 11.8 %own_logits.1.refs_0_ = f32[128,8192]{1,0:T(8,128)S(1)} custom-call(bf16[128,2048]{1,0:T(8,128)(2,1)S(1)} %get-tuple-element.97.x_ref, bf16[2048,8192]{1,0:T(8,128)(2,1)} %head_ref.17), custom_call_target="tpu_custom_call" | custom-call | flops 1024 | bytes 1024 | tf_op jit(solution)/shard_map/own_logits/pallas_call | solution.py:178
  20.8 2.0 copy-done.2
  22.7 6.8 %far_codes.2 = (s16[64,4224]{1,0:T(8,128)(2,1)S(1)}, s16[64,4224]{1,0:T(8,128)(2,1)S(1)}) custom-call(bf16[128,2304]{1,0:T(8,128)(2,1)S(1)} %collective-permute-done.2.x_ref, bf16[2048,8192]{1,0:T(8,128)(2,1)} %head_ref.17), custom_call_target="tpu_custom_call" | custom-call | flops 1024 | bytes 1024 | tf_op jit(solution)/shard_map/far_codes/pallas_call | solution.py:117
  29.7 2.0 collective-permute-start.4
  31.7 2.7 %collective-permute-done.x_ref = bf16[128,2176]{1,0:T(8,128)(2,1)S(1)} collective-permute-done((bf16[128,2176]{1,0:T(8,128)(2,1)S(1)}, bf16[128,2176]{1,0:T(8,128)(2,1)S(1)}, u32[]{:S(2)}, u32[]{:S(2)}) %collective-permute-start) | collective-permute-done | bytes 557088 | tf_op jit(solution)/shard_map/ppermute | solution.py:465
  34.4 6.8 %far_codes.3 = (s16[64,4224]{1,0:T(8,128)(2,1)S(1)}, s16[64,4224]{1,0:T(8,128)(2,1)S(1)}) custom-call(bf16[128,2304]{1,0:T(8,128)(2,1)S(1)} %collective-permute-done.2.x_ref, bf16[2048,8192]{1,0:T(8,128)(2,1)} %head_ref.17), custom_call_target="tpu_custom_call" | custom-call | flops 1024 | bytes 1024 | tf_op jit(solution)/shard_map/far_codes/pallas_call | solution.py:117
  41.3 0.6 collective-permute-start.5
  42.2 3.8 %collective-permute-done.3.by_x_ref = s16[64,4224]{1,0:T(8,128)(2,1)S(1)} collective-permute-done((s16[64,4224]{1,0:T(8,128)(2,1)S(1)}, s16[64,4224]{1,0:T(8,128)(2,1)S(1)}, u32[]{:S(2)}, u32[]{:S(2)}) %collective-permute-start.3) | collective-permute-done | bytes 540704 | tf_op jit(solution)/shard_map/ppermute | solution.py:465
  46.0 9.3 %near_codes.2 = (s16[64,4224]{1,0:T(8,128)(2,1)S(1)}, s16[64,4224]{1,0:T(8,128)(2,1)}, s16[64,4224]{1,0:T(8,128)(2,1)}, s16[64,4224]{1,0:T(8,128)(2,1)S(1)}) custom-call(bf16[128,2176]{1,0:T(8,128)(2,1)S(1)} %collective-permute-done.x_ref, bf16[128,2176]{1,0:T(8,128)(2,1)S(1)} %collective-permute-done.1.y_ref, bf16[2048,8192]{1,0:T(8,128)(2,1)} %head_ref.17, ...), custom_call_target="tpu_custom_call" | custom-call | flops 1024 | bytes 1024 | tf_op jit(solution)/shard_map/near_codes/pallas_call | solution.py:155
  55.3 0.6 collective-permute-start.11
  56.4 9.1 %near_codes.3 = (s16[64,4224]{1,0:T(8,128)(2,1)}, s16[64,4224]{1,0:T(8,128)(2,1)S(1)}, s16[64,4224]{1,0:T(8,128)(2,1)}, s16[64,4224]{1,0:T(8,128)(2,1)S(1)}) custom-call(bf16[128,2176]{1,0:T(8,128)(2,1)S(1)} %collective-permute-done.x_ref, bf16[128,2176]{1,0:T(8,128)(2,1)S(1)} %collective-permute-done.1.y_ref, bf16[2048,8192]{1,0:T(8,128)(2,1)} %head_ref.17, ...), custom_call_target="tpu_custom_call" | custom-call | flops 1024 | bytes 1024 | tf_op jit(solution)/shard_map/near_codes/pallas_call | solution.py:155
  65.6 0.8 copy-done.6
  66.4 0.8 copy-done.7
  67.2 1.0 collective-permute-start.12
  68.1 1.0 collective-permute-start.13
  69.1 1.0 collective-permute-start.14
  70.3 1.1 collective-permute-start.7
  71.4 1.0 collective-permute-start.8
  72.4 10.2 %collective-permute-done.12.refs_2_ = s16[64,4224]{1,0:T(8,128)(2,1)S(1)} collective-permute-done((s16[64,4224]{1,0:T(8,128)(2,1)}, s16[64,4224]{1,0:T(8,128)(2,1)S(1)}, u32[]{:S(2)}, u32[]{:S(2)}) %collective-permute-start.12) | collective-permute-done | bytes 540704 | tf_op jit(solution)/shard_map/ppermute | solution.py:465
  82.6 1.4 collective-permute-start.9
  84.0 0.6 collective-permute-start.10
  85.0 10.2 %collective-permute-done.14.refs_4_ = s16[64,4224]{1,0:T(8,128)(2,1)S(1)} collective-permute-done((s16[64,4224]{1,0:T(8,128)(2,1)}, s16[64,4224]{1,0:T(8,128)(2,1)S(1)}, u32[]{:S(2)}, u32[]{:S(2)}) %collective-permute-start.14) | collective-permute-done | bytes 540704 | tf_op jit(solution)/shard_map/ppermute | solution.py:465
  95.2 2.2 copy-done.3
  97.4 5.9 %row_stats.2 = (f32[64,8192]{1,0:T(8,128)S(1)}, f32[64,8192]{1,0:T(8,128)S(1)}, f32[64,128]{1,0:T(8,128)S(1)}) custom-call(f32[128,8192]{1,0:T(8,128)S(1)} %copy-done.3, s16[64,4224]{1,0:T(8,128)(2,1)S(1)} %collective-permute-done.11.refs_1_, s16[64,4224]{1,0:T(8,128)(2,1)S(1)} %collective-permute-done.12.refs_2_, ...), custom_call_target="tpu_custom_call" | custom-call | flops 1024 | bytes 1024 | tf_op jit(solution)/shard_map/row_stats/pallas_call | solution.py:241
  103.2 14.6 %all-gather = f32[512,128]{1,0:T(8,128)S(1)} all-gather(f32[64,128]{1,0:T(8,128)S(1)} %get-tuple-element.68), channel_id=2, replica_groups=mesh['prompt'=4,'vocab'=8] {'vocab'}, dimensions={0}, use_global_device_ids=true | all-gather | bytes 294912 | tf_op jit(solution)/shard_map/all_gather | solution.py:517
  117.8 2.2 logit_grads.2
  120.0 1.0 collective-permute-start.15
  121.0 1.5 collective-permute-start.17
  122.5 6.9 %row_stats.3 = (f32[64,8192]{1,0:T(8,128)S(1)}, f32[64,8192]{1,0:T(8,128)S(1)}, f32[64,128]{1,0:T(8,128)S(1)}) custom-call(f32[128,8192]{1,0:T(8,128)S(1)} %copy-done.4, s16[64,4224]{1,0:T(8,128)(2,1)S(1)} %collective-permute-done.7.refs_1_, s16[64,4224]{1,0:T(8,128)(2,1)S(1)} %collective-permute-done.8.refs_2_, ...), custom_call_target="tpu_custom_call" | custom-call | flops 1024 | bytes 1024 | tf_op jit(solution)/shard_map/row_stats/pallas_call | solution.py:241
  129.4 14.5 %all-gather.1 = f32[512,128]{1,0:T(8,128)S(1)} all-gather(f32[64,128]{1,0:T(8,128)S(1)} %get-tuple-element.73), channel_id=3, replica_groups=mesh['prompt'=4,'vocab'=8] {'vocab'}, dimensions={0}, use_global_device_ids=true | all-gather | bytes 294912 | tf_op jit(solution)/shard_map/all_gather | solution.py:517
  143.9 2.2 logit_grads.3
  146.3 0.8 collective-permute-start.16
  147.2 1.3 collective-permute-start.18
  148.7 12.0 %collective-permute-done.16 = bf16[32,8320]{1,0:T(8,128)(2,1)S(1)} collective-permute-done((bf16[32,8320]{1,0:T(8,128)(2,1)S(1)}, bf16[32,8320]{1,0:T(8,128)(2,1)S(1)}, u32[]{:S(2)}, u32[]{:S(2)}) %collective-permute-start.16) | collective-permute-done | bytes 532512 | tf_op jit(solution)/shard_map/ppermute | solution.py:465
  161.1 1.1 collective-permute-start.19
  162.1 1.2 collective-permute-start.20
  163.5 10.0 %grad_rows.4 = s16[256,1152]{1,0:T(8,128)(2,1)S(1)} custom-call(s32[2]{0:T(128)S(1)} %pad_add_fusion.place_ref, bf16[256,8320]{1,0:T(8,128)(2,1)S(1)} %constant_dynamic-update-slice_fusion.grad_ref.beside_ref, bf16[256,8320]{1,0:T(8,128)(2,1)S(1)} %constant_dynamic-update-slice_fusion.grad_ref.beside_ref, bf16[2048,8192]{1,0:T(8,128)(2,1)} %head_ref.17), custom_call_target="tpu_custom_call" | custom-call | flops 1024 | bytes 1024 | tf_op jit(solution)/shard_map/grad_rows/pallas_call | solution.py:370
  173.7 9.7 %grad_rows.5.keep_ref = f32[256,1152]{1,0:T(8,128)S(1)} custom-call(s32[2]{0:T(128)S(1)} %pad_add_fusion.1.place_ref, bf16[256,8320]{1,0:T(8,128)(2,1)S(1)} %constant_dynamic-update-slice_fusion.grad_ref.beside_ref, bf16[256,8320]{1,0:T(8,128)(2,1)S(1)} %constant_dynamic-update-slice_fusion.grad_ref.beside_ref, bf16[2048,8192]{1,0:T(8,128)(2,1)} %head_ref.17), custom_call_target="tpu_custom_call" | custom-call | flops 1024 | bytes 1024 | tf_op jit(solution)/shard_map/grad_rows/pallas_call | solution.py:370
  183.4 2.2 collective-permute-done.19
  186.2 1.6 collective-permute-start.26
  187.8 1.2 collective-permute-start.27
  189.0 1.1 group_sum.2
  190.1 1.5 collective-permute-start.22
  191.6 2.4 collective-permute-start.23
  194.8 1.3 collective-permute-done.22.refs_0_
  196.1 7.2 %collective-permute-done.23.refs_1_ = s16[64,1152]{1,0:T(8,128)(2,1)S(1)} collective-permute-done((s16[64,1152]{1,0:T(8,128)(2,1)S(1)}, s16[64,1152]{1,0:T(8,128)(2,1)S(1)}, u32[]{:S(2)}, u32[]{:S(2)}) %collective-permute-start.23) | collective-permute-done | bytes 147488 | tf_op jit(solution)/shard_map/ppermute | solution.py:541
  203.5 10.7 %grad_rows.6 = s16[256,1152]{1,0:T(8,128)(2,1)S(1)} custom-call(s32[2]{0:T(128)S(1)} %pad_add_fusion.place_ref, bf16[256,8320]{1,0:T(8,128)(2,1)S(1)} %constant_dynamic-update-slice_fusion.5.grad_ref.beside_ref, bf16[256,8320]{1,0:T(8,128)(2,1)S(1)} %constant_dynamic-update-slice_fusion.5.grad_ref.beside_ref, bf16[2048,8192]{1,0:T(8,128)(2,1)} %head_ref.17), custom_call_target="tpu_custom_call" | custom-call | flops 1024 | bytes 1024 | tf_op jit(solution)/shard_map/grad_rows/pallas_call | solution.py:370
  214.7 3.9 %collective-permute-start.25 = (s16[64,1152]{1,0:T(8,128)(2,1)S(1)}, s16[64,1152]{1,0:T(8,128)(2,1)S(1)}, u32[]{:S(2)}, u32[]{:S(2)}) collective-permute-start(s16[64,1152]{1,0:T(8,128)(2,1)S(1)} %last_sum.2), channel_id=1, source_target_pairs={{0,0},{1,1},{2,8},{3,9},{4,16},{5,17},{6,24},{7,25},{8,2},{9,3},{1... | collective-permute-start | bytes 442376 | tf_op jit(solution)/shard_map/ppermute | solution.py:552
  218.7 2.2 copy-done.1
  220.9 9.7 %grad_rows.7.keep_ref = f32[256,1152]{1,0:T(8,128)S(1)} custom-call(s32[2]{0:T(128)S(1)} %pad_add_fusion.1.place_ref, bf16[256,8320]{1,0:T(8,128)(2,1)S(1)} %copy-done.1, bf16[256,8320]{1,0:T(8,128)(2,1)S(1)} %copy-done.1, bf16[2048,8192]{1,0:T(8,128)(2,1)} %head_ref.17), custom_call_target="tpu_custom_call" | custom-call | flops 1024 | bytes 1024 | tf_op jit(solution)/shard_map/grad_rows/pallas_call | solution.py:370
  230.6 1.0 group_sum.3
  231.7 3.2 %collective-permute-start.30 = (s16[64,1152]{1,0:T(8,128)(2,1)S(1)}, s16[64,1152]{1,0:T(8,128)(2,1)S(1)}, u32[]{:S(2)}, u32[]{:S(2)}) collective-permute-start(s16[64,1152]{1,0:T(8,128)(2,1)S(1)} %get-tuple-element.92), channel_id=1, source_target_pairs={{0,4},{1,5},{2,6},{3,7},{4,0},{5,1},{6,2},{7,3},{8,12},{9,13},{10,... | collective-permute-start | bytes 442376 | tf_op jit(solution)/shard_map/ppermute | solution.py:541
  235.0 1.1 collective-permute-start.31
  236.2 0.6 pad_maximum_fusion
  236.8 3.6 %collective-permute-done.29.refs_0_ = s16[64,1152]{1,0:T(8,128)(2,1)S(1)} collective-permute-done((s16[64,1152]{1,0:T(8,128)(2,1)S(1)}, s16[64,1152]{1,0:T(8,128)(2,1)S(1)}, u32[]{:S(2)}, u32[]{:S(2)}) %collective-permute-start.29) | collective-permute-done | bytes 147488 | tf_op jit(solution)/shard_map/ppermute | solution.py:541
  240.4 5.6 %collective-permute-done.30.refs_1_ = s16[64,1152]{1,0:T(8,128)(2,1)S(1)} collective-permute-done((s16[64,1152]{1,0:T(8,128)(2,1)S(1)}, s16[64,1152]{1,0:T(8,128)(2,1)S(1)}, u32[]{:S(2)}, u32[]{:S(2)}) %collective-permute-start.30) | collective-permute-done | bytes 147488 | tf_op jit(solution)/shard_map/ppermute | solution.py:541
  246.3 5.2 %collective-permute-start.32 = (s16[64,1152]{1,0:T(8,128)(2,1)S(1)}, s16[64,1152]{1,0:T(8,128)(2,1)S(1)}, u32[]{:S(2)}, u32[]{:S(2)}) collective-permute-start(s16[64,1152]{1,0:T(8,128)(2,1)S(1)} %last_sum.3), channel_id=1, source_target_pairs={{0,0},{1,1},{2,8},{3,9},{4,16},{5,17},{6,24},{7,25},{8,2},{9,3},{1... | collective-permute-start | bytes 442376 | tf_op jit(solution)/shard_map/ppermute | solution.py:552
  251.5 9.4 %collective-permute-done.32 = s16[64,1152]{1,0:T(8,128)(2,1)S(1)} collective-permute-done((s16[64,1152]{1,0:T(8,128)(2,1)S(1)}, s16[64,1152]{1,0:T(8,128)(2,1)S(1)}, u32[]{:S(2)}, u32[]{:S(2)}) %collective-permute-start.32) | collective-permute-done | bytes 147488 | tf_op jit(solution)/shard_map/ppermute | solution.py:552
  261.3 2.0 multiply_subtract_fusion
  (81 shorter events, 5.7 us)
Async XLA Ops:
  5.2 17.5 %collective-permute-start.2 = (bf16[128,2304]{1,0:T(8,128)(2,1)S(1)}, bf16[128,2304]{1,0:T(8,128)(2,1)S(1)}, u32[]{:S(2)}, u32[]{:S(2)}) collective-permute-start(bf16[128,2304]{1,0:T(8,128)(2,1)S(1)} %pad.13), channel_id=1, source_target_pairs={{0,24},{8,16},{16,8},{24,0},{1,25},{9,17},{17,9},{25,1},{2,26},{10... | collective-permute-start | bytes 1769480 | tf_op jit(solution)/shard_map/ppermute | solution.py:465
  6.8 27.6 %collective-permute-start = (bf16[128,2176]{1,0:T(8,128)(2,1)S(1)}, bf16[128,2176]{1,0:T(8,128)(2,1)S(1)}, u32[]{:S(2)}, u32[]{:S(2)}) collective-permute-start(bf16[128,2176]{1,0:T(8,128)(2,1)S(1)} %pad.11), channel_id=1, source_target_pairs={{0,8},{8,0},{16,24},{24,16},{1,9},{9,1},{17,25},{25,17},{2,10},{10... | collective-permute-start | bytes 1671176 | tf_op jit(solution)/shard_map/ppermute | solution.py:465
  8.4 26.0 %collective-permute-start.1 = (bf16[128,2176]{1,0:T(8,128)(2,1)S(1)}, bf16[128,2176]{1,0:T(8,128)(2,1)S(1)}, u32[]{:S(2)}, u32[]{:S(2)}) collective-permute-start(bf16[128,2176]{1,0:T(8,128)(2,1)S(1)} %pad.12), channel_id=1, source_target_pairs={{0,16},{8,24},{16,0},{24,8},{1,17},{9,25},{17,1},{25,9},{2,18},{10... | collective-permute-start | bytes 1671176 | tf_op jit(solution)/shard_map/ppermute | solution.py:465
  20.8 2.0 copy-start.2
  29.6 16.4 %collective-permute-start.3 = (s16[64,4224]{1,0:T(8,128)(2,1)S(1)}, s16[64,4224]{1,0:T(8,128)(2,1)S(1)}, u32[]{:S(2)}, u32[]{:S(2)}) collective-permute-start(s16[64,4224]{1,0:T(8,128)(2,1)S(1)} %get-tuple-element.49), channel_id=1, source_target_pairs={{0,8},{8,0},{16,24},{24,16},{1,9},{9,1},{17,25},{25,17},{2,10},{10... | collective-permute-start | bytes 1622024 | tf_op jit(solution)/shard_map/ppermute | solution.py:465
  29.7 16.3 %collective-permute-start.4 = (s16[64,4224]{1,0:T(8,128)(2,1)S(1)}, s16[64,4224]{1,0:T(8,128)(2,1)S(1)}, u32[]{:S(2)}, u32[]{:S(2)}) collective-permute-start(s16[64,4224]{1,0:T(8,128)(2,1)S(1)} %get-tuple-element.50), channel_id=1, source_target_pairs={{0,16},{8,24},{16,0},{24,8},{1,17},{9,25},{17,1},{25,9},{2,18},{10... | collective-permute-start | bytes 1622024 | tf_op jit(solution)/shard_map/ppermute | solution.py:465
  41.3 15.2 %collective-permute-start.5 = (s16[64,4224]{1,0:T(8,128)(2,1)S(1)}, s16[64,4224]{1,0:T(8,128)(2,1)S(1)}, u32[]{:S(2)}, u32[]{:S(2)}) collective-permute-start(s16[64,4224]{1,0:T(8,128)(2,1)S(1)} %get-tuple-element.53), channel_id=1, source_target_pairs={{0,8},{8,0},{16,24},{24,16},{1,9},{9,1},{17,25},{25,17},{2,10},{10... | collective-permute-start | bytes 1622024 | tf_op jit(solution)/shard_map/ppermute | solution.py:465
  41.9 14.6 %collective-permute-start.6 = (s16[64,4224]{1,0:T(8,128)(2,1)S(1)}, s16[64,4224]{1,0:T(8,128)(2,1)S(1)}, u32[]{:S(2)}, u32[]{:S(2)}) collective-permute-start(s16[64,4224]{1,0:T(8,128)(2,1)S(1)} %get-tuple-element.54), channel_id=1, source_target_pairs={{0,16},{8,24},{16,0},{24,8},{1,17},{9,25},{17,1},{25,9},{2,18},{10... | collective-permute-start | bytes 1622024 | tf_op jit(solution)/shard_map/ppermute | solution.py:465
  55.3 10.3 %copy-start.5 = (s16[64,4224]{1,0:T(8,128)(2,1)}, s16[64,4224]{1,0:T(8,128)(2,1)S(1)}, u32[]{:S(2)}) copy-start(s16[64,4224]{1,0:T(8,128)(2,1)S(1)} %get-tuple-element.60) | copy-start | bytes 1622020
  55.3 14.9 %copy-start.8 = (s32[128,16]{0,1:T(8,128)S(1)}, s32[128,16]{0,1:T(8,128)}, u32[]{:S(2)}) copy-start(s32[128,16]{0,1:T(8,128)} %param.9) | copy-start | bytes 24580
  55.3 29.3 %copy-start.9 = (s32[128]{0:T(128)S(1)}, s32[128]{0:T(128)}, u32[]{:S(2)}) copy-start(s32[128]{0:T(128)} %param.10) | copy-start | bytes 1540
  55.3 29.4 %copy-start.10 = (f32[128]{0:T(128)S(1)}, f32[128]{0:T(128)}, u32[]{:S(2)}) copy-start(f32[128]{0:T(128)} %param.11) | copy-start | bytes 1540
  55.3 16.1 %collective-permute-start.11 = (s16[64,4224]{1,0:T(8,128)(2,1)S(1)}, s16[64,4224]{1,0:T(8,128)(2,1)S(1)}, u32[]{:S(2)}, u32[]{:S(2)}) collective-permute-start(s16[64,4224]{1,0:T(8,128)(2,1)S(1)} %get-tuple-element.63), channel_id=1, source_target_pairs={{0,8},{8,0},{16,24},{24,16},{1,9},{9,1},{17,25},{25,17},{2,10},{10... | collective-permute-start | bytes 1622024 | tf_op jit(solution)/shard_map/ppermute | solution.py:465
  65.6 0.8 copy-start.6
  66.4 0.8 copy-start.7
  67.2 15.4 %collective-permute-start.12 = (s16[64,4224]{1,0:T(8,128)(2,1)}, s16[64,4224]{1,0:T(8,128)(2,1)S(1)}, u32[]{:S(2)}, u32[]{:S(2)}) collective-permute-start(s16[64,4224]{1,0:T(8,128)(2,1)} %get-tuple-element.55), channel_id=1, source_target_pairs={{0,8},{8,0},{16,24},{24,16},{1,9},{9,1},{17,25},{25,17},{2,10},{10... | collective-permute-start | bytes 1622024 | tf_op jit(solution)/shard_map/ppermute | solution.py:465
  68.1 15.9 %collective-permute-start.13 = (s16[64,4224]{1,0:T(8,128)(2,1)}, s16[64,4224]{1,0:T(8,128)(2,1)S(1)}, u32[]{:S(2)}, u32[]{:S(2)}) collective-permute-start(s16[64,4224]{1,0:T(8,128)(2,1)} %get-tuple-element.64), channel_id=1, source_target_pairs={{0,16},{8,24},{16,0},{24,8},{1,17},{9,25},{17,1},{25,9},{2,18},{10... | collective-permute-start | bytes 1622024 | tf_op jit(solution)/shard_map/ppermute | solution.py:465
  69.1 26.0 %collective-permute-start.14 = (s16[64,4224]{1,0:T(8,128)(2,1)}, s16[64,4224]{1,0:T(8,128)(2,1)S(1)}, u32[]{:S(2)}, u32[]{:S(2)}) collective-permute-start(s16[64,4224]{1,0:T(8,128)(2,1)} %get-tuple-element.65), channel_id=1, source_target_pairs={{0,16},{8,24},{16,0},{24,8},{1,17},{9,25},{17,1},{25,9},{2,18},{10... | collective-permute-start | bytes 1622024 | tf_op jit(solution)/shard_map/ppermute | solution.py:465
  70.3 50.7 %collective-permute-start.7 = (s16[64,4224]{1,0:T(8,128)(2,1)}, s16[64,4224]{1,0:T(8,128)(2,1)S(1)}, u32[]{:S(2)}, u32[]{:S(2)}) collective-permute-start(s16[64,4224]{1,0:T(8,128)(2,1)} %get-tuple-element.56), channel_id=1, source_target_pairs={{0,8},{8,0},{16,24},{24,16},{1,9},{9,1},{17,25},{25,17},{2,10},{10... | collective-permute-start | bytes 1622024 | tf_op jit(solution)/shard_map/ppermute | solution.py:465
  71.4 51.1 %collective-permute-start.8 = (s16[64,4224]{1,0:T(8,128)(2,1)}, s16[64,4224]{1,0:T(8,128)(2,1)S(1)}, u32[]{:S(2)}, u32[]{:S(2)}) collective-permute-start(s16[64,4224]{1,0:T(8,128)(2,1)} %copy-done.7), channel_id=1, source_target_pairs={{0,8},{8,0},{16,24},{24,16},{1,9},{9,1},{17,25},{25,17},{2,10},{10... | collective-permute-start | bytes 1622024 | tf_op jit(solution)/shard_map/ppermute | solution.py:465
  82.6 39.9 %collective-permute-start.9 = (s16[64,4224]{1,0:T(8,128)(2,1)}, s16[64,4224]{1,0:T(8,128)(2,1)}, u32[]{:S(2)}, u32[]{:S(2)}) collective-permute-start(s16[64,4224]{1,0:T(8,128)(2,1)} %copy-done.5), channel_id=1, source_target_pairs={{0,16},{8,24},{16,0},{24,8},{1,17},{9,25},{17,1},{25,9},{2,18},{10... | collective-permute-start | bytes 1622024 | tf_op jit(solution)/shard_map/ppermute | solution.py:465
  84.0 38.5 %collective-permute-start.10 = (s16[64,4224]{1,0:T(8,128)(2,1)}, s16[64,4224]{1,0:T(8,128)(2,1)}, u32[]{:S(2)}, u32[]{:S(2)}) collective-permute-start(s16[64,4224]{1,0:T(8,128)(2,1)} %copy-done.6), channel_id=1, source_target_pairs={{0,16},{8,24},{16,0},{24,8},{1,17},{9,25},{17,1},{25,9},{2,18},{10... | collective-permute-start | bytes 1622024 | tf_op jit(solution)/shard_map/ppermute | solution.py:465
  95.2 2.2 copy-start.3
  97.3 25.2 %copy-start.4 = (f32[128,8192]{1,0:T(8,128)S(1)}, f32[128,8192]{1,0:T(8,128)}, u32[]{:S(2)}) copy-start(f32[128,8192]{1,0:T(8,128)} %copy-done.2) | copy-start | bytes 12582916
  120.0 26.3 %collective-permute-start.15 = (bf16[64,8320]{1,0:T(8,128)(2,1)S(1)}, bf16[64,8320]{1,0:T(8,128)(2,1)S(1)}, u32[]{:S(2)}, u32[]{:S(2)}) collective-permute-start(bf16[64,8320]{1,0:T(8,128)(2,1)S(1)} %get-tuple-element.75), channel_id=1, source_target_pairs={{0,16},{8,24},{16,0},{24,8},{1,17},{9,25},{17,1},{25,9},{2,18},{10... | collective-permute-start | bytes 3194888 | tf_op jit(solution)/shard_map/ppermute | solution.py:465
  121.0 26.1 %collective-permute-start.17 = (bf16[64,8320]{1,0:T(8,128)(2,1)S(1)}, bf16[64,8320]{1,0:T(8,128)(2,1)S(1)}, u32[]{:S(2)}, u32[]{:S(2)}) collective-permute-start(bf16[64,8320]{1,0:T(8,128)(2,1)S(1)} %get-tuple-element.75), channel_id=1, source_target_pairs={{0,8},{8,0},{16,24},{24,16},{1,9},{9,1},{17,25},{25,17},{2,10},{10... | collective-permute-start | bytes 3194888 | tf_op jit(solution)/shard_map/ppermute | solution.py:465
  146.3 14.4 %collective-permute-start.16 = (bf16[32,8320]{1,0:T(8,128)(2,1)S(1)}, bf16[32,8320]{1,0:T(8,128)(2,1)S(1)}, u32[]{:S(2)}, u32[]{:S(2)}) collective-permute-start(bf16[32,8320]{1,0:T(8,128)(2,1)S(1)} %slice.33), channel_id=1, source_target_pairs={{0,8},{8,0},{16,24},{24,16},{1,9},{9,1},{17,25},{25,17},{2,10},{10... | collective-permute-start | bytes 1597448 | tf_op jit(solution)/shard_map/ppermute | solution.py:465
  147.2 13.9 %collective-permute-start.18 = (bf16[32,8320]{1,0:T(8,128)(2,1)S(1)}, bf16[32,8320]{1,0:T(8,128)(2,1)S(1)}, u32[]{:S(2)}, u32[]{:S(2)}) collective-permute-start(bf16[32,8320]{1,0:T(8,128)(2,1)S(1)} %slice.34), channel_id=1, source_target_pairs={{0,16},{8,24},{16,0},{24,8},{1,17},{9,25},{17,1},{25,9},{2,18},{10... | collective-permute-start | bytes 1597448 | tf_op jit(solution)/shard_map/ppermute | solution.py:465
  161.1 24.6 %collective-permute-start.19 = (bf16[64,8320]{1,0:T(8,128)(2,1)S(1)}, bf16[64,8320]{1,0:T(8,128)(2,1)S(1)}, u32[]{:S(2)}, u32[]{:S(2)}) collective-permute-start(bf16[64,8320]{1,0:T(8,128)(2,1)S(1)} %get-tuple-element.79), channel_id=1, source_target_pairs={{0,16},{8,24},{16,0},{24,8},{1,17},{9,25},{17,1},{25,9},{2,18},{10... | collective-permute-start | bytes 3194888 | tf_op jit(solution)/shard_map/ppermute | solution.py:465
  162.1 24.0 %collective-permute-start.20 = (bf16[64,8320]{1,0:T(8,128)(2,1)S(1)}, bf16[64,8320]{1,0:T(8,128)(2,1)S(1)}, u32[]{:S(2)}, u32[]{:S(2)}) collective-permute-start(bf16[64,8320]{1,0:T(8,128)(2,1)S(1)} %get-tuple-element.79), channel_id=1, source_target_pairs={{0,8},{8,0},{16,24},{24,16},{1,9},{9,1},{17,25},{25,17},{2,10},{10... | collective-permute-start | bytes 3194888 | tf_op jit(solution)/shard_map/ppermute | solution.py:465
  173.5 15.5 %collective-permute-start.21 = (s16[256,1152]{1,0:T(8,128)(2,1)S(1)}, s16[256,1152]{1,0:T(8,128)(2,1)S(1)}, u32[]{:S(2)}, u32[]{:S(2)}) collective-permute-start(s16[256,1152]{1,0:T(8,128)(2,1)S(1)} %grad_rows.4), channel_id=1, source_target_pairs={{0,1},{1,0},{2,3},{3,2},{4,5},{5,4},{6,7},{7,6},{8,9},{9,8},{10,11... | collective-permute-start | bytes 1769480 | tf_op jit(solution)/shard_map/ppermute | solution.py:534
  186.2 17.1 %collective-permute-start.26 = (bf16[32,8320]{1,0:T(8,128)(2,1)S(1)}, bf16[32,8320]{1,0:T(8,128)(2,1)S(1)}, u32[]{:S(2)}, u32[]{:S(2)}) collective-permute-start(bf16[32,8320]{1,0:T(8,128)(2,1)S(1)} %slice.35), channel_id=1, source_target_pairs={{0,8},{8,0},{16,24},{24,16},{1,9},{9,1},{17,25},{25,17},{2,10},{10... | collective-permute-start | bytes 1597448 | tf_op jit(solution)/shard_map/ppermute | solution.py:465
  187.8 15.6 %collective-permute-start.27 = (bf16[32,8320]{1,0:T(8,128)(2,1)S(1)}, bf16[32,8320]{1,0:T(8,128)(2,1)S(1)}, u32[]{:S(2)}, u32[]{:S(2)}) collective-permute-start(bf16[32,8320]{1,0:T(8,128)(2,1)S(1)} %slice.36), channel_id=1, source_target_pairs={{0,16},{8,24},{16,0},{24,8},{1,17},{9,25},{17,1},{25,9},{2,18},{10... | collective-permute-start | bytes 1597448 | tf_op jit(solution)/shard_map/ppermute | solution.py:465
  190.1 6.0 %collective-permute-start.22 = (s16[64,1152]{1,0:T(8,128)(2,1)S(1)}, s16[64,1152]{1,0:T(8,128)(2,1)S(1)}, u32[]{:S(2)}, u32[]{:S(2)}) collective-permute-start(s16[64,1152]{1,0:T(8,128)(2,1)S(1)} %get-tuple-element.85), channel_id=1, source_target_pairs={{0,2},{1,3},{2,0},{3,1},{4,6},{5,7},{6,4},{7,5},{8,10},{9,11},{10,... | collective-permute-start | bytes 442376 | tf_op jit(solution)/shard_map/ppermute | solution.py:541
  191.6 11.7 %collective-permute-start.23 = (s16[64,1152]{1,0:T(8,128)(2,1)S(1)}, s16[64,1152]{1,0:T(8,128)(2,1)S(1)}, u32[]{:S(2)}, u32[]{:S(2)}) collective-permute-start(s16[64,1152]{1,0:T(8,128)(2,1)S(1)} %get-tuple-element.86), channel_id=1, source_target_pairs={{0,4},{1,5},{2,6},{3,7},{4,0},{5,1},{6,2},{7,3},{8,12},{9,13},{10,... | collective-permute-start | bytes 442376 | tf_op jit(solution)/shard_map/ppermute | solution.py:541
  194.0 9.3 %collective-permute-start.24 = (s16[64,1152]{1,0:T(8,128)(2,1)S(1)}, s16[64,1152]{1,0:T(8,128)(2,1)S(1)}, u32[]{:S(2)}, u32[]{:S(2)}) collective-permute-start(s16[64,1152]{1,0:T(8,128)(2,1)S(1)} %get-tuple-element.87), channel_id=1, source_target_pairs={{0,6},{1,7},{2,4},{3,5},{4,2},{5,3},{6,0},{7,1},{8,14},{9,15},{10,... | collective-permute-start | bytes 442376 | tf_op jit(solution)/shard_map/ppermute | solution.py:541
  203.5 10.7 %copy-start = (bf16[256,8320]{1,0:T(8,128)(2,1)}, bf16[256,8320]{1,0:T(8,128)(2,1)S(1)}, u32[]{:S(2)}) copy-start(bf16[256,8320]{1,0:T(8,128)(2,1)S(1)} %constant_dynamic-update-slice_fusion.5.grad_ref.beside_ref) | copy-start | bytes 12779524
  214.2 16.4 %collective-permute-start.28 = (s16[256,1152]{1,0:T(8,128)(2,1)S(1)}, s16[256,1152]{1,0:T(8,128)(2,1)S(1)}, u32[]{:S(2)}, u32[]{:S(2)}) collective-permute-start(s16[256,1152]{1,0:T(8,128)(2,1)S(1)} %grad_rows.6), channel_id=1, source_target_pairs={{0,1},{1,0},{2,3},{3,2},{4,5},{5,4},{6,7},{7,6},{8,9},{9,8},{10,11... | collective-permute-start | bytes 1769480 | tf_op jit(solution)/shard_map/ppermute | solution.py:534
  214.7 36.8 %collective-permute-start.25 = (s16[64,1152]{1,0:T(8,128)(2,1)S(1)}, s16[64,1152]{1,0:T(8,128)(2,1)S(1)}, u32[]{:S(2)}, u32[]{:S(2)}) collective-permute-start(s16[64,1152]{1,0:T(8,128)(2,1)S(1)} %last_sum.2), channel_id=1, source_target_pairs={{0,0},{1,1},{2,8},{3,9},{4,16},{5,17},{6,24},{7,25},{8,2},{9,3},{1... | collective-permute-start | bytes 442376 | tf_op jit(solution)/shard_map/ppermute | solution.py:552
  218.6 2.2 copy-start.1
  220.8 40.4 %dynamic-slice-start = ((f32[8192]{0:T(1024)}, s32[]{:T(128)}), f32[1024]{0:T(1024)S(1)}, s32[]{:S(2)}) async-start(f32[8192]{0:T(1024)} %param.8, s32[]{:T(128)} %select_n.37), calls=%async_computation | async-start | bytes 8704 | tf_op jit(solution)/shard_map/dynamic_slice | solution.py:562
  231.7 8.8 %collective-permute-start.29 = (s16[64,1152]{1,0:T(8,128)(2,1)S(1)}, s16[64,1152]{1,0:T(8,128)(2,1)S(1)}, u32[]{:S(2)}, u32[]{:S(2)}) collective-permute-start(s16[64,1152]{1,0:T(8,128)(2,1)S(1)} %get-tuple-element.91), channel_id=1, source_target_pairs={{0,2},{1,3},{2,0},{3,1},{4,6},{5,7},{6,4},{7,5},{8,10},{9,11},{10,... | collective-permute-start | bytes 442376 | tf_op jit(solution)/shard_map/ppermute | solution.py:541
  231.7 14.3 %collective-permute-start.30 = (s16[64,1152]{1,0:T(8,128)(2,1)S(1)}, s16[64,1152]{1,0:T(8,128)(2,1)S(1)}, u32[]{:S(2)}, u32[]{:S(2)}) collective-permute-start(s16[64,1152]{1,0:T(8,128)(2,1)S(1)} %get-tuple-element.92), channel_id=1, source_target_pairs={{0,4},{1,5},{2,6},{3,7},{4,0},{5,1},{6,2},{7,3},{8,12},{9,13},{10,... | collective-permute-start | bytes 442376 | tf_op jit(solution)/shard_map/ppermute | solution.py:541
  235.0 11.0 %collective-permute-start.31 = (s16[64,1152]{1,0:T(8,128)(2,1)S(1)}, s16[64,1152]{1,0:T(8,128)(2,1)S(1)}, u32[]{:S(2)}, u32[]{:S(2)}) collective-permute-start(s16[64,1152]{1,0:T(8,128)(2,1)S(1)} %get-tuple-element.93), channel_id=1, source_target_pairs={{0,6},{1,7},{2,4},{3,5},{4,2},{5,3},{6,0},{7,1},{8,14},{9,15},{10,... | collective-permute-start | bytes 442376 | tf_op jit(solution)/shard_map/ppermute | solution.py:541
  246.3 14.7 %collective-permute-start.32 = (s16[64,1152]{1,0:T(8,128)(2,1)S(1)}, s16[64,1152]{1,0:T(8,128)(2,1)S(1)}, u32[]{:S(2)}, u32[]{:S(2)}) collective-permute-start(s16[64,1152]{1,0:T(8,128)(2,1)S(1)} %last_sum.3), channel_id=1, source_target_pairs={{0,0},{1,1},{2,8},{3,9},{4,16},{5,17},{6,24},{7,25},{8,2},{9,3},{1... | collective-permute-start | bytes 442376 | tf_op jit(solution)/shard_map/ppermute | solution.py:552
